TPU v7x, 32 devices: a whole 2x2x4 slice. The times are simulated.
32 devices in a mesh: row: 8 (over z, x), col: 2 (over core), rep: 2 (over y).
Axes of the slice: x: 2, y: 2, z: 4, core: 2. Of those that a mesh axis runs over, the one named last changes fastest.
Arguments:
- left_values: float32 [8, 2, 2, 3, 8, 2, 128, 128], P('row', 'rep', 'col'), may hold values from -0.5 to 0.5
- left_rows: int32 [8, 2, 2, 3, 8, 2], P('row', 'rep', 'col'), may hold values from 0 to 3, as said below
- right_values: float32 [2, 8, 2, 8, 4, 128, 128], P('rep', 'row', 'col'), may hold values from -1.5 to 1.5
- right_cols: int32 [2, 8, 2, 8, 4], P('rep', 'row', 'col'), may hold values from 0 to 7
- result_slots: int32 [8, 2, 24], P('row', 'col'), may hold values from 0 to 31, as said below
Outputs:
- result_blocks: float32 [8, 2, 24, 128, 128], P('row', 'col', 'rep')
Inputs may be any that keep to these rules, and one draw needn't show every extreme that they name: `result_slots`: within one result tile the 24 slots are distinct; slot value p stands for the block at block row p // 8 and block column p % 8 of the tile. `left_rows`: the 2 block rows of one block column of a panel are distinct.
All inputs are finite; a program needn't handle non-finite values.
Results may differ from a plain program's by a relative error of at most 0.0003.
Values sent between devices are 32-bit elements; how exact they have to be, the bound alone decides.
No kernel may reach another device: no remote copies, remote signals or barrier semaphores. Data moves between devices by JAX's collectives and lax.ppermute only.
A program may use at most 64 MiB of HBM per device.

v0:
```python
import jax
import jax.numpy as jnp
from jax import lax
from jax.sharding import PartitionSpec as P

STEPS = 4
CB = 8


highest = lax.Precision.HIGHEST


def from_behind(x, axis, by):
    peers = lax.axis_size(axis)
    return lax.ppermute(x, axis, [(i, (i + by) % peers) for i in range(peers)])


def turn_products(left_blocks, left_places, right_blocks, right_places, listed):
    products = jnp.einsum("kaxy,kbyz->kabxz", left_blocks, right_blocks, precision=highest)
    block_codes = left_places[:, :, None] * CB + right_places[:, None, :]
    onehot = (block_codes[:, :, :, None] == listed[None, None, None, :]).astype(jnp.float32)
    return jnp.einsum("kabc,kabxz->cxz", onehot, products, precision=highest)


def shards(left_values, left_rows, right_values, right_cols, result_slots):
    column_count = lax.axis_size("col")
    column_at = lax.axis_index("col")
    panels = left_values[0, 0, 0]
    panel_rows = left_rows[0, 0, 0]
    right_first = right_values[0, 0, 0]
    right_first_cols = right_cols[0, 0, 0]
    listed = result_slots[0, 0]
    totals = jnp.zeros((listed.shape[0], panels.shape[-2], panels.shape[-1]), jnp.float32)
    held_values = panels
    held_rows = panel_rows
    right_blocks = right_first
    right_places = right_first_cols
    for turn_index in range(STEPS):
        if turn_index > 0:
            held_values, held_rows = from_behind((held_values, held_rows), "col", -1)
        slot_index = (column_at + turn_index) // column_count
        left_blocks = lax.dynamic_index_in_dim(held_values, slot_index, 0, keepdims=False)
        left_places = lax.dynamic_index_in_dim(held_rows, slot_index, 0, keepdims=False)
        if turn_index > 0:
            right_blocks, right_places = from_behind((right_blocks, right_places), "row", -1)
        totals = totals + turn_products(
            left_blocks, left_places, right_blocks, right_places, listed
        )
    shares = lax.psum_scatter(totals, "rep", scatter_dimension=0, tiled=True)
    return shares[None, None]


def solution(mesh):
    in_specs = (
        P("row", "rep", "col", None, None, None, None, None),
        P("row", "rep", "col", None, None, None),
        P("rep", "row", "col", None, None, None, None),
        P("rep", "row", "col", None, None),
        P("row", "col", None),
    )
    out_specs = P("row", "col", "rep", None, None)
    return jax.shard_map(shards, mesh=mesh, in_specs=in_specs, out_specs=out_specs, check_vma=False)
```

profile of v0, /device:TPU:0, one launch (start us, length us, event | category | flops | bytes accessed | tf_op | source)
XLA Modules:
  0.0 221.8 jit_solution(7221704601129321231)
XLA Ops:
  6.5 0.0 reduce-scatter.2.cloned.1.call-start
  6.5 0.5 collective-permute-start.2
  7.0 5.6 %collective-permute-done.2 = f32[3,8,2,128,128]{4,3,2,1,0:T(8,128)} collective-permute-done((f32[3,8,2,128,128]{4,3,2,1,0:T(8,128)}, f32[3,8,2,128,128]{4,3,2,1,0:T(8,128)}, u32[]{:S(2)}, u32[]{:S(2)}) %collective-permute-start.2) | collective-permute-done | bytes 3145760 | tf_op jit(solution)/shard_map/ppermute | solution.py:15
  12.6 0.4 collective-permute-start.6
  13.0 5.7 %collective-permute-start.3 = (f32[8,4,128,128]{3,2,1,0:T(8,128)}, f32[8,4,128,128]{3,2,1,0:T(8,128)}, u32[]{:S(2)}, u32[]{:S(2)}) collective-permute-start(f32[8,4,128,128]{3,2,1,0:T(8,128)} %bitcast.112), channel_id=1, source_target_pairs={{0,28},{4,0},{8,4},{12,8},{16,12},{20,16},{24,20},{28,24},{1,29},{... | collective-permute-start | bytes 6291464 | tf_op jit(solution)/shard_map/ppermute | solution.py:15
  18.7 45.7 %collective-permute-done.3 = f32[8,4,128,128]{3,2,1,0:T(8,128)} collective-permute-done((f32[8,4,128,128]{3,2,1,0:T(8,128)}, f32[8,4,128,128]{3,2,1,0:T(8,128)}, u32[]{:S(2)}, u32[]{:S(2)}) %collective-permute-start.3) | collective-permute-done | bytes 2097184 | tf_op jit(solution)/shard_map/ppermute | solution.py:15
  64.4 5.2 %collective-permute-start.7 = (f32[8,4,128,128]{3,2,1,0:T(8,128)}, f32[8,4,128,128]{3,2,1,0:T(8,128)S(1)}, u32[]{:S(2)}, u32[]{:S(2)}) collective-permute-start(f32[8,4,128,128]{3,2,1,0:T(8,128)} %collective-permute-done.3), channel_id=1, source_target_pairs={{0,28},{4,0},{8,4},{12,8},{16,12},{20,16},{24,20},{28,24},{1,29},{... | collective-permute-start | bytes 6291464 | tf_op jit(solution)/shard_map/ppermute | solution.py:15
  69.6 0.0 collective-permute-start.1
  69.6 0.0 collective-permute-start
  69.6 0.0 collective-permute-done.6
  69.6 0.5 collective-permute-start.10
  70.1 0.7 fusion.43
  70.8 0.7 broadcast_add_fusion.3
  71.5 7.4 %convolution_bitcast_fusion.3 = f32[8,2,4,128,128]{4,3,2,1,0:T(8,128)} fusion(f32[1,1,1,8,4,128,128]{6,5,4,3,2,1,0:T(8,128)} %param.7, f32[1,1,1,3,8,2,128,128]{7,6,5,4,3,2,1,0:T(8,128)} %param.5, s32[]{:T(128)S(6)} %select_n.33), kind=kOutput, calls=%fused_computation.11 | convolution fusion | flops 1610612736 | bytes 7340036 | tf_op jit(solution)/shard_map/kaxy,kbyz->kabxz/dot_general | solution.py:19
  78.9 35.6 %collective-permute-done.1 = s32[8,4]{0,1:T(4,128)S(1)} collective-permute-done((s32[8,4]{0,1:T(4,128)}, s32[8,4]{0,1:T(4,128)S(1)}, u32[]{:S(2)}, u32[]{:S(2)}) %collective-permute-start.1) | collective-permute-done | bytes 160 | tf_op jit(solution)/shard_map/ppermute | solution.py:15
  114.5 5.1 %collective-permute-start.5 = (s32[8,4]{0,1:T(4,128)S(1)}, s32[8,4]{0,1:T(4,128)S(1)}, u32[]{:S(2)}, u32[]{:S(2)}) collective-permute-start(s32[8,4]{0,1:T(4,128)S(1)} %collective-permute-done.1), channel_id=1, source_target_pairs={{0,28},{4,0},{8,4},{12,8},{16,12},{20,16},{24,20},{28,24},{1,29},{... | collective-permute-start | bytes 392 | tf_op jit(solution)/shard_map/ppermute | solution.py:15
  119.6 0.0 collective-permute-done
  119.6 0.0 collective-permute-start.4
  119.6 1.3 collective-permute-done.5
  120.9 5.0 %collective-permute-start.9 = (s32[8,4]{0,1:T(4,128)S(1)}, s32[8,4]{0,1:T(4,128)S(1)}, u32[]{:S(2)}, u32[]{:S(2)}) collective-permute-start(s32[8,4]{0,1:T(4,128)S(1)} %collective-permute-done.5), channel_id=1, source_target_pairs={{0,28},{4,0},{8,4},{12,8},{16,12},{20,16},{24,20},{28,24},{1,29},{... | collective-permute-start | bytes 392 | tf_op jit(solution)/shard_map/ppermute | solution.py:15
  125.9 0.0 collective-permute-done.4
  125.9 0.0 collective-permute-start.8
  125.9 0.0 collective-permute-done.7
  125.9 0.2 collective-permute-start.11
  126.2 0.9 collective-permute-done.8
  127.1 0.1 collective-permute-done.9
  127.2 0.0 copy-start.1
  127.2 5.7 %convolution_bitcast_fusion.2 = f32[8,2,4,128,128]{4,3,2,1,0:T(8,128)S(1)} fusion(f32[8,4,128,128]{3,2,1,0:T(8,128)} %collective-permute-done.3, f32[3,8,2,128,128]{4,3,2,1,0:T(8,128)} %collective-permute-done.2, s32[]{:T(128)S(6)} %select_n.35), kind=kOutput, calls=%fused_computation.10 | convolution fusion | flops 1610612736 | bytes 7340036 | tf_op jit(solution)/shard_map/kaxy,kbyz->kabxz/dot_general | solution.py:19
  132.9 0.0 copy-done.1
  132.9 4.0 %fusion.4 = f32[24,128,128,1,1]{2,0,4,1,3:T(8,128)S(1)} fusion(f32[8,2,4,128,128]{4,3,2,1,0:T(8,128)S(1)} %convolution_bitcast_fusion.2, s32[8,2,4]{0,2,1:T(4,128)S(1)} %broadcast_add_fusion.2, s32[24]{0:T(128)S(1)} %bitcast.114), kind=kOutput, calls=%fused_computation.4 | convolution fusion | flops 301991424 | bytes 5767520 | tf_op jit(solution)/shard_map/kabc,kabxz->cxz/dot_general | solution.py:22
  136.9 5.0 %convolution_bitcast_fusion.1 = f32[8,2,4,128,128]{4,3,2,1,0:T(8,128)S(1)} fusion(f32[8,4,128,128]{3,2,1,0:T(8,128)S(1)} %collective-permute-done.7, f32[3,8,2,128,128]{4,3,2,1,0:T(8,128)} %collective-permute-done.6, s32[]{:T(128)S(6)} %select_n.37), kind=kOutput, calls=%fused_computation.9 | convolution fusion | flops 1610612736 | bytes 7340036 | tf_op jit(solution)/shard_map/kaxy,kbyz->kabxz/dot_general | solution.py:19
  141.9 4.2 %fusion.2 = f32[24,128,128,1,1]{2,0,4,1,3:T(8,128)S(1)} fusion(f32[8,2,4,128,128]{4,3,2,1,0:T(8,128)S(1)} %convolution_bitcast_fusion.1, s32[8,2,4]{0,2,1:T(4,128)S(1)} %broadcast_add_fusion.1, s32[24]{0:T(128)S(1)} %bitcast.115), kind=kOutput, calls=%fused_computation.2 | convolution fusion | flops 301991424 | bytes 5767520 | tf_op jit(solution)/shard_map/kabc,kabxz->cxz/dot_general | solution.py:22
  146.2 27.8 %collective-permute-done.11 = f32[8,4,128,128]{3,2,1,0:T(8,128)S(1)} collective-permute-done((f32[8,4,128,128]{3,2,1,0:T(8,128)S(1)}, f32[8,4,128,128]{3,2,1,0:T(8,128)S(1)}, u32[]{:S(2)}, u32[]{:S(2)}) %collective-permute-start.11) | collective-permute-done | bytes 2097184 | tf_op jit(solution)/shard_map/ppermute | solution.py:15
  174.0 0.0 collective-permute-done.10
  174.0 5.0 %convolution_bitcast_fusion = f32[8,2,4,128,128]{4,3,2,1,0:T(8,128)S(1)} fusion(f32[8,4,128,128]{3,2,1,0:T(8,128)S(1)} %collective-permute-done.11, f32[3,8,2,128,128]{4,3,2,1,0:T(8,128)} %collective-permute-done.10, s32[]{:T(128)S(6)} %select_n.39), kind=kOutput, calls=%fused_computation.8 | convolution fusion | flops 1610612736 | bytes 7340036 | tf_op jit(solution)/shard_map/kaxy,kbyz->kabxz/dot_general | solution.py:19
  178.9 0.0 copy-start
  178.9 4.0 %fusion = f32[24,128,128,1,1]{2,0,4,1,3:T(8,128)S(1)} fusion(f32[8,2,4,128,128]{4,3,2,1,0:T(8,128)S(1)} %convolution_bitcast_fusion, s32[8,2,4]{0,2,1:T(4,128)S(1)} %broadcast_add_fusion, s32[24]{0:T(128)S(1)} %bitcast.116), kind=kOutput, calls=%fused_computation | convolution fusion | flops 301991424 | bytes 5767520 | tf_op jit(solution)/shard_map/kabc,kabxz->cxz/dot_general | solution.py:22
  183.0 0.0 copy-done
  183.0 4.6 %bitcast_add_fusion = f32[24,128,128]{2,0,1:T(8,128)S(1)} fusion(f32[24,128,128,1,1]{2,0,4,1,3:T(8,128)S(1)} %fusion, f32[24,128,128,1,1]{2,0,4,1,3:T(8,128)S(1)} %fusion.2, f32[24,128,128,1,1]{2,0,4,1,3:T(8,128)S(1)} %fusion.4, f32[8,2,4,128,128]{4,3,2,1,0:T(8,128)S(1)} %copy-done, s32[24]{0:T(128)S(1)} %bitcast.117, s32[8,2,4]{0,2,1:T(4,128)S(1)} %broadcast_add_fusion.3), kind=kOutput, calls=%fused_computation.16 | convolution fusion | flops 303171072 | bytes 10486112 | tf_op jit(solution)/shard_map/kabc,kabxz->cxz/dot_general | solution.py:22
  187.6 1.5 copy.7
  189.0 0.0 reduce-scatter.2.cloned.1.call-update
  189.0 26.0 %reduce-scatter.2.cloned.1.call-done = f32[12,128,128]{2,1,0:T(8,128)} async-done(((f32[24,128,128]{2,1,0:T(8,128)}), f32[12,128,128]{2,1,0:T(8,128)}) %reduce-scatter.2.cloned.1.call-update) | async-done | bytes 786448 | tf_op jit(solution)/shard_map/reduce_scatter | solution.py:49
  (6 shorter events, 0.0 us)
Async XLA Ops:
  6.5 208.5 %reduce-scatter.2.cloned.1.call-start = ((), (), s32[]{:S(2)}) async-start(), calls=%async_computation.1 | async-start | bytes 2359296 | tf_op jit(solution)/shard_map/reduce_scatter | solution.py:49
  6.5 6.1 %collective-permute-start.2 = (f32[3,8,2,128,128]{4,3,2,1,0:T(8,128)}, f32[3,8,2,128,128]{4,3,2,1,0:T(8,128)}, u32[]{:S(2)}, u32[]{:S(2)}) collective-permute-start(f32[3,8,2,128,128]{4,3,2,1,0:T(8,128)} %bitcast.113), channel_id=1, source_target_pairs={{0,2},{2,0},{1,3},{3,1},{4,6},{6,4},{5,7},{7,5},{8,10},{10,8},{9,1... | collective-permute-start | bytes 9437192 | tf_op jit(solution)/shard_map/ppermute | solution.py:15
  12.6 57.0 %collective-permute-start.6 = (f32[3,8,2,128,128]{4,3,2,1,0:T(8,128)}, f32[3,8,2,128,128]{4,3,2,1,0:T(8,128)}, u32[]{:S(2)}, u32[]{:S(2)}) collective-permute-start(f32[3,8,2,128,128]{4,3,2,1,0:T(8,128)} %collective-permute-done.2), channel_id=1, source_target_pairs={{0,2},{2,0},{1,3},{3,1},{4,6},{6,4},{5,7},{7,5},{8,10},{10,8},{9,1... | collective-permute-start | bytes 9437192 | tf_op jit(solution)/shard_map/ppermute | solution.py:15
  13.0 51.4 %collective-permute-start.3 = (f32[8,4,128,128]{3,2,1,0:T(8,128)}, f32[8,4,128,128]{3,2,1,0:T(8,128)}, u32[]{:S(2)}, u32[]{:S(2)}) collective-permute-start(f32[8,4,128,128]{3,2,1,0:T(8,128)} %bitcast.112), channel_id=1, source_target_pairs={{0,28},{4,0},{8,4},{12,8},{16,12},{20,16},{24,20},{28,24},{1,29},{... | collective-permute-start | bytes 6291464 | tf_op jit(solution)/shard_map/ppermute | solution.py:15
  64.4 61.5 %collective-permute-start.7 = (f32[8,4,128,128]{3,2,1,0:T(8,128)}, f32[8,4,128,128]{3,2,1,0:T(8,128)S(1)}, u32[]{:S(2)}, u32[]{:S(2)}) collective-permute-start(f32[8,4,128,128]{3,2,1,0:T(8,128)} %collective-permute-done.3), channel_id=1, source_target_pairs={{0,28},{4,0},{8,4},{12,8},{16,12},{20,16},{24,20},{28,24},{1,29},{... | collective-permute-start | bytes 6291464 | tf_op jit(solution)/shard_map/ppermute | solution.py:15
  69.6 44.9 %collective-permute-start.1 = (s32[8,4]{0,1:T(4,128)}, s32[8,4]{0,1:T(4,128)S(1)}, u32[]{:S(2)}, u32[]{:S(2)}) collective-permute-start(s32[8,4]{0,1:T(4,128)} %bitcast.118), channel_id=1, source_target_pairs={{0,28},{4,0},{8,4},{12,8},{16,12},{20,16},{24,20},{28,24},{1,29},{... | collective-permute-start | bytes 392 | tf_op jit(solution)/shard_map/ppermute | solution.py:15
  69.6 50.0 %collective-permute-start = (s32[3,8,2]{1,2,0:T(2,128)}, s32[3,8,2]{1,2,0:T(2,128)S(1)}, u32[]{:S(2)}, u32[]{:S(2)}) collective-permute-start(s32[3,8,2]{1,2,0:T(2,128)} %bitcast.120), channel_id=1, source_target_pairs={{0,2},{2,0},{1,3},{3,1},{4,6},{6,4},{5,7},{7,5},{8,10},{10,8},{9,1... | collective-permute-start | bytes 584 | tf_op jit(solution)/shard_map/ppermute | solution.py:15
  69.6 104.3 %collective-permute-start.10 = (f32[3,8,2,128,128]{4,3,2,1,0:T(8,128)}, f32[3,8,2,128,128]{4,3,2,1,0:T(8,128)}, u32[]{:S(2)}, u32[]{:S(2)}) collective-permute-start(f32[3,8,2,128,128]{4,3,2,1,0:T(8,128)} %collective-permute-done.6), channel_id=1, source_target_pairs={{0,2},{2,0},{1,3},{3,1},{4,6},{6,4},{5,7},{7,5},{8,10},{10,8},{9,1... | collective-permute-start | bytes 9437192 | tf_op jit(solution)/shard_map/ppermute | solution.py:15
  114.5 6.4 %collective-permute-start.5 = (s32[8,4]{0,1:T(4,128)S(1)}, s32[8,4]{0,1:T(4,128)S(1)}, u32[]{:S(2)}, u32[]{:S(2)}) collective-permute-start(s32[8,4]{0,1:T(4,128)S(1)} %collective-permute-done.1), channel_id=1, source_target_pairs={{0,28},{4,0},{8,4},{12,8},{16,12},{20,16},{24,20},{28,24},{1,29},{... | collective-permute-start | bytes 392 | tf_op jit(solution)/shard_map/ppermute | solution.py:15
  119.6 6.3 %collective-permute-start.4 = (s32[3,8,2]{1,2,0:T(2,128)S(1)}, s32[3,8,2]{1,2,0:T(2,128)S(1)}, u32[]{:S(2)}, u32[]{:S(2)}) collective-permute-start(s32[3,8,2]{1,2,0:T(2,128)S(1)} %collective-permute-done), channel_id=1, source_target_pairs={{0,2},{2,0},{1,3},{3,1},{4,6},{6,4},{5,7},{7,5},{8,10},{10,8},{9,1... | collective-permute-start | bytes 584 | tf_op jit(solution)/shard_map/ppermute | solution.py:15
  120.9 6.3 %collective-permute-start.9 = (s32[8,4]{0,1:T(4,128)S(1)}, s32[8,4]{0,1:T(4,128)S(1)}, u32[]{:S(2)}, u32[]{:S(2)}) collective-permute-start(s32[8,4]{0,1:T(4,128)S(1)} %collective-permute-done.5), channel_id=1, source_target_pairs={{0,28},{4,0},{8,4},{12,8},{16,12},{20,16},{24,20},{28,24},{1,29},{... | collective-permute-start | bytes 392 | tf_op jit(solution)/shard_map/ppermute | solution.py:15
  125.9 1.2 collective-permute-start.8
  125.9 48.0 %collective-permute-start.11 = (f32[8,4,128,128]{3,2,1,0:T(8,128)S(1)}, f32[8,4,128,128]{3,2,1,0:T(8,128)S(1)}, u32[]{:S(2)}, u32[]{:S(2)}) collective-permute-start(f32[8,4,128,128]{3,2,1,0:T(8,128)S(1)} %collective-permute-done.7), channel_id=1, source_target_pairs={{0,28},{4,0},{8,4},{12,8},{16,12},{20,16},{24,20},{28,24},{1,29},{... | collective-permute-start | bytes 6291464 | tf_op jit(solution)/shard_map/ppermute | solution.py:15
  127.2 5.7 %copy-start.1 = (s32[1,1,24]{2,1,0:T(1,128)S(1)}, s32[1,1,24]{2,1,0:T(1,128)}, u32[]{:S(2)}) copy-start(s32[1,1,24]{2,1,0:T(1,128)} %param.9) | copy-start | bytes 292
  178.9 4.1 %copy-start = (f32[8,2,4,128,128]{4,3,2,1,0:T(8,128)S(1)}, f32[8,2,4,128,128]{4,3,2,1,0:T(8,128)}, u32[]{:S(2)}) copy-start(f32[8,2,4,128,128]{4,3,2,1,0:T(8,128)} %convolution_bitcast_fusion.3) | copy-start | bytes 12582916
Sparse Core Ops, SparseCore 0:
  189.2 25.7 reduce-scatter.1
where the time goes:
time: 222 us
  waiting for transfers between devices  143 us (64%)
  matrix products  39.9 us (18%)
  starting transfers between devices  22.5 us (10%)
  between operations  13.5 us (6%)
    ppermute x12, waiting for transfers between devices, from_behind(): return lax.ppermute(x, axis, [(i, (i + by) % peers) for i in range(peers)])  117 us
    reduce_scatter x1, waiting for transfers between devices, shards(): shares = lax.psum_scatter(totals, 'rep', scatter_dimension=0, tiled=True)  26 us
    dot_general x4, matrix products, turn_products(): jnp.einsum('kaxy,kbyz->kabxz', left_blocks, right_blocks, precision=highest)  23 us
    ppermute x12, starting transfers between devices, from_behind(): return lax.ppermute(x, axis, [(i, (i + by) % peers) for i in range(peers)])  22.5 us
    dot_general x4, matrix products, turn_products(): return jnp.einsum('kabc,kabxz->cxz', onehot, products, precision=highest)  16.9 us
  transfers between devices with their start and end apart: 13, of which 8 were waited for; matrix products, arithmetic and copies ran while one was open for 12% of the time, Pallas kernels for 0%

commit v1 on v0

v1 whole, which is shorter than its diff:
```python
import functools

import jax
import jax.numpy as jnp
from jax import lax
from jax.experimental import pallas as pl
from jax.experimental.pallas import tpu as pltpu
from jax.sharding import PartitionSpec as P

STEPS = 4
CB = 8
QUARTERS = 4

bf16 = jnp.bfloat16
f32 = jnp.float32

Z_EVEN = ((1, 2, 0), (1, 2, 1), (1, 2, 2), (1, 2, 3), (1, 3, 0), (0, 0, 0), (0, 0, 0))
Z_ODD = ((1, 2, 1), (1, 2, 2), (1, 2, 3), (1, 3, 0), (1, 3, 1), (1, 3, 2), (1, 3, 3))
X_EVEN = ((1, 1, 0), (1, 1, 1), (1, 1, 2), (1, 1, 3), (1, 3, 1), (1, 3, 2), (1, 3, 3))
X_ODD = ((0, 0, 0), (0, 0, 0), (1, 1, 0), (1, 1, 1), (1, 1, 2), (1, 1, 3), (1, 2, 0))
OWN = tuple((1, 0, q) for q in range(QUARTERS))
STAGES = len(Z_EVEN)


def split_panels(left_refs, out_ref):
    for turn, left_ref in enumerate(left_refs):
        block = left_ref[0].reshape(-1, left_ref.shape[-1])
        high = block.astype(bf16)
        low = (block - high.astype(f32)).astype(bf16)
        out_ref[turn, 0] = jnp.concatenate([high, low], axis=1)


def split_left(panels):
    kb, lpb, bs, _ = panels[0].shape
    turns = len(panels)

    def body(*refs):
        split_panels(refs[:-1], refs[-1])

    return pl.pallas_call(
        body,
        grid=(kb,),
        in_specs=[pl.BlockSpec((1, lpb, bs, bs), lambda k: (k, 0, 0, 0))] * turns,
        out_specs=pl.BlockSpec((turns, 1, lpb * bs, 2 * bs), lambda k: (0, k, 0, 0)),
        out_shape=jax.ShapeDtypeStruct((turns, kb, lpb * bs, 2 * bs), bf16),
        cost_estimate=pl.CostEstimate(flops=4 * turns * kb * lpb * bs * bs, bytes_accessed=8 * turns * kb * lpb * bs * bs, transcendentals=0),
        name="split_left",
    )(*panels)


def accumulate(places, picks, table, left_cat, chunks, totals, kb):
    rows_all, cols_all, slots, where_at = places
    count = len(chunks)
    nc = slots.shape[0]
    turns, _, lrows, lcat = left_cat.shape
    bs = lcat // 2
    lpb = lrows // bs
    per = kb // QUARTERS
    bpr = chunks[0][0].shape[1]
    first = totals is None

    def kernel(table_ref, rows_ref, cols_ref, slots_ref, at_ref, *refs):
        left_refs = refs[:count]
        right_refs = refs[count:2 * count]
        out_ref, place_ref = refs[-2:]
        if first:
            out_ref[...] = jnp.zeros_like(out_ref)
        else:
            out_ref[...] = refs[2 * count][...]
        row, rows_n, col, cols_n, slots_m, rep = (at_ref[n] for n in range(6))
        for code in range(CB * CB):
            place_ref[code] = nc
        half = nc // 2
        for n in range(nc):
            local = lax.rem(n + nc - half * rep, nc)
            place_ref[slots_ref[n]] = local
        for c, (_, _, pick) in enumerate(chunks):
            counts = table_ref[3 * pick]
            turn = table_ref[3 * pick + 1]
            quarter = table_ref[3 * pick + 2]

            def do(c=c, turn=turn, quarter=quarter):
                c_at = lax.rem(col + turn, cols_n)
                m_at = lax.div(col + turn, cols_n)
                rows_base = ((c_at * slots_m + m_at) * kb + quarter * per) * lpb
                cols_base = (lax.rem(row + turn, rows_n) * kb + quarter * per) * bpr
                for k in range(per):
                    cat = left_refs[c][0, k]
                    left3 = jnp.concatenate([cat, cat[:, :bs]], axis=1)
                    right = jnp.concatenate([right_refs[c][k, b] for b in range(bpr)], axis=1)
                    high = right.astype(bf16)
                    low = (right - high.astype(f32)).astype(bf16)
                    right3 = jnp.concatenate([high, high, low], axis=0)
                    out = jnp.dot(left3, right3, preferred_element_type=f32)
                    for a in range(lpb):
                        left_place = rows_ref[rows_base + k * lpb + a] * CB
                        for b in range(bpr):
                            code = left_place + cols_ref[cols_base + k * bpr + b]
                            n = place_ref[code]
                            out_ref[n] += out[a * bs:(a + 1) * bs, b * bs:(b + 1) * bs]

            pl.when(counts > 0)(do)

    def left_spec(pick):
        return pl.BlockSpec((1, per, lrows, lcat), lambda g, tab, *_: (tab[3 * pick + 1], tab[3 * pick + 2], 0, 0))

    def right_spec(at):
        return pl.BlockSpec((per, bpr, bs, bs), lambda g, *_: (at, 0, 0, 0))

    total_spec = pl.BlockSpec((nc + 1, bs, bs), lambda g, *_: (0, 0, 0))
    operands = [left_cat] * count + [c[0] for c in chunks] + ([] if first else [totals])
    in_specs = [left_spec(c[2]) for c in chunks] + [right_spec(c[1]) for c in chunks] + ([] if first else [total_spec])
    flops = count * per * 2 * lrows * 3 * bs * bpr * bs
    moved = 4 * (count * per * bpr * bs * bs + 2 * (nc + 1) * bs * bs)
    return pl.pallas_call(
        kernel,
        grid_spec=pltpu.PrefetchScalarGridSpec(
            num_scalar_prefetch=5,
            grid=(1,),
            in_specs=in_specs,
            out_specs=total_spec,
            scratch_shapes=[pltpu.SMEM((CB * CB,), jnp.int32)],
        ),
        out_shape=jax.ShapeDtypeStruct((nc + 1, bs, bs), f32),
        input_output_aliases={} if first else {5 + 2 * count: 0},
        compiler_params=pltpu.CompilerParams(vmem_limit_bytes=32 * 1024 * 1024),
        cost_estimate=pl.CostEstimate(flops=flops, bytes_accessed=moved, transcendentals=0),
        name="accumulate",
    )(table, rows_all, cols_all, slots, where_at, *operands)


def after(x, *others):
    return lax.optimization_barrier((x,) + others)[0]


def shards(left_values, left_rows, right_values, right_cols, result_slots):
    rows_n, cols_n, reps = (lax.axis_size(a) for a in ("row", "col", "rep"))
    row, col, rep = (lax.axis_index(a) for a in ("row", "col", "rep"))
    panels = left_values[0, 0, 0]
    slots_m, kb = panels.shape[:2]
    right = right_values[0, 0, 0]
    slots = result_slots[0, 0]
    nc = slots.shape[0]
    per = kb // QUARTERS
    odd = row % 2 == 1

    z_pairs = [(r, (r - 2) % rows_n) for r in range(rows_n)]
    x_pairs = [(r, r ^ 1) for r in range(rows_n)]

    def along_z(even_chunk, odd_chunk):
        return lax.ppermute(jnp.where(odd, odd_chunk, even_chunk), "row", z_pairs)

    def along_x(even_chunk, odd_chunk):
        return lax.ppermute(jnp.where(odd, odd_chunk, even_chunk), "row", x_pairs)

    own = [right[q * per:(q + 1) * per] for q in range(QUARTERS)]

    def left_of(turn):
        to = (col - turn) % cols_n
        panel = lax.dynamic_index_in_dim(panels, (to + turn) // cols_n, 0, keepdims=False)
        if turn % cols_n == 0:
            return panel
        return lax.ppermute(panel, "col", [(c, (c - turn) % cols_n) for c in range(cols_n)])

    z = {}
    x = {}
    z[1] = along_z(own[0], own[1])
    x[1] = along_x(own[0], own[0])
    lefts = [left_of(turn) for turn in range(STEPS)]
    z[2] = along_z(own[1], own[2])

    rows_all = lax.all_gather(left_rows[0, 0, 0], "col").reshape(-1)
    cols_all = lax.all_gather(right_cols[0, 0, 0], "row").reshape(-1)
    where_at = jnp.stack([row, jnp.int32(rows_n), col, jnp.int32(cols_n), jnp.int32(slots_m), rep]).astype(jnp.int32)
    even_table = jnp.array(Z_EVEN + X_EVEN + OWN, jnp.int32).reshape(-1)
    odd_table = jnp.array(Z_ODD + X_ODD + OWN, jnp.int32).reshape(-1)
    table = jnp.where(odd, odd_table, even_table)
    places = (rows_all, cols_all, slots, where_at)
    left_cat = split_left(lefts)

    def add(totals, chunks):
        return accumulate(places, None, table, left_cat, chunks, totals, kb)

    def received(stage):
        return [(z[stage], 0, stage - 1), (x[stage], 0, STAGES + stage - 1)]

    totals = add(None, [(right, q, 2 * STAGES + q) for q in range(QUARTERS)])
    x[2] = along_x(z[1], own[1])
    z[3] = along_z(own[2], own[3])
    x[3] = along_x(z[1], own[2])
    totals = add(totals, received(1))
    z[4] = along_z(own[3], x[3])
    x[4] = along_x(z[2], own[3])
    totals = add(totals, received(2))
    z[5] = along_z(x[1], x[4])
    x[5] = along_x(z[3], z[1])
    totals = add(totals, received(3))
    z[6] = along_z(x[5], x[5])
    x[6] = along_x(z[4], z[2])
    totals = add(totals, received(4))
    z[7] = along_z(x[6], x[6])
    x[7] = along_x(z[5], z[3])
    totals = add(totals, received(5))
    totals = add(totals, received(6))
    totals = add(totals, received(7))
    half = nc // 2
    other = lax.ppermute(totals[half:nc], "rep", [(0, 1), (1, 0)])
    return (totals[:half] + other)[None, None]


def solution(mesh):
    in_specs = (
        P("row", "rep", "col", None, None, None, None, None),
        P("row", "rep", "col", None, None, None),
        P("rep", "row", "col", None, None, None, None),
        P("rep", "row", "col", None, None),
        P("row", "col", None),
    )
    out_specs = P("row", "col", "rep", None, None)
    return jax.shard_map(shards, mesh=mesh, in_specs=in_specs, out_specs=out_specs, check_vma=False)
```

time: 222 us -> 188 us (0.85)
  waiting for transfers between devices: 143 us -> 69.7 us
  blocking collectives: 0 us -> 42.4 us
  matrix products: 39.9 us -> 0 us
  Pallas kernels: 0 us -> 27.6 us
  between operations: 13.5 us -> 0.21 us
  other arithmetic: 1.39 us -> 9.59 us
  local copies, waits for them, and re-layouts: 1.46 us -> 8.93 us
  starting transfers between devices: 22.5 us -> 28.8 us
    ppermute x12 -> x17, waiting for transfers between devices: 117 us -> 69.7 us  [the longest x7 29.6 us: along_x(): return lax.ppermute(jnp.where(odd, odd_chunk, even_chunk), 'row', x_pairs)]
    all_gather x0 -> x2, blocking collectives: none -> 42.4 us  [the longest x1 40.6 us: shards(): cols_all = lax.all_gather(right_cols[0, 0, 0], 'row').reshape(-1)]
    dot_general x8 -> x0, matrix products: 39.9 us -> none  [the longest x4 23 us: turn_products(): jnp.einsum('kaxy,kbyz->kabxz', left_blocks, right_blocks, precision=highest)]
    pallas_call x0 -> x9, Pallas kernels: none -> 27.6 us  [the longest x8 20.8 us: accumulate(): pl.pallas_call(kernel, grid_spec=pltpu.PrefetchScalarGridSpec(num_scalar_...]
    reduce_scatter x1 -> x0, waiting for transfers between devices: 26 us -> none  [shards(): shares = lax.psum_scatter(totals, 'rep', scatter_dimension=0, tiled=True)]
    select_n x0 -> x7, other arithmetic: none -> 8.62 us  [the longest x3 5.17 us: along_x(): return lax.ppermute(jnp.where(odd, odd_chunk, even_chunk), 'row', x_pairs)]
    ppermute x12 -> x17, starting transfers between devices: 22.5 us -> 28.8 us  [the longest x7 18.4 us: along_z(): return lax.ppermute(jnp.where(odd, odd_chunk, even_chunk), 'row', z_pairs)]
    squeeze x0 -> x1, local copies, waits for them, and re-layouts: none -> 4.36 us  [left_of(): lax.dynamic_index_in_dim(panels, (to + turn) // cols_n, 0, keepdims=False)]
  transfers between devices with their start and end apart: 13 -> 17, of which waited for: 8 -> 8; matrix products, arithmetic and copies ran while one was open for 12% -> 6% of each run, Pallas kernels for 0% -> 13%
where the time goes in v1:
time: 188 us; the launch traced here: 187 us
  waiting for transfers between devices  69.7 us (37%)
  blocking collectives  42.4 us (23%)
  starting transfers between devices  28.8 us (15%)
  Pallas kernels  27.6 us (15%)
  other arithmetic  9.59 us (5%)
  local copies, waits for them, and re-layouts  8.93 us (5%)
    all_gather x1, blocking collectives, shards(): cols_all = lax.all_gather(right_cols[0, 0, 0], 'row').reshape(-1)  40.6 us
    ppermute x7, waiting for transfers between devices, along_x(): return lax.ppermute(jnp.where(odd, odd_chunk, even_chunk), 'row', x_pairs)  29.6 us
    ppermute x7, waiting for transfers between devices, along_z(): return lax.ppermute(jnp.where(odd, odd_chunk, even_chunk), 'row', z_pairs)  21.9 us
    pallas_call x8, Pallas kernels, accumulate(): pl.pallas_call(kernel, grid_spec=pltpu.PrefetchScalarGridSpec(num_scalar_...  20.8 us
    ppermute x7, starting transfers between devices, along_z(): return lax.ppermute(jnp.where(odd, odd_chunk, even_chunk), 'row', z_pairs)  18.4 us
    ppermute x1, waiting for transfers between devices, shards(): other = lax.ppermute(totals[half:nc], 'rep', [(0, 1), (1, 0)])  18.1 us
    ppermute x7, starting transfers between devices, along_x(): return lax.ppermute(jnp.where(odd, odd_chunk, even_chunk), 'row', x_pairs)  8.28 us
    pallas_call x1, Pallas kernels, split_left(): pl.pallas_call(body, grid=(kb,), in_specs=[pl.BlockSpec((1, lpb, bs, bs),...  6.78 us
  transfers between devices with their start and end apart: 17, of which 8 were waited for; matrix products, arithmetic and copies ran while one was open for 6% of the time, Pallas kernels for 13%

profile of v1, /device:TPU:0, one launch (start us, length us, event | category | flops | bytes accessed | tf_op | source)
XLA Modules:
  0.0 187.2 jit_solution(7097138526852203458)
XLA Ops:
  0.0 1.6 bitcast_select_fusion.4
  1.6 5.1 %collective-permute-start.3 = (f32[2,4,128,128]{3,2,1,0:T(8,128)S(1)}, f32[2,4,128,128]{3,2,1,0:T(8,128)S(1)}, u32[]{:S(2)}, u32[]{:S(2)}) collective-permute-start(f32[2,4,128,128]{3,2,1,0:T(8,128)S(1)} %get-tuple-element.13), channel_id=1, source_target_pairs={{0,24},{4,28},{8,0},{12,4},{16,8},{20,12},{24,16},{28,20},{1,25},{... | collective-permute-start | bytes 1572872 | tf_op jit(solution)/shard_map/ppermute | solution.py:151
  6.7 0.4 collective-permute-start.2
  7.2 1.6 collective-permute-start.10
  8.8 10.3 %collective-permute-done.3.refs_2_ = f32[2,4,128,128]{3,2,1,0:T(8,128)S(1)} collective-permute-done((f32[2,4,128,128]{3,2,1,0:T(8,128)S(1)}, f32[2,4,128,128]{3,2,1,0:T(8,128)S(1)}, u32[]{:S(2)}, u32[]{:S(2)}) %collective-permute-start.3) | collective-permute-done | bytes 524320 | tf_op jit(solution)/shard_map/ppermute | solution.py:151
  19.0 10.1 %collective-permute-done.2.refs_2_ = f32[2,4,128,128]{3,2,1,0:T(8,128)S(1)} collective-permute-done((f32[2,4,128,128]{3,2,1,0:T(8,128)S(1)}, f32[2,4,128,128]{3,2,1,0:T(8,128)S(1)}, u32[]{:S(2)}, u32[]{:S(2)}) %collective-permute-start.2) | collective-permute-done | bytes 524320 | tf_op jit(solution)/shard_map/ppermute | solution.py:151
  29.1 1.2 bitcast_select_fusion.3
  30.3 1.5 collective-permute-start.9
  31.8 0.5 collective-permute-start.4
  32.3 4.3 %collective-permute-start.8 = (f32[2,4,128,128]{3,2,1,0:T(8,128)}, f32[2,4,128,128]{3,2,1,0:T(8,128)}, u32[]{:S(2)}, u32[]{:S(2)}) collective-permute-start(f32[2,4,128,128]{3,2,1,0:T(8,128)} %get-tuple-element.12), channel_id=1, source_target_pairs={{0,24},{4,28},{8,0},{12,4},{16,8},{20,12},{24,16},{28,20},{1,25},{... | collective-permute-start | bytes 1572872 | tf_op jit(solution)/shard_map/ppermute | solution.py:151
  36.6 8.6 %collective-permute-done.9.refs_3_ = f32[2,4,128,128]{3,2,1,0:T(8,128)S(1)} collective-permute-done((f32[2,4,128,128]{3,2,1,0:T(8,128)S(1)}, f32[2,4,128,128]{3,2,1,0:T(8,128)S(1)}, u32[]{:S(2)}, u32[]{:S(2)}) %collective-permute-start.9) | collective-permute-done | bytes 524320 | tf_op jit(solution)/shard_map/ppermute | solution.py:154
  45.2 1.0 broadcast_select_fusion.2
  46.2 0.8 copy-done.2
  47.0 4.3 %collective-permute-start.11 = (f32[2,4,128,128]{3,2,1,0:T(8,128)}, f32[2,4,128,128]{3,2,1,0:T(8,128)}, u32[]{:S(2)}, u32[]{:S(2)}) collective-permute-start(f32[2,4,128,128]{3,2,1,0:T(8,128)} %broadcast_select_fusion.2), channel_id=1, source_target_pairs={{0,24},{4,28},{8,0},{12,4},{16,8},{20,12},{24,16},{28,20},{1,25},{... | collective-permute-start | bytes 1572872 | tf_op jit(solution)/shard_map/ppermute | solution.py:151
  51.3 3.1 %collective-permute-done.4.refs_3_ = f32[2,4,128,128]{3,2,1,0:T(8,128)S(1)} collective-permute-done((f32[2,4,128,128]{3,2,1,0:T(8,128)S(1)}, f32[2,4,128,128]{3,2,1,0:T(8,128)S(1)}, u32[]{:S(2)}, u32[]{:S(2)}) %collective-permute-start.4) | collective-permute-done | bytes 524320 | tf_op jit(solution)/shard_map/ppermute | solution.py:154
  54.3 0.9 bitcast_select_fusion.2
  55.2 0.8 copy-done.6
  56.0 4.3 %collective-permute-start.5 = (f32[2,4,128,128]{3,2,1,0:T(8,128)}, f32[2,4,128,128]{3,2,1,0:T(8,128)}, u32[]{:S(2)}, u32[]{:S(2)}) collective-permute-start(f32[2,4,128,128]{3,2,1,0:T(8,128)} %bitcast_select_fusion.2), channel_id=1, source_target_pairs={{0,24},{4,28},{8,0},{12,4},{16,8},{20,12},{24,16},{28,20},{1,25},{... | collective-permute-start | bytes 1572872 | tf_op jit(solution)/shard_map/ppermute | solution.py:151
  60.3 4.4 %dynamic-slice_bitcast_fusion = (f32[8,2,128,128]{3,2,1,0:T(8,128)}, f32[8,2,128,128]{3,2,1,0:T(8,128)}, f32[8,2,128,128]{3,2,1,0:T(8,128)}, f32[8,2,128,128]{3,2,1,0:T(8,128)}) fusion(f32[1,1,1,3,8,2,128,128]{7,6,5,4,3,2,1,0:T(8,128)} %param.7, s32[]{:T(128)S(6)} %select_n.128, s32[]{:T(128)S(6)} %select_n.122, s32[]{:T(128)S(6)} %select_n.119, s32[]{:T(128)S(6)} %select_n.125), kind=kLoop, calls=%fused_computation | loop fusion | bytes 8388624 | tf_op jit(solution)/shard_map/jit(dynamic_index_in_dim)/squeeze | solution.py:160
  64.7 0.5 collective-permute-start.1
  65.3 2.1 %broadcast_select_fusion = (f32[2,4,128,128]{3,2,1,0:T(8,128)S(1)}, f32[2,4,128,128]{3,2,1,0:T(8,128)}) fusion(f32[2,4,128,128]{3,2,1,0:T(8,128)S(1)} %collective-permute-done.3.refs_2_, f32[2,4,128,128]{3,2,1,0:T(8,128)} %collective-permute-done.8.refs_2_, pred[]{:T(512)S(6)} %eq.9, f32[2,4,128,128]{3,2,1,0:T(8,128)} %collective-permute-done.11.refs_2_), kind=kLoop, calls=%fused_computation.14 | loop fusion | flops 262144 | bytes 2621441 | tf_op jit(solution)/shard_map/jit(_where)/select_n | solution.py:154
  67.4 1.3 collective-permute-start.13
  68.7 1.5 collective-permute-done.5.refs_2_
  70.2 1.9 %broadcast_select_fusion.3 = f32[2,4,128,128]{3,2,1,0:T(8,128)} fusion(f32[2,4,128,128]{3,2,1,0:T(8,128)S(1)} %collective-permute-done.2.refs_2_, f32[2,4,128,128]{3,2,1,0:T(8,128)} %collective-permute-done.5.refs_2_, pred[]{:T(512)S(6)} %eq.9), kind=kLoop, calls=%fused_computation.17 | loop fusion | flops 131072 | bytes 1572865 | tf_op jit(solution)/shard_map/jit(_where)/select_n | solution.py:154
  72.1 0.5 collective-permute-start.6
  72.6 1.6 collective-permute-start.15
  74.1 8.1 %collective-permute-done.13.refs_3_ = f32[2,4,128,128]{3,2,1,0:T(8,128)} collective-permute-done((f32[2,4,128,128]{3,2,1,0:T(8,128)S(1)}, f32[2,4,128,128]{3,2,1,0:T(8,128)}, u32[]{:S(2)}, u32[]{:S(2)}) %collective-permute-start.13) | collective-permute-done | bytes 524320 | tf_op jit(solution)/shard_map/ppermute | solution.py:154
  82.3 1.3 collective-permute-start.12
  83.6 9.9 %collective-permute-done.6.refs_3_ = f32[2,4,128,128]{3,2,1,0:T(8,128)} collective-permute-done((f32[2,4,128,128]{3,2,1,0:T(8,128)}, f32[2,4,128,128]{3,2,1,0:T(8,128)}, u32[]{:S(2)}, u32[]{:S(2)}) %collective-permute-start.6) | collective-permute-done | bytes 524320 | tf_op jit(solution)/shard_map/ppermute | solution.py:154
  93.6 40.6 %all-gather.1 = s32[8,1,1,8,4]{3,4,2,1,0:T(4,128)S(1)} all-gather(s32[1,1,1,8,4]{3,4,2,1,0:T(4,128)S(1)} %copy-done.12), channel_id=3, replica_groups=mesh['row'=8,'col'=2,'rep'=2] {'row'}, dimensions={0}, use_global_device_ids=true | all-gather | bytes 1152 | tf_op jit(solution)/shard_map/all_gather | solution.py:173
  134.2 0.1 copy.19
  134.3 0.1 reshape.23.cols_ref
  134.4 1.8 all-gather
  136.2 0.1 copy.18
  136.3 0.1 reshape.22.rows_ref
  136.5 6.8 %split_left.1.refs_0_.refs_1_.refs_2_.refs_3_ = bf16[4,8,256,256]{3,2,1,0:T(8,128)(2,1)} custom-call(f32[8,2,128,128]{3,2,1,0:T(8,128)} %get-tuple-element.7.refs_0_, f32[8,2,128,128]{3,2,1,0:T(8,128)} %collective-permute-done.refs_1_, f32[8,2,128,128]{3,2,1,0:T(8,128)} %get-tuple-element.8.refs_2_, f32[8,2,128,128]{3,2,1,0:T(8,128)} %collective-permute-done.1.refs_3_), custom_call_target="tpu_custom_call" | custom-call | flops 4194304 | bytes 8388608 | tf_op jit(solution)/shard_map/split_left/pallas_call | solution.py:40
  143.3 2.2 %copy-done = bf16[4,8,256,256]{3,2,1,0:T(8,128)(2,1)S(1)} copy-done((bf16[4,8,256,256]{3,2,1,0:T(8,128)(2,1)S(1)}, bf16[4,8,256,256]{3,2,1,0:T(8,128)(2,1)}, u32[]{:S(2)}) %copy-start) | copy-done | bytes 4194328
  145.5 2.6 %accumulate.8.refs_4_ = f32[25,128,128]{2,1,0:T(8,128)S(1)} custom-call(s32[54]{0:T(128)S(1)} %select_n.116.table_ref, s32[96]{0:T(128)S(1)} %reshape.22.rows_ref, s32[256]{0:T(256)S(1)} %reshape.23.cols_ref, s32[24]{0:T(128)S(1)} %bitcast.43, s32[6]{0:T(128)S(1)} %stack.15.at_ref, bf16[4,8,256,256]{3,2,1,0:T(8,128)(2,1)S(1)} %copy-done, ...), custom_call_target="tpu_custom_call" | custom-call | flops 805306368 | bytes 5373952 | tf_op jit(solution)/shard_map/accumulate/pallas_call | solution.py:115
  148.1 1.8 accumulate.9.refs_4_
  149.9 2.8 %accumulate.10.refs_4_ = f32[25,128,128]{2,1,0:T(8,128)S(1)} custom-call(s32[54]{0:T(128)S(1)} %select_n.116.table_ref, s32[96]{0:T(128)S(1)} %reshape.22.rows_ref, s32[256]{0:T(256)S(1)} %reshape.23.cols_ref, s32[24]{0:T(128)S(1)} %bitcast.45, s32[6]{0:T(128)S(1)} %stack.15.at_ref, ...), custom_call_target="tpu_custom_call", output_to_operand_aliasing={{}: (9, {})} | custom-call | flops 402653184 | bytes 4325376 | tf_op jit(solution)/shard_map/accumulate/pallas_call | solution.py:115
  152.8 2.8 %accumulate.11.refs_4_ = f32[25,128,128]{2,1,0:T(8,128)S(1)} custom-call(s32[54]{0:T(128)S(1)} %select_n.116.table_ref, s32[96]{0:T(128)S(1)} %reshape.22.rows_ref, s32[256]{0:T(256)S(1)} %reshape.23.cols_ref, s32[24]{0:T(128)S(1)} %bitcast.46, s32[6]{0:T(128)S(1)} %stack.15.at_ref, ...), custom_call_target="tpu_custom_call", output_to_operand_aliasing={{}: (9, {})} | custom-call | flops 402653184 | bytes 4325376 | tf_op jit(solution)/shard_map/accumulate/pallas_call | solution.py:115
  155.6 2.8 %accumulate.12.refs_4_ = f32[25,128,128]{2,1,0:T(8,128)S(1)} custom-call(s32[54]{0:T(128)S(1)} %select_n.116.table_ref, s32[96]{0:T(128)S(1)} %reshape.22.rows_ref, s32[256]{0:T(256)S(1)} %reshape.23.cols_ref, s32[24]{0:T(128)S(1)} %bitcast.47, s32[6]{0:T(128)S(1)} %stack.15.at_ref, ...), custom_call_target="tpu_custom_call", output_to_operand_aliasing={{}: (9, {})} | custom-call | flops 402653184 | bytes 4325376 | tf_op jit(solution)/shard_map/accumulate/pallas_call | solution.py:115
  158.4 3.0 %accumulate.13.refs_4_ = f32[25,128,128]{2,1,0:T(8,128)S(1)} custom-call(s32[54]{0:T(128)S(1)} %select_n.116.table_ref, s32[96]{0:T(128)S(1)} %reshape.22.rows_ref, s32[256]{0:T(256)S(1)} %reshape.23.cols_ref, s32[24]{0:T(128)S(1)} %bitcast.48, s32[6]{0:T(128)S(1)} %stack.15.at_ref, ...), custom_call_target="tpu_custom_call", output_to_operand_aliasing={{}: (9, {})} | custom-call | flops 402653184 | bytes 4325376 | tf_op jit(solution)/shard_map/accumulate/pallas_call | solution.py:115
  161.4 2.5 %accumulate.14.refs_4_ = f32[25,128,128]{2,1,0:T(8,128)S(1)} custom-call(s32[54]{0:T(128)S(1)} %select_n.116.table_ref, s32[96]{0:T(128)S(1)} %reshape.22.rows_ref, s32[256]{0:T(256)S(1)} %reshape.23.cols_ref, s32[24]{0:T(128)S(1)} %bitcast.49, s32[6]{0:T(128)S(1)} %stack.15.at_ref, ...), custom_call_target="tpu_custom_call", output_to_operand_aliasing={{}: (9, {})} | custom-call | flops 402653184 | bytes 4325376 | tf_op jit(solution)/shard_map/accumulate/pallas_call | solution.py:115
  163.9 2.5 %accumulate.15 = f32[25,128,128]{2,1,0:T(8,128)S(1)} custom-call(s32[54]{0:T(128)S(1)} %select_n.116.table_ref, s32[96]{0:T(128)S(1)} %reshape.22.rows_ref, s32[256]{0:T(256)S(1)} %reshape.23.cols_ref, s32[24]{0:T(128)S(1)} %bitcast.50, s32[6]{0:T(128)S(1)} %stack.15.at_ref, bf16[4,8,256,256]{3,2,1,0:T(8,128)(2,1)S(1)} %copy-done, ...), custom_call_target="tpu_custom_call", output_to_operand_aliasing={{}: (9, {})} | custom-call | flops 402653184 | bytes 4325376 | tf_op jit(solution)/shard_map/accumulate/pallas_call | solution.py:115
  166.5 1.6 collective-permute-start.16
  168.1 18.1 %collective-permute-done.16 = f32[12,128,128]{2,1,0:T(8,128)S(1)} collective-permute-done((f32[12,128,128]{2,1,0:T(8,128)S(1)}, f32[12,128,128]{2,1,0:T(8,128)S(1)}, u32[]{:S(2)}, u32[]{:S(2)}) %collective-permute-start.16) | collective-permute-done | bytes 786464 | tf_op jit(solution)/shard_map/ppermute | solution.py:207
  186.2 1.0 fusion
  (40 shorter events, 0.4 us)
Async XLA Ops:
  0.0 7.2 %copy-start.1 = (f32[1,1,1,8,4,128,128]{6,5,4,3,2,1,0:T(8,128)S(1)}, f32[1,1,1,8,4,128,128]{6,5,4,3,2,1,0:T(8,128)}, u32[]{:S(2)}) copy-start(f32[1,1,1,8,4,128,128]{6,5,4,3,2,1,0:T(8,128)} %param.9) | copy-start | bytes 6291460
  1.6 17.4 %collective-permute-start.3 = (f32[2,4,128,128]{3,2,1,0:T(8,128)S(1)}, f32[2,4,128,128]{3,2,1,0:T(8,128)S(1)}, u32[]{:S(2)}, u32[]{:S(2)}) collective-permute-start(f32[2,4,128,128]{3,2,1,0:T(8,128)S(1)} %get-tuple-element.13), channel_id=1, source_target_pairs={{0,24},{4,28},{8,0},{12,4},{16,8},{20,12},{24,16},{28,20},{1,25},{... | collective-permute-start | bytes 1572872 | tf_op jit(solution)/shard_map/ppermute | solution.py:151
  6.7 22.4 %collective-permute-start.2 = (f32[2,4,128,128]{3,2,1,0:T(8,128)S(1)}, f32[2,4,128,128]{3,2,1,0:T(8,128)S(1)}, u32[]{:S(2)}, u32[]{:S(2)}) collective-permute-start(f32[2,4,128,128]{3,2,1,0:T(8,128)S(1)} %get-tuple-element.14), channel_id=1, source_target_pairs={{0,24},{4,28},{8,0},{12,4},{16,8},{20,12},{24,16},{28,20},{1,25},{... | collective-permute-start | bytes 1572872 | tf_op jit(solution)/shard_map/ppermute | solution.py:151
  7.2 29.4 %collective-permute-start.10 = (f32[2,4,128,128]{3,2,1,0:T(8,128)S(1)}, f32[2,4,128,128]{3,2,1,0:T(8,128)S(1)}, u32[]{:S(2)}, u32[]{:S(2)}) collective-permute-start(f32[2,4,128,128]{3,2,1,0:T(8,128)S(1)} %slice_bitcast_fusion), channel_id=1, source_target_pairs={{0,4},{4,0},{8,12},{12,8},{16,20},{20,16},{24,28},{28,24},{1,5},{5... | collective-permute-start | bytes 1572872 | tf_op jit(solution)/shard_map/ppermute | solution.py:154
  30.3 14.9 %collective-permute-start.9 = (f32[2,4,128,128]{3,2,1,0:T(8,128)S(1)}, f32[2,4,128,128]{3,2,1,0:T(8,128)S(1)}, u32[]{:S(2)}, u32[]{:S(2)}) collective-permute-start(f32[2,4,128,128]{3,2,1,0:T(8,128)S(1)} %get-tuple-element.11), channel_id=1, source_target_pairs={{0,4},{4,0},{8,12},{12,8},{16,20},{20,16},{24,28},{28,24},{1,5},{5... | collective-permute-start | bytes 1572872 | tf_op jit(solution)/shard_map/ppermute | solution.py:154
  31.8 22.5 %collective-permute-start.4 = (f32[2,4,128,128]{3,2,1,0:T(8,128)S(1)}, f32[2,4,128,128]{3,2,1,0:T(8,128)S(1)}, u32[]{:S(2)}, u32[]{:S(2)}) collective-permute-start(f32[2,4,128,128]{3,2,1,0:T(8,128)S(1)} %get-tuple-element.10), channel_id=1, source_target_pairs={{0,4},{4,0},{8,12},{12,8},{16,20},{20,16},{24,28},{28,24},{1,5},{5... | collective-permute-start | bytes 1572872 | tf_op jit(solution)/shard_map/ppermute | solution.py:154
  32.3 32.9 %collective-permute-start.8 = (f32[2,4,128,128]{3,2,1,0:T(8,128)}, f32[2,4,128,128]{3,2,1,0:T(8,128)}, u32[]{:S(2)}, u32[]{:S(2)}) collective-permute-start(f32[2,4,128,128]{3,2,1,0:T(8,128)} %get-tuple-element.12), channel_id=1, source_target_pairs={{0,24},{4,28},{8,0},{12,4},{16,8},{20,12},{24,16},{28,20},{1,25},{... | collective-permute-start | bytes 1572872 | tf_op jit(solution)/shard_map/ppermute | solution.py:151
  45.2 1.0 copy-start.4
  46.2 0.8 copy-start.2
  47.0 18.3 %collective-permute-start.11 = (f32[2,4,128,128]{3,2,1,0:T(8,128)}, f32[2,4,128,128]{3,2,1,0:T(8,128)}, u32[]{:S(2)}, u32[]{:S(2)}) collective-permute-start(f32[2,4,128,128]{3,2,1,0:T(8,128)} %broadcast_select_fusion.2), channel_id=1, source_target_pairs={{0,24},{4,28},{8,0},{12,4},{16,8},{20,12},{24,16},{28,20},{1,25},{... | collective-permute-start | bytes 1572872 | tf_op jit(solution)/shard_map/ppermute | solution.py:151
  55.2 0.8 copy-start.6
  56.0 14.2 %collective-permute-start.5 = (f32[2,4,128,128]{3,2,1,0:T(8,128)}, f32[2,4,128,128]{3,2,1,0:T(8,128)}, u32[]{:S(2)}, u32[]{:S(2)}) collective-permute-start(f32[2,4,128,128]{3,2,1,0:T(8,128)} %bitcast_select_fusion.2), channel_id=1, source_target_pairs={{0,24},{4,28},{8,0},{12,4},{16,8},{20,12},{24,16},{28,20},{1,25},{... | collective-permute-start | bytes 1572872 | tf_op jit(solution)/shard_map/ppermute | solution.py:151
  64.7 17.6 %collective-permute-start = (f32[8,2,128,128]{3,2,1,0:T(8,128)}, f32[8,2,128,128]{3,2,1,0:T(8,128)}, u32[]{:S(2)}, u32[]{:S(2)}) collective-permute-start(f32[8,2,128,128]{3,2,1,0:T(8,128)} %get-tuple-element.6), channel_id=1, source_target_pairs={{0,2},{2,0},{1,3},{3,1},{4,6},{6,4},{5,7},{7,5},{8,10},{10,8},{9,1... | collective-permute-start | bytes 3145736 | tf_op jit(solution)/shard_map/ppermute | solution.py:163
  64.7 28.8 %copy-start.9 = (s32[18,3]{1,0:T(8,128)S(1)}, s32[18,3]{1,0:T(8,128)}, u32[]{:S(2)}) copy-start(s32[18,3]{1,0:T(8,128)} %constant.105.clone) | copy-start | bytes 652
  64.7 28.8 %copy-start.10 = (s32[18,3]{1,0:T(8,128)S(1)}, s32[18,3]{1,0:T(8,128)}, u32[]{:S(2)}) copy-start(s32[18,3]{1,0:T(8,128)} %constant.106.clone) | copy-start | bytes 652
  64.7 28.9 %copy-start.12 = (s32[1,1,1,8,4]{3,4,2,1,0:T(4,128)S(1)}, s32[1,1,1,8,4]{3,4,2,1,0:T(4,128)}, u32[]{:S(2)}) copy-start(s32[1,1,1,8,4]{3,4,2,1,0:T(4,128)} %param.10) | copy-start | bytes 388
  64.7 69.7 %copy-start.11 = (s32[1,1,1,3,8,2]{4,5,3,2,1,0:T(2,128)S(1)}, s32[1,1,1,3,8,2]{4,5,3,2,1,0:T(2,128)}, u32[]{:S(2)}) copy-start(s32[1,1,1,3,8,2]{4,5,3,2,1,0:T(2,128)} %param.8) | copy-start | bytes 580
  64.7 71.9 %collective-permute-start.1 = (f32[8,2,128,128]{3,2,1,0:T(8,128)}, f32[8,2,128,128]{3,2,1,0:T(8,128)}, u32[]{:S(2)}, u32[]{:S(2)}) collective-permute-start(f32[8,2,128,128]{3,2,1,0:T(8,128)} %get-tuple-element.5), channel_id=1, source_target_pairs={{0,2},{2,0},{1,3},{3,1},{4,6},{6,4},{5,7},{7,5},{8,10},{10,8},{9,1... | collective-permute-start | bytes 3145736 | tf_op jit(solution)/shard_map/ppermute | solution.py:163
  67.4 14.9 %collective-permute-start.13 = (f32[2,4,128,128]{3,2,1,0:T(8,128)S(1)}, f32[2,4,128,128]{3,2,1,0:T(8,128)}, u32[]{:S(2)}, u32[]{:S(2)}) collective-permute-start(f32[2,4,128,128]{3,2,1,0:T(8,128)S(1)} %get-tuple-element.15), channel_id=1, source_target_pairs={{0,4},{4,0},{8,12},{12,8},{16,20},{20,16},{24,28},{28,24},{1,5},{5... | collective-permute-start | bytes 1572872 | tf_op jit(solution)/shard_map/ppermute | solution.py:154
  72.1 21.4 %collective-permute-start.6 = (f32[2,4,128,128]{3,2,1,0:T(8,128)}, f32[2,4,128,128]{3,2,1,0:T(8,128)}, u32[]{:S(2)}, u32[]{:S(2)}) collective-permute-start(f32[2,4,128,128]{3,2,1,0:T(8,128)} %broadcast_select_fusion.3), channel_id=1, source_target_pairs={{0,4},{4,0},{8,12},{12,8},{16,20},{20,16},{24,28},{28,24},{1,5},{5... | collective-permute-start | bytes 1572872 | tf_op jit(solution)/shard_map/ppermute | solution.py:154
  72.6 77.4 %collective-permute-start.15 = (f32[2,4,128,128]{3,2,1,0:T(8,128)}, f32[2,4,128,128]{3,2,1,0:T(8,128)}, u32[]{:S(2)}, u32[]{:S(2)}) collective-permute-start(f32[2,4,128,128]{3,2,1,0:T(8,128)} %get-tuple-element.9), channel_id=1, source_target_pairs={{0,4},{4,0},{8,12},{12,8},{16,20},{20,16},{24,28},{28,24},{1,5},{5... | collective-permute-start | bytes 1572872 | tf_op jit(solution)/shard_map/ppermute | solution.py:154
  82.2 79.1 %collective-permute-start.14 = (f32[2,4,128,128]{3,2,1,0:T(8,128)}, f32[2,4,128,128]{3,2,1,0:T(8,128)}, u32[]{:S(2)}, u32[]{:S(2)}) collective-permute-start(f32[2,4,128,128]{3,2,1,0:T(8,128)} %collective-permute-done.13.refs_3_), channel_id=1, source_target_pairs={{0,24},{4,28},{8,0},{12,4},{16,8},{20,12},{24,16},{28,20},{1,25},{... | collective-permute-start | bytes 1572872 | tf_op jit(solution)/shard_map/ppermute | solution.py:151
  82.3 81.6 %collective-permute-start.12 = (f32[2,4,128,128]{3,2,1,0:T(8,128)}, f32[2,4,128,128]{3,2,1,0:T(8,128)}, u32[]{:S(2)}, u32[]{:S(2)}) collective-permute-start(f32[2,4,128,128]{3,2,1,0:T(8,128)} %get-tuple-element.16), channel_id=1, source_target_pairs={{0,4},{4,0},{8,12},{12,8},{16,20},{20,16},{24,28},{28,24},{1,5},{5... | collective-permute-start | bytes 1572872 | tf_op jit(solution)/shard_map/ppermute | solution.py:154
  93.5 70.4 %collective-permute-start.7 = (f32[2,4,128,128]{3,2,1,0:T(8,128)}, f32[2,4,128,128]{3,2,1,0:T(8,128)}, u32[]{:S(2)}, u32[]{:S(2)}) collective-permute-start(f32[2,4,128,128]{3,2,1,0:T(8,128)} %collective-permute-done.6.refs_3_), channel_id=1, source_target_pairs={{0,24},{4,28},{8,0},{12,4},{16,8},{20,12},{24,16},{28,20},{1,25},{... | collective-permute-start | bytes 1572872 | tf_op jit(solution)/shard_map/ppermute | solution.py:151
  136.5 6.8 %copy-start.8 = (s32[1,1,24]{2,1,0:T(1,128)S(1)}, s32[1,1,24]{2,1,0:T(1,128)}, u32[]{:S(2)}) copy-start(s32[1,1,24]{2,1,0:T(1,128)} %param.11) | copy-start | bytes 292
  143.3 2.2 %copy-start = (bf16[4,8,256,256]{3,2,1,0:T(8,128)(2,1)S(1)}, bf16[4,8,256,256]{3,2,1,0:T(8,128)(2,1)}, u32[]{:S(2)}) copy-start(bf16[4,8,256,256]{3,2,1,0:T(8,128)(2,1)} %split_left.1.refs_0_.refs_1_.refs_2_.refs_3_) | copy-start | bytes 12582916
  145.5 2.6 %copy-start.3 = (f32[2,4,128,128]{3,2,1,0:T(8,128)S(1)}, f32[2,4,128,128]{3,2,1,0:T(8,128)}, u32[]{:S(2)}) copy-start(f32[2,4,128,128]{3,2,1,0:T(8,128)} %copy-done.2) | copy-start | bytes 1572868
  149.9 2.8 %copy-start.7 = (f32[2,4,128,128]{3,2,1,0:T(8,128)S(1)}, f32[2,4,128,128]{3,2,1,0:T(8,128)}, u32[]{:S(2)}) copy-start(f32[2,4,128,128]{3,2,1,0:T(8,128)} %copy-done.6) | copy-start | bytes 1572868
  152.8 2.8 %copy-start.5 = (f32[2,4,128,128]{3,2,1,0:T(8,128)S(1)}, f32[2,4,128,128]{3,2,1,0:T(8,128)}, u32[]{:S(2)}) copy-start(f32[2,4,128,128]{3,2,1,0:T(8,128)} %copy-done.4) | copy-start | bytes 1572868
  166.5 19.7 %collective-permute-start.16 = (f32[12,128,128]{2,1,0:T(8,128)S(1)}, f32[12,128,128]{2,1,0:T(8,128)S(1)}, u32[]{:S(2)}, u32[]{:S(2)}) collective-permute-start(f32[12,128,128]{2,1,0:T(8,128)S(1)} %slice.41), channel_id=1, source_target_pairs={{0,1},{1,0},{2,3},{3,2},{4,5},{5,4},{6,7},{7,6},{8,9},{9,8},{10,11... | collective-permute-start | bytes 2359304 | tf_op jit(solution)/shard_map/ppermute | solution.py:207

commit v2 on v0

v2 whole, which is shorter than its diff:
```python
import jax
import jax.numpy as jnp
from jax import lax
from jax.experimental import pallas as pl
from jax.experimental.pallas import tpu as pltpu
from jax.sharding import PartitionSpec as P

STEPS = 4
CB = 8
QUARTERS = 4

bf16 = jnp.bfloat16
f32 = jnp.float32

Z_CHUNKS = (
    ((2, 0), (2, 0)),
    ((2, 1), (2, 1)),
    ((2, 2), (2, 2)),
    ((2, 3), (3, 0)),
    ((3, 3), (3, 1)),
    (None, (3, 2)),
    (None, (3, 3)),
)
X_CHUNKS = (
    ((1, 3), None),
    ((1, 0), None),
    ((1, 1), (1, 0)),
    ((1, 2), (1, 1)),
    ((3, 0), (1, 2)),
    ((3, 1), (1, 3)),
    ((3, 2), (2, 3)),
)


def copy_call(kernel, scalar, operands, out_shapes, name):
    any_spec = pl.BlockSpec(memory_space=pl.ANY)
    moved = sum(8 * shape.size for shape in out_shapes)
    return pl.pallas_call(
        kernel,
        in_specs=[pl.BlockSpec(memory_space=pltpu.SMEM)] + [any_spec] * len(operands),
        out_specs=[any_spec] * len(out_shapes),
        out_shape=out_shapes,
        scratch_shapes=[pltpu.SemaphoreType.DMA((len(out_shapes),))],
        cost_estimate=pl.CostEstimate(flops=0, bytes_accessed=moved, transcendentals=0),
        name=name,
    )(scalar, *operands)


def pick(odd, per, even_part, odd_part, *others):
    (even_from, even_at), (odd_from, odd_at) = even_part, odd_part

    def kernel(odd_ref, even_ref, other_ref, *refs):
        out_ref, sems = refs[-2:]

        def copy_from(ref, at):
            copy = pltpu.make_async_copy(ref.at[pl.ds(at * per, per)], out_ref, sems.at[0])
            copy.start()
            copy.wait()

        if even_part is odd_part:
            copy_from(even_ref, even_at)
        else:
            pl.when(odd_ref[0] == 0)(lambda: copy_from(even_ref, even_at))
            pl.when(odd_ref[0] != 0)(lambda: copy_from(other_ref, odd_at))

    out_shape = jax.ShapeDtypeStruct((per,) + even_from.shape[1:], even_from.dtype)
    return copy_call(kernel, odd, [even_from, odd_from, *others], [out_shape], "pick")[0]


def pick_panels(panels, which):
    count = which.shape[0]

    def kernel(which_ref, panels_ref, *refs):
        sems = refs[-1]
        copies = [pltpu.make_async_copy(panels_ref.at[which_ref[n]], refs[n], sems.at[n]) for n in range(count)]
        for copy in copies:
            copy.start()
        for copy in copies:
            copy.wait()

    out_shape = jax.ShapeDtypeStruct(panels.shape[1:], panels.dtype)
    return copy_call(kernel, which, [panels], [out_shape] * count, "pick_panels")


def accumulate(scalars, lefts, chunks, totals, nc):
    _, kb, lpb, bs, _ = lefts[0][0].shape
    per = kb // QUARTERS
    bpr = chunks[0][0].shape[1]
    products = lpb * bpr
    odd_at = STEPS * kb * products
    first = totals is None
    sides = [(c, side) for c in range(len(chunks)) for side in range(2) if chunks[c][2][side] is not None]
    sides = [(c, side) for c, side in sides if side == 0 or chunks[c][2][0] != chunks[c][2][1]]

    def kernel(scalar_ref, *refs):
        left_refs = dict(zip(sides, refs))
        right_refs = refs[len(sides):len(sides) + len(chunks)]
        out_ref = refs[-1]
        odd = scalar_ref[odd_at]
        if first:
            out_ref[...] = jnp.zeros_like(out_ref)
        else:
            out_ref[...] = refs[-2][...]
        for c, (_, _, (even_is, odd_is)) in enumerate(chunks):
            def one(c=c, even_is=even_is, odd_is=odd_is):
                both = even_is != odd_is and even_is is not None and odd_is is not None
                base = [0 if what is None else (what[0] * kb + what[1] * per) * products for what in (even_is, odd_is)]
                base_at = jnp.where(odd == 0, base[0], base[1]) if both else base[0] if even_is else base[1]
                for k in range(per):
                    if both:
                        left = jnp.where(odd == 0, left_refs[c, 0][0, k], left_refs[c, 1][0, k])
                    else:
                        left = left_refs[c, 0 if even_is else 1][0, k]
                    left = left.reshape(lpb * bs, bs)
                    left_high = left.astype(bf16)
                    left_low = (left - left_high.astype(f32)).astype(bf16)
                    right = jnp.concatenate([right_refs[c][k, b] for b in range(bpr)], axis=1)
                    high = right.astype(bf16)
                    low = (right - high.astype(f32)).astype(bf16)
                    out = jnp.dot(
                        jnp.concatenate([left_high, left_low, left_high], axis=1),
                        jnp.concatenate([high, high, low], axis=0),
                        preferred_element_type=f32,
                    )
                    for a in range(lpb):
                        for b in range(bpr):
                            n = scalar_ref[base_at + k * products + a * bpr + b]
                            out_ref[n] += out[a * bs:(a + 1) * bs, b * bs:(b + 1) * bs]

            if even_is is None:
                pl.when(odd != 0)(one)
            elif odd_is is None:
                pl.when(odd == 0)(one)
            else:
                one()

    def left_spec(turn, quarter):
        held_at = lefts[turn][1]
        return pl.BlockSpec((1, per, lpb, bs, bs), lambda g, *_: (held_at, quarter, 0, 0, 0))

    def right_spec(at):
        return pl.BlockSpec((per, bpr, bs, bs), lambda g, *_: (at, 0, 0, 0))

    total_spec = pl.BlockSpec((nc + 1, bs, bs), lambda g, *_: (0, 0, 0))
    operands = [lefts[chunks[c][2][side][0]][0] for c, side in sides] + [c[0] for c in chunks]
    in_specs = [left_spec(*chunks[c][2][side]) for c, side in sides]
    in_specs += [right_spec(at) for _, at, _ in chunks]
    if not first:
        operands.append(totals)
        in_specs.append(total_spec)
    flops = len(chunks) * per * 2 * lpb * bs * 3 * bs * bpr * bs
    moved = 4 * (len(chunks) * per * (bpr + lpb) * bs * bs + 2 * (nc + 1) * bs * bs)
    return pl.pallas_call(
        kernel,
        grid_spec=pltpu.PrefetchScalarGridSpec(
            num_scalar_prefetch=1,
            grid=(1,),
            in_specs=in_specs,
            out_specs=total_spec,
        ),
        out_shape=jax.ShapeDtypeStruct((nc + 1, bs, bs), f32),
        input_output_aliases={} if first else {len(operands): 0},
        compiler_params=pltpu.CompilerParams(vmem_limit_bytes=32 * 1024 * 1024),
        cost_estimate=pl.CostEstimate(flops=flops, bytes_accessed=moved, transcendentals=0),
        name="accumulate",
    )(scalars, *operands)


def shards(left_values, left_rows, right_values, right_cols, result_slots):
    rows_n, cols_n = (lax.axis_size(a) for a in ("row", "col"))
    row, col, rep = (lax.axis_index(a) for a in ("row", "col", "rep"))
    panels = left_values[0, 0, 0]
    panel_rows = left_rows[0, 0, 0]
    right = right_values[0, 0, 0]
    right_places = right_cols[0, 0, 0]
    slots = result_slots[0, 0]
    kb = right.shape[0]
    nc = slots.shape[0]
    half = nc // 2
    per = kb // QUARTERS
    odd = (row % 2).astype(jnp.int32).reshape(1)

    z_pairs = [(r, (r - 2) % rows_n) for r in range(rows_n)]
    x_pairs = [(r, r ^ 1) for r in range(rows_n)]

    def along_z(chunk):
        return lax.ppermute(chunk, "row", z_pairs)

    def along_x(chunk):
        return lax.ppermute(chunk, "row", x_pairs)

    def sent(even_part, odd_part=None, *others):
        even_part = even_part if isinstance(even_part, tuple) else (even_part, 0)
        odd_part = even_part if odd_part is None else odd_part if isinstance(odd_part, tuple) else (odd_part, 0)
        return pick(odd, per, even_part, odd_part, *others)

    z = {}
    x = {}
    z[1] = along_z(sent((right, 0)))
    x[1] = along_x(sent((right, 3)))
    z[2] = along_z(sent((right, 1)))

    def to_reader(held, turn):
        return lax.ppermute(held, "col", [(c, (c - turn) % cols_n) for c in range(cols_n)])

    moving = [turn for turn in range(STEPS) if turn % cols_n]
    place = [turn // cols_n if turn % cols_n == 0 else ((col - turn) % cols_n + turn) // cols_n for turn in range(STEPS)]
    lefts = [(panels, place[turn]) for turn in range(STEPS)]
    row_turns = [panel_rows[place[turn]] for turn in range(STEPS)]
    if moving:
        picked = pick_panels(panels, jnp.stack([place[turn] for turn in moving]).astype(jnp.int32))
        for turn, panel in zip(moving, picked):
            lefts[turn] = (to_reader(panel, turn)[None], 0)
            row_turns[turn] = to_reader(row_turns[turn], turn)

    def right_of(held, turn):
        if turn % rows_n == 0:
            return held
        return lax.ppermute(held, "row", [(r, (r - turn) % rows_n) for r in range(rows_n)])

    rows_at = jnp.stack(row_turns)
    cols_at = jnp.stack([right_of(right_places, turn) for turn in range(STEPS)])
    codes = rows_at[:, :, :, None] * CB + cols_at[:, :, None, :]
    order = (jnp.arange(nc, dtype=jnp.int32) + nc - half * rep) % nc
    listed = codes[..., None] == slots
    where_to = nc - jnp.sum(jnp.where(listed, nc - order, 0), axis=-1, dtype=jnp.int32)
    scalars = jnp.concatenate([where_to.reshape(-1), odd])

    def add(totals, chunks):
        return accumulate(scalars, lefts, chunks, totals, nc)

    def received(stage):
        return [(z[stage], 0, Z_CHUNKS[stage - 1]), (x[stage], 0, X_CHUNKS[stage - 1])]

    x[2] = along_x(sent((right, 0)))
    totals = add(None, [(right, q, ((0, q), (0, q))) for q in range(QUARTERS)])
    z[3] = along_z(sent((right, 2), None, z[1], totals))
    x[3] = along_x(sent(z[1], (right, 1), x[1], totals))
    totals = add(totals, received(1))
    x[4] = along_x(sent(z[2], (right, 2), x[2], totals))
    z[4] = along_z(sent((right, 3), x[3], totals))
    totals = add(totals, received(2))
    x[5] = along_x(sent(z[3], z[1], totals))
    z[5] = along_z(sent(x[1], x[4], totals))
    totals = add(totals, received(3))
    x[6] = along_x(sent(z[4], z[2], totals))
    z[6] = along_z(x[5])
    totals = add(totals, received(4))
    x[7] = along_x(sent(z[5], z[3], totals))
    z[7] = along_z(x[6])
    totals = add(totals, received(5))
    totals = add(totals, received(6))
    totals = add(totals, received(7))
    other = lax.ppermute(totals[half:nc], "rep", [(0, 1), (1, 0)])
    return (totals[:half] + other)[None, None]


def solution(mesh):
    in_specs = (
        P("row", "rep", "col", None, None, None, None, None),
        P("row", "rep", "col", None, None, None),
        P("rep", "row", "col", None, None, None, None),
        P("rep", "row", "col", None, None),
        P("row", "col", None),
    )
    out_specs = P("row", "col", "rep", None, None)
    return jax.shard_map(shards, mesh=mesh, in_specs=in_specs, out_specs=out_specs, check_vma=False)
```

time: 222 us -> 359 us (1.62)
  Pallas kernels: 0 us -> 274 us
  waiting for transfers between devices: 143 us -> 40.1 us
  matrix products: 39.9 us -> 0 us
  local copies, waits for them, and re-layouts: 1.46 us -> 16.5 us
  between operations: 13.5 us -> 0.42 us
    pallas_call x0 -> x20, Pallas kernels: none -> 274 us  [the longest x12 252 us: copy_call(): pl.pallas_call(kernel, in_specs=[pl.BlockSpec(memory_space=pltpu.SMEM)] +...]
    ppermute x12 -> x22, waiting for transfers between devices: 117 us -> 40.1 us  [the longest x7 23.8 us: along_x(): return lax.ppermute(chunk, 'row', x_pairs)]
    dot_general x8 -> x0, matrix products: 39.9 us -> none  [the longest x4 23 us: turn_products(): jnp.einsum('kaxy,kbyz->kabxz', left_blocks, right_blocks, precision=highest)]
    reduce_scatter x1 -> x0, waiting for transfers between devices: 26 us -> none  [shards(): shares = lax.psum_scatter(totals, 'rep', scatter_dimension=0, tiled=True)]
    unnamed x4 -> x40, local copies, waits for them, and re-layouts: 0.01 us -> 15.4 us
    ppermute x12 -> x22, starting transfers between devices: 22.5 us -> 25.2 us  [the longest x7 9.97 us: along_z(): return lax.ppermute(chunk, 'row', z_pairs)]
  transfers between devices with their start and end apart: 13 -> 22, of which waited for: 8 -> 5; matrix products, arithmetic and copies ran while one was open for 12% -> 1% of each run, Pallas kernels for 0% -> 76%
where the time goes in v2:
time: 359 us
  Pallas kernels  274 us (76%)
  waiting for transfers between devices  40.1 us (11%)
  starting transfers between devices  25.2 us (7%)
  local copies, waits for them, and re-layouts  16.5 us (5%)
    pallas_call x12, Pallas kernels, copy_call(): pl.pallas_call(kernel, in_specs=[pl.BlockSpec(memory_space=pltpu.SMEM)] +...  252 us
    ppermute x7, waiting for transfers between devices, along_x(): return lax.ppermute(chunk, 'row', x_pairs)  23.8 us
    pallas_call x8, Pallas kernels, accumulate(): pl.pallas_call(kernel, grid_spec=pltpu.PrefetchScalarGridSpec(num_scalar_...  21.7 us
    unnamed x40, local copies, waits for them, and re-layouts  15.4 us
    ppermute x1, waiting for transfers between devices, shards(): other = lax.ppermute(totals[half:nc], 'rep', [(0, 1), (1, 0)])  14.4 us
    ppermute x7, starting transfers between devices, along_z(): return lax.ppermute(chunk, 'row', z_pairs)  9.97 us
  transfers between devices with their start and end apart: 22, of which 5 were waited for; matrix products, arithmetic and copies ran while one was open for 1% of the time, Pallas kernels for 76%

profile of v2, /device:TPU:0, one launch (start us, length us, event | category | flops | bytes accessed | tf_op | source)
XLA Modules:
  0.0 358.5 jit_solution(17652864417784870485)
XLA Ops:
  0.0 5.0 %collective-permute-start.4 = (s32[8,4]{0,1:T(4,128)}, s32[8,4]{0,1:T(4,128)S(1)}, u32[]{:S(2)}, u32[]{:S(2)}) collective-permute-start(s32[8,4]{0,1:T(4,128)} %bitcast.58), channel_id=1, source_target_pairs={{0,20},{4,24},{8,28},{12,0},{16,4},{20,8},{24,12},{28,16},{1,21},{... | collective-permute-start | bytes 392 | tf_op jit(solution)/shard_map/ppermute | solution.py:219
  5.0 1.3 collective-permute-start.3
  6.8 0.8 slice_bitcast_fusion.1
  8.1 17.0 %pick.11 = f32[2,4,128,128]{3,2,1,0:T(8,128)} custom-call(s32[1]{0:T(128)} %bitcast.12.odd_ref, f32[8,4,128,128]{3,2,1,0:T(8,128)} %bitcast.25, f32[8,4,128,128]{3,2,1,0:T(8,128)} %bitcast.26), custom_call_target="tpu_custom_call" | custom-call | bytes 1048576 | tf_op jit(solution)/shard_map/pick/pallas_call | solution.py:38
  25.1 17.0 %pick.15 = f32[2,4,128,128]{3,2,1,0:T(8,128)} custom-call(s32[1]{0:T(128)} %bitcast.12.odd_ref, f32[8,4,128,128]{3,2,1,0:T(8,128)} %bitcast.27, f32[8,4,128,128]{3,2,1,0:T(8,128)} %bitcast.28), custom_call_target="tpu_custom_call" | custom-call | bytes 1048576 | tf_op jit(solution)/shard_map/pick/pallas_call | solution.py:38
  42.1 17.0 %pick.12 = f32[2,4,128,128]{3,2,1,0:T(8,128)} custom-call(s32[1]{0:T(128)} %bitcast.12.odd_ref, f32[8,4,128,128]{3,2,1,0:T(8,128)} %bitcast.29, f32[8,4,128,128]{3,2,1,0:T(8,128)} %bitcast.30), custom_call_target="tpu_custom_call" | custom-call | bytes 1048576 | tf_op jit(solution)/shard_map/pick/pallas_call | solution.py:38
  59.8 65.4 %pick_panels.1 = (f32[8,2,128,128]{3,2,1,0:T(8,128)}, f32[8,2,128,128]{3,2,1,0:T(8,128)}) custom-call(s32[2]{0:T(128)} %pad_add_fusion.2.which_ref, f32[3,8,2,128,128]{4,3,2,1,0:T(8,128)} %bitcast.40), custom_call_target="tpu_custom_call" | custom-call | bytes 4194304 | tf_op jit(solution)/shard_map/pick_panels/pallas_call | solution.py:38
  125.2 1.6 collective-permute-start.13
  127.4 4.0 %collective-permute-start.11 = (f32[2,4,128,128]{3,2,1,0:T(8,128)}, f32[2,4,128,128]{3,2,1,0:T(8,128)}, u32[]{:S(2)}, u32[]{:S(2)}) collective-permute-start(f32[2,4,128,128]{3,2,1,0:T(8,128)} %pick.15), channel_id=1, source_target_pairs={{0,24},{4,28},{8,0},{12,4},{16,8},{20,12},{24,16},{28,20},{1,25},{... | collective-permute-start | bytes 1572872 | tf_op jit(solution)/shard_map/ppermute | solution.py:187
  131.5 0.7 select_reduce_fusion
  132.5 1.9 copy-done.11
  134.4 2.0 accumulate.8.refs_1_.refs_4_
  136.4 1.2 copy-done.1
  137.6 13.1 %collective-permute-done.7.refs_0_.refs_3_.even_ref = f32[2,4,128,128]{3,2,1,0:T(8,128)} collective-permute-done((f32[2,4,128,128]{3,2,1,0:T(8,128)}, f32[2,4,128,128]{3,2,1,0:T(8,128)}, u32[]{:S(2)}, u32[]{:S(2)}) %collective-permute-start.7) | collective-permute-done | bytes 524320 | tf_op jit(solution)/shard_map/ppermute | solution.py:190
  150.7 17.0 %pick.13 = f32[2,4,128,128]{3,2,1,0:T(8,128)} custom-call(s32[1]{0:T(128)} %bitcast.12.odd_ref, f32[2,4,128,128]{3,2,1,0:T(8,128)} %collective-permute-done.6.even_ref.refs_2_.refs_0_.other_ref, f32[8,4,128,128]{3,2,1,0:T(8,128)} %bitcast.31, f32[2,4,128,128]{3,2,1,0:T(8,128)} %collective-permute-done.7.refs_0_.refs_3_.even_ref, f32[25,128,128]{2,1,0:T(8,128)} %copy-done.1), custom_call_target="tpu_custom_call" | custom-call | bytes 1048576 | tf_op jit(solution)/shard_map/pick/pallas_call | solution.py:38
  167.7 1.6 collective-permute-start.8
  169.2 17.0 %pick.16 = f32[2,4,128,128]{3,2,1,0:T(8,128)} custom-call(s32[1]{0:T(128)} %bitcast.12.odd_ref, f32[8,4,128,128]{3,2,1,0:T(8,128)} %bitcast.32, f32[8,4,128,128]{3,2,1,0:T(8,128)} %bitcast.33, f32[2,4,128,128]{3,2,1,0:T(8,128)} %collective-permute-done.6.even_ref.refs_2_.refs_0_.other_ref, f32[25,128,128]{2,1,0:T(8,128)} %copy-done.1), custom_call_target="tpu_custom_call" | custom-call | bytes 1048576 | tf_op jit(solution)/shard_map/pick/pallas_call | solution.py:38
  186.7 1.9 copy-done.12
  188.6 2.9 accumulate.9.refs_0_.refs_4_.refs_1_
  191.6 1.2 copy-done.3
  192.7 17.0 %pick.18 = f32[2,4,128,128]{3,2,1,0:T(8,128)} custom-call(s32[1]{0:T(128)} %bitcast.12.odd_ref, f32[2,4,128,128]{3,2,1,0:T(8,128)} %collective-permute-done.11.refs_2_.other_ref.even_ref, f32[8,4,128,128]{3,2,1,0:T(8,128)} %bitcast.34, f32[2,4,128,128]{3,2,1,0:T(8,128)} %collective-permute-done.13.refs_3_.refs_0_, f32[25,128,128]{2,1,0:T(8,128)} %copy-done.3), custom_call_target="tpu_custom_call" | custom-call | bytes 1048576 | tf_op jit(solution)/shard_map/pick/pallas_call | solution.py:38
  209.9 17.0 %pick.14 = f32[2,4,128,128]{3,2,1,0:T(8,128)} custom-call(s32[1]{0:T(128)} %bitcast.12.odd_ref, f32[8,4,128,128]{3,2,1,0:T(8,128)} %bitcast.35, f32[2,4,128,128]{3,2,1,0:T(8,128)} %collective-permute-done.8.other_ref.refs_4_, f32[25,128,128]{2,1,0:T(8,128)} %copy-done.3), custom_call_target="tpu_custom_call" | custom-call | bytes 1048576 | tf_op jit(solution)/shard_map/pick/pallas_call | solution.py:38
  226.9 3.6 %collective-permute-start.10 = (f32[2,4,128,128]{3,2,1,0:T(8,128)}, f32[2,4,128,128]{3,2,1,0:T(8,128)}, u32[]{:S(2)}, u32[]{:S(2)}) collective-permute-start(f32[2,4,128,128]{3,2,1,0:T(8,128)} %pick.14), channel_id=1, source_target_pairs={{0,24},{4,28},{8,0},{12,4},{16,8},{20,12},{24,16},{28,20},{1,25},{... | collective-permute-start | bytes 1572872 | tf_op jit(solution)/shard_map/ppermute | solution.py:187
  230.5 1.9 copy-done.13
  232.4 2.9 accumulate.10.refs_5_.refs_0_
  235.3 1.2 copy-done.5
  236.5 17.0 %pick.21 = f32[2,4,128,128]{3,2,1,0:T(8,128)} custom-call(s32[1]{0:T(128)} %bitcast.12.odd_ref, f32[2,4,128,128]{3,2,1,0:T(8,128)} %collective-permute-done.12.refs_3_.other_ref.even_ref, f32[2,4,128,128]{3,2,1,0:T(8,128)} %collective-permute-done.6.even_ref.refs_2_.refs_0_.other_ref, f32[25,128,128]{2,1,0:T(8,128)} %copy-done.5), custom_call_target="tpu_custom_call" | custom-call | bytes 1048576 | tf_op jit(solution)/shard_map/pick/pallas_call | solution.py:38
  253.5 0.7 collective-permute-start.19
  254.2 17.0 %pick.19 = f32[2,4,128,128]{3,2,1,0:T(8,128)} custom-call(s32[1]{0:T(128)} %bitcast.12.odd_ref, f32[2,4,128,128]{3,2,1,0:T(8,128)} %collective-permute-done.7.refs_0_.refs_3_.even_ref, f32[2,4,128,128]{3,2,1,0:T(8,128)} %collective-permute-done.16.other_ref.refs_5_, f32[25,128,128]{2,1,0:T(8,128)} %copy-done.5), custom_call_target="tpu_custom_call" | custom-call | bytes 1048576 | tf_op jit(solution)/shard_map/pick/pallas_call | solution.py:38
  271.2 1.9 copy-done.14
  273.1 2.7 accumulate.11.refs_0_.refs_6_
  275.9 1.2 copy-done.7
  277.0 17.0 %pick.17 = f32[2,4,128,128]{3,2,1,0:T(8,128)} custom-call(s32[1]{0:T(128)} %bitcast.12.odd_ref, f32[2,4,128,128]{3,2,1,0:T(8,128)} %collective-permute-done.10.even_ref.refs_4_, f32[2,4,128,128]{3,2,1,0:T(8,128)} %collective-permute-done.11.refs_2_.other_ref.even_ref, f32[25,128,128]{2,1,0:T(8,128)} %copy-done.7), custom_call_target="tpu_custom_call" | custom-call | bytes 1048576 | tf_op jit(solution)/shard_map/pick/pallas_call | solution.py:38
  294.0 1.5 collective-permute-start.14
  296.5 1.9 copy-done.15
  298.4 2.8 accumulate.12.refs_0_.refs_6_
  301.2 1.2 copy-done.9
  302.4 5.8 %collective-permute-done.14.refs_4_ = f32[2,4,128,128]{3,2,1,0:T(8,128)} collective-permute-done((f32[2,4,128,128]{3,2,1,0:T(8,128)}, f32[2,4,128,128]{3,2,1,0:T(8,128)}, u32[]{:S(2)}, u32[]{:S(2)}) %collective-permute-start.14) | collective-permute-done | bytes 524320 | tf_op jit(solution)/shard_map/ppermute | solution.py:190
  308.6 1.8 collective-permute-done.17.even_ref.refs_4_
  310.5 17.0 %pick.20 = f32[2,4,128,128]{3,2,1,0:T(8,128)} custom-call(s32[1]{0:T(128)} %bitcast.12.odd_ref, f32[2,4,128,128]{3,2,1,0:T(8,128)} %collective-permute-done.17.even_ref.refs_4_, f32[2,4,128,128]{3,2,1,0:T(8,128)} %collective-permute-done.12.refs_3_.other_ref.even_ref, f32[25,128,128]{2,1,0:T(8,128)} %copy-done.9), custom_call_target="tpu_custom_call" | custom-call | bytes 1048576 | tf_op jit(solution)/shard_map/pick/pallas_call | solution.py:38
  327.5 0.7 collective-permute-start.18
  328.1 3.0 accumulate.13.refs_5_
  331.2 2.9 accumulate.14.refs_5_
  334.1 4.9 %collective-permute-done.18.refs_4_ = f32[2,4,128,128]{3,2,1,0:T(8,128)S(1)} collective-permute-done((f32[2,4,128,128]{3,2,1,0:T(8,128)}, f32[2,4,128,128]{3,2,1,0:T(8,128)S(1)}, u32[]{:S(2)}, u32[]{:S(2)}) %collective-permute-start.18) | collective-permute-done | bytes 524320 | tf_op jit(solution)/shard_map/ppermute | solution.py:190
  339.0 2.4 accumulate.15
  341.5 1.6 collective-permute-start.21
  343.1 14.4 %collective-permute-done.21 = f32[12,128,128]{2,1,0:T(8,128)S(1)} collective-permute-done((f32[12,128,128]{2,1,0:T(8,128)S(1)}, f32[12,128,128]{2,1,0:T(8,128)S(1)}, u32[]{:S(2)}, u32[]{:S(2)}) %collective-permute-start.21) | collective-permute-done | bytes 786464 | tf_op jit(solution)/shard_map/ppermute | solution.py:254
  357.5 1.0 fusion
  (69 shorter events, 4.8 us)
Async XLA Ops:
  0.0 127.2 %collective-permute-start.4 = (s32[8,4]{0,1:T(4,128)}, s32[8,4]{0,1:T(4,128)S(1)}, u32[]{:S(2)}, u32[]{:S(2)}) collective-permute-start(s32[8,4]{0,1:T(4,128)} %bitcast.58), channel_id=1, source_target_pairs={{0,20},{4,24},{8,28},{12,0},{16,4},{20,8},{24,12},{28,16},{1,21},{... | collective-permute-start | bytes 392 | tf_op jit(solution)/shard_map/ppermute | solution.py:219
  5.0 122.5 %collective-permute-start.3 = (s32[8,4]{0,1:T(4,128)}, s32[8,4]{0,1:T(4,128)S(1)}, u32[]{:S(2)}, u32[]{:S(2)}) collective-permute-start(s32[8,4]{0,1:T(4,128)} %bitcast.59), channel_id=1, source_target_pairs={{0,24},{4,28},{8,0},{12,4},{16,8},{20,12},{24,16},{28,20},{1,25},{... | collective-permute-start | bytes 392 | tf_op jit(solution)/shard_map/ppermute | solution.py:219
  6.3 125.1 %collective-permute-start.2 = (s32[8,4]{0,1:T(4,128)}, s32[8,4]{0,1:T(4,128)S(1)}, u32[]{:S(2)}, u32[]{:S(2)}) collective-permute-start(s32[8,4]{0,1:T(4,128)} %bitcast.60), channel_id=1, source_target_pairs={{0,28},{4,0},{8,4},{12,8},{16,12},{20,16},{24,20},{28,24},{1,29},{... | collective-permute-start | bytes 392 | tf_op jit(solution)/shard_map/ppermute | solution.py:219
  7.6 117.6 %collective-permute-start = (s32[8,2]{0,1:T(2,128)S(1)}, s32[8,2]{0,1:T(2,128)S(1)}, u32[]{:S(2)}, u32[]{:S(2)}) collective-permute-start(s32[8,2]{0,1:T(2,128)S(1)} %get-tuple-element.10), channel_id=1, source_target_pairs={{0,2},{2,0},{1,3},{3,1},{4,6},{6,4},{5,7},{7,5},{8,10},{10,8},{9,1... | collective-permute-start | bytes 200 | tf_op jit(solution)/shard_map/ppermute | solution.py:204
  7.6 119.2 %collective-permute-start.1 = (s32[8,2]{0,1:T(2,128)S(1)}, s32[8,2]{0,1:T(2,128)S(1)}, u32[]{:S(2)}, u32[]{:S(2)}) collective-permute-start(s32[8,2]{0,1:T(2,128)S(1)} %get-tuple-element.11), channel_id=1, source_target_pairs={{0,2},{2,0},{1,3},{3,1},{4,6},{6,4},{5,7},{7,5},{8,10},{10,8},{9,1... | collective-permute-start | bytes 200 | tf_op jit(solution)/shard_map/ppermute | solution.py:204
  59.1 72.3 %copy-start.18 = (s32[1,1,1,8,4]{3,4,2,1,0:T(4,128)S(1)}, s32[1,1,1,8,4]{3,4,2,1,0:T(4,128)}, u32[]{:S(2)}) copy-start(s32[1,1,1,8,4]{3,4,2,1,0:T(4,128)} %param.8) | copy-start | bytes 388
  59.1 72.4 %copy-start.19 = (s32[1,1,24]{2,1,0:T(1,128)S(1)}, s32[1,1,24]{2,1,0:T(1,128)}, u32[]{:S(2)}) copy-start(s32[1,1,24]{2,1,0:T(1,128)} %param.9) | copy-start | bytes 292
  59.8 72.7 %copy-start = (f32[1,1,1,8,4,128,128]{6,5,4,3,2,1,0:T(8,128)S(1)}, f32[1,1,1,8,4,128,128]{6,5,4,3,2,1,0:T(8,128)}, u32[]{:S(2)}) copy-start(f32[1,1,1,8,4,128,128]{6,5,4,3,2,1,0:T(8,128)} %param.7) | copy-start | bytes 6291460
  125.2 67.5 %collective-permute-start.13 = (f32[2,4,128,128]{3,2,1,0:T(8,128)}, f32[2,4,128,128]{3,2,1,0:T(8,128)}, u32[]{:S(2)}, u32[]{:S(2)}) collective-permute-start(f32[2,4,128,128]{3,2,1,0:T(8,128)} %pick.11), channel_id=1, source_target_pairs={{0,4},{4,0},{8,12},{12,8},{16,20},{20,16},{24,28},{28,24},{1,5},{5... | collective-permute-start | bytes 1572872 | tf_op jit(solution)/shard_map/ppermute | solution.py:190
  126.8 23.9 %collective-permute-start.6 = (f32[2,4,128,128]{3,2,1,0:T(8,128)}, f32[2,4,128,128]{3,2,1,0:T(8,128)}, u32[]{:S(2)}, u32[]{:S(2)}) collective-permute-start(f32[2,4,128,128]{3,2,1,0:T(8,128)} %pick.11), channel_id=1, source_target_pairs={{0,24},{4,28},{8,0},{12,4},{16,8},{20,12},{24,16},{28,20},{1,25},{... | collective-permute-start | bytes 1572872 | tf_op jit(solution)/shard_map/ppermute | solution.py:187
  127.2 23.4 %collective-permute-start.7 = (f32[2,4,128,128]{3,2,1,0:T(8,128)}, f32[2,4,128,128]{3,2,1,0:T(8,128)}, u32[]{:S(2)}, u32[]{:S(2)}) collective-permute-start(f32[2,4,128,128]{3,2,1,0:T(8,128)} %pick.12), channel_id=1, source_target_pairs={{0,4},{4,0},{8,12},{12,8},{16,20},{20,16},{24,28},{28,24},{1,5},{5... | collective-permute-start | bytes 1572872 | tf_op jit(solution)/shard_map/ppermute | solution.py:190
  127.4 65.3 %collective-permute-start.11 = (f32[2,4,128,128]{3,2,1,0:T(8,128)}, f32[2,4,128,128]{3,2,1,0:T(8,128)}, u32[]{:S(2)}, u32[]{:S(2)}) collective-permute-start(f32[2,4,128,128]{3,2,1,0:T(8,128)} %pick.15), channel_id=1, source_target_pairs={{0,24},{4,28},{8,0},{12,4},{16,8},{20,12},{24,16},{28,20},{1,25},{... | collective-permute-start | bytes 1572872 | tf_op jit(solution)/shard_map/ppermute | solution.py:187
  131.5 55.3 %collective-permute-start.9 = (f32[8,2,128,128]{3,2,1,0:T(8,128)}, f32[8,2,128,128]{3,2,1,0:T(8,128)S(1)}, u32[]{:S(2)}, u32[]{:S(2)}) collective-permute-start(f32[8,2,128,128]{3,2,1,0:T(8,128)} %get-tuple-element.8), channel_id=1, source_target_pairs={{0,2},{2,0},{1,3},{3,1},{4,6},{6,4},{5,7},{7,5},{8,10},{10,8},{9,1... | collective-permute-start | bytes 3145736 | tf_op jit(solution)/shard_map/ppermute | solution.py:204
  132.5 1.9 copy-start.11
  136.4 1.2 copy-start.1
  167.7 19.1 %copy-start.2 = (f32[25,128,128]{2,1,0:T(8,128)S(1)}, f32[25,128,128]{2,1,0:T(8,128)}, u32[]{:S(2)}) copy-start(f32[25,128,128]{2,1,0:T(8,128)} %copy-done.1) | copy-start | bytes 4915204
  167.7 42.2 %collective-permute-start.8 = (f32[2,4,128,128]{3,2,1,0:T(8,128)}, f32[2,4,128,128]{3,2,1,0:T(8,128)}, u32[]{:S(2)}, u32[]{:S(2)}) collective-permute-start(f32[2,4,128,128]{3,2,1,0:T(8,128)} %pick.13), channel_id=1, source_target_pairs={{0,4},{4,0},{8,12},{12,8},{16,20},{20,16},{24,28},{28,24},{1,5},{5... | collective-permute-start | bytes 1572872 | tf_op jit(solution)/shard_map/ppermute | solution.py:190
  186.2 50.3 %collective-permute-start.12 = (f32[2,4,128,128]{3,2,1,0:T(8,128)}, f32[2,4,128,128]{3,2,1,0:T(8,128)}, u32[]{:S(2)}, u32[]{:S(2)}) collective-permute-start(f32[2,4,128,128]{3,2,1,0:T(8,128)} %pick.16), channel_id=1, source_target_pairs={{0,24},{4,28},{8,0},{12,4},{16,8},{20,12},{24,16},{28,20},{1,25},{... | collective-permute-start | bytes 1572872 | tf_op jit(solution)/shard_map/ppermute | solution.py:187
  186.7 1.9 copy-start.12
  191.5 1.2 copy-start.3
  209.7 44.5 %collective-permute-start.16 = (f32[2,4,128,128]{3,2,1,0:T(8,128)}, f32[2,4,128,128]{3,2,1,0:T(8,128)}, u32[]{:S(2)}, u32[]{:S(2)}) collective-permute-start(f32[2,4,128,128]{3,2,1,0:T(8,128)} %pick.18), channel_id=1, source_target_pairs={{0,4},{4,0},{8,12},{12,8},{16,20},{20,16},{24,28},{28,24},{1,5},{5... | collective-permute-start | bytes 1572872 | tf_op jit(solution)/shard_map/ppermute | solution.py:190
  209.8 20.7 %copy-start.4 = (f32[25,128,128]{2,1,0:T(8,128)S(1)}, f32[25,128,128]{2,1,0:T(8,128)}, u32[]{:S(2)}) copy-start(f32[25,128,128]{2,1,0:T(8,128)} %copy-done.3) | copy-start | bytes 4915204
  209.8 86.7 %collective-permute-start.5 = (f32[8,2,128,128]{3,2,1,0:T(8,128)}, f32[8,2,128,128]{3,2,1,0:T(8,128)}, u32[]{:S(2)}, u32[]{:S(2)}) collective-permute-start(f32[8,2,128,128]{3,2,1,0:T(8,128)} %get-tuple-element.7), channel_id=1, source_target_pairs={{0,2},{2,0},{1,3},{3,1},{4,6},{6,4},{5,7},{7,5},{8,10},{10,8},{9,1... | collective-permute-start | bytes 3145736 | tf_op jit(solution)/shard_map/ppermute | solution.py:204
  226.9 50.1 %collective-permute-start.10 = (f32[2,4,128,128]{3,2,1,0:T(8,128)}, f32[2,4,128,128]{3,2,1,0:T(8,128)}, u32[]{:S(2)}, u32[]{:S(2)}) collective-permute-start(f32[2,4,128,128]{3,2,1,0:T(8,128)} %pick.14), channel_id=1, source_target_pairs={{0,24},{4,28},{8,0},{12,4},{16,8},{20,12},{24,16},{28,20},{1,25},{... | collective-permute-start | bytes 1572872 | tf_op jit(solution)/shard_map/ppermute | solution.py:187
  230.5 1.9 copy-start.13
  235.3 1.2 copy-start.5
  253.5 17.7 %copy-start.6 = (f32[25,128,128]{2,1,0:T(8,128)S(1)}, f32[25,128,128]{2,1,0:T(8,128)}, u32[]{:S(2)}) copy-start(f32[25,128,128]{2,1,0:T(8,128)} %copy-done.5) | copy-start | bytes 4915204
  253.5 42.5 %collective-permute-start.19 = (f32[2,4,128,128]{3,2,1,0:T(8,128)}, f32[2,4,128,128]{3,2,1,0:T(8,128)}, u32[]{:S(2)}, u32[]{:S(2)}) collective-permute-start(f32[2,4,128,128]{3,2,1,0:T(8,128)} %pick.21), channel_id=1, source_target_pairs={{0,4},{4,0},{8,12},{12,8},{16,20},{20,16},{24,28},{28,24},{1,5},{5... | collective-permute-start | bytes 1572872 | tf_op jit(solution)/shard_map/ppermute | solution.py:190
  271.2 1.9 copy-start.14
  275.8 1.2 copy-start.7
  277.0 18.5 %copy-start.17 = (f32[2,4,128,128]{3,2,1,0:T(8,128)S(1)}, f32[2,4,128,128]{3,2,1,0:T(8,128)}, u32[]{:S(2)}) copy-start(f32[2,4,128,128]{3,2,1,0:T(8,128)} %pick.19) | copy-start | bytes 1572868
  277.0 19.4 %copy-start.8 = (f32[25,128,128]{2,1,0:T(8,128)S(1)}, f32[25,128,128]{2,1,0:T(8,128)}, u32[]{:S(2)}) copy-start(f32[25,128,128]{2,1,0:T(8,128)} %copy-done.7) | copy-start | bytes 4915204
  294.0 14.1 %collective-permute-start.14 = (f32[2,4,128,128]{3,2,1,0:T(8,128)}, f32[2,4,128,128]{3,2,1,0:T(8,128)}, u32[]{:S(2)}, u32[]{:S(2)}) collective-permute-start(f32[2,4,128,128]{3,2,1,0:T(8,128)} %pick.17), channel_id=1, source_target_pairs={{0,4},{4,0},{8,12},{12,8},{16,20},{20,16},{24,28},{28,24},{1,5},{5... | collective-permute-start | bytes 1572872 | tf_op jit(solution)/shard_map/ppermute | solution.py:190
  295.5 14.9 %collective-permute-start.17 = (f32[2,4,128,128]{3,2,1,0:T(8,128)S(1)}, f32[2,4,128,128]{3,2,1,0:T(8,128)}, u32[]{:S(2)}, u32[]{:S(2)}) collective-permute-start(f32[2,4,128,128]{3,2,1,0:T(8,128)S(1)} %copy-done.17), channel_id=1, source_target_pairs={{0,24},{4,28},{8,0},{12,4},{16,8},{20,12},{24,16},{28,20},{1,25},{... | collective-permute-start | bytes 1572872 | tf_op jit(solution)/shard_map/ppermute | solution.py:187
  296.0 35.2 %collective-permute-start.20 = (f32[2,4,128,128]{3,2,1,0:T(8,128)}, f32[2,4,128,128]{3,2,1,0:T(8,128)}, u32[]{:S(2)}, u32[]{:S(2)}) collective-permute-start(f32[2,4,128,128]{3,2,1,0:T(8,128)} %collective-permute-done.19.refs_5_), channel_id=1, source_target_pairs={{0,24},{4,28},{8,0},{12,4},{16,8},{20,12},{24,16},{28,20},{1,25},{... | collective-permute-start | bytes 1572872 | tf_op jit(solution)/shard_map/ppermute | solution.py:187
  296.5 1.9 copy-start.15
  301.2 1.2 copy-start.9
  308.2 20.0 %copy-start.10 = (f32[25,128,128]{2,1,0:T(8,128)S(1)}, f32[25,128,128]{2,1,0:T(8,128)}, u32[]{:S(2)}) copy-start(f32[25,128,128]{2,1,0:T(8,128)} %copy-done.9) | copy-start | bytes 4915204
  308.2 25.9 %collective-permute-start.15 = (f32[2,4,128,128]{3,2,1,0:T(8,128)}, f32[2,4,128,128]{3,2,1,0:T(8,128)}, u32[]{:S(2)}, u32[]{:S(2)}) collective-permute-start(f32[2,4,128,128]{3,2,1,0:T(8,128)} %collective-permute-done.14.refs_4_), channel_id=1, source_target_pairs={{0,24},{4,28},{8,0},{12,4},{16,8},{20,12},{24,16},{28,20},{1,25},{... | collective-permute-start | bytes 1572872 | tf_op jit(solution)/shard_map/ppermute | solution.py:187
  327.5 11.5 %collective-permute-start.18 = (f32[2,4,128,128]{3,2,1,0:T(8,128)}, f32[2,4,128,128]{3,2,1,0:T(8,128)S(1)}, u32[]{:S(2)}, u32[]{:S(2)}) collective-permute-start(f32[2,4,128,128]{3,2,1,0:T(8,128)} %pick.20), channel_id=1, source_target_pairs={{0,4},{4,0},{8,12},{12,8},{16,20},{20,16},{24,28},{28,24},{1,5},{5... | collective-permute-start | bytes 1572872 | tf_op jit(solution)/shard_map/ppermute | solution.py:190
  331.2 7.8 %copy-start.16 = (f32[1,1,1,3,8,2,128,128]{7,6,5,4,3,2,1,0:T(8,128)S(1)}, f32[1,1,1,3,8,2,128,128]{7,6,5,4,3,2,1,0:T(8,128)}, u32[]{:S(2)}) copy-start(f32[1,1,1,3,8,2,128,128]{7,6,5,4,3,2,1,0:T(8,128)} %param.5) | copy-start | bytes 9437188
  341.5 16.0 %collective-permute-start.21 = (f32[12,128,128]{2,1,0:T(8,128)S(1)}, f32[12,128,128]{2,1,0:T(8,128)S(1)}, u32[]{:S(2)}, u32[]{:S(2)}) collective-permute-start(f32[12,128,128]{2,1,0:T(8,128)S(1)} %slice.19), channel_id=1, source_target_pairs={{0,1},{1,0},{2,3},{3,2},{4,5},{5,4},{6,7},{7,6},{8,9},{9,8},{10,11... | collective-permute-start | bytes 2359304 | tf_op jit(solution)/shard_map/ppermute | solution.py:254

commit v3 on v2

--- a/solution.py
+++ b/solution.py
@@ -32,54 +32,60 @@
 )
 
 
-def copy_call(kernel, scalar, operands, out_shapes, name):
-    any_spec = pl.BlockSpec(memory_space=pl.ANY)
-    moved = sum(8 * shape.size for shape in out_shapes)
+def pick(odd, per, even_part, odd_part, *others):
+    parts = [even_part] if even_part is odd_part else [even_part, odd_part]
+    array = even_part[0]
+
+    def kernel(odd_ref, *refs):
+        out_ref = refs[-1]
+        if len(parts) == 1:
+            out_ref[...] = refs[0][...]
+            return
+
+        def copy_from(ref):
+            out_ref[...] = ref[...]
+
+        pl.when(odd_ref[0] == 0)(lambda: copy_from(refs[0]))
+        pl.when(odd_ref[0] != 0)(lambda: copy_from(refs[1]))
+
+    def spec(at):
+        return pl.BlockSpec((per,) + array.shape[1:], lambda g, *_: (at, 0, 0, 0))
+
+    out_shape = jax.ShapeDtypeStruct((per,) + array.shape[1:], array.dtype)
     return pl.pallas_call(
         kernel,
-        in_specs=[pl.BlockSpec(memory_space=pltpu.SMEM)] + [any_spec] * len(operands),
-        out_specs=[any_spec] * len(out_shapes),
-        out_shape=out_shapes,
-        scratch_shapes=[pltpu.SemaphoreType.DMA((len(out_shapes),))],
-        cost_estimate=pl.CostEstimate(flops=0, bytes_accessed=moved, transcendentals=0),
-        name=name,
-    )(scalar, *operands)
-
-
-def pick(odd, per, even_part, odd_part, *others):
-    (even_from, even_at), (odd_from, odd_at) = even_part, odd_part
-
-    def kernel(odd_ref, even_ref, other_ref, *refs):
-        out_ref, sems = refs[-2:]
-
-        def copy_from(ref, at):
-            copy = pltpu.make_async_copy(ref.at[pl.ds(at * per, per)], out_ref, sems.at[0])
-            copy.start()
-            copy.wait()
-
-        if even_part is odd_part:
-            copy_from(even_ref, even_at)
-        else:
-            pl.when(odd_ref[0] == 0)(lambda: copy_from(even_ref, even_at))
-            pl.when(odd_ref[0] != 0)(lambda: copy_from(other_ref, odd_at))
-
-    out_shape = jax.ShapeDtypeStruct((per,) + even_from.shape[1:], even_from.dtype)
-    return copy_call(kernel, odd, [even_from, odd_from, *others], [out_shape], "pick")[0]
-
-
-def pick_panels(panels, which):
-    count = which.shape[0]
-
-    def kernel(which_ref, panels_ref, *refs):
-        sems = refs[-1]
-        copies = [pltpu.make_async_copy(panels_ref.at[which_ref[n]], refs[n], sems.at[n]) for n in range(count)]
-        for copy in copies:
-            copy.start()
-        for copy in copies:
-            copy.wait()
-
-    out_shape = jax.ShapeDtypeStruct(panels.shape[1:], panels.dtype)
-    return copy_call(kernel, which, [panels], [out_shape] * count, "pick_panels")
+        grid_spec=pltpu.PrefetchScalarGridSpec(
+            num_scalar_prefetch=1,
+            grid=(1,),
+            in_specs=[spec(at) for _, at in parts] + [pl.BlockSpec(memory_space=pl.ANY)] * len(others),
+            out_specs=spec(0),
+        ),
+        out_shape=out_shape,
+        compiler_params=pltpu.CompilerParams(vmem_limit_bytes=16 * 1024 * 1024),
+        cost_estimate=pl.CostEstimate(flops=0, bytes_accessed=8 * out_shape.size, transcendentals=0),
+        name="pick",
+    )(odd, *[part for part, _ in parts], *others)
+
+
+def pick_panel(panels, which):
+    _, kb, lpb, bs, _ = panels.shape
+    per = kb // QUARTERS
+
+    def kernel(which_ref, panel_ref, out_ref):
+        out_ref[...] = panel_ref[0]
+
+    return pl.pallas_call(
+        kernel,
+        grid_spec=pltpu.PrefetchScalarGridSpec(
+            num_scalar_prefetch=1,
+            grid=(QUARTERS,),
+            in_specs=[pl.BlockSpec((1, per, lpb, bs, bs), lambda g, which_ref: (which_ref[0], g, 0, 0, 0))],
+            out_specs=pl.BlockSpec((per, lpb, bs, bs), lambda g, which_ref: (g, 0, 0, 0)),
+        ),
+        out_shape=jax.ShapeDtypeStruct(panels.shape[1:], panels.dtype),
+        cost_estimate=pl.CostEstimate(flops=0, bytes_accessed=8 * kb * lpb * bs * bs, transcendentals=0),
+        name="pick_panel",
+    )(which.astype(jnp.int32).reshape(1), panels)
 
 
 def accumulate(scalars, lefts, chunks, totals, nc):
@@ -95,12 +101,13 @@
     def kernel(scalar_ref, *refs):
         left_refs = dict(zip(sides, refs))
         right_refs = refs[len(sides):len(sides) + len(chunks)]
-        out_ref = refs[-1]
+        out_ref, token_ref = refs[-2:]
+        token_ref[...] = jnp.zeros_like(token_ref)
         odd = scalar_ref[odd_at]
         if first:
             out_ref[...] = jnp.zeros_like(out_ref)
         else:
-            out_ref[...] = refs[-2][...]
+            out_ref[...] = refs[-3][...]
         for c, (_, _, (even_is, odd_is)) in enumerate(chunks):
             def one(c=c, even_is=even_is, odd_is=odd_is):
                 both = even_is != odd_is and even_is is not None and odd_is is not None
@@ -156,9 +163,9 @@
             num_scalar_prefetch=1,
             grid=(1,),
             in_specs=in_specs,
-            out_specs=total_spec,
+            out_specs=[total_spec, pl.BlockSpec((8, 128), lambda g, *_: (0, 0))],
         ),
-        out_shape=jax.ShapeDtypeStruct((nc + 1, bs, bs), f32),
+        out_shape=[jax.ShapeDtypeStruct((nc + 1, bs, bs), f32), jax.ShapeDtypeStruct((8, 128), f32)],
         input_output_aliases={} if first else {len(operands): 0},
         compiler_params=pltpu.CompilerParams(vmem_limit_bytes=32 * 1024 * 1024),
         cost_estimate=pl.CostEstimate(flops=flops, bytes_accessed=moved, transcendentals=0),
@@ -208,9 +215,8 @@
     lefts = [(panels, place[turn]) for turn in range(STEPS)]
     row_turns = [panel_rows[place[turn]] for turn in range(STEPS)]
     if moving:
-        picked = pick_panels(panels, jnp.stack([place[turn] for turn in moving]).astype(jnp.int32))
-        for turn, panel in zip(moving, picked):
-            lefts[turn] = (to_reader(panel, turn)[None], 0)
+        for turn in moving:
+            lefts[turn] = (to_reader(pick_panel(panels, place[turn]), turn)[None], 0)
             row_turns[turn] = to_reader(row_turns[turn], turn)
 
     def right_of(held, turn):
@@ -233,24 +239,24 @@
         return [(z[stage], 0, Z_CHUNKS[stage - 1]), (x[stage], 0, X_CHUNKS[stage - 1])]
 
     x[2] = along_x(sent((right, 0)))
-    totals = add(None, [(right, q, ((0, q), (0, q))) for q in range(QUARTERS)])
-    z[3] = along_z(sent((right, 2), None, z[1], totals))
-    x[3] = along_x(sent(z[1], (right, 1), x[1], totals))
-    totals = add(totals, received(1))
-    x[4] = along_x(sent(z[2], (right, 2), x[2], totals))
-    z[4] = along_z(sent((right, 3), x[3], totals))
-    totals = add(totals, received(2))
-    x[5] = along_x(sent(z[3], z[1], totals))
-    z[5] = along_z(sent(x[1], x[4], totals))
-    totals = add(totals, received(3))
-    x[6] = along_x(sent(z[4], z[2], totals))
+    totals, done = add(None, [(right, q, ((0, q), (0, q))) for q in range(QUARTERS)])
+    z[3] = along_z(sent((right, 2), None, z[1], done))
+    x[3] = along_x(sent(z[1], (right, 1), x[1], done))
+    totals, done = add(totals, received(1))
+    x[4] = along_x(sent(z[2], (right, 2), x[2], done))
+    z[4] = along_z(sent((right, 3), x[3], done))
+    totals, done = add(totals, received(2))
+    x[5] = along_x(sent(z[3], z[1], done))
+    z[5] = along_z(sent(x[1], x[4], done))
+    totals, done = add(totals, received(3))
+    x[6] = along_x(sent(z[4], z[2], done))
     z[6] = along_z(x[5])
-    totals = add(totals, received(4))
-    x[7] = along_x(sent(z[5], z[3], totals))
+    totals, done = add(totals, received(4))
+    x[7] = along_x(sent(z[5], z[3], done))
     z[7] = along_z(x[6])
-    totals = add(totals, received(5))
-    totals = add(totals, received(6))
-    totals = add(totals, received(7))
+    totals, done = add(totals, received(5))
+    totals, done = add(totals, received(6))
+    totals, done = add(totals, received(7))
     other = lax.ppermute(totals[half:nc], "rep", [(0, 1), (1, 0)])
     return (totals[:half] + other)[None, None]
 

time: 359 us -> 129 us (0.36)
  Pallas kernels: 274 us -> 32.7 us
  waiting for transfers between devices: 40.1 us -> 54 us
  local copies, waits for them, and re-layouts: 16.5 us -> 10.7 us
  starting transfers between devices: 25.2 us -> 28.9 us
    pallas_call x12 -> x13, Pallas kernels: 252 us -> 12.7 us  [the longest x2 7.03 us: pick_panel(): pl.pallas_call(kernel, grid_spec=pltpu.PrefetchScalarGridSpec(num_scalar_...]
    ppermute x7, waiting for transfers between devices: 1.86 us -> 9.04 us  [along_z(): return lax.ppermute(chunk, 'row', z_pairs)]
    unnamed x40 -> x28, local copies, waits for them, and re-layouts: 15.4 us -> 9.67 us
    ppermute x7, waiting for transfers between devices: 23.8 us -> 27.8 us  [along_x(): return lax.ppermute(chunk, 'row', x_pairs)]
  transfers between devices with their start and end apart: 22 -> 22, of which waited for: 5 -> 10; matrix products, arithmetic and copies ran while one was open for 1% -> 1% of each run, Pallas kernels for 76% -> 24%
where the time goes in v3:
time: 129 us; the launch traced here: 128 us
  waiting for transfers between devices  54 us (42%)
  Pallas kernels  32.7 us (25%)
  starting transfers between devices  28.9 us (22%)
  local copies, waits for them, and re-layouts  10.7 us (8%)
  other arithmetic  1.72 us (1%)
    ppermute x7, waiting for transfers between devices, along_x(): return lax.ppermute(chunk, 'row', x_pairs)  27.8 us
    pallas_call x8, Pallas kernels, accumulate(): pl.pallas_call(kernel, grid_spec=pltpu.PrefetchScalarGridSpec(num_scalar_...  20 us
    ppermute x1, waiting for transfers between devices, shards(): other = lax.ppermute(totals[half:nc], 'rep', [(0, 1), (1, 0)])  17.1 us
    ppermute x7, starting transfers between devices, along_z(): return lax.ppermute(chunk, 'row', z_pairs)  11.2 us
    unnamed x28, local copies, waits for them, and re-layouts  9.67 us
    ppermute x7, waiting for transfers between devices, along_z(): return lax.ppermute(chunk, 'row', z_pairs)  9.04 us
    ppermute x7, starting transfers between devices, along_x(): return lax.ppermute(chunk, 'row', x_pairs)  8.67 us
    pallas_call x2, Pallas kernels, pick_panel(): pl.pallas_call(kernel, grid_spec=pltpu.PrefetchScalarGridSpec(num_scalar_...  7.03 us
  transfers between devices with their start and end apart: 22, of which 10 were waited for; matrix products, arithmetic and copies ran while one was open for 1% of the time, Pallas kernels for 24%

profile of v3, /device:TPU:0, one launch (start us, length us, event | category | flops | bytes accessed | tf_op | source)
XLA Modules:
  0.0 128.3 jit_solution(7282916238907014910)
XLA Ops:
  0.0 5.0 %collective-permute-start.4 = (s32[8,4]{0,1:T(4,128)}, s32[8,4]{0,1:T(4,128)S(1)}, u32[]{:S(2)}, u32[]{:S(2)}) collective-permute-start(s32[8,4]{0,1:T(4,128)} %bitcast.55), channel_id=1, source_target_pairs={{0,20},{4,24},{8,28},{12,0},{16,4},{20,8},{24,12},{28,16},{1,21},{... | collective-permute-start | bytes 392 | tf_op jit(solution)/shard_map/ppermute | solution.py:225
  5.0 1.4 %collective-permute-start.2 = (s32[8,4]{0,1:T(4,128)}, s32[8,4]{0,1:T(4,128)S(1)}, u32[]{:S(2)}, u32[]{:S(2)}) collective-permute-start(s32[8,4]{0,1:T(4,128)} %bitcast.56), channel_id=1, source_target_pairs={{0,28},{4,0},{8,4},{12,8},{16,12},{20,16},{24,20},{28,24},{1,29},{... | collective-permute-start | bytes 392 | tf_op jit(solution)/shard_map/ppermute | solution.py:225
  6.8 0.8 slice_bitcast_fusion.1
  8.1 1.6 %copy-done.2 = f32[1,1,1,8,4,128,128]{6,5,4,3,2,1,0:T(8,128)S(1)} copy-done((f32[1,1,1,8,4,128,128]{6,5,4,3,2,1,0:T(8,128)S(1)}, f32[1,1,1,8,4,128,128]{6,5,4,3,2,1,0:T(8,128)}, u32[]{:S(2)}) %copy-start.2) | copy-done | bytes 2097176
  9.8 0.8 copy-done.9
  10.6 0.8 copy-done.11
  11.4 0.8 copy-done.10
  12.3 3.5 %pick_panel.3 = f32[8,2,128,128]{3,2,1,0:T(8,128)} custom-call(s32[1]{0:T(128)} %bitcast.17.which_ref, f32[3,8,2,128,128]{4,3,2,1,0:T(8,128)} %bitcast.25), custom_call_target="tpu_custom_call" | custom-call | bytes 2097152 | tf_op jit(solution)/shard_map/pick_panel/pallas_call | solution.py:77
  15.9 1.9 %collective-permute-start.13 = (f32[2,4,128,128]{3,2,1,0:T(8,128)}, f32[2,4,128,128]{3,2,1,0:T(8,128)}, u32[]{:S(2)}, u32[]{:S(2)}) collective-permute-start(f32[2,4,128,128]{3,2,1,0:T(8,128)} %copy-done.9), channel_id=1, source_target_pairs={{0,4},{4,0},{8,12},{12,8},{16,20},{20,16},{24,28},{28,24},{1,5},{5... | collective-permute-start | bytes 1572872 | tf_op jit(solution)/shard_map/ppermute | solution.py:197
  18.1 4.0 %collective-permute-start.11 = (f32[2,4,128,128]{3,2,1,0:T(8,128)}, f32[2,4,128,128]{3,2,1,0:T(8,128)}, u32[]{:S(2)}, u32[]{:S(2)}) collective-permute-start(f32[2,4,128,128]{3,2,1,0:T(8,128)} %copy-done.10), channel_id=1, source_target_pairs={{0,24},{4,28},{8,0},{12,4},{16,8},{20,12},{24,16},{28,20},{1,25},{... | collective-permute-start | bytes 1572872 | tf_op jit(solution)/shard_map/ppermute | solution.py:194
  23.1 1.6 %copy-done.3 = f32[1,1,1,8,4,128,128]{6,5,4,3,2,1,0:T(8,128)S(1)} copy-done((f32[1,1,1,8,4,128,128]{6,5,4,3,2,1,0:T(8,128)S(1)}, f32[1,1,1,8,4,128,128]{6,5,4,3,2,1,0:T(8,128)}, u32[]{:S(2)}) %copy-start.3) | copy-done | bytes 2097176
  24.7 2.0 %accumulate.8 = (f32[25,128,128]{2,1,0:T(8,128)S(1)}, f32[8,128]{1,0:T(8,128)S(1)}) custom-call(s32[257]{0:T(512)S(1)} %pad_add_fusion.1.scalar_ref, f32[3,8,2,128,128]{4,3,2,1,0:T(8,128)S(1)} %bitcast.27, f32[3,8,2,128,128]{4,3,2,1,0:T(8,128)S(1)} %bitcast.28, f32[3,8,2,128,128]{4,3,2,1,0:T(8,128)S(1)} %bitcast.29, f32[3,8,2,128,128]{4,3,2,1,0:T(8,128)S(1)} %bitcast.30, ...), custom_call_target="tpu_custom_call" | custom-call | flops 805306368 | bytes 6422528 | tf_op jit(solution)/shard_map/accumulate/pallas_call | solution.py:160
  26.7 4.2 %collective-permute-done.6.refs_0_.refs_2_.refs_1_ = f32[2,4,128,128]{3,2,1,0:T(8,128)} collective-permute-done((f32[2,4,128,128]{3,2,1,0:T(8,128)}, f32[2,4,128,128]{3,2,1,0:T(8,128)}, u32[]{:S(2)}, u32[]{:S(2)}) %collective-permute-start.6) | collective-permute-done | bytes 524320 | tf_op jit(solution)/shard_map/ppermute | solution.py:194
  30.9 10.3 %collective-permute-done.7.refs_2_.refs_3_.refs_0_ = f32[2,4,128,128]{3,2,1,0:T(8,128)} collective-permute-done((f32[2,4,128,128]{3,2,1,0:T(8,128)}, f32[2,4,128,128]{3,2,1,0:T(8,128)}, u32[]{:S(2)}, u32[]{:S(2)}) %collective-permute-start.7) | collective-permute-done | bytes 524320 | tf_op jit(solution)/shard_map/ppermute | solution.py:197
  41.3 1.1 pick.13
  42.4 1.6 %collective-permute-start.8 = (f32[2,4,128,128]{3,2,1,0:T(8,128)S(1)}, f32[2,4,128,128]{3,2,1,0:T(8,128)S(1)}, u32[]{:S(2)}, u32[]{:S(2)}) collective-permute-start(f32[2,4,128,128]{3,2,1,0:T(8,128)S(1)} %pick.13), channel_id=1, source_target_pairs={{0,4},{4,0},{8,12},{12,8},{16,20},{20,16},{24,28},{28,24},{1,5},{5... | collective-permute-start | bytes 1572872 | tf_op jit(solution)/shard_map/ppermute | solution.py:197
  44.0 3.5 %pick_panel.2 = f32[8,2,128,128]{3,2,1,0:T(8,128)} custom-call(s32[1]{0:T(128)} %bitcast.13.which_ref, f32[3,8,2,128,128]{4,3,2,1,0:T(8,128)} %bitcast.26), custom_call_target="tpu_custom_call" | custom-call | bytes 2097152 | tf_op jit(solution)/shard_map/pick_panel/pallas_call | solution.py:77
  47.6 2.8 %collective-permute-start.12 = (f32[2,4,128,128]{3,2,1,0:T(8,128)S(1)}, f32[2,4,128,128]{3,2,1,0:T(8,128)S(1)}, u32[]{:S(2)}, u32[]{:S(2)}) collective-permute-start(f32[2,4,128,128]{3,2,1,0:T(8,128)S(1)} %pick.16), channel_id=1, source_target_pairs={{0,24},{4,28},{8,0},{12,4},{16,8},{20,12},{24,16},{28,20},{1,25},{... | collective-permute-start | bytes 1572872 | tf_op jit(solution)/shard_map/ppermute | solution.py:194
  50.4 1.4 %copy-done.6 = f32[25,128,128]{2,1,0:T(8,128)S(1)} copy-done((f32[25,128,128]{2,1,0:T(8,128)S(1)}, f32[25,128,128]{2,1,0:T(8,128)}, u32[]{:S(2)}) %copy-start.6) | copy-done | bytes 1638424
  51.8 3.0 %accumulate.9 = (f32[25,128,128]{2,1,0:T(8,128)S(1)}, f32[8,128]{1,0:T(8,128)S(1)}) custom-call(s32[257]{0:T(512)S(1)} %pad_add_fusion.1.scalar_ref, f32[3,8,2,128,128]{4,3,2,1,0:T(8,128)S(1)} %bitcast.31, f32[1,8,2,128,128]{4,3,2,1,0:T(8,128)} %bitcast.18.refs_1_.refs_2_.refs_3_, ...), custom_call_target="tpu_custom_call", output_to_operand_aliasing={{0}: (5, {})} | custom-call | flops 402653184 | bytes 4849664 | tf_op jit(solution)/shard_map/accumulate/pallas_call | solution.py:160
  54.8 1.1 pick.18
  55.9 1.0 collective-permute-start.16
  57.0 1.9 %collective-permute-start.10 = (f32[2,4,128,128]{3,2,1,0:T(8,128)S(1)}, f32[2,4,128,128]{3,2,1,0:T(8,128)S(1)}, u32[]{:S(2)}, u32[]{:S(2)}) collective-permute-start(f32[2,4,128,128]{3,2,1,0:T(8,128)S(1)} %pick.14), channel_id=1, source_target_pairs={{0,24},{4,28},{8,0},{12,4},{16,8},{20,12},{24,16},{28,20},{1,25},{... | collective-permute-start | bytes 1572872 | tf_op jit(solution)/shard_map/ppermute | solution.py:194
  58.9 3.0 %accumulate.10 = (f32[25,128,128]{2,1,0:T(8,128)S(1)}, f32[8,128]{1,0:T(8,128)S(1)}) custom-call(s32[257]{0:T(512)S(1)} %pad_add_fusion.1.scalar_ref, f32[3,8,2,128,128]{4,3,2,1,0:T(8,128)S(1)} %bitcast.32, f32[1,8,2,128,128]{4,3,2,1,0:T(8,128)} %bitcast.18.refs_1_.refs_2_.refs_3_, ...), custom_call_target="tpu_custom_call", output_to_operand_aliasing={{0}: (5, {})} | custom-call | flops 402653184 | bytes 4849664 | tf_op jit(solution)/shard_map/accumulate/pallas_call | solution.py:160
  61.9 0.7 collective-permute-done.12.refs_3_.refs_1_.refs_0_
  62.6 1.1 pick.21
  63.7 1.5 %collective-permute-start.19 = (f32[2,4,128,128]{3,2,1,0:T(8,128)S(1)}, f32[2,4,128,128]{3,2,1,0:T(8,128)S(1)}, u32[]{:S(2)}, u32[]{:S(2)}) collective-permute-start(f32[2,4,128,128]{3,2,1,0:T(8,128)S(1)} %pick.21), channel_id=1, source_target_pairs={{0,4},{4,0},{8,12},{12,8},{16,20},{20,16},{24,28},{28,24},{1,5},{5... | collective-permute-start | bytes 1572872 | tf_op jit(solution)/shard_map/ppermute | solution.py:197
  65.2 2.6 %accumulate.11 = (f32[25,128,128]{2,1,0:T(8,128)S(1)}, f32[8,128]{1,0:T(8,128)S(1)}) custom-call(s32[257]{0:T(512)S(1)} %pad_add_fusion.1.scalar_ref, f32[3,8,2,128,128]{4,3,2,1,0:T(8,128)S(1)} %bitcast.33, f32[1,8,2,128,128]{4,3,2,1,0:T(8,128)} %bitcast.18.refs_1_.refs_2_.refs_3_, ...), custom_call_target="tpu_custom_call", output_to_operand_aliasing={{0}: (6, {})} | custom-call | flops 402653184 | bytes 4849664 | tf_op jit(solution)/shard_map/accumulate/pallas_call | solution.py:160
  67.8 3.0 %collective-permute-done.16.refs_1_.refs_5_ = f32[2,4,128,128]{3,2,1,0:T(8,128)S(1)} collective-permute-done((f32[2,4,128,128]{3,2,1,0:T(8,128)S(1)}, f32[2,4,128,128]{3,2,1,0:T(8,128)S(1)}, u32[]{:S(2)}, u32[]{:S(2)}) %collective-permute-start.16) | collective-permute-done | bytes 524320 | tf_op jit(solution)/shard_map/ppermute | solution.py:197
  70.7 1.1 pick.19
  71.8 1.4 %collective-permute-start.17 = (f32[2,4,128,128]{3,2,1,0:T(8,128)S(1)}, f32[2,4,128,128]{3,2,1,0:T(8,128)S(1)}, u32[]{:S(2)}, u32[]{:S(2)}) collective-permute-start(f32[2,4,128,128]{3,2,1,0:T(8,128)S(1)} %pick.19), channel_id=1, source_target_pairs={{0,24},{4,28},{8,0},{12,4},{16,8},{20,12},{24,16},{28,20},{1,25},{... | collective-permute-start | bytes 1572872 | tf_op jit(solution)/shard_map/ppermute | solution.py:194
  73.8 1.1 pick.17
  74.9 1.5 %collective-permute-start.14 = (f32[2,4,128,128]{3,2,1,0:T(8,128)S(1)}, f32[2,4,128,128]{3,2,1,0:T(8,128)S(1)}, u32[]{:S(2)}, u32[]{:S(2)}) collective-permute-start(f32[2,4,128,128]{3,2,1,0:T(8,128)S(1)} %pick.17), channel_id=1, source_target_pairs={{0,4},{4,0},{8,12},{12,8},{16,20},{20,16},{24,28},{28,24},{1,5},{5... | collective-permute-start | bytes 1572872 | tf_op jit(solution)/shard_map/ppermute | solution.py:197
  76.4 5.5 %collective-permute-done.19.refs_5_ = f32[2,4,128,128]{3,2,1,0:T(8,128)S(1)} collective-permute-done((f32[2,4,128,128]{3,2,1,0:T(8,128)S(1)}, f32[2,4,128,128]{3,2,1,0:T(8,128)S(1)}, u32[]{:S(2)}, u32[]{:S(2)}) %collective-permute-start.19) | collective-permute-done | bytes 524320 | tf_op jit(solution)/shard_map/ppermute | solution.py:197
  82.1 2.6 %accumulate.12 = (f32[25,128,128]{2,1,0:T(8,128)S(1)}, f32[8,128]{1,0:T(8,128)S(1)}) custom-call(s32[257]{0:T(512)S(1)} %pad_add_fusion.1.scalar_ref, f32[3,8,2,128,128]{4,3,2,1,0:T(8,128)S(1)} %bitcast.34, f32[1,8,2,128,128]{4,3,2,1,0:T(8,128)S(1)} %bitcast.47, ...), custom_call_target="tpu_custom_call", output_to_operand_aliasing={{0}: (7, {})} | custom-call | flops 402653184 | bytes 4849664 | tf_op jit(solution)/shard_map/accumulate/pallas_call | solution.py:160
  84.7 1.2 copy-done.7
  86.0 0.9 collective-permute-start.18
  86.8 6.4 %collective-permute-done.14.refs_4_ = f32[2,4,128,128]{3,2,1,0:T(8,128)S(1)} collective-permute-done((f32[2,4,128,128]{3,2,1,0:T(8,128)S(1)}, f32[2,4,128,128]{3,2,1,0:T(8,128)S(1)}, u32[]{:S(2)}, u32[]{:S(2)}) %collective-permute-start.14) | collective-permute-done | bytes 524320 | tf_op jit(solution)/shard_map/ppermute | solution.py:197
  93.2 0.9 collective-permute-start.15
  94.1 1.4 %copy-done.8 = f32[25,128,128]{2,1,0:T(8,128)S(1)} copy-done((f32[25,128,128]{2,1,0:T(8,128)S(1)}, f32[25,128,128]{2,1,0:T(8,128)}, u32[]{:S(2)}) %copy-start.8) | copy-done | bytes 1638424
  95.6 3.0 %accumulate.13 = (f32[25,128,128]{2,1,0:T(8,128)S(1)}, f32[8,128]{1,0:T(8,128)}) custom-call(s32[257]{0:T(512)S(1)} %pad_add_fusion.1.scalar_ref, f32[1,8,2,128,128]{4,3,2,1,0:T(8,128)S(1)} %bitcast.48, f32[1,8,2,128,128]{4,3,2,1,0:T(8,128)S(1)} %bitcast.49, f32[1,8,2,128,128]{4,3,2,1,0:T(8,128)S(1)} %bitcast.50, ...), custom_call_target="tpu_custom_call", output_to_operand_aliasing={{0}: (7, {})} | custom-call | flops 402653184 | bytes 4849664 | tf_op jit(solution)/shard_map/accumulate/pallas_call | solution.py:160
  98.6 2.6 %accumulate.14 = (f32[25,128,128]{2,1,0:T(8,128)S(1)}, f32[8,128]{1,0:T(8,128)}) custom-call(s32[257]{0:T(512)S(1)} %pad_add_fusion.1.scalar_ref, f32[1,8,2,128,128]{4,3,2,1,0:T(8,128)S(1)} %bitcast.51, f32[1,8,2,128,128]{4,3,2,1,0:T(8,128)S(1)} %bitcast.52, f32[1,8,2,128,128]{4,3,2,1,0:T(8,128)} %bitcast.18.refs_1_.refs_2_.refs_3_, ...), custom_call_target="tpu_custom_call", output_to_operand_aliasing={{0}: (6, {})} | custom-call | flops 402653184 | bytes 4849664 | tf_op jit(solution)/shard_map/accumulate/pallas_call | solution.py:160
  101.2 2.6 %collective-permute-done.18.refs_4_ = f32[2,4,128,128]{3,2,1,0:T(8,128)S(1)} collective-permute-done((f32[2,4,128,128]{3,2,1,0:T(8,128)S(1)}, f32[2,4,128,128]{3,2,1,0:T(8,128)S(1)}, u32[]{:S(2)}, u32[]{:S(2)}) %collective-permute-start.18) | collective-permute-done | bytes 524320 | tf_op jit(solution)/shard_map/ppermute | solution.py:197
  103.7 3.4 %collective-permute-done.15.refs_3_ = f32[2,4,128,128]{3,2,1,0:T(8,128)S(1)} collective-permute-done((f32[2,4,128,128]{3,2,1,0:T(8,128)S(1)}, f32[2,4,128,128]{3,2,1,0:T(8,128)S(1)}, u32[]{:S(2)}, u32[]{:S(2)}) %collective-permute-start.15) | collective-permute-done | bytes 524320 | tf_op jit(solution)/shard_map/ppermute | solution.py:194
  107.2 1.4 %accumulate.15 = (f32[25,128,128]{2,1,0:T(8,128)S(1)}, f32[8,128]{1,0:T(8,128)}) custom-call(s32[257]{0:T(512)S(1)} %pad_add_fusion.1.scalar_ref, f32[1,8,2,128,128]{4,3,2,1,0:T(8,128)S(1)} %bitcast.53, f32[1,8,2,128,128]{4,3,2,1,0:T(8,128)S(1)} %bitcast.54, f32[3,8,2,128,128]{4,3,2,1,0:T(8,128)S(1)} %bitcast.35, ...), custom_call_target="tpu_custom_call", output_to_operand_aliasing={{0}: (6, {})} | custom-call | flops 402653184 | bytes 4849664 | tf_op jit(solution)/shard_map/accumulate/pallas_call | solution.py:160
  108.6 1.6 %collective-permute-start.21 = (f32[12,128,128]{2,1,0:T(8,128)S(1)}, f32[12,128,128]{2,1,0:T(8,128)S(1)}, u32[]{:S(2)}, u32[]{:S(2)}) collective-permute-start(f32[12,128,128]{2,1,0:T(8,128)S(1)} %slice.17), channel_id=1, source_target_pairs={{0,1},{1,0},{2,3},{3,2},{4,5},{5,4},{6,7},{7,6},{8,9},{9,8},{10,11... | collective-permute-start | bytes 2359304 | tf_op jit(solution)/shard_map/ppermute | solution.py:260
  110.2 17.1 %collective-permute-done.21 = f32[12,128,128]{2,1,0:T(8,128)S(1)} collective-permute-done((f32[12,128,128]{2,1,0:T(8,128)S(1)}, f32[12,128,128]{2,1,0:T(8,128)S(1)}, u32[]{:S(2)}, u32[]{:S(2)}) %collective-permute-start.21) | collective-permute-done | bytes 786464 | tf_op jit(solution)/shard_map/ppermute | solution.py:260
  127.3 1.0 add_bitcast_fusion
  (57 shorter events, 3.4 us)
Async XLA Ops:
  0.0 17.8 %collective-permute-start.4 = (s32[8,4]{0,1:T(4,128)}, s32[8,4]{0,1:T(4,128)S(1)}, u32[]{:S(2)}, u32[]{:S(2)}) collective-permute-start(s32[8,4]{0,1:T(4,128)} %bitcast.55), channel_id=1, source_target_pairs={{0,20},{4,24},{8,28},{12,0},{16,4},{20,8},{24,12},{28,16},{1,21},{... | collective-permute-start | bytes 392 | tf_op jit(solution)/shard_map/ppermute | solution.py:225
  5.0 12.9 %collective-permute-start.2 = (s32[8,4]{0,1:T(4,128)}, s32[8,4]{0,1:T(4,128)S(1)}, u32[]{:S(2)}, u32[]{:S(2)}) collective-permute-start(s32[8,4]{0,1:T(4,128)} %bitcast.56), channel_id=1, source_target_pairs={{0,28},{4,0},{8,4},{12,8},{16,12},{20,16},{24,20},{28,24},{1,29},{... | collective-permute-start | bytes 392 | tf_op jit(solution)/shard_map/ppermute | solution.py:225
  6.4 11.7 %collective-permute-start.3 = (s32[8,4]{0,1:T(4,128)}, s32[8,4]{0,1:T(4,128)S(1)}, u32[]{:S(2)}, u32[]{:S(2)}) collective-permute-start(s32[8,4]{0,1:T(4,128)} %bitcast.57), channel_id=1, source_target_pairs={{0,24},{4,28},{8,0},{12,4},{16,8},{20,12},{24,16},{28,20},{1,25},{... | collective-permute-start | bytes 392 | tf_op jit(solution)/shard_map/ppermute | solution.py:225
  7.6 8.2 %collective-permute-start = (s32[8,2]{0,1:T(2,128)S(1)}, s32[8,2]{0,1:T(2,128)S(1)}, u32[]{:S(2)}, u32[]{:S(2)}) collective-permute-start(s32[8,2]{0,1:T(2,128)S(1)} %get-tuple-element.32), channel_id=1, source_target_pairs={{0,2},{2,0},{1,3},{3,1},{4,6},{6,4},{5,7},{7,5},{8,10},{10,8},{9,1... | collective-permute-start | bytes 200 | tf_op jit(solution)/shard_map/ppermute | solution.py:211
  7.6 8.2 %collective-permute-start.1 = (s32[8,2]{0,1:T(2,128)S(1)}, s32[8,2]{0,1:T(2,128)S(1)}, u32[]{:S(2)}, u32[]{:S(2)}) collective-permute-start(s32[8,2]{0,1:T(2,128)S(1)} %get-tuple-element.33), channel_id=1, source_target_pairs={{0,2},{2,0},{1,3},{3,1},{4,6},{6,4},{5,7},{7,5},{8,10},{10,8},{9,1... | collective-permute-start | bytes 200 | tf_op jit(solution)/shard_map/ppermute | solution.py:211
  8.1 1.6 %copy-start.2 = (f32[1,1,1,8,4,128,128]{6,5,4,3,2,1,0:T(8,128)S(1)}, f32[1,1,1,8,4,128,128]{6,5,4,3,2,1,0:T(8,128)}, u32[]{:S(2)}) copy-start(f32[1,1,1,8,4,128,128]{6,5,4,3,2,1,0:T(8,128)} %param.7) | copy-start | bytes 6291460
  9.7 0.8 copy-start.9
  10.6 0.8 copy-start.11
  11.4 0.8 copy-start.10
  12.3 9.8 %copy-start.12 = (s32[1,1,1,8,4]{3,4,2,1,0:T(4,128)S(1)}, s32[1,1,1,8,4]{3,4,2,1,0:T(4,128)}, u32[]{:S(2)}) copy-start(s32[1,1,1,8,4]{3,4,2,1,0:T(4,128)} %param.8) | copy-start | bytes 388
  12.3 9.8 %copy-start.13 = (s32[1,1,24]{2,1,0:T(1,128)S(1)}, s32[1,1,24]{2,1,0:T(1,128)}, u32[]{:S(2)}) copy-start(s32[1,1,24]{2,1,0:T(1,128)} %param.9) | copy-start | bytes 292
  12.3 10.8 %copy-start = (f32[1,1,1,3,8,2,128,128]{7,6,5,4,3,2,1,0:T(8,128)S(1)}, f32[1,1,1,3,8,2,128,128]{7,6,5,4,3,2,1,0:T(8,128)}, u32[]{:S(2)}) copy-start(f32[1,1,1,3,8,2,128,128]{7,6,5,4,3,2,1,0:T(8,128)} %param.5) | copy-start | bytes 9437188
  15.8 15.1 %collective-permute-start.6 = (f32[2,4,128,128]{3,2,1,0:T(8,128)}, f32[2,4,128,128]{3,2,1,0:T(8,128)}, u32[]{:S(2)}, u32[]{:S(2)}) collective-permute-start(f32[2,4,128,128]{3,2,1,0:T(8,128)} %copy-done.9), channel_id=1, source_target_pairs={{0,24},{4,28},{8,0},{12,4},{16,8},{20,12},{24,16},{28,20},{1,25},{... | collective-permute-start | bytes 1572872 | tf_op jit(solution)/shard_map/ppermute | solution.py:194
  15.9 38.9 %collective-permute-start.13 = (f32[2,4,128,128]{3,2,1,0:T(8,128)}, f32[2,4,128,128]{3,2,1,0:T(8,128)}, u32[]{:S(2)}, u32[]{:S(2)}) collective-permute-start(f32[2,4,128,128]{3,2,1,0:T(8,128)} %copy-done.9), channel_id=1, source_target_pairs={{0,4},{4,0},{8,12},{12,8},{16,20},{20,16},{24,28},{28,24},{1,5},{5... | collective-permute-start | bytes 1572872 | tf_op jit(solution)/shard_map/ppermute | solution.py:197
  17.8 29.8 %collective-permute-start.9 = (f32[8,2,128,128]{3,2,1,0:T(8,128)}, f32[8,2,128,128]{3,2,1,0:T(8,128)}, u32[]{:S(2)}, u32[]{:S(2)}) collective-permute-start(f32[8,2,128,128]{3,2,1,0:T(8,128)} %pick_panel.3), channel_id=1, source_target_pairs={{0,2},{2,0},{1,3},{3,1},{4,6},{6,4},{5,7},{7,5},{8,10},{10,8},{9,1... | collective-permute-start | bytes 3145736 | tf_op jit(solution)/shard_map/ppermute | solution.py:211
  17.9 23.4 %collective-permute-start.7 = (f32[2,4,128,128]{3,2,1,0:T(8,128)}, f32[2,4,128,128]{3,2,1,0:T(8,128)}, u32[]{:S(2)}, u32[]{:S(2)}) collective-permute-start(f32[2,4,128,128]{3,2,1,0:T(8,128)} %copy-done.11), channel_id=1, source_target_pairs={{0,4},{4,0},{8,12},{12,8},{16,20},{20,16},{24,28},{28,24},{1,5},{5... | collective-permute-start | bytes 1572872 | tf_op jit(solution)/shard_map/ppermute | solution.py:197
  18.1 36.7 %collective-permute-start.11 = (f32[2,4,128,128]{3,2,1,0:T(8,128)}, f32[2,4,128,128]{3,2,1,0:T(8,128)}, u32[]{:S(2)}, u32[]{:S(2)}) collective-permute-start(f32[2,4,128,128]{3,2,1,0:T(8,128)} %copy-done.10), channel_id=1, source_target_pairs={{0,24},{4,28},{8,0},{12,4},{16,8},{20,12},{24,16},{28,20},{1,25},{... | collective-permute-start | bytes 1572872 | tf_op jit(solution)/shard_map/ppermute | solution.py:194
  23.1 1.6 %copy-start.3 = (f32[1,1,1,8,4,128,128]{6,5,4,3,2,1,0:T(8,128)S(1)}, f32[1,1,1,8,4,128,128]{6,5,4,3,2,1,0:T(8,128)}, u32[]{:S(2)}) copy-start(f32[1,1,1,8,4,128,128]{6,5,4,3,2,1,0:T(8,128)} %param.7) | copy-start | bytes 6291460
  26.7 15.7 %copy-start.5 = (f32[25,128,128]{2,1,0:T(8,128)}, f32[25,128,128]{2,1,0:T(8,128)S(1)}, u32[]{:S(2)}) copy-start(f32[25,128,128]{2,1,0:T(8,128)S(1)} %get-tuple-element.19.refs_4_) | copy-start | bytes 4915204
  42.4 14.6 %collective-permute-start.8 = (f32[2,4,128,128]{3,2,1,0:T(8,128)S(1)}, f32[2,4,128,128]{3,2,1,0:T(8,128)S(1)}, u32[]{:S(2)}, u32[]{:S(2)}) collective-permute-start(f32[2,4,128,128]{3,2,1,0:T(8,128)S(1)} %pick.13), channel_id=1, source_target_pairs={{0,4},{4,0},{8,12},{12,8},{16,20},{20,16},{24,28},{28,24},{1,5},{5... | collective-permute-start | bytes 1572872 | tf_op jit(solution)/shard_map/ppermute | solution.py:197
  44.0 3.5 %copy-start.4 = (f32[1,1,1,8,4,128,128]{6,5,4,3,2,1,0:T(8,128)S(1)}, f32[1,1,1,8,4,128,128]{6,5,4,3,2,1,0:T(8,128)}, u32[]{:S(2)}) copy-start(f32[1,1,1,8,4,128,128]{6,5,4,3,2,1,0:T(8,128)} %param.7) | copy-start | bytes 6291460
  47.5 2.8 %copy-start.1 = (f32[1,1,1,3,8,2,128,128]{7,6,5,4,3,2,1,0:T(8,128)S(1)}, f32[1,1,1,3,8,2,128,128]{7,6,5,4,3,2,1,0:T(8,128)}, u32[]{:S(2)}) copy-start(f32[1,1,1,3,8,2,128,128]{7,6,5,4,3,2,1,0:T(8,128)} %param.5) | copy-start | bytes 9437188
  47.5 34.6 %collective-permute-start.5 = (f32[8,2,128,128]{3,2,1,0:T(8,128)}, f32[8,2,128,128]{3,2,1,0:T(8,128)S(1)}, u32[]{:S(2)}, u32[]{:S(2)}) collective-permute-start(f32[8,2,128,128]{3,2,1,0:T(8,128)} %pick_panel.2), channel_id=1, source_target_pairs={{0,2},{2,0},{1,3},{3,1},{4,6},{6,4},{5,7},{7,5},{8,10},{10,8},{9,1... | collective-permute-start | bytes 3145736 | tf_op jit(solution)/shard_map/ppermute | solution.py:211
  47.6 15.0 %collective-permute-start.12 = (f32[2,4,128,128]{3,2,1,0:T(8,128)S(1)}, f32[2,4,128,128]{3,2,1,0:T(8,128)S(1)}, u32[]{:S(2)}, u32[]{:S(2)}) collective-permute-start(f32[2,4,128,128]{3,2,1,0:T(8,128)S(1)} %pick.16), channel_id=1, source_target_pairs={{0,24},{4,28},{8,0},{12,4},{16,8},{20,12},{24,16},{28,20},{1,25},{... | collective-permute-start | bytes 1572872 | tf_op jit(solution)/shard_map/ppermute | solution.py:194
  50.4 1.4 %copy-start.6 = (f32[25,128,128]{2,1,0:T(8,128)S(1)}, f32[25,128,128]{2,1,0:T(8,128)}, u32[]{:S(2)}) copy-start(f32[25,128,128]{2,1,0:T(8,128)} %copy-done.5) | copy-start | bytes 4915204
  55.9 14.8 %collective-permute-start.16 = (f32[2,4,128,128]{3,2,1,0:T(8,128)S(1)}, f32[2,4,128,128]{3,2,1,0:T(8,128)S(1)}, u32[]{:S(2)}, u32[]{:S(2)}) collective-permute-start(f32[2,4,128,128]{3,2,1,0:T(8,128)S(1)} %pick.18), channel_id=1, source_target_pairs={{0,4},{4,0},{8,12},{12,8},{16,20},{20,16},{24,28},{28,24},{1,5},{5... | collective-permute-start | bytes 1572872 | tf_op jit(solution)/shard_map/ppermute | solution.py:197
  57.0 16.9 %collective-permute-start.10 = (f32[2,4,128,128]{3,2,1,0:T(8,128)S(1)}, f32[2,4,128,128]{3,2,1,0:T(8,128)S(1)}, u32[]{:S(2)}, u32[]{:S(2)}) collective-permute-start(f32[2,4,128,128]{3,2,1,0:T(8,128)S(1)} %pick.14), channel_id=1, source_target_pairs={{0,24},{4,28},{8,0},{12,4},{16,8},{20,12},{24,16},{28,20},{1,25},{... | collective-permute-start | bytes 1572872 | tf_op jit(solution)/shard_map/ppermute | solution.py:194
  63.7 18.3 %collective-permute-start.19 = (f32[2,4,128,128]{3,2,1,0:T(8,128)S(1)}, f32[2,4,128,128]{3,2,1,0:T(8,128)S(1)}, u32[]{:S(2)}, u32[]{:S(2)}) collective-permute-start(f32[2,4,128,128]{3,2,1,0:T(8,128)S(1)} %pick.21), channel_id=1, source_target_pairs={{0,4},{4,0},{8,12},{12,8},{16,20},{20,16},{24,28},{28,24},{1,5},{5... | collective-permute-start | bytes 1572872 | tf_op jit(solution)/shard_map/ppermute | solution.py:197
  71.8 14.1 %collective-permute-start.17 = (f32[2,4,128,128]{3,2,1,0:T(8,128)S(1)}, f32[2,4,128,128]{3,2,1,0:T(8,128)S(1)}, u32[]{:S(2)}, u32[]{:S(2)}) collective-permute-start(f32[2,4,128,128]{3,2,1,0:T(8,128)S(1)} %pick.19), channel_id=1, source_target_pairs={{0,24},{4,28},{8,0},{12,4},{16,8},{20,12},{24,16},{28,20},{1,25},{... | collective-permute-start | bytes 1572872 | tf_op jit(solution)/shard_map/ppermute | solution.py:194
  74.9 18.3 %collective-permute-start.14 = (f32[2,4,128,128]{3,2,1,0:T(8,128)S(1)}, f32[2,4,128,128]{3,2,1,0:T(8,128)S(1)}, u32[]{:S(2)}, u32[]{:S(2)}) collective-permute-start(f32[2,4,128,128]{3,2,1,0:T(8,128)S(1)} %pick.17), channel_id=1, source_target_pairs={{0,4},{4,0},{8,12},{12,8},{16,20},{20,16},{24,28},{28,24},{1,5},{5... | collective-permute-start | bytes 1572872 | tf_op jit(solution)/shard_map/ppermute | solution.py:197
  82.0 16.6 %collective-permute-start.20 = (f32[2,4,128,128]{3,2,1,0:T(8,128)S(1)}, f32[2,4,128,128]{3,2,1,0:T(8,128)S(1)}, u32[]{:S(2)}, u32[]{:S(2)}) collective-permute-start(f32[2,4,128,128]{3,2,1,0:T(8,128)S(1)} %collective-permute-done.19.refs_5_), channel_id=1, source_target_pairs={{0,24},{4,28},{8,0},{12,4},{16,8},{20,12},{24,16},{28,20},{1,25},{... | collective-permute-start | bytes 1572872 | tf_op jit(solution)/shard_map/ppermute | solution.py:194
  84.7 1.2 copy-start.7
  86.0 17.8 %collective-permute-start.18 = (f32[2,4,128,128]{3,2,1,0:T(8,128)S(1)}, f32[2,4,128,128]{3,2,1,0:T(8,128)S(1)}, u32[]{:S(2)}, u32[]{:S(2)}) collective-permute-start(f32[2,4,128,128]{3,2,1,0:T(8,128)S(1)} %pick.20), channel_id=1, source_target_pairs={{0,4},{4,0},{8,12},{12,8},{16,20},{20,16},{24,28},{28,24},{1,5},{5... | collective-permute-start | bytes 1572872 | tf_op jit(solution)/shard_map/ppermute | solution.py:197
  93.2 14.0 %collective-permute-start.15 = (f32[2,4,128,128]{3,2,1,0:T(8,128)S(1)}, f32[2,4,128,128]{3,2,1,0:T(8,128)S(1)}, u32[]{:S(2)}, u32[]{:S(2)}) collective-permute-start(f32[2,4,128,128]{3,2,1,0:T(8,128)S(1)} %collective-permute-done.14.refs_4_), channel_id=1, source_target_pairs={{0,24},{4,28},{8,0},{12,4},{16,8},{20,12},{24,16},{28,20},{1,25},{... | collective-permute-start | bytes 1572872 | tf_op jit(solution)/shard_map/ppermute | solution.py:194
  94.1 1.4 %copy-start.8 = (f32[25,128,128]{2,1,0:T(8,128)S(1)}, f32[25,128,128]{2,1,0:T(8,128)}, u32[]{:S(2)}) copy-start(f32[25,128,128]{2,1,0:T(8,128)} %copy-done.7) | copy-start | bytes 4915204
  108.6 18.7 %collective-permute-start.21 = (f32[12,128,128]{2,1,0:T(8,128)S(1)}, f32[12,128,128]{2,1,0:T(8,128)S(1)}, u32[]{:S(2)}, u32[]{:S(2)}) collective-permute-start(f32[12,128,128]{2,1,0:T(8,128)S(1)} %slice.17), channel_id=1, source_target_pairs={{0,1},{1,0},{2,3},{3,2},{4,5},{5,4},{6,7},{7,6},{8,9},{9,8},{10,11... | collective-permute-start | bytes 2359304 | tf_op jit(solution)/shard_map/ppermute | solution.py:260

commit v4 on v3

--- a/solution.py
+++ b/solution.py
@@ -12,27 +12,27 @@
 bf16 = jnp.bfloat16
 f32 = jnp.float32
 
-Z_CHUNKS = (
-    ((2, 0), (2, 0)),
-    ((2, 1), (2, 1)),
-    ((2, 2), (2, 2)),
-    ((2, 3), (3, 0)),
-    ((3, 3), (3, 1)),
-    (None, (3, 2)),
-    (None, (3, 3)),
-)
-X_CHUNKS = (
-    ((1, 3), None),
-    ((1, 0), None),
-    ((1, 1), (1, 0)),
-    ((1, 2), (1, 1)),
-    ((3, 0), (1, 2)),
-    ((3, 1), (1, 3)),
-    ((3, 2), (2, 3)),
-)
-
-
-def pick(odd, per, even_part, odd_part, *others):
+Z_CHUNKS = {
+    1: ((2, 0), (2, 0)),
+    2: ((2, 1), (2, 1)),
+    3: ((2, 2), (2, 2)),
+    4: ((2, 3), (3, 0)),
+    5: ((3, 3), (3, 1)),
+    6: (None, (3, 2)),
+    7: (None, (3, 3)),
+}
+X_CHUNKS = {
+    1: ((1, 2), None),
+    2: ((1, 3), None),
+    3: ((1, 0), (1, 0)),
+    4: ((1, 1), (1, 1)),
+    5: ((3, 0), (1, 2)),
+    6: ((3, 1), (1, 3)),
+    7: ((3, 2), (2, 3)),
+}
+
+
+def pick(odd, size, even_part, odd_part, *others):
     parts = [even_part] if even_part is odd_part else [even_part, odd_part]
     array = even_part[0]
 
@@ -49,9 +49,9 @@
         pl.when(odd_ref[0] != 0)(lambda: copy_from(refs[1]))
 
     def spec(at):
-        return pl.BlockSpec((per,) + array.shape[1:], lambda g, *_: (at, 0, 0, 0))
-
-    out_shape = jax.ShapeDtypeStruct((per,) + array.shape[1:], array.dtype)
+        return pl.BlockSpec((size,) + array.shape[1:], lambda g, *_: (at, 0, 0, 0))
+
+    out_shape = jax.ShapeDtypeStruct((size,) + array.shape[1:], array.dtype)
     return pl.pallas_call(
         kernel,
         grid_spec=pltpu.PrefetchScalarGridSpec(
@@ -67,29 +67,8 @@
     )(odd, *[part for part, _ in parts], *others)
 
 
-def pick_panel(panels, which):
-    _, kb, lpb, bs, _ = panels.shape
-    per = kb // QUARTERS
-
-    def kernel(which_ref, panel_ref, out_ref):
-        out_ref[...] = panel_ref[0]
-
-    return pl.pallas_call(
-        kernel,
-        grid_spec=pltpu.PrefetchScalarGridSpec(
-            num_scalar_prefetch=1,
-            grid=(QUARTERS,),
-            in_specs=[pl.BlockSpec((1, per, lpb, bs, bs), lambda g, which_ref: (which_ref[0], g, 0, 0, 0))],
-            out_specs=pl.BlockSpec((per, lpb, bs, bs), lambda g, which_ref: (g, 0, 0, 0)),
-        ),
-        out_shape=jax.ShapeDtypeStruct(panels.shape[1:], panels.dtype),
-        cost_estimate=pl.CostEstimate(flops=0, bytes_accessed=8 * kb * lpb * bs * bs, transcendentals=0),
-        name="pick_panel",
-    )(which.astype(jnp.int32).reshape(1), panels)
-
-
 def accumulate(scalars, lefts, chunks, totals, nc):
-    _, kb, lpb, bs, _ = lefts[0][0].shape
+    _, kb, lpb, bs, _ = lefts[0].shape
     per = kb // QUARTERS
     bpr = chunks[0][0].shape[1]
     products = lpb * bpr
@@ -142,14 +121,13 @@
                 one()
 
     def left_spec(turn, quarter):
-        held_at = lefts[turn][1]
-        return pl.BlockSpec((1, per, lpb, bs, bs), lambda g, *_: (held_at, quarter, 0, 0, 0))
+        return pl.BlockSpec((1, per, lpb, bs, bs), lambda g, s: (s[odd_at + 1 + turn], quarter, 0, 0, 0))
 
     def right_spec(at):
         return pl.BlockSpec((per, bpr, bs, bs), lambda g, *_: (at, 0, 0, 0))
 
     total_spec = pl.BlockSpec((nc + 1, bs, bs), lambda g, *_: (0, 0, 0))
-    operands = [lefts[chunks[c][2][side][0]][0] for c, side in sides] + [c[0] for c in chunks]
+    operands = [lefts[chunks[c][2][side][0]] for c, side in sides] + [c[0] for c in chunks]
     in_specs = [left_spec(*chunks[c][2][side]) for c, side in sides]
     in_specs += [right_spec(at) for _, at, _ in chunks]
     if not first:
@@ -204,50 +182,46 @@
     z = {}
     x = {}
     z[1] = along_z(sent((right, 0)))
-    x[1] = along_x(sent((right, 3)))
+    x[1] = along_x(pick(odd, 2 * per, *[(right, QUARTERS // 2 - 1)] * 2))
     z[2] = along_z(sent((right, 1)))
 
-    def to_reader(held, turn):
-        return lax.ppermute(held, "col", [(c, (c - turn) % cols_n) for c in range(cols_n)])
-
-    moving = [turn for turn in range(STEPS) if turn % cols_n]
-    place = [turn // cols_n if turn % cols_n == 0 else ((col - turn) % cols_n + turn) // cols_n for turn in range(STEPS)]
-    lefts = [(panels, place[turn]) for turn in range(STEPS)]
-    row_turns = [panel_rows[place[turn]] for turn in range(STEPS)]
-    if moving:
-        for turn in moving:
-            lefts[turn] = (to_reader(pick_panel(panels, place[turn]), turn)[None], 0)
-            row_turns[turn] = to_reader(row_turns[turn], turn)
+    shifts = sorted({turn % cols_n for turn in range(STEPS)})
+    held = {
+        shift: (panels, panel_rows) if shift == 0 else lax.ppermute((panels, panel_rows), "col", [(c, (c - shift) % cols_n) for c in range(cols_n)])
+        for shift in shifts
+    }
+    place = [(col + turn) // cols_n for turn in range(STEPS)]
+    lefts = [held[turn % cols_n][0] for turn in range(STEPS)]
+    rows_at = jnp.stack([held[turn % cols_n][1][place[turn]] for turn in range(STEPS)])
 
     def right_of(held, turn):
         if turn % rows_n == 0:
             return held
         return lax.ppermute(held, "row", [(r, (r - turn) % rows_n) for r in range(rows_n)])
 
-    rows_at = jnp.stack(row_turns)
     cols_at = jnp.stack([right_of(right_places, turn) for turn in range(STEPS)])
     codes = rows_at[:, :, :, None] * CB + cols_at[:, :, None, :]
     order = (jnp.arange(nc, dtype=jnp.int32) + nc - half * rep) % nc
     listed = codes[..., None] == slots
     where_to = nc - jnp.sum(jnp.where(listed, nc - order, 0), axis=-1, dtype=jnp.int32)
-    scalars = jnp.concatenate([where_to.reshape(-1), odd])
+    scalars = jnp.concatenate([where_to.reshape(-1), odd, jnp.stack(place).astype(jnp.int32)])
 
     def add(totals, chunks):
         return accumulate(scalars, lefts, chunks, totals, nc)
 
     def received(stage):
-        return [(z[stage], 0, Z_CHUNKS[stage - 1]), (x[stage], 0, X_CHUNKS[stage - 1])]
-
-    x[2] = along_x(sent((right, 0)))
+        along_x_part = (x[1], stage - 1) if stage < 3 else (x[stage], 0)
+        return [(z[stage], 0, Z_CHUNKS[stage]), (*along_x_part, X_CHUNKS[stage])]
+
     totals, done = add(None, [(right, q, ((0, q), (0, q))) for q in range(QUARTERS)])
+    x[3] = along_x(sent(z[1], (right, 0), done))
     z[3] = along_z(sent((right, 2), None, z[1], done))
-    x[3] = along_x(sent(z[1], (right, 1), x[1], done))
     totals, done = add(totals, received(1))
-    x[4] = along_x(sent(z[2], (right, 2), x[2], done))
+    x[4] = along_x(sent(z[2], (right, 1), done))
     z[4] = along_z(sent((right, 3), x[3], done))
     totals, done = add(totals, received(2))
     x[5] = along_x(sent(z[3], z[1], done))
-    z[5] = along_z(sent(x[1], x[4], done))
+    z[5] = along_z(sent((x[1], 1), x[4], done))
     totals, done = add(totals, received(3))
     x[6] = along_x(sent(z[4], z[2], done))
     z[6] = along_z(x[5])

time: 129 us -> 120 us (0.930)
  waiting for transfers between devices: 54 us -> 67.6 us
  Pallas kernels: 32.7 us -> 21.8 us
  starting transfers between devices: 28.9 us -> 20.5 us
  local copies, waits for them, and re-layouts: 10.7 us -> 8.05 us
    ppermute x7 -> x6, waiting for transfers between devices: 27.8 us -> 43.6 us  [along_x(): return lax.ppermute(chunk, 'row', x_pairs)]
    pallas_call x2 -> x0, Pallas kernels: 7.03 us -> none  [pick_panel(): pl.pallas_call(kernel, grid_spec=pltpu.PrefetchScalarGridSpec(num_scalar_...]
    ppermute x7 -> x6, starting transfers between devices: 8.67 us -> 3.8 us  [along_x(): return lax.ppermute(chunk, 'row', x_pairs)]
    pallas_call x8, Pallas kernels: 20 us -> 16.1 us  [accumulate(): pl.pallas_call(kernel, grid_spec=pltpu.PrefetchScalarGridSpec(num_scalar_...]
    ppermute x7, starting transfers between devices: 11.2 us -> 8.31 us  [along_z(): return lax.ppermute(chunk, 'row', z_pairs)]
    unnamed x28 -> x22, local copies, waits for them, and re-layouts: 9.67 us -> 7.64 us
  transfers between devices with their start and end apart: 22 -> 19, of which waited for: 10 -> 11; matrix products, arithmetic and copies ran while one was open for 1% -> 1% of each run, Pallas kernels for 24% -> 17%
where the time goes in v4:
time: 120 us
  waiting for transfers between devices  67.6 us (56%)
  Pallas kernels  21.8 us (18%)
  starting transfers between devices  20.5 us (17%)
  local copies, waits for them, and re-layouts  8.05 us (7%)
  other arithmetic  1.71 us (1%)
    ppermute x6, waiting for transfers between devices, along_x(): return lax.ppermute(chunk, 'row', x_pairs)  43.6 us
    ppermute x1, waiting for transfers between devices, shards(): other = lax.ppermute(totals[half:nc], 'rep', [(0, 1), (1, 0)])  16.2 us
    pallas_call x8, Pallas kernels, accumulate(): pl.pallas_call(kernel, grid_spec=pltpu.PrefetchScalarGridSpec(num_scalar_...  16.1 us
    ppermute x7, starting transfers between devices, along_z(): return lax.ppermute(chunk, 'row', z_pairs)  8.31 us
    ppermute x7, waiting for transfers between devices, along_z(): return lax.ppermute(chunk, 'row', z_pairs)  7.76 us
    unnamed x22, local copies, waits for them, and re-layouts  7.64 us
    ppermute x3, starting transfers between devices, right_of(): lax.ppermute(held, 'row', [(r, (r - turn) % rows_n) for r in range(rows_n)])  6.4 us
    pallas_call x11, Pallas kernels, pick(): pl.pallas_call(kernel, grid_spec=pltpu.PrefetchScalarGridSpec(num_scalar_...  5.66 us
  transfers between devices with their start and end apart: 19, of which 11 were waited for; matrix products, arithmetic and copies ran while one was open for 1% of the time, Pallas kernels for 17%

profile of v4, /device:TPU:0, one launch (start us, length us, event | category | flops | bytes accessed | tf_op | source)
XLA Modules:
  0.0 119.9 jit_solution(6495558482156235268)
XLA Ops:
  0.0 0.5 collective-permute-start.4
  0.5 4.5 %collective-permute-start.3 = (s32[8,4]{0,1:T(4,128)}, s32[8,4]{0,1:T(4,128)S(1)}, u32[]{:S(2)}, u32[]{:S(2)}) collective-permute-start(s32[8,4]{0,1:T(4,128)} %bitcast.41), channel_id=1, source_target_pairs={{0,20},{4,24},{8,28},{12,0},{16,4},{20,8},{24,12},{28,16},{1,21},{... | collective-permute-start | bytes 392 | tf_op jit(solution)/shard_map/ppermute | solution.py:200
  5.0 1.3 %collective-permute-start.2 = (s32[8,4]{0,1:T(4,128)}, s32[8,4]{0,1:T(4,128)S(1)}, u32[]{:S(2)}, u32[]{:S(2)}) collective-permute-start(s32[8,4]{0,1:T(4,128)} %bitcast.42), channel_id=1, source_target_pairs={{0,24},{4,28},{8,0},{12,4},{16,8},{20,12},{24,16},{28,20},{1,25},{... | collective-permute-start | bytes 392 | tf_op jit(solution)/shard_map/ppermute | solution.py:200
  6.3 0.5 collective-permute-start.1
  6.9 1.6 %copy-done.2 = f32[1,1,1,8,4,128,128]{6,5,4,3,2,1,0:T(8,128)S(1)} copy-done((f32[1,1,1,8,4,128,128]{6,5,4,3,2,1,0:T(8,128)S(1)}, f32[1,1,1,8,4,128,128]{6,5,4,3,2,1,0:T(8,128)}, u32[]{:S(2)}) %copy-start.2) | copy-done | bytes 2097176
  8.5 0.8 copy-done.6
  9.3 0.8 copy-done.7
  10.2 1.0 copy-done.5
  11.2 0.3 collective-permute-start.5
  11.5 3.8 %collective-permute-start.9 = (f32[2,4,128,128]{3,2,1,0:T(8,128)}, f32[2,4,128,128]{3,2,1,0:T(8,128)}, u32[]{:S(2)}, u32[]{:S(2)}) collective-permute-start(f32[2,4,128,128]{3,2,1,0:T(8,128)} %copy-done.6), channel_id=1, source_target_pairs={{0,24},{4,28},{8,0},{12,4},{16,8},{20,12},{24,16},{28,20},{1,25},{... | collective-permute-start | bytes 1572872 | tf_op jit(solution)/shard_map/ppermute | solution.py:172
  15.3 0.6 collective-permute-start.7
  16.0 0.7 select_reduce_fusion
  17.1 1.9 %copy-done = f32[1,1,1,3,8,2,128,128]{7,6,5,4,3,2,1,0:T(8,128)S(1)} copy-done((f32[1,1,1,3,8,2,128,128]{7,6,5,4,3,2,1,0:T(8,128)S(1)}, f32[1,1,1,3,8,2,128,128]{7,6,5,4,3,2,1,0:T(8,128)}, u32[]{:S(2)}) %copy-start) | copy-done | bytes 3145752
  19.0 1.6 %copy-done.3 = f32[1,1,1,8,4,128,128]{6,5,4,3,2,1,0:T(8,128)S(1)} copy-done((f32[1,1,1,8,4,128,128]{6,5,4,3,2,1,0:T(8,128)S(1)}, f32[1,1,1,8,4,128,128]{6,5,4,3,2,1,0:T(8,128)}, u32[]{:S(2)}) %copy-start.3) | copy-done | bytes 2097176
  20.6 2.0 %accumulate.8 = (f32[25,128,128]{2,1,0:T(8,128)S(1)}, f32[8,128]{1,0:T(8,128)S(1)}) custom-call(s32[261]{0:T(512)S(1)} %concatenate.7.scalar_ref, f32[3,8,2,128,128]{4,3,2,1,0:T(8,128)S(1)} %bitcast.21, f32[3,8,2,128,128]{4,3,2,1,0:T(8,128)S(1)} %bitcast.22, f32[3,8,2,128,128]{4,3,2,1,0:T(8,128)S(1)} %bitcast.23, f32[3,8,2,128,128]{4,3,2,1,0:T(8,128)S(1)} %bitcast.24, ...), custom_call_target="tpu_custom_call" | custom-call | flops 805306368 | bytes 6422528 | tf_op jit(solution)/shard_map/accumulate/pallas_call | solution.py:138
  22.6 3.8 %collective-permute-done.5.refs_0_.refs_2_.refs_1_ = f32[2,4,128,128]{3,2,1,0:T(8,128)} collective-permute-done((f32[2,4,128,128]{3,2,1,0:T(8,128)}, f32[2,4,128,128]{3,2,1,0:T(8,128)}, u32[]{:S(2)}, u32[]{:S(2)}) %collective-permute-start.5) | collective-permute-done | bytes 524320 | tf_op jit(solution)/shard_map/ppermute | solution.py:172
  26.3 1.1 pick.12
  27.4 1.5 %collective-permute-start.6 = (f32[2,4,128,128]{3,2,1,0:T(8,128)S(1)}, f32[2,4,128,128]{3,2,1,0:T(8,128)S(1)}, u32[]{:S(2)}, u32[]{:S(2)}) collective-permute-start(f32[2,4,128,128]{3,2,1,0:T(8,128)S(1)} %pick.12), channel_id=1, source_target_pairs={{0,4},{4,0},{8,12},{12,8},{16,20},{20,16},{24,28},{28,24},{1,5},{5... | collective-permute-start | bytes 1572872 | tf_op jit(solution)/shard_map/ppermute | solution.py:175
  29.0 2.3 %collective-permute-start.10 = (f32[2,4,128,128]{3,2,1,0:T(8,128)S(1)}, f32[2,4,128,128]{3,2,1,0:T(8,128)S(1)}, u32[]{:S(2)}, u32[]{:S(2)}) collective-permute-start(f32[2,4,128,128]{3,2,1,0:T(8,128)S(1)} %pick.16), channel_id=1, source_target_pairs={{0,24},{4,28},{8,0},{12,4},{16,8},{20,12},{24,16},{28,20},{1,25},{... | collective-permute-start | bytes 1572872 | tf_op jit(solution)/shard_map/ppermute | solution.py:172
  31.3 10.4 %collective-permute-done.7.refs_3_.refs_0_ = f32[4,4,128,128]{3,2,1,0:T(8,128)} collective-permute-done((f32[4,4,128,128]{3,2,1,0:T(8,128)}, f32[4,4,128,128]{3,2,1,0:T(8,128)}, u32[]{:S(2)}, u32[]{:S(2)}) %collective-permute-start.7) | collective-permute-done | bytes 1048608 | tf_op jit(solution)/shard_map/ppermute | solution.py:175
  41.7 3.0 %accumulate.9 = (f32[25,128,128]{2,1,0:T(8,128)S(1)}, f32[8,128]{1,0:T(8,128)S(1)}) custom-call(s32[261]{0:T(512)S(1)} %concatenate.7.scalar_ref, f32[3,8,2,128,128]{4,3,2,1,0:T(8,128)S(1)} %bitcast.25, f32[3,8,2,128,128]{4,3,2,1,0:T(8,128)S(1)} %collective-permute-done.4.refs_1_.refs_2_.refs_0_.refs_3_, ...), custom_call_target="tpu_custom_call", output_to_operand_aliasing={{0}: (5, {})} | custom-call | flops 402653184 | bytes 4849664 | tf_op jit(solution)/shard_map/accumulate/pallas_call | solution.py:138
  44.7 1.1 pick.18
  46.0 6.8 %collective-permute-done.6.refs_1_.refs_3_ = f32[2,4,128,128]{3,2,1,0:T(8,128)S(1)} collective-permute-done((f32[2,4,128,128]{3,2,1,0:T(8,128)S(1)}, f32[2,4,128,128]{3,2,1,0:T(8,128)S(1)}, u32[]{:S(2)}, u32[]{:S(2)}) %collective-permute-start.6) | collective-permute-done | bytes 524320 | tf_op jit(solution)/shard_map/ppermute | solution.py:175
  52.9 0.5 collective-permute-start.8
  53.4 2.9 %accumulate.10 = (f32[25,128,128]{2,1,0:T(8,128)S(1)}, f32[8,128]{1,0:T(8,128)S(1)}) custom-call(s32[261]{0:T(512)S(1)} %concatenate.7.scalar_ref, f32[3,8,2,128,128]{4,3,2,1,0:T(8,128)S(1)} %bitcast.26, f32[3,8,2,128,128]{4,3,2,1,0:T(8,128)S(1)} %collective-permute-done.4.refs_1_.refs_2_.refs_0_.refs_3_, ...), custom_call_target="tpu_custom_call", output_to_operand_aliasing={{0}: (5, {})} | custom-call | flops 402653184 | bytes 4849664 | tf_op jit(solution)/shard_map/accumulate/pallas_call | solution.py:138
  56.3 1.1 pick.21
  57.6 1.6 %accumulate.11 = (f32[25,128,128]{2,1,0:T(8,128)S(1)}, f32[8,128]{1,0:T(8,128)S(1)}) custom-call(s32[261]{0:T(512)S(1)} %concatenate.7.scalar_ref, f32[3,8,2,128,128]{4,3,2,1,0:T(8,128)S(1)} %bitcast.27, f32[3,8,2,128,128]{4,3,2,1,0:T(8,128)S(1)} %collective-permute-done.4.refs_1_.refs_2_.refs_0_.refs_3_, ...), custom_call_target="tpu_custom_call", output_to_operand_aliasing={{0}: (5, {})} | custom-call | flops 402653184 | bytes 4849664 | tf_op jit(solution)/shard_map/accumulate/pallas_call | solution.py:138
  59.1 4.9 %collective-permute-done.13.refs_1_.refs_4_ = f32[2,4,128,128]{3,2,1,0:T(8,128)S(1)} collective-permute-done((f32[2,4,128,128]{3,2,1,0:T(8,128)S(1)}, f32[2,4,128,128]{3,2,1,0:T(8,128)S(1)}, u32[]{:S(2)}, u32[]{:S(2)}) %collective-permute-start.13) | collective-permute-done | bytes 524320 | tf_op jit(solution)/shard_map/ppermute | solution.py:175
  64.1 1.1 pick.19
  65.1 0.5 collective-permute-start.14
  65.7 1.1 pick.17
  66.7 0.6 collective-permute-start.11
  67.4 7.9 %collective-permute-done.16.refs_5_ = f32[2,4,128,128]{3,2,1,0:T(8,128)S(1)} collective-permute-done((f32[2,4,128,128]{3,2,1,0:T(8,128)S(1)}, f32[2,4,128,128]{3,2,1,0:T(8,128)S(1)}, u32[]{:S(2)}, u32[]{:S(2)}) %collective-permute-start.16) | collective-permute-done | bytes 524320 | tf_op jit(solution)/shard_map/ppermute | solution.py:175
  75.3 0.4 collective-permute-start.17
  75.7 1.6 %accumulate.12 = (f32[25,128,128]{2,1,0:T(8,128)S(1)}, f32[8,128]{1,0:T(8,128)S(1)}) custom-call(s32[261]{0:T(512)S(1)} %concatenate.7.scalar_ref, f32[3,8,2,128,128]{4,3,2,1,0:T(8,128)S(1)} %bitcast.28, f32[3,8,2,128,128]{4,3,2,1,0:T(8,128)S(1)} %collective-permute-done.4.refs_1_.refs_2_.refs_0_.refs_3_, ...), custom_call_target="tpu_custom_call", output_to_operand_aliasing={{0}: (6, {})} | custom-call | flops 402653184 | bytes 4849664 | tf_op jit(solution)/shard_map/accumulate/pallas_call | solution.py:138
  77.3 0.8 collective-permute-done.14.refs_0_.refs_4_
  78.2 0.6 collective-permute-start.15
  78.9 7.7 %collective-permute-done.11.refs_4_ = f32[2,4,128,128]{3,2,1,0:T(8,128)S(1)} collective-permute-done((f32[2,4,128,128]{3,2,1,0:T(8,128)S(1)}, f32[2,4,128,128]{3,2,1,0:T(8,128)S(1)}, u32[]{:S(2)}, u32[]{:S(2)}) %collective-permute-start.11) | collective-permute-done | bytes 524320 | tf_op jit(solution)/shard_map/ppermute | solution.py:175
  86.5 0.4 collective-permute-start.12
  87.0 2.1 %accumulate.13 = (f32[25,128,128]{2,1,0:T(8,128)S(1)}, f32[8,128]{1,0:T(8,128)}) custom-call(s32[261]{0:T(512)S(1)} %concatenate.7.scalar_ref, f32[3,8,2,128,128]{4,3,2,1,0:T(8,128)S(1)} %collective-permute-done.4.refs_1_.refs_2_.refs_0_.refs_3_, ...), custom_call_target="tpu_custom_call", output_to_operand_aliasing={{0}: (7, {})} | custom-call | flops 402653184 | bytes 4849664 | tf_op jit(solution)/shard_map/accumulate/pallas_call | solution.py:138
  89.1 0.3 collective-permute-done.17.refs_3_
  89.4 1.5 %accumulate.14 = (f32[25,128,128]{2,1,0:T(8,128)S(1)}, f32[8,128]{1,0:T(8,128)}) custom-call(s32[261]{0:T(512)S(1)} %concatenate.7.scalar_ref, f32[3,8,2,128,128]{4,3,2,1,0:T(8,128)S(1)} %collective-permute-done.4.refs_1_.refs_2_.refs_0_.refs_3_, ...), custom_call_target="tpu_custom_call", output_to_operand_aliasing={{0}: (6, {})} | custom-call | flops 402653184 | bytes 4849664 | tf_op jit(solution)/shard_map/accumulate/pallas_call | solution.py:138
  90.9 5.8 %collective-permute-done.15.refs_4_ = f32[2,4,128,128]{3,2,1,0:T(8,128)S(1)} collective-permute-done((f32[2,4,128,128]{3,2,1,0:T(8,128)S(1)}, f32[2,4,128,128]{3,2,1,0:T(8,128)S(1)}, u32[]{:S(2)}, u32[]{:S(2)}) %collective-permute-start.15) | collective-permute-done | bytes 524320 | tf_op jit(solution)/shard_map/ppermute | solution.py:175
  96.7 2.8 %collective-permute-done.12.refs_3_ = f32[2,4,128,128]{3,2,1,0:T(8,128)S(1)} collective-permute-done((f32[2,4,128,128]{3,2,1,0:T(8,128)S(1)}, f32[2,4,128,128]{3,2,1,0:T(8,128)S(1)}, u32[]{:S(2)}, u32[]{:S(2)}) %collective-permute-start.12) | collective-permute-done | bytes 524320 | tf_op jit(solution)/shard_map/ppermute | solution.py:172
  99.6 1.5 %accumulate.15 = (f32[25,128,128]{2,1,0:T(8,128)S(1)}, f32[8,128]{1,0:T(8,128)}) custom-call(s32[261]{0:T(512)S(1)} %concatenate.7.scalar_ref, f32[3,8,2,128,128]{4,3,2,1,0:T(8,128)S(1)} %collective-permute-done.4.refs_1_.refs_2_.refs_0_.refs_3_, ...), custom_call_target="tpu_custom_call", output_to_operand_aliasing={{0}: (6, {})} | custom-call | flops 402653184 | bytes 4849664 | tf_op jit(solution)/shard_map/accumulate/pallas_call | solution.py:138
  101.1 1.6 %collective-permute-start.18 = (f32[12,128,128]{2,1,0:T(8,128)S(1)}, f32[12,128,128]{2,1,0:T(8,128)S(1)}, u32[]{:S(2)}, u32[]{:S(2)}) collective-permute-start(f32[12,128,128]{2,1,0:T(8,128)S(1)} %slice.7), channel_id=1, source_target_pairs={{0,1},{1,0},{2,3},{3,2},{4,5},{5,4},{6,7},{7,6},{8,9},{9,8},{10,11... | collective-permute-start | bytes 2359304 | tf_op jit(solution)/shard_map/ppermute | solution.py:234
  102.7 16.2 %collective-permute-done.18 = f32[12,128,128]{2,1,0:T(8,128)S(1)} collective-permute-done((f32[12,128,128]{2,1,0:T(8,128)S(1)}, f32[12,128,128]{2,1,0:T(8,128)S(1)}, u32[]{:S(2)}, u32[]{:S(2)}) %collective-permute-start.18) | collective-permute-done | bytes 786464 | tf_op jit(solution)/shard_map/ppermute | solution.py:234
  118.9 1.0 add_bitcast_fusion
  (44 shorter events, 1.1 us)
Async XLA Ops:
  0.0 41.7 %collective-permute-start.4 = (f32[3,8,2,128,128]{4,3,2,1,0:T(8,128)}, f32[3,8,2,128,128]{4,3,2,1,0:T(8,128)S(1)}, u32[]{:S(2)}, u32[]{:S(2)}) collective-permute-start(f32[3,8,2,128,128]{4,3,2,1,0:T(8,128)} %bitcast.20), channel_id=1, source_target_pairs={{0,2},{2,0},{1,3},{3,1},{4,6},{6,4},{5,7},{7,5},{8,10},{10,8},{9,1... | collective-permute-start | bytes 9437192 | tf_op jit(solution)/shard_map/ppermute | solution.py:190
  0.5 10.8 %collective-permute-start.3 = (s32[8,4]{0,1:T(4,128)}, s32[8,4]{0,1:T(4,128)S(1)}, u32[]{:S(2)}, u32[]{:S(2)}) collective-permute-start(s32[8,4]{0,1:T(4,128)} %bitcast.41), channel_id=1, source_target_pairs={{0,20},{4,24},{8,28},{12,0},{16,4},{20,8},{24,12},{28,16},{1,21},{... | collective-permute-start | bytes 392 | tf_op jit(solution)/shard_map/ppermute | solution.py:200
  5.0 6.6 %collective-permute-start.2 = (s32[8,4]{0,1:T(4,128)}, s32[8,4]{0,1:T(4,128)S(1)}, u32[]{:S(2)}, u32[]{:S(2)}) collective-permute-start(s32[8,4]{0,1:T(4,128)} %bitcast.42), channel_id=1, source_target_pairs={{0,24},{4,28},{8,0},{12,4},{16,8},{20,12},{24,16},{28,20},{1,25},{... | collective-permute-start | bytes 392 | tf_op jit(solution)/shard_map/ppermute | solution.py:200
  6.3 9.0 %collective-permute-start.1 = (s32[8,4]{0,1:T(4,128)}, s32[8,4]{0,1:T(4,128)S(1)}, u32[]{:S(2)}, u32[]{:S(2)}) collective-permute-start(s32[8,4]{0,1:T(4,128)} %bitcast.43), channel_id=1, source_target_pairs={{0,28},{4,0},{8,4},{12,8},{16,12},{20,16},{24,20},{28,24},{1,29},{... | collective-permute-start | bytes 392 | tf_op jit(solution)/shard_map/ppermute | solution.py:200
  6.9 9.1 %collective-permute-start = (s32[3,8,2]{1,2,0:T(2,128)}, s32[3,8,2]{1,2,0:T(2,128)S(1)}, u32[]{:S(2)}, u32[]{:S(2)}) collective-permute-start(s32[3,8,2]{1,2,0:T(2,128)} %bitcast.48), channel_id=1, source_target_pairs={{0,2},{2,0},{1,3},{3,1},{4,6},{6,4},{5,7},{7,5},{8,10},{10,8},{9,1... | collective-permute-start | bytes 584 | tf_op jit(solution)/shard_map/ppermute | solution.py:190
  6.9 1.6 %copy-start.2 = (f32[1,1,1,8,4,128,128]{6,5,4,3,2,1,0:T(8,128)S(1)}, f32[1,1,1,8,4,128,128]{6,5,4,3,2,1,0:T(8,128)}, u32[]{:S(2)}) copy-start(f32[1,1,1,8,4,128,128]{6,5,4,3,2,1,0:T(8,128)} %param.7) | copy-start | bytes 6291460
  8.5 0.8 copy-start.6
  9.3 0.8 copy-start.7
  10.1 1.1 copy-start.9
  10.1 5.8 %copy-start.8 = (s32[1,1,1,8,4]{3,4,2,1,0:T(4,128)S(1)}, s32[1,1,1,8,4]{3,4,2,1,0:T(4,128)}, u32[]{:S(2)}) copy-start(s32[1,1,1,8,4]{3,4,2,1,0:T(4,128)} %param.8) | copy-start | bytes 388
  10.1 5.9 %copy-start.10 = (s32[1,1,24]{2,1,0:T(1,128)S(1)}, s32[1,1,24]{2,1,0:T(1,128)}, u32[]{:S(2)}) copy-start(s32[1,1,24]{2,1,0:T(1,128)} %param.9) | copy-start | bytes 292
  10.2 1.0 copy-start.5
  11.2 15.1 %collective-permute-start.5 = (f32[2,4,128,128]{3,2,1,0:T(8,128)}, f32[2,4,128,128]{3,2,1,0:T(8,128)}, u32[]{:S(2)}, u32[]{:S(2)}) collective-permute-start(f32[2,4,128,128]{3,2,1,0:T(8,128)} %copy-done.7), channel_id=1, source_target_pairs={{0,24},{4,28},{8,0},{12,4},{16,8},{20,12},{24,16},{28,20},{1,25},{... | collective-permute-start | bytes 1572872 | tf_op jit(solution)/shard_map/ppermute | solution.py:172
  11.5 33.1 %collective-permute-start.9 = (f32[2,4,128,128]{3,2,1,0:T(8,128)}, f32[2,4,128,128]{3,2,1,0:T(8,128)}, u32[]{:S(2)}, u32[]{:S(2)}) collective-permute-start(f32[2,4,128,128]{3,2,1,0:T(8,128)} %copy-done.6), channel_id=1, source_target_pairs={{0,24},{4,28},{8,0},{12,4},{16,8},{20,12},{24,16},{28,20},{1,25},{... | collective-permute-start | bytes 1572872 | tf_op jit(solution)/shard_map/ppermute | solution.py:172
  15.3 26.3 %collective-permute-start.7 = (f32[4,4,128,128]{3,2,1,0:T(8,128)}, f32[4,4,128,128]{3,2,1,0:T(8,128)}, u32[]{:S(2)}, u32[]{:S(2)}) collective-permute-start(f32[4,4,128,128]{3,2,1,0:T(8,128)} %copy-done.5), channel_id=1, source_target_pairs={{0,4},{4,0},{8,12},{12,8},{16,20},{20,16},{24,28},{28,24},{1,5},{5... | collective-permute-start | bytes 3145736 | tf_op jit(solution)/shard_map/ppermute | solution.py:175
  17.1 1.9 %copy-start = (f32[1,1,1,3,8,2,128,128]{7,6,5,4,3,2,1,0:T(8,128)S(1)}, f32[1,1,1,3,8,2,128,128]{7,6,5,4,3,2,1,0:T(8,128)}, u32[]{:S(2)}) copy-start(f32[1,1,1,3,8,2,128,128]{7,6,5,4,3,2,1,0:T(8,128)} %param.5) | copy-start | bytes 9437188
  19.0 1.6 %copy-start.3 = (f32[1,1,1,8,4,128,128]{6,5,4,3,2,1,0:T(8,128)S(1)}, f32[1,1,1,8,4,128,128]{6,5,4,3,2,1,0:T(8,128)}, u32[]{:S(2)}) copy-start(f32[1,1,1,8,4,128,128]{6,5,4,3,2,1,0:T(8,128)} %param.7) | copy-start | bytes 6291460
  27.4 14.3 %copy-start.1 = (f32[1,1,1,3,8,2,128,128]{7,6,5,4,3,2,1,0:T(8,128)S(1)}, f32[1,1,1,3,8,2,128,128]{7,6,5,4,3,2,1,0:T(8,128)}, u32[]{:S(2)}) copy-start(f32[1,1,1,3,8,2,128,128]{7,6,5,4,3,2,1,0:T(8,128)} %param.5) | copy-start | bytes 9437188
  27.4 25.4 %collective-permute-start.6 = (f32[2,4,128,128]{3,2,1,0:T(8,128)S(1)}, f32[2,4,128,128]{3,2,1,0:T(8,128)S(1)}, u32[]{:S(2)}, u32[]{:S(2)}) collective-permute-start(f32[2,4,128,128]{3,2,1,0:T(8,128)S(1)} %pick.12), channel_id=1, source_target_pairs={{0,4},{4,0},{8,12},{12,8},{16,20},{20,16},{24,28},{28,24},{1,5},{5... | collective-permute-start | bytes 1572872 | tf_op jit(solution)/shard_map/ppermute | solution.py:175
  29.0 27.3 %collective-permute-start.10 = (f32[2,4,128,128]{3,2,1,0:T(8,128)S(1)}, f32[2,4,128,128]{3,2,1,0:T(8,128)S(1)}, u32[]{:S(2)}, u32[]{:S(2)}) collective-permute-start(f32[2,4,128,128]{3,2,1,0:T(8,128)S(1)} %pick.16), channel_id=1, source_target_pairs={{0,24},{4,28},{8,0},{12,4},{16,8},{20,12},{24,16},{28,20},{1,25},{... | collective-permute-start | bytes 1572872 | tf_op jit(solution)/shard_map/ppermute | solution.py:172
  41.7 3.0 %copy-start.4 = (f32[1,1,1,8,4,128,128]{6,5,4,3,2,1,0:T(8,128)S(1)}, f32[1,1,1,8,4,128,128]{6,5,4,3,2,1,0:T(8,128)}, u32[]{:S(2)}) copy-start(f32[1,1,1,8,4,128,128]{6,5,4,3,2,1,0:T(8,128)} %param.7) | copy-start | bytes 6291460
  45.8 18.3 %collective-permute-start.13 = (f32[2,4,128,128]{3,2,1,0:T(8,128)S(1)}, f32[2,4,128,128]{3,2,1,0:T(8,128)S(1)}, u32[]{:S(2)}, u32[]{:S(2)}) collective-permute-start(f32[2,4,128,128]{3,2,1,0:T(8,128)S(1)} %pick.18), channel_id=1, source_target_pairs={{0,4},{4,0},{8,12},{12,8},{16,20},{20,16},{24,28},{28,24},{1,5},{5... | collective-permute-start | bytes 1572872 | tf_op jit(solution)/shard_map/ppermute | solution.py:175
  52.9 12.8 %collective-permute-start.8 = (f32[2,4,128,128]{3,2,1,0:T(8,128)S(1)}, f32[2,4,128,128]{3,2,1,0:T(8,128)S(1)}, u32[]{:S(2)}, u32[]{:S(2)}) collective-permute-start(f32[2,4,128,128]{3,2,1,0:T(8,128)S(1)} %pick.14), channel_id=1, source_target_pairs={{0,24},{4,28},{8,0},{12,4},{16,8},{20,12},{24,16},{28,20},{1,25},{... | collective-permute-start | bytes 1572872 | tf_op jit(solution)/shard_map/ppermute | solution.py:172
  57.4 17.9 %collective-permute-start.16 = (f32[2,4,128,128]{3,2,1,0:T(8,128)S(1)}, f32[2,4,128,128]{3,2,1,0:T(8,128)S(1)}, u32[]{:S(2)}, u32[]{:S(2)}) collective-permute-start(f32[2,4,128,128]{3,2,1,0:T(8,128)S(1)} %pick.21), channel_id=1, source_target_pairs={{0,4},{4,0},{8,12},{12,8},{16,20},{20,16},{24,28},{28,24},{1,5},{5... | collective-permute-start | bytes 1572872 | tf_op jit(solution)/shard_map/ppermute | solution.py:175
  65.1 13.0 %collective-permute-start.14 = (f32[2,4,128,128]{3,2,1,0:T(8,128)S(1)}, f32[2,4,128,128]{3,2,1,0:T(8,128)S(1)}, u32[]{:S(2)}, u32[]{:S(2)}) collective-permute-start(f32[2,4,128,128]{3,2,1,0:T(8,128)S(1)} %pick.19), channel_id=1, source_target_pairs={{0,24},{4,28},{8,0},{12,4},{16,8},{20,12},{24,16},{28,20},{1,25},{... | collective-permute-start | bytes 1572872 | tf_op jit(solution)/shard_map/ppermute | solution.py:172
  66.7 19.8 %collective-permute-start.11 = (f32[2,4,128,128]{3,2,1,0:T(8,128)S(1)}, f32[2,4,128,128]{3,2,1,0:T(8,128)S(1)}, u32[]{:S(2)}, u32[]{:S(2)}) collective-permute-start(f32[2,4,128,128]{3,2,1,0:T(8,128)S(1)} %pick.17), channel_id=1, source_target_pairs={{0,4},{4,0},{8,12},{12,8},{16,20},{20,16},{24,28},{28,24},{1,5},{5... | collective-permute-start | bytes 1572872 | tf_op jit(solution)/shard_map/ppermute | solution.py:175
  75.3 14.1 %collective-permute-start.17 = (f32[2,4,128,128]{3,2,1,0:T(8,128)S(1)}, f32[2,4,128,128]{3,2,1,0:T(8,128)S(1)}, u32[]{:S(2)}, u32[]{:S(2)}) collective-permute-start(f32[2,4,128,128]{3,2,1,0:T(8,128)S(1)} %collective-permute-done.16.refs_5_), channel_id=1, source_target_pairs={{0,24},{4,28},{8,0},{12,4},{16,8},{20,12},{24,16},{28,20},{1,25},{... | collective-permute-start | bytes 1572872 | tf_op jit(solution)/shard_map/ppermute | solution.py:172
  78.2 18.5 %collective-permute-start.15 = (f32[2,4,128,128]{3,2,1,0:T(8,128)S(1)}, f32[2,4,128,128]{3,2,1,0:T(8,128)S(1)}, u32[]{:S(2)}, u32[]{:S(2)}) collective-permute-start(f32[2,4,128,128]{3,2,1,0:T(8,128)S(1)} %pick.20), channel_id=1, source_target_pairs={{0,4},{4,0},{8,12},{12,8},{16,20},{20,16},{24,28},{28,24},{1,5},{5... | collective-permute-start | bytes 1572872 | tf_op jit(solution)/shard_map/ppermute | solution.py:175
  86.5 13.0 %collective-permute-start.12 = (f32[2,4,128,128]{3,2,1,0:T(8,128)S(1)}, f32[2,4,128,128]{3,2,1,0:T(8,128)S(1)}, u32[]{:S(2)}, u32[]{:S(2)}) collective-permute-start(f32[2,4,128,128]{3,2,1,0:T(8,128)S(1)} %collective-permute-done.11.refs_4_), channel_id=1, source_target_pairs={{0,24},{4,28},{8,0},{12,4},{16,8},{20,12},{24,16},{28,20},{1,25},{... | collective-permute-start | bytes 1572872 | tf_op jit(solution)/shard_map/ppermute | solution.py:172
  101.1 17.8 %collective-permute-start.18 = (f32[12,128,128]{2,1,0:T(8,128)S(1)}, f32[12,128,128]{2,1,0:T(8,128)S(1)}, u32[]{:S(2)}, u32[]{:S(2)}) collective-permute-start(f32[12,128,128]{2,1,0:T(8,128)S(1)} %slice.7), channel_id=1, source_target_pairs={{0,1},{1,0},{2,3},{3,2},{4,5},{5,4},{6,7},{7,6},{8,9},{9,8},{10,11... | collective-permute-start | bytes 2359304 | tf_op jit(solution)/shard_map/ppermute | solution.py:234

commit v5 on v4

v5 whole, which is shorter than its diff:
```python
import jax
import jax.numpy as jnp
from jax import lax
from jax.experimental import pallas as pl
from jax.experimental.pallas import tpu as pltpu
from jax.sharding import PartitionSpec as P

STEPS = 4
CB = 8
HALVES = 2
QUARTERS = HALVES * HALVES

bf16 = jnp.bfloat16
f32 = jnp.float32

Z_CHUNKS = {
    1: ((2, 0), (2, 0)),
    2: ((2, 1), (2, 1)),
    3: ((2, 2), (2, 2)),
    4: ((2, 3), (3, 0)),
    5: ((3, 3), (3, 1)),
    6: (None, (3, 2)),
    7: (None, (3, 3)),
}
X_CHUNKS = {
    1: ((1, 2), None),
    2: ((1, 3), None),
    3: ((1, 0), (1, 0)),
    4: ((1, 1), (1, 1)),
    5: ((3, 0), (1, 2)),
    6: ((3, 1), (1, 3)),
    7: ((3, 2), (2, 3)),
}

in_vmem = pl.BlockSpec(memory_space=pltpu.VMEM)
anywhere = pl.BlockSpec(memory_space=pl.ANY)


def whole(shape):
    return pl.BlockSpec(shape, lambda *_: (0,) * len(shape))


def lower_lanes(shape):
    return lax.broadcasted_iota(jnp.int32, shape, len(shape) - 1) < shape[-1] // 2


def swap_lanes(x):
    return pltpu.roll(x, x.shape[-1] // 2, x.ndim - 1)


def cut(right_ref, out_ref, half, at=0):
    per, bpr, bs, _ = right_ref.shape
    lower = lower_lanes((bs, bs))
    for k in range(per):
        for pair in range(bpr // 2):
            even, odd = right_ref[k, 2 * pair], right_ref[k, 2 * pair + 1]
            if half == 0:
                both = jnp.where(lower, even, swap_lanes(odd))
            else:
                both = jnp.where(lower, swap_lanes(even), odd)
            out_ref[at + k, :, pair * bs:(pair + 1) * bs] = both


def own_spec(right, k_half):
    return pl.BlockSpec((right.shape[0] // HALVES,) + right.shape[1:], lambda *_: (k_half, 0, 0, 0))


def quarter_shape(right):
    kb, bpr, bs, _ = right.shape
    return (kb // HALVES, bs, bpr * bs // HALVES)


def own_quarters(right, quarters, *others):
    per, bs, width = quarter_shape(right)

    def kernel(*refs):
        for n, quarter in enumerate(quarters):
            cut(refs[n], refs[-1], quarter // HALVES, n * per)

    out_shape = jax.ShapeDtypeStruct((len(quarters) * per, bs, width), right.dtype)
    return pl.pallas_call(
        kernel,
        grid=(1,),
        in_specs=[own_spec(right, quarter % HALVES) for quarter in quarters] + [anywhere] * len(others),
        out_specs=whole(out_shape.shape),
        out_shape=out_shape,
        compiler_params=pltpu.CompilerParams(vmem_limit_bytes=12 * 1024 * 1024),
        cost_estimate=pl.CostEstimate(flops=0, bytes_accessed=12 * out_shape.size, transcendentals=0),
        name="own_quarters",
    )(*[right] * len(quarters), *others)


def pick(odd, right, even_part, odd_part, *others):
    parts = (even_part, odd_part)
    per, bs, width = quarter_shape(right)

    def kernel(odd_ref, *refs):
        out_ref = refs[-1]

        def copy_from(n):
            array, at = parts[n]
            if array is None:
                cut(refs[n], out_ref, at // HALVES)
            else:
                out_ref[...] = refs[n][at * per:(at + 1) * per]

        pl.when(odd_ref[0] == 0)(lambda: copy_from(0))
        pl.when(odd_ref[0] != 0)(lambda: copy_from(1))

    out_shape = jax.ShapeDtypeStruct((per, bs, width), right.dtype)
    specs = [own_spec(right, at % HALVES) if array is None else in_vmem for array, at in parts]
    return pl.pallas_call(
        kernel,
        grid=(1,),
        in_specs=[pl.BlockSpec(memory_space=pltpu.SMEM)] + specs + [anywhere] * len(others),
        out_specs=whole(out_shape.shape),
        out_shape=out_shape,
        compiler_params=pltpu.CompilerParams(vmem_limit_bytes=8 * 1024 * 1024),
        cost_estimate=pl.CostEstimate(flops=0, bytes_accessed=8 * out_shape.size, transcendentals=0),
        name="pick",
    )(odd, *[right if array is None else array for array, _ in parts], *others)


def accumulate(scalars, lefts, chunks, totals, nc, finish=None):
    _, kb, lpb, bs, _ = lefts[0].shape
    per = kb // HALVES
    own = totals is None
    bpr = chunks[0][0].shape[1] if own else HALVES * chunks[0][0].shape[2] // bs
    width = bpr * bs // HALVES
    lanes = bs // HALVES
    products = lpb * bpr
    odd_at = STEPS * kb * products
    packed = nc // 4
    if own:
        touched = list(range(HALVES))
    else:
        touched = sorted({what[1] // HALVES for _, _, both in chunks for what in both if what is not None})
    sides = [(c, side) for c in range(len(chunks)) for side in range(2) if chunks[c][2][side] is not None]
    sides = [(c, side) for c, side in sides if side == 0 or chunks[c][2][0] != chunks[c][2][1]]

    def kernel(scalar_ref, *refs):
        left_refs = dict(zip(sides, refs))
        right_refs = refs[len(sides):len(sides) + len(chunks)]
        outs = refs[len(sides) + len(chunks) + (0 if own else len(touched)):]
        total_refs = dict(zip(touched, outs))
        outs = outs[len(touched):]
        outs[0][...] = jnp.zeros_like(outs[0])
        odd = scalar_ref[odd_at]
        if own:
            for ref in total_refs.values():
                ref[...] = jnp.zeros_like(ref)

        def products_of(left, right):
            left = left.reshape(lpb * bs, bs)
            left_high = left.astype(bf16)
            left_low = (left - left_high.astype(f32)).astype(bf16)
            high = right.astype(bf16)
            low = (right - high.astype(f32)).astype(bf16)
            return jnp.dot(
                jnp.concatenate([left_high, left_low, left_high], axis=1),
                jnp.concatenate([high, high, low], axis=0),
                preferred_element_type=f32,
            )

        def add_own(left_ref, right_ref):
            for k in range(kb):
                out = products_of(left_ref[0, k], jnp.concatenate([right_ref[k, b] for b in range(bpr)], axis=1))
                for a in range(lpb):
                    for b in range(bpr):
                        n = scalar_ref[k * products + a * bpr + b]
                        for half in range(HALVES):
                            at = slice(half * lanes, (half + 1) * lanes)
                            total_refs[half][n, :, at] += out[a * bs:(a + 1) * bs, b * bs:(b + 1) * bs][:, at]

        def add(c, side):
            turn, quarter = chunks[c][2][side]
            half, k_half = divmod(quarter, HALVES)
            base = (turn * kb + k_half * per) * products
            left_ref, right_ref, total_ref = left_refs[c, side], right_refs[c], total_refs[half]
            for k in range(per):
                out = products_of(left_ref[0, k], right_ref[chunks[c][1] * per + k])
                for a in range(lpb):
                    for b in range(bpr):
                        n = scalar_ref[base + k * products + a * bpr + b]
                        at = (b % HALVES) * lanes
                        total_ref[n, :, at:at + lanes] += out[a * bs:(a + 1) * bs, b * lanes:(b + 1) * lanes]

        if own:
            add_own(left_refs[0, 0], right_refs[0])
            return
        for c, (_, _, both) in enumerate(chunks):
            if both[0] == both[1]:
                add(c, 0)
                continue
            if both[0] is not None:
                pl.when(odd == 0)(lambda c=c: add(c, 0))
            if both[1] is not None:
                pl.when(odd != 0)(lambda c=c: add(c, 1))
        if finish is not None:
            lower = lower_lanes((bs, bs))
            for kept, ref in enumerate(outs[1:]):
                for p in range(packed):
                    n = 2 * packed * kept + p
                    one, two = total_refs[finish][n], total_refs[finish][n + packed]
                    ref[p] = jnp.where(lower, one + swap_lanes(one), two + swap_lanes(two))

    def left_spec(turn, quarter):
        return pl.BlockSpec((1, per, lpb, bs, bs), lambda g, s: (s[odd_at + 1 + turn], quarter % HALVES, 0, 0, 0))

    operands = [lefts[chunks[c][2][side][0]] for c, side in sides] + [c[0] for c in chunks]
    if own:
        in_specs = [pl.BlockSpec((1, kb, lpb, bs, bs), lambda g, s: (s[odd_at + 1], 0, 0, 0, 0)), whole(chunks[0][0].shape)]
    else:
        in_specs = [left_spec(*chunks[c][2][side]) for c, side in sides] + [in_vmem] * len(chunks)
    held = len(operands) + 1
    if not own:
        operands += [totals[half] for half in touched]
        in_specs += [in_vmem] * len(touched)
    outs = [jax.ShapeDtypeStruct((nc + 1, bs, bs), f32)] * len(touched) + [jax.ShapeDtypeStruct((8, 128), jnp.int32)]
    if finish is not None:
        outs += [jax.ShapeDtypeStruct((packed, bs, bs), f32)] * 2
    parts = QUARTERS if own else len(chunks)
    flops = parts * per * 2 * lpb * bs * 3 * bs * width
    moved = 4 * parts * per * (lpb * bs * bs + bs * width)
    results = pl.pallas_call(
        kernel,
        grid_spec=pltpu.PrefetchScalarGridSpec(
            num_scalar_prefetch=1,
            grid=(1,),
            in_specs=in_specs,
            out_specs=[in_vmem] * len(outs),
        ),
        out_shape=outs,
        input_output_aliases={} if own else {held + n: n for n in range(len(touched))},
        compiler_params=pltpu.CompilerParams(vmem_limit_bytes=16 * 1024 * 1024),
        cost_estimate=pl.CostEstimate(flops=flops, bytes_accessed=moved, transcendentals=0),
        name="accumulate",
    )(scalars, *operands)
    totals = [None] * HALVES if own else list(totals)
    for half, total in zip(touched, results):
        totals[half] = total
    return (totals, *results[len(touched):])


def combine(kept, other):
    packed, bs, _ = kept[0].shape
    steps = 2 if packed % 2 == 0 else 1
    per = packed // steps

    def kernel(kept_0, kept_1, other_0, other_1, out_ref):
        lower = lower_lanes((bs, bs))
        for p in range(per):
            left = kept_0[p] + other_0[p]
            right = kept_1[p] + other_1[p]
            out_ref[0, p] = jnp.where(lower, left, swap_lanes(right))
            out_ref[1, p] = jnp.where(lower, swap_lanes(left), right)

    return pl.pallas_call(
        kernel,
        grid=(steps,),
        in_specs=[pl.BlockSpec((per, bs, bs), lambda g: (g, 0, 0))] * 4,
        out_specs=pl.BlockSpec((2, per, bs, bs), lambda g: (0, g, 0, 0)),
        out_shape=jax.ShapeDtypeStruct((2, packed, bs, bs), f32),
        name="combine",
    )(*kept, *other).reshape(2 * packed, bs, bs)


def shards(left_values, left_rows, right_values, right_cols, result_slots):
    rows_n, cols_n = (lax.axis_size(a) for a in ("row", "col"))
    row, col, rep = (lax.axis_index(a) for a in ("row", "col", "rep"))
    panels = left_values[0, 0, 0]
    panel_rows = left_rows[0, 0, 0]
    right = right_values[0, 0, 0]
    right_places = right_cols[0, 0, 0]
    slots = result_slots[0, 0]
    kb = right.shape[0]
    nc = slots.shape[0]
    per = kb // HALVES
    odd = (row % 2).astype(jnp.int32).reshape(1)

    z_pairs = [(r, (r - 2) % rows_n) for r in range(rows_n)]
    x_pairs = [(r, r ^ 1) for r in range(rows_n)]

    def along_z(chunk):
        return lax.ppermute(chunk, "row", z_pairs)

    def along_x(chunk):
        return lax.ppermute(chunk, "row", x_pairs)

    def sent(even_part, odd_part, *others):
        return pick(odd, right, even_part, odd_part, *others)

    z = {}
    x = {}
    z[1] = along_z(own_quarters(right, (0,)))
    x[1] = along_x(own_quarters(right, (2, 3)))

    shifts = sorted({turn % cols_n for turn in range(STEPS)})
    held = {
        shift: (panels, panel_rows) if shift == 0 else lax.ppermute((panels, panel_rows), "col", [(c, (c - shift) % cols_n) for c in range(cols_n)])
        for shift in shifts
    }
    place = [(col + turn) // cols_n for turn in range(STEPS)]
    lefts = [held[turn % cols_n][0] for turn in range(STEPS)]
    rows_at = jnp.stack([held[turn % cols_n][1][place[turn]] for turn in range(STEPS)])

    def right_of(held, turn):
        if turn % rows_n == 0:
            return held
        return lax.ppermute(held, "row", [(r, (r - turn) % rows_n) for r in range(rows_n)])

    cols_at = jnp.stack([right_of(right_places, turn) for turn in range(STEPS)])
    codes = rows_at[:, :, :, None] * CB + cols_at[:, :, None, :]
    order = (jnp.arange(nc, dtype=jnp.int32) + nc - nc // 2 * rep) % nc
    listed = codes[..., None] == slots
    where_to = nc - jnp.sum(jnp.where(listed, nc - order, 0), axis=-1, dtype=jnp.int32)
    scalars = jnp.concatenate([where_to.reshape(-1), odd, jnp.stack(place).astype(jnp.int32)])

    def add(totals, chunks, finish=None):
        return accumulate(scalars, lefts, chunks, totals, nc, finish)

    def along_z_part(stage):
        return (z[stage], 0, Z_CHUNKS[stage])

    def along_x_part(stage):
        return (*((x[1], stage - 1) if stage < 3 else (x[stage], 0)), X_CHUNKS[stage])

    def received(stage):
        return [along_z_part(stage), along_x_part(stage)]

    totals, done = add(None, [(right, 0, ((0, 0), (0, 0)))])
    z[2] = along_z(own_quarters(right, (1,), done))
    x[3] = along_x(sent((z[1], 0), (None, 0), done))
    z[3] = along_z(own_quarters(right, (2,), z[1], done))
    totals, done = add(totals, received(1))
    x[4] = along_x(sent((z[2], 0), (None, 1), done))
    z[4] = along_z(sent((None, 3), (x[3], 0), done))
    totals, done = add(totals, received(2))
    x[5] = along_x(sent((z[3], 0), (z[1], 0), done))
    z[5] = along_z(sent((x[1], 1), (x[4], 0), done))
    totals, done = add(totals, received(3))
    x[6] = along_x(sent((z[4], 0), (z[2], 0), done))
    z[6] = along_z(x[5])
    totals, done = add(totals, received(4))
    x[7] = along_x(sent((z[5], 0), (z[3], 0), done))
    z[7] = along_z(x[6])
    totals, done = add(totals, received(5))

    def to_partner(blocks):
        return lax.ppermute(blocks, "rep", [(0, 1), (1, 0)])

    totals, done, kept_0, send_0 = add(totals, [along_x_part(6)], 0)
    other_0 = to_partner(send_0)
    totals, done, kept_1, send_1 = add(totals, [along_z_part(6), along_x_part(7), along_z_part(7)], 1)
    other_1 = to_partner(send_1)
    return combine((kept_0, kept_1), (other_0, other_1))[None, None]


def solution(mesh):
    in_specs = (
        P("row", "rep", "col", None, None, None, None, None),
        P("row", "rep", "col", None, None, None),
        P("rep", "row", "col", None, None, None, None),
        P("rep", "row", "col", None, None),
        P("row", "col", None),
    )
    out_specs = P("row", "col", "rep", None, None)
    return jax.shard_map(shards, mesh=mesh, in_specs=in_specs, out_specs=out_specs, check_vma=False)
```

time: 120 us -> 114 us (0.950)
  waiting for transfers between devices: 67.6 us -> 44.1 us
  starting transfers between devices: 20.5 us -> 34.5 us
  Pallas kernels: 21.8 us -> 24.8 us
    ppermute x6, waiting for transfers between devices: 43.6 us -> 28.1 us  [along_x(): return lax.ppermute(chunk, 'row', x_pairs)]
    ppermute x7, starting transfers between devices: 8.31 us -> 19.3 us  [along_z(): return lax.ppermute(chunk, 'row', z_pairs)]
    ppermute x1 -> x2, waiting for transfers between devices: 16.2 us -> 8.35 us  [to_partner(): return lax.ppermute(blocks, 'rep', [(0, 1), (1, 0)])]
    pallas_call x8, Pallas kernels: 16.1 us -> 17.8 us  [accumulate(): pl.pallas_call(kernel, grid_spec=pltpu.PrefetchScalarGridSpec(num_scalar_...]
    ppermute x6, starting transfers between devices: 3.8 us -> 5.33 us  [along_x(): return lax.ppermute(chunk, 'row', x_pairs)]
    ppermute x1 -> x2, starting transfers between devices: 1.58 us -> 3.02 us  [to_partner(): return lax.ppermute(blocks, 'rep', [(0, 1), (1, 0)])]
    pallas_call x11 -> x12, Pallas kernels: 5.66 us -> 7.05 us  [the longest x7 3.77 us: pick(): pl.pallas_call(kernel, grid=(1,), in_specs=[pl.BlockSpec(memory_space=plt...]
    unnamed x22 -> x28, local copies, waits for them, and re-layouts: 7.64 us -> 8.37 us
  transfers between devices with their start and end apart: 19 -> 20, of which waited for: 11 -> 9; matrix products, arithmetic and copies ran while one was open for 1% -> 1% of each run, Pallas kernels for 17% -> 20%
where the time goes in v5:
time: 114 us; the launch traced here: 113 us
  waiting for transfers between devices  44.1 us (39%)
  starting transfers between devices  34.5 us (30%)
  Pallas kernels  24.8 us (22%)
  local copies, waits for them, and re-layouts  8.72 us (8%)
    ppermute x6, waiting for transfers between devices, along_x(): return lax.ppermute(chunk, 'row', x_pairs)  28.1 us
    ppermute x7, starting transfers between devices, along_z(): return lax.ppermute(chunk, 'row', z_pairs)  19.3 us
    pallas_call x8, Pallas kernels, accumulate(): pl.pallas_call(kernel, grid_spec=pltpu.PrefetchScalarGridSpec(num_scalar_...  17.8 us
    unnamed x28, local copies, waits for them, and re-layouts  8.37 us
    ppermute x2, waiting for transfers between devices, to_partner(): return lax.ppermute(blocks, 'rep', [(0, 1), (1, 0)])  8.35 us
    ppermute x7, waiting for transfers between devices, along_z(): return lax.ppermute(chunk, 'row', z_pairs)  7.71 us
    ppermute x3, starting transfers between devices, right_of(): lax.ppermute(held, 'row', [(r, (r - turn) % rows_n) for r in range(rows_n)])  6.4 us
    ppermute x6, starting transfers between devices, along_x(): return lax.ppermute(chunk, 'row', x_pairs)  5.33 us
  transfers between devices with their start and end apart: 20, of which 9 were waited for; matrix products, arithmetic and copies ran while one was open for 1% of the time, Pallas kernels for 20%

profile of v5, /device:TPU:0, one launch (start us, length us, event | category | flops | bytes accessed | tf_op | source)
XLA Modules:
  0.0 113.3 jit_solution(12920762994101959980)
XLA Ops:
  0.0 0.5 collective-permute-start.4
  0.5 4.5 %collective-permute-start.3 = (s32[8,4]{0,1:T(4,128)}, s32[8,4]{0,1:T(4,128)S(1)}, u32[]{:S(2)}, u32[]{:S(2)}) collective-permute-start(s32[8,4]{0,1:T(4,128)} %bitcast.35), channel_id=1, source_target_pairs={{0,20},{4,24},{8,28},{12,0},{16,4},{20,8},{24,12},{28,16},{1,21},{... | collective-permute-start | bytes 392 | tf_op jit(solution)/shard_map/ppermute | solution.py:310
  5.0 1.3 %collective-permute-start.2 = (s32[8,4]{0,1:T(4,128)}, s32[8,4]{0,1:T(4,128)S(1)}, u32[]{:S(2)}, u32[]{:S(2)}) collective-permute-start(s32[8,4]{0,1:T(4,128)} %bitcast.36), channel_id=1, source_target_pairs={{0,24},{4,28},{8,0},{12,4},{16,8},{20,12},{24,16},{28,20},{1,25},{... | collective-permute-start | bytes 392 | tf_op jit(solution)/shard_map/ppermute | solution.py:310
  6.3 0.5 collective-permute-start.1
  6.9 1.6 %copy-done = f32[1,1,1,8,4,128,128]{6,5,4,3,2,1,0:T(8,128)S(1)} copy-done((f32[1,1,1,8,4,128,128]{6,5,4,3,2,1,0:T(8,128)S(1)}, f32[1,1,1,8,4,128,128]{6,5,4,3,2,1,0:T(8,128)}, u32[]{:S(2)}) %copy-start) | copy-done | bytes 2097176
  8.7 0.8 copy-done.6
  9.5 0.3 own_quarters.5
  9.8 1.0 copy-done.5
  10.8 0.7 collective-permute-start.5
  11.5 1.3 %collective-permute-start.7 = (f32[8,128,256]{2,1,0:T(8,128)}, f32[8,128,256]{2,1,0:T(8,128)}, u32[]{:S(2)}, u32[]{:S(2)}) collective-permute-start(f32[8,128,256]{2,1,0:T(8,128)} %copy-done.5), channel_id=1, source_target_pairs={{0,4},{4,0},{8,12},{12,8},{16,20},{20,16},{24,28},{28,24},{1,5},{5... | collective-permute-start | bytes 3145736 | tf_op jit(solution)/shard_map/ppermute | solution.py:288
  12.9 0.7 select_reduce_fusion
  14.0 1.6 %copy-done.1 = f32[1,1,1,8,4,128,128]{6,5,4,3,2,1,0:T(8,128)S(1)} copy-done((f32[1,1,1,8,4,128,128]{6,5,4,3,2,1,0:T(8,128)S(1)}, f32[1,1,1,8,4,128,128]{6,5,4,3,2,1,0:T(8,128)}, u32[]{:S(2)}) %copy-start.1) | copy-done | bytes 2097176
  15.6 1.9 %copy-done.3 = f32[1,1,1,3,8,2,128,128]{7,6,5,4,3,2,1,0:T(8,128)S(1)} copy-done((f32[1,1,1,3,8,2,128,128]{7,6,5,4,3,2,1,0:T(8,128)S(1)}, f32[1,1,1,3,8,2,128,128]{7,6,5,4,3,2,1,0:T(8,128)}, u32[]{:S(2)}) %copy-start.3) | copy-done | bytes 3145752
  17.5 2.3 %accumulate.8 = (f32[25,128,128]{2,1,0:T(8,128)S(1)}, f32[25,128,128]{2,1,0:T(8,128)S(1)}, s32[8,128]{1,0:T(8,128)S(1)}) custom-call(s32[261]{0:T(512)S(1)} %concatenate.7.scalar_ref, f32[3,8,2,128,128]{4,3,2,1,0:T(8,128)S(1)} %bitcast.29, f32[8,4,128,128]{3,2,1,0:T(8,128)S(1)} %bitcast.22), custom_call_target="tpu_custom_call" | custom-call | flops 805306368 | bytes 4194304 | tf_op jit(solution)/shard_map/accumulate/pallas_call | solution.py:225
  20.0 2.8 %collective-permute-start.9 = (f32[4,128,256]{2,1,0:T(8,128)S(1)}, f32[4,128,256]{2,1,0:T(8,128)S(1)}, u32[]{:S(2)}, u32[]{:S(2)}) collective-permute-start(f32[4,128,256]{2,1,0:T(8,128)S(1)} %own_quarters.6), channel_id=1, source_target_pairs={{0,24},{4,28},{8,0},{12,4},{16,8},{20,12},{24,16},{28,20},{1,25},{... | collective-permute-start | bytes 1572872 | tf_op jit(solution)/shard_map/ppermute | solution.py:285
  22.8 3.2 %collective-permute-done.5.refs_0_.refs_2_.refs_1_ = f32[4,128,256]{2,1,0:T(8,128)} collective-permute-done((f32[4,128,256]{2,1,0:T(8,128)}, f32[4,128,256]{2,1,0:T(8,128)}, u32[]{:S(2)}, u32[]{:S(2)}) %collective-permute-start.5) | collective-permute-done | bytes 524320 | tf_op jit(solution)/shard_map/ppermute | solution.py:285
  25.9 1.1 pick.7
  27.0 1.7 %collective-permute-start.6 = (f32[4,128,256]{2,1,0:T(8,128)S(1)}, f32[4,128,256]{2,1,0:T(8,128)S(1)}, u32[]{:S(2)}, u32[]{:S(2)}) collective-permute-start(f32[4,128,256]{2,1,0:T(8,128)S(1)} %pick.7), channel_id=1, source_target_pairs={{0,4},{4,0},{8,12},{12,8},{16,20},{20,16},{24,28},{28,24},{1,5},{5... | collective-permute-start | bytes 1572872 | tf_op jit(solution)/shard_map/ppermute | solution.py:288
  28.9 2.3 %collective-permute-start.10 = (f32[4,128,256]{2,1,0:T(8,128)S(1)}, f32[4,128,256]{2,1,0:T(8,128)S(1)}, u32[]{:S(2)}, u32[]{:S(2)}) collective-permute-start(f32[4,128,256]{2,1,0:T(8,128)S(1)} %own_quarters.7), channel_id=1, source_target_pairs={{0,24},{4,28},{8,0},{12,4},{16,8},{20,12},{24,16},{28,20},{1,25},{... | collective-permute-start | bytes 1572872 | tf_op jit(solution)/shard_map/ppermute | solution.py:285
  31.2 6.7 %collective-permute-done.7.refs_3_.refs_0_ = f32[8,128,256]{2,1,0:T(8,128)} collective-permute-done((f32[8,128,256]{2,1,0:T(8,128)}, f32[8,128,256]{2,1,0:T(8,128)}, u32[]{:S(2)}, u32[]{:S(2)}) %collective-permute-start.7) | collective-permute-done | bytes 1048608 | tf_op jit(solution)/shard_map/ppermute | solution.py:288
  37.9 3.1 %accumulate.9 = (f32[25,128,128]{2,1,0:T(8,128)S(1)}, f32[25,128,128]{2,1,0:T(8,128)S(1)}, s32[8,128]{1,0:T(8,128)S(1)}) custom-call(s32[261]{0:T(512)S(1)} %concatenate.7.scalar_ref, f32[3,8,2,128,128]{4,3,2,1,0:T(8,128)S(1)} %bitcast.30, ...), custom_call_target="tpu_custom_call", output_to_operand_aliasing={{0}: (5, {}), {1}: (6, {})} | custom-call | flops 402653184 | bytes 2097152 | tf_op jit(solution)/shard_map/accumulate/pallas_call | solution.py:225
  41.0 0.9 collective-permute-start.12
  42.0 7.0 %collective-permute-done.6.refs_1_.refs_3_ = f32[4,128,256]{2,1,0:T(8,128)S(1)} collective-permute-done((f32[4,128,256]{2,1,0:T(8,128)S(1)}, f32[4,128,256]{2,1,0:T(8,128)S(1)}, u32[]{:S(2)}, u32[]{:S(2)}) %collective-permute-start.6) | collective-permute-done | bytes 524320 | tf_op jit(solution)/shard_map/ppermute | solution.py:288
  49.2 3.4 %collective-permute-start.8 = (f32[4,128,256]{2,1,0:T(8,128)S(1)}, f32[4,128,256]{2,1,0:T(8,128)S(1)}, u32[]{:S(2)}, u32[]{:S(2)}) collective-permute-start(f32[4,128,256]{2,1,0:T(8,128)S(1)} %pick.8), channel_id=1, source_target_pairs={{0,24},{4,28},{8,0},{12,4},{16,8},{20,12},{24,16},{28,20},{1,25},{... | collective-permute-start | bytes 1572872 | tf_op jit(solution)/shard_map/ppermute | solution.py:285
  52.7 2.8 %accumulate.10 = (f32[25,128,128]{2,1,0:T(8,128)S(1)}, f32[25,128,128]{2,1,0:T(8,128)S(1)}, s32[8,128]{1,0:T(8,128)S(1)}) custom-call(s32[261]{0:T(512)S(1)} %concatenate.7.scalar_ref, f32[3,8,2,128,128]{4,3,2,1,0:T(8,128)S(1)} %bitcast.31, ...), custom_call_target="tpu_custom_call", output_to_operand_aliasing={{0}: (5, {}), {1}: (6, {})} | custom-call | flops 402653184 | bytes 2097152 | tf_op jit(solution)/shard_map/accumulate/pallas_call | solution.py:225
  55.5 1.1 pick.12
  56.7 1.4 %accumulate.11 = (f32[25,128,128]{2,1,0:T(8,128)S(1)}, f32[25,128,128]{2,1,0:T(8,128)S(1)}, s32[8,128]{1,0:T(8,128)S(1)}) custom-call(s32[261]{0:T(512)S(1)} %concatenate.7.scalar_ref, f32[3,8,2,128,128]{4,3,2,1,0:T(8,128)S(1)} %bitcast.32, ...), custom_call_target="tpu_custom_call", output_to_operand_aliasing={{0}: (5, {}), {1}: (6, {})} | custom-call | flops 402653184 | bytes 2097152 | tf_op jit(solution)/shard_map/accumulate/pallas_call | solution.py:225
  58.1 2.2 %collective-permute-done.12.refs_1_.refs_4_ = f32[4,128,256]{2,1,0:T(8,128)S(1)} collective-permute-done((f32[4,128,256]{2,1,0:T(8,128)S(1)}, f32[4,128,256]{2,1,0:T(8,128)S(1)}, u32[]{:S(2)}, u32[]{:S(2)}) %collective-permute-start.12) | collective-permute-done | bytes 524320 | tf_op jit(solution)/shard_map/ppermute | solution.py:288
  60.3 1.3 %pick.11 = f32[4,128,256]{2,1,0:T(8,128)S(1)} custom-call(s32[1]{0:T(128)} %bitcast.9.odd_ref, f32[8,128,256]{2,1,0:T(8,128)} %collective-permute-done.7.refs_3_.refs_0_, f32[4,128,256]{2,1,0:T(8,128)S(1)} %collective-permute-done.12.refs_1_.refs_4_, s32[8,128]{1,0:T(8,128)S(1)} %get-tuple-element.36.refs_2_), custom_call_target="tpu_custom_call" | custom-call | bytes 1048576 | tf_op jit(solution)/shard_map/pick/pallas_call | solution.py:112
  61.5 3.4 %collective-permute-start.13 = (f32[4,128,256]{2,1,0:T(8,128)S(1)}, f32[4,128,256]{2,1,0:T(8,128)S(1)}, u32[]{:S(2)}, u32[]{:S(2)}) collective-permute-start(f32[4,128,256]{2,1,0:T(8,128)S(1)} %pick.11), channel_id=1, source_target_pairs={{0,24},{4,28},{8,0},{12,4},{16,8},{20,12},{24,16},{28,20},{1,25},{... | collective-permute-start | bytes 1572872 | tf_op jit(solution)/shard_map/ppermute | solution.py:285
  65.0 0.6 collective-permute-start.11
  65.6 5.9 %collective-permute-done.14.refs_5_ = f32[4,128,256]{2,1,0:T(8,128)S(1)} collective-permute-done((f32[4,128,256]{2,1,0:T(8,128)S(1)}, f32[4,128,256]{2,1,0:T(8,128)S(1)}, u32[]{:S(2)}, u32[]{:S(2)}) %collective-permute-start.14) | collective-permute-done | bytes 524320 | tf_op jit(solution)/shard_map/ppermute | solution.py:288
  71.5 3.4 %collective-permute-start.15 = (f32[4,128,256]{2,1,0:T(8,128)S(1)}, f32[4,128,256]{2,1,0:T(8,128)S(1)}, u32[]{:S(2)}, u32[]{:S(2)}) collective-permute-start(f32[4,128,256]{2,1,0:T(8,128)S(1)} %collective-permute-done.14.refs_5_), channel_id=1, source_target_pairs={{0,24},{4,28},{8,0},{12,4},{16,8},{20,12},{24,16},{28,20},{1,25},{... | collective-permute-start | bytes 1572872 | tf_op jit(solution)/shard_map/ppermute | solution.py:285
  74.9 1.6 %accumulate.12 = (f32[25,128,128]{2,1,0:T(8,128)S(1)}, f32[25,128,128]{2,1,0:T(8,128)S(1)}, s32[8,128]{1,0:T(8,128)S(1)}) custom-call(s32[261]{0:T(512)S(1)} %concatenate.7.scalar_ref, f32[3,8,2,128,128]{4,3,2,1,0:T(8,128)S(1)} %bitcast.33, ...), custom_call_target="tpu_custom_call", output_to_operand_aliasing={{0}: (6, {}), {1}: (7, {})} | custom-call | flops 402653184 | bytes 2097152 | tf_op jit(solution)/shard_map/accumulate/pallas_call | solution.py:225
  76.5 0.7 collective-permute-start.16
  77.2 5.5 %collective-permute-done.11.refs_2_ = f32[4,128,256]{2,1,0:T(8,128)S(1)} collective-permute-done((f32[4,128,256]{2,1,0:T(8,128)S(1)}, f32[4,128,256]{2,1,0:T(8,128)S(1)}, u32[]{:S(2)}, u32[]{:S(2)}) %collective-permute-start.11) | collective-permute-done | bytes 524320 | tf_op jit(solution)/shard_map/ppermute | solution.py:288
  82.7 3.4 %collective-permute-start.17 = (f32[4,128,256]{2,1,0:T(8,128)S(1)}, f32[4,128,256]{2,1,0:T(8,128)S(1)}, u32[]{:S(2)}, u32[]{:S(2)}) collective-permute-start(f32[4,128,256]{2,1,0:T(8,128)S(1)} %collective-permute-done.11.refs_2_), channel_id=1, source_target_pairs={{0,24},{4,28},{8,0},{12,4},{16,8},{20,12},{24,16},{28,20},{1,25},{... | collective-permute-start | bytes 1572872 | tf_op jit(solution)/shard_map/ppermute | solution.py:285
  86.1 2.2 %accumulate.13 = (f32[25,128,128]{2,1,0:T(8,128)S(1)}, f32[25,128,128]{2,1,0:T(8,128)S(1)}, s32[8,128]{1,0:T(8,128)}) custom-call(s32[261]{0:T(512)S(1)} %concatenate.7.scalar_ref, f32[3,8,2,128,128]{4,3,2,1,0:T(8,128)S(1)} %collective-permute-done.4.refs_1_.refs_2_.refs_0_.refs_3_, ...), custom_call_target="tpu_custom_call", output_to_operand_aliasing={{0}: (7, {}), {1}: (8, {})} | custom-call | flops 402653184 | bytes 2097152 | tf_op jit(solution)/shard_map/accumulate/pallas_call | solution.py:225
  88.3 2.3 %accumulate.14 = (f32[25,128,128]{2,1,0:T(8,128)S(1)}, f32[25,128,128]{2,1,0:T(8,128)S(1)}, s32[8,128]{1,0:T(8,128)}, f32[6,128,128]{2,1,0:T(8,128)S(1)}, f32[6,128,128]{2,1,0:T(8,128)S(1)}) custom-call(s32[261]{0:T(512)S(1)} %concatenate.7.scalar_ref, ...), custom_call_target="tpu_custom_call", output_to_operand_aliasing={{0}: (4, {}), {1}: (5, {})} | custom-call | flops 201326592 | bytes 1048576 | tf_op jit(solution)/shard_map/accumulate/pallas_call | solution.py:225
  90.6 1.5 %collective-permute-start.18 = (f32[6,128,128]{2,1,0:T(8,128)S(1)}, f32[6,128,128]{2,1,0:T(8,128)S(1)}, u32[]{:S(2)}, u32[]{:S(2)}) collective-permute-start(f32[6,128,128]{2,1,0:T(8,128)S(1)} %get-tuple-element.47), channel_id=1, source_target_pairs={{0,1},{1,0},{2,3},{3,2},{4,5},{5,4},{6,7},{7,6},{8,9},{9,8},{10,11... | collective-permute-start | bytes 1179656 | tf_op jit(solution)/shard_map/ppermute | solution.py:350
  92.1 0.8 collective-permute-done.16.refs_5_
  92.9 4.5 %collective-permute-done.17.refs_6_ = f32[4,128,256]{2,1,0:T(8,128)S(1)} collective-permute-done((f32[4,128,256]{2,1,0:T(8,128)S(1)}, f32[4,128,256]{2,1,0:T(8,128)S(1)}, u32[]{:S(2)}, u32[]{:S(2)}) %collective-permute-start.17) | collective-permute-done | bytes 524320 | tf_op jit(solution)/shard_map/ppermute | solution.py:285
  97.5 2.1 %accumulate.15 = (f32[25,128,128]{2,1,0:T(8,128)S(1)}, s32[8,128]{1,0:T(8,128)}, f32[6,128,128]{2,1,0:T(8,128)S(1)}, f32[6,128,128]{2,1,0:T(8,128)S(1)}) custom-call(s32[261]{0:T(512)S(1)} %concatenate.7.scalar_ref, f32[3,8,2,128,128]{4,3,2,1,0:T(8,128)S(1)} %collective-permute-done.4.refs_1_.refs_2_.refs_0_.refs_3_, ...), custom_call_target="tpu_custom_call", output_to_operand_aliasing={{0}: (8, {})} | custom-call | flops 603979776 | bytes 3145728 | tf_op jit(solution)/shard_map/accumulate/pallas_call | solution.py:225
  99.6 0.8 copy-done.8
  100.3 1.5 %collective-permute-start.19 = (f32[6,128,128]{2,1,0:T(8,128)S(1)}, f32[6,128,128]{2,1,0:T(8,128)S(1)}, u32[]{:S(2)}, u32[]{:S(2)}) collective-permute-start(f32[6,128,128]{2,1,0:T(8,128)S(1)} %get-tuple-element.48), channel_id=1, source_target_pairs={{0,1},{1,0},{2,3},{3,2},{4,5},{5,4},{6,7},{7,6},{8,9},{9,8},{10,11... | collective-permute-start | bytes 1179656 | tf_op jit(solution)/shard_map/ppermute | solution.py:350
  101.8 8.4 %collective-permute-done.19.other_1 = f32[6,128,128]{2,1,0:T(8,128)S(1)} collective-permute-done((f32[6,128,128]{2,1,0:T(8,128)S(1)}, f32[6,128,128]{2,1,0:T(8,128)S(1)}, u32[]{:S(2)}, u32[]{:S(2)}) %collective-permute-start.19) | collective-permute-done | bytes 393248 | tf_op jit(solution)/shard_map/ppermute | solution.py:350
  110.2 0.7 copy-done.10
  110.9 2.4 %combine.1 = f32[2,6,128,128]{3,2,1,0:T(8,128)} custom-call(f32[6,128,128]{2,1,0:T(8,128)} %copy-done.7, f32[6,128,128]{2,1,0:T(8,128)} %copy-done.8, f32[6,128,128]{2,1,0:T(8,128)} %copy-done.9, f32[6,128,128]{2,1,0:T(8,128)} %copy-done.10), custom_call_target="tpu_custom_call" | custom-call | tf_op jit(solution)/shard_map/combine/pallas_call | solution.py:258
  (51 shorter events, 1.5 us)
Async XLA Ops:
  0.0 37.9 %collective-permute-start.4 = (f32[3,8,2,128,128]{4,3,2,1,0:T(8,128)}, f32[3,8,2,128,128]{4,3,2,1,0:T(8,128)S(1)}, u32[]{:S(2)}, u32[]{:S(2)}) collective-permute-start(f32[3,8,2,128,128]{4,3,2,1,0:T(8,128)} %bitcast.28), channel_id=1, source_target_pairs={{0,2},{2,0},{1,3},{3,1},{4,6},{6,4},{5,7},{7,5},{8,10},{10,8},{9,1... | collective-permute-start | bytes 9437192 | tf_op jit(solution)/shard_map/ppermute | solution.py:300
  0.5 10.4 %collective-permute-start.3 = (s32[8,4]{0,1:T(4,128)}, s32[8,4]{0,1:T(4,128)S(1)}, u32[]{:S(2)}, u32[]{:S(2)}) collective-permute-start(s32[8,4]{0,1:T(4,128)} %bitcast.35), channel_id=1, source_target_pairs={{0,20},{4,24},{8,28},{12,0},{16,4},{20,8},{24,12},{28,16},{1,21},{... | collective-permute-start | bytes 392 | tf_op jit(solution)/shard_map/ppermute | solution.py:310
  5.0 6.6 %collective-permute-start.2 = (s32[8,4]{0,1:T(4,128)}, s32[8,4]{0,1:T(4,128)S(1)}, u32[]{:S(2)}, u32[]{:S(2)}) collective-permute-start(s32[8,4]{0,1:T(4,128)} %bitcast.36), channel_id=1, source_target_pairs={{0,24},{4,28},{8,0},{12,4},{16,8},{20,12},{24,16},{28,20},{1,25},{... | collective-permute-start | bytes 392 | tf_op jit(solution)/shard_map/ppermute | solution.py:310
  6.3 6.5 %collective-permute-start.1 = (s32[8,4]{0,1:T(4,128)}, s32[8,4]{0,1:T(4,128)S(1)}, u32[]{:S(2)}, u32[]{:S(2)}) collective-permute-start(s32[8,4]{0,1:T(4,128)} %bitcast.37), channel_id=1, source_target_pairs={{0,28},{4,0},{8,4},{12,8},{16,12},{20,16},{24,20},{28,24},{1,29},{... | collective-permute-start | bytes 392 | tf_op jit(solution)/shard_map/ppermute | solution.py:310
  6.9 6.0 %collective-permute-start = (s32[3,8,2]{1,2,0:T(2,128)}, s32[3,8,2]{1,2,0:T(2,128)S(1)}, u32[]{:S(2)}, u32[]{:S(2)}) collective-permute-start(s32[3,8,2]{1,2,0:T(2,128)} %bitcast.42), channel_id=1, source_target_pairs={{0,2},{2,0},{1,3},{3,1},{4,6},{6,4},{5,7},{7,5},{8,10},{10,8},{9,1... | collective-permute-start | bytes 584 | tf_op jit(solution)/shard_map/ppermute | solution.py:300
  6.9 1.6 %copy-start = (f32[1,1,1,8,4,128,128]{6,5,4,3,2,1,0:T(8,128)S(1)}, f32[1,1,1,8,4,128,128]{6,5,4,3,2,1,0:T(8,128)}, u32[]{:S(2)}) copy-start(f32[1,1,1,8,4,128,128]{6,5,4,3,2,1,0:T(8,128)} %param.7) | copy-start | bytes 6291460
  8.7 0.8 copy-start.6
  9.4 1.4 %copy-start.12 = (s32[1,1,1,3,8,2]{4,5,3,2,1,0:T(2,128)S(1)}, s32[1,1,1,3,8,2]{4,5,3,2,1,0:T(2,128)}, u32[]{:S(2)}) copy-start(s32[1,1,1,3,8,2]{4,5,3,2,1,0:T(2,128)} %param.6) | copy-start | bytes 580
  9.4 3.4 %copy-start.11 = (s32[1,1,1,8,4]{3,4,2,1,0:T(4,128)S(1)}, s32[1,1,1,8,4]{3,4,2,1,0:T(4,128)}, u32[]{:S(2)}) copy-start(s32[1,1,1,8,4]{3,4,2,1,0:T(4,128)} %param.8) | copy-start | bytes 388
  9.5 3.5 %copy-start.13 = (s32[1,1,24]{2,1,0:T(1,128)S(1)}, s32[1,1,24]{2,1,0:T(1,128)}, u32[]{:S(2)}) copy-start(s32[1,1,24]{2,1,0:T(1,128)} %param.9) | copy-start | bytes 292
  9.8 1.0 copy-start.5
  10.8 15.1 %collective-permute-start.5 = (f32[4,128,256]{2,1,0:T(8,128)}, f32[4,128,256]{2,1,0:T(8,128)}, u32[]{:S(2)}, u32[]{:S(2)}) collective-permute-start(f32[4,128,256]{2,1,0:T(8,128)} %copy-done.6), channel_id=1, source_target_pairs={{0,24},{4,28},{8,0},{12,4},{16,8},{20,12},{24,16},{28,20},{1,25},{... | collective-permute-start | bytes 1572872 | tf_op jit(solution)/shard_map/ppermute | solution.py:285
  11.5 26.3 %collective-permute-start.7 = (f32[8,128,256]{2,1,0:T(8,128)}, f32[8,128,256]{2,1,0:T(8,128)}, u32[]{:S(2)}, u32[]{:S(2)}) collective-permute-start(f32[8,128,256]{2,1,0:T(8,128)} %copy-done.5), channel_id=1, source_target_pairs={{0,4},{4,0},{8,12},{12,8},{16,20},{20,16},{24,28},{28,24},{1,5},{5... | collective-permute-start | bytes 3145736 | tf_op jit(solution)/shard_map/ppermute | solution.py:288
  14.0 1.6 %copy-start.1 = (f32[1,1,1,8,4,128,128]{6,5,4,3,2,1,0:T(8,128)S(1)}, f32[1,1,1,8,4,128,128]{6,5,4,3,2,1,0:T(8,128)}, u32[]{:S(2)}) copy-start(f32[1,1,1,8,4,128,128]{6,5,4,3,2,1,0:T(8,128)} %param.7) | copy-start | bytes 6291460
  15.6 1.9 %copy-start.3 = (f32[1,1,1,3,8,2,128,128]{7,6,5,4,3,2,1,0:T(8,128)S(1)}, f32[1,1,1,3,8,2,128,128]{7,6,5,4,3,2,1,0:T(8,128)}, u32[]{:S(2)}) copy-start(f32[1,1,1,3,8,2,128,128]{7,6,5,4,3,2,1,0:T(8,128)} %param.5) | copy-start | bytes 9437188
  20.0 21.0 %collective-permute-start.9 = (f32[4,128,256]{2,1,0:T(8,128)S(1)}, f32[4,128,256]{2,1,0:T(8,128)S(1)}, u32[]{:S(2)}, u32[]{:S(2)}) collective-permute-start(f32[4,128,256]{2,1,0:T(8,128)S(1)} %own_quarters.6), channel_id=1, source_target_pairs={{0,24},{4,28},{8,0},{12,4},{16,8},{20,12},{24,16},{28,20},{1,25},{... | collective-permute-start | bytes 1572872 | tf_op jit(solution)/shard_map/ppermute | solution.py:285
  27.0 10.9 %copy-start.4 = (f32[1,1,1,3,8,2,128,128]{7,6,5,4,3,2,1,0:T(8,128)S(1)}, f32[1,1,1,3,8,2,128,128]{7,6,5,4,3,2,1,0:T(8,128)}, u32[]{:S(2)}) copy-start(f32[1,1,1,3,8,2,128,128]{7,6,5,4,3,2,1,0:T(8,128)} %param.5) | copy-start | bytes 9437188
  27.0 22.0 %collective-permute-start.6 = (f32[4,128,256]{2,1,0:T(8,128)S(1)}, f32[4,128,256]{2,1,0:T(8,128)S(1)}, u32[]{:S(2)}, u32[]{:S(2)}) collective-permute-start(f32[4,128,256]{2,1,0:T(8,128)S(1)} %pick.7), channel_id=1, source_target_pairs={{0,4},{4,0},{8,12},{12,8},{16,20},{20,16},{24,28},{28,24},{1,5},{5... | collective-permute-start | bytes 1572872 | tf_op jit(solution)/shard_map/ppermute | solution.py:288
  28.9 26.5 %collective-permute-start.10 = (f32[4,128,256]{2,1,0:T(8,128)S(1)}, f32[4,128,256]{2,1,0:T(8,128)S(1)}, u32[]{:S(2)}, u32[]{:S(2)}) collective-permute-start(f32[4,128,256]{2,1,0:T(8,128)S(1)} %own_quarters.7), channel_id=1, source_target_pairs={{0,24},{4,28},{8,0},{12,4},{16,8},{20,12},{24,16},{28,20},{1,25},{... | collective-permute-start | bytes 1572872 | tf_op jit(solution)/shard_map/ppermute | solution.py:285
  37.9 3.1 %copy-start.2 = (f32[1,1,1,8,4,128,128]{6,5,4,3,2,1,0:T(8,128)S(1)}, f32[1,1,1,8,4,128,128]{6,5,4,3,2,1,0:T(8,128)}, u32[]{:S(2)}) copy-start(f32[1,1,1,8,4,128,128]{6,5,4,3,2,1,0:T(8,128)} %param.7) | copy-start | bytes 6291460
  41.0 19.2 %collective-permute-start.12 = (f32[4,128,256]{2,1,0:T(8,128)S(1)}, f32[4,128,256]{2,1,0:T(8,128)S(1)}, u32[]{:S(2)}, u32[]{:S(2)}) collective-permute-start(f32[4,128,256]{2,1,0:T(8,128)S(1)} %pick.10), channel_id=1, source_target_pairs={{0,4},{4,0},{8,12},{12,8},{16,20},{20,16},{24,28},{28,24},{1,5},{5... | collective-permute-start | bytes 1572872 | tf_op jit(solution)/shard_map/ppermute | solution.py:288
  49.2 15.7 %collective-permute-start.8 = (f32[4,128,256]{2,1,0:T(8,128)S(1)}, f32[4,128,256]{2,1,0:T(8,128)S(1)}, u32[]{:S(2)}, u32[]{:S(2)}) collective-permute-start(f32[4,128,256]{2,1,0:T(8,128)S(1)} %pick.8), channel_id=1, source_target_pairs={{0,24},{4,28},{8,0},{12,4},{16,8},{20,12},{24,16},{28,20},{1,25},{... | collective-permute-start | bytes 1572872 | tf_op jit(solution)/shard_map/ppermute | solution.py:285
  56.6 14.9 %collective-permute-start.14 = (f32[4,128,256]{2,1,0:T(8,128)S(1)}, f32[4,128,256]{2,1,0:T(8,128)S(1)}, u32[]{:S(2)}, u32[]{:S(2)}) collective-permute-start(f32[4,128,256]{2,1,0:T(8,128)S(1)} %pick.12), channel_id=1, source_target_pairs={{0,4},{4,0},{8,12},{12,8},{16,20},{20,16},{24,28},{28,24},{1,5},{5... | collective-permute-start | bytes 1572872 | tf_op jit(solution)/shard_map/ppermute | solution.py:288
  61.5 14.9 %collective-permute-start.13 = (f32[4,128,256]{2,1,0:T(8,128)S(1)}, f32[4,128,256]{2,1,0:T(8,128)S(1)}, u32[]{:S(2)}, u32[]{:S(2)}) collective-permute-start(f32[4,128,256]{2,1,0:T(8,128)S(1)} %pick.11), channel_id=1, source_target_pairs={{0,24},{4,28},{8,0},{12,4},{16,8},{20,12},{24,16},{28,20},{1,25},{... | collective-permute-start | bytes 1572872 | tf_op jit(solution)/shard_map/ppermute | solution.py:285
  65.0 17.7 %collective-permute-start.11 = (f32[4,128,256]{2,1,0:T(8,128)S(1)}, f32[4,128,256]{2,1,0:T(8,128)S(1)}, u32[]{:S(2)}, u32[]{:S(2)}) collective-permute-start(f32[4,128,256]{2,1,0:T(8,128)S(1)} %pick.9), channel_id=1, source_target_pairs={{0,4},{4,0},{8,12},{12,8},{16,20},{20,16},{24,28},{28,24},{1,5},{5... | collective-permute-start | bytes 1572872 | tf_op jit(solution)/shard_map/ppermute | solution.py:288
  71.5 20.6 %collective-permute-start.15 = (f32[4,128,256]{2,1,0:T(8,128)S(1)}, f32[4,128,256]{2,1,0:T(8,128)S(1)}, u32[]{:S(2)}, u32[]{:S(2)}) collective-permute-start(f32[4,128,256]{2,1,0:T(8,128)S(1)} %collective-permute-done.14.refs_5_), channel_id=1, source_target_pairs={{0,24},{4,28},{8,0},{12,4},{16,8},{20,12},{24,16},{28,20},{1,25},{... | collective-permute-start | bytes 1572872 | tf_op jit(solution)/shard_map/ppermute | solution.py:285
  76.5 16.4 %collective-permute-start.16 = (f32[4,128,256]{2,1,0:T(8,128)S(1)}, f32[4,128,256]{2,1,0:T(8,128)S(1)}, u32[]{:S(2)}, u32[]{:S(2)}) collective-permute-start(f32[4,128,256]{2,1,0:T(8,128)S(1)} %pick.13), channel_id=1, source_target_pairs={{0,4},{4,0},{8,12},{12,8},{16,20},{20,16},{24,28},{28,24},{1,5},{5... | collective-permute-start | bytes 1572872 | tf_op jit(solution)/shard_map/ppermute | solution.py:288
  82.7 14.7 %collective-permute-start.17 = (f32[4,128,256]{2,1,0:T(8,128)S(1)}, f32[4,128,256]{2,1,0:T(8,128)S(1)}, u32[]{:S(2)}, u32[]{:S(2)}) collective-permute-start(f32[4,128,256]{2,1,0:T(8,128)S(1)} %collective-permute-done.11.refs_2_), channel_id=1, source_target_pairs={{0,24},{4,28},{8,0},{12,4},{16,8},{20,12},{24,16},{28,20},{1,25},{... | collective-permute-start | bytes 1572872 | tf_op jit(solution)/shard_map/ppermute | solution.py:285
  90.6 9.0 %copy-start.7 = (f32[6,128,128]{2,1,0:T(8,128)}, f32[6,128,128]{2,1,0:T(8,128)S(1)}, u32[]{:S(2)}) copy-start(f32[6,128,128]{2,1,0:T(8,128)S(1)} %get-tuple-element.43.kept_0) | copy-start | bytes 1179652
  90.6 11.2 %collective-permute-start.18 = (f32[6,128,128]{2,1,0:T(8,128)S(1)}, f32[6,128,128]{2,1,0:T(8,128)S(1)}, u32[]{:S(2)}, u32[]{:S(2)}) collective-permute-start(f32[6,128,128]{2,1,0:T(8,128)S(1)} %get-tuple-element.47), channel_id=1, source_target_pairs={{0,1},{1,0},{2,3},{3,2},{4,5},{5,4},{6,7},{7,6},{8,9},{9,8},{10,11... | collective-permute-start | bytes 1179656 | tf_op jit(solution)/shard_map/ppermute | solution.py:350
  99.6 0.8 copy-start.8
  100.3 9.9 %collective-permute-start.19 = (f32[6,128,128]{2,1,0:T(8,128)S(1)}, f32[6,128,128]{2,1,0:T(8,128)S(1)}, u32[]{:S(2)}, u32[]{:S(2)}) collective-permute-start(f32[6,128,128]{2,1,0:T(8,128)S(1)} %get-tuple-element.48), channel_id=1, source_target_pairs={{0,1},{1,0},{2,3},{3,2},{4,5},{5,4},{6,7},{7,6},{8,9},{9,8},{10,11... | collective-permute-start | bytes 1179656 | tf_op jit(solution)/shard_map/ppermute | solution.py:350
  101.8 8.4 %copy-start.9 = (f32[6,128,128]{2,1,0:T(8,128)}, f32[6,128,128]{2,1,0:T(8,128)S(1)}, u32[]{:S(2)}) copy-start(f32[6,128,128]{2,1,0:T(8,128)S(1)} %collective-permute-done.18.other_0) | copy-start | bytes 1179652
  110.2 0.7 copy-start.10

commit v6 on v5

v6 whole, which is shorter than its diff:
```python
import jax
import jax.numpy as jnp
from jax import lax
from jax.experimental import pallas as pl
from jax.experimental.pallas import tpu as pltpu
from jax.sharding import PartitionSpec as P

STEPS = 4
CB = 8
HALVES = 2
QUARTERS = HALVES * HALVES

bf16 = jnp.bfloat16
f32 = jnp.float32

Z_CHUNKS = {
    1: ((2, 0), (2, 0)),
    2: ((2, 1), (2, 1)),
    3: ((2, 2), (2, 2)),
    4: ((2, 3), (3, 0)),
    5: ((3, 3), (3, 1)),
    6: (None, (3, 2)),
    7: (None, (3, 3)),
}
X_CHUNKS = {
    1: ((1, 2), None),
    2: ((1, 3), None),
    3: ((1, 0), (1, 0)),
    4: ((1, 1), (1, 1)),
    5: ((3, 0), (1, 2)),
    6: ((3, 1), (1, 3)),
    7: ((3, 2), (2, 3)),
}
EXTRA = 8

in_smem = pl.BlockSpec(memory_space=pltpu.SMEM)
in_vmem = pl.BlockSpec(memory_space=pltpu.VMEM)
anywhere = pl.BlockSpec(memory_space=pl.ANY)


def whole(shape):
    return pl.BlockSpec(shape, lambda *_: (0,) * len(shape))


def lower_lanes(shape):
    return lax.broadcasted_iota(jnp.int32, shape, len(shape) - 1) < shape[-1] // 2


def swap_lanes(x):
    return pltpu.roll(x, x.shape[-1] // 2, x.ndim - 1)


def cut(right_ref, out_ref, half, at=0):
    per, bpr, bs, _ = right_ref.shape
    lower = lower_lanes((bs, bs))
    for k in range(per):
        for pair in range(bpr // 2):
            even, odd = right_ref[k, 2 * pair], right_ref[k, 2 * pair + 1]
            if half == 0:
                both = jnp.where(lower, even, swap_lanes(odd))
            else:
                both = jnp.where(lower, swap_lanes(even), odd)
            out_ref[at + k * bs:at + (k + 1) * bs, pair * bs:(pair + 1) * bs] = both


def own_spec(right, k_half):
    return pl.BlockSpec((right.shape[0] // HALVES,) + right.shape[1:], lambda *_: (k_half, 0, 0, 0))


def quarter_shape(right):
    kb, bpr, bs, _ = right.shape
    return kb // HALVES * bs, bpr * bs // HALVES


def own_quarters(right, quarters, cols, *others):
    rows, width = quarter_shape(right)
    extra = [] if cols is None else [cols]

    def kernel(*refs):
        out_ref = refs[-1]
        for n, quarter in enumerate(quarters):
            cut(refs[n], out_ref, quarter // HALVES, n * rows)
        if extra:
            out_ref[len(quarters) * rows:, :] = refs[len(quarters)][...]

    out_shape = jax.ShapeDtypeStruct((len(quarters) * rows + EXTRA * len(extra), width), right.dtype)
    return pl.pallas_call(
        kernel,
        grid=(1,),
        in_specs=[own_spec(right, quarter % HALVES) for quarter in quarters] + [whole(x.shape) for x in extra] + [anywhere] * len(others),
        out_specs=whole(out_shape.shape),
        out_shape=out_shape,
        compiler_params=pltpu.CompilerParams(vmem_limit_bytes=12 * 1024 * 1024),
        cost_estimate=pl.CostEstimate(flops=0, bytes_accessed=12 * out_shape.size, transcendentals=0),
        name="own_quarters",
    )(*[right] * len(quarters), *extra, *others)


def pick(info, right, cols, even_part, odd_part, *others):
    parts = (even_part, odd_part)
    rows, width = quarter_shape(right)
    extra = [] if cols is None else [cols]

    def taken(array, at):
        return array.shape[0] if extra and at == 0 and array.shape[0] == rows + EXTRA else rows

    def kernel(info_ref, *refs):
        out_ref = refs[-1]

        def copy_from(n):
            array, at = parts[n]
            if array is None:
                cut(refs[n], out_ref, at // HALVES)
                if extra:
                    out_ref[rows:, :] = refs[2][...]
                return
            out_ref[:refs[n].shape[0]] = refs[n][...]
            if extra and refs[n].shape[0] == rows:
                out_ref[rows:, :] = jnp.zeros((EXTRA, width), right.dtype)

        pl.when(info_ref[0] == 0)(lambda: copy_from(0))
        pl.when(info_ref[0] != 0)(lambda: copy_from(1))

    def spec(array, at):
        if array is None:
            return own_spec(right, at % HALVES)
        return pl.BlockSpec((taken(array, at), width), lambda *_: (at, 0))

    out_shape = jax.ShapeDtypeStruct((rows + EXTRA * len(extra), width), right.dtype)
    return pl.pallas_call(
        kernel,
        grid=(1,),
        in_specs=[in_smem] + [spec(*part) for part in parts] + [whole(x.shape) for x in extra] + [anywhere] * len(others),
        out_specs=whole(out_shape.shape),
        out_shape=out_shape,
        compiler_params=pltpu.CompilerParams(vmem_limit_bytes=8 * 1024 * 1024),
        cost_estimate=pl.CostEstimate(flops=0, bytes_accessed=8 * out_shape.size, transcendentals=0),
        name="pick",
    )(info, *[right if array is None else array for array, _ in parts], *extra, *others)


def accumulate(info, places, lefts, chunks, totals, nc, finish=None):
    _, kb, lpb, bs, _ = lefts[0].shape
    per = kb // HALVES
    own = totals is None
    bpr = chunks[0][0].shape[1] if own else HALVES * chunks[0][0].shape[1] // bs
    width = bpr * bs // HALVES
    lanes = bs // HALVES
    products = lpb * bpr
    turns = sorted({what[0] for _, _, both in chunks for what in both if what is not None})
    packed = nc // 4
    if own:
        touched = list(range(HALVES))
    else:
        touched = sorted({what[1] // HALVES for _, _, both in chunks for what in both if what is not None})
    sides = [(c, side) for c in range(len(chunks)) for side in range(2) if chunks[c][2][side] is not None]
    sides = [(c, side) for c, side in sides if side == 0 or chunks[c][2][0] != chunks[c][2][1]]

    def kernel(info_ref, *refs):
        place_refs = dict(zip(turns, refs))
        refs = refs[len(turns):]
        left_refs = dict(zip(sides, refs))
        right_refs = refs[len(sides):len(sides) + len(chunks)]
        outs = refs[len(sides) + len(chunks) + (0 if own else len(touched)):]
        total_refs = dict(zip(touched, outs))
        outs = outs[len(touched):]
        outs[0][...] = jnp.zeros_like(outs[0])
        odd = info_ref[0]
        if own:
            for ref in total_refs.values():
                ref[...] = jnp.zeros_like(ref)

        def products_of(left, right):
            left = left.reshape(lpb * bs, bs)
            left_high = left.astype(bf16)
            left_low = (left - left_high.astype(f32)).astype(bf16)
            high = right.astype(bf16)
            low = (right - high.astype(f32)).astype(bf16)
            return jnp.dot(
                jnp.concatenate([left_high, left_low, left_high], axis=1),
                jnp.concatenate([high, high, low], axis=0),
                preferred_element_type=f32,
            )

        def add_own(left_ref, right_ref):
            for k in range(kb):
                out = products_of(left_ref[0, k], jnp.concatenate([right_ref[k, b] for b in range(bpr)], axis=1))
                for a in range(lpb):
                    for b in range(bpr):
                        n = place_refs[0][k * products + a * bpr + b]
                        for half in range(HALVES):
                            at = slice(half * lanes, (half + 1) * lanes)
                            total_refs[half][n, :, at] += out[a * bs:(a + 1) * bs, b * bs:(b + 1) * bs][:, at]

        def add(c, side):
            turn, quarter = chunks[c][2][side]
            half, k_half = divmod(quarter, HALVES)
            base = k_half * per * products
            left_ref, right_ref, total_ref = left_refs[c, side], right_refs[c], total_refs[half]
            for k in range(per):
                out = products_of(left_ref[0, k], right_ref[k * bs:(k + 1) * bs])
                for a in range(lpb):
                    for b in range(bpr):
                        n = place_refs[turn][base + k * products + a * bpr + b]
                        at = (b % HALVES) * lanes
                        total_ref[n, :, at:at + lanes] += out[a * bs:(a + 1) * bs, b * lanes:(b + 1) * lanes]

        if own:
            add_own(left_refs[0, 0], right_refs[0])
            return
        for c, (_, _, both) in enumerate(chunks):
            if both[0] == both[1]:
                add(c, 0)
                continue
            if both[0] is not None:
                pl.when(odd == 0)(lambda c=c: add(c, 0))
            if both[1] is not None:
                pl.when(odd != 0)(lambda c=c: add(c, 1))
        if finish is not None:
            lower = lower_lanes((bs, bs))
            for kept, ref in enumerate(outs[1:]):
                for p in range(packed):
                    n = 2 * packed * kept + p
                    one, two = total_refs[finish][n], total_refs[finish][n + packed]
                    ref[p] = jnp.where(lower, one + swap_lanes(one), two + swap_lanes(two))

    def left_spec(turn, quarter):
        return pl.BlockSpec((1, per, lpb, bs, bs), lambda g, info_ref, *_: (info_ref[1 + turn], quarter % HALVES, 0, 0, 0))

    operands = [lefts[chunks[c][2][side][0]] for c, side in sides] + [c[0] for c in chunks]
    if own:
        in_specs = [pl.BlockSpec((1, kb, lpb, bs, bs), lambda g, info_ref, *_: (info_ref[1], 0, 0, 0, 0)), whole(chunks[0][0].shape)]
    else:
        in_specs = [left_spec(*chunks[c][2][side]) for c, side in sides] + [pl.BlockSpec((per * bs, width), lambda g, *_, at=at: (at, 0)) for _, at, _ in chunks]
    held = len(operands) + 1 + len(turns)
    if not own:
        operands += [totals[half] for half in touched]
        in_specs += [in_vmem] * len(touched)
    outs = [jax.ShapeDtypeStruct((nc + 1, bs, bs), f32)] * len(touched) + [jax.ShapeDtypeStruct((8, 128), jnp.int32)]
    if finish is not None:
        outs += [jax.ShapeDtypeStruct((packed, bs, bs), f32)] * 2
    parts = QUARTERS if own else len(chunks)
    flops = parts * per * 2 * lpb * bs * 3 * bs * width
    moved = 4 * parts * per * (lpb * bs * bs + bs * width)
    results = pl.pallas_call(
        kernel,
        grid_spec=pltpu.PrefetchScalarGridSpec(
            num_scalar_prefetch=1 + len(turns),
            grid=(1,),
            in_specs=in_specs,
            out_specs=[in_vmem] * len(touched) + [whole(x.shape) for x in outs[len(touched):]],
        ),
        out_shape=outs,
        input_output_aliases={} if own else {held + n: n for n in range(len(touched))},
        compiler_params=pltpu.CompilerParams(vmem_limit_bytes=16 * 1024 * 1024),
        cost_estimate=pl.CostEstimate(flops=flops, bytes_accessed=moved, transcendentals=0),
        name="accumulate",
    )(info, *[places[turn] for turn in turns], *operands)
    totals = [None] * HALVES if own else list(totals)
    for half, total in zip(touched, results):
        totals[half] = total
    return (totals, *results[len(touched):])


def own_places(info, slots, rows, cols, kb, lpb):
    nc = slots.shape[0]
    bpr = cols.shape[0] // kb

    def kernel(info_ref, slots_ref, rows_ref, cols_ref, table_ref, out_ref):
        for code in range(CB * CB):
            table_ref[code] = nc
        behind = nc - nc // 2 * info_ref[1 + STEPS]
        for n in range(nc):
            table_ref[slots_ref[n]] = lax.rem(n + behind, nc)
        fill_places(info_ref[1], table_ref, rows_ref, lambda n: cols_ref[n], out_ref, kb, lpb, bpr)

    return pl.pallas_call(
        kernel,
        in_specs=[in_smem] * 4,
        out_specs=[in_smem] * 2,
        out_shape=[jax.ShapeDtypeStruct((CB * CB,), jnp.int32), jax.ShapeDtypeStruct((kb * lpb * bpr,), jnp.int32)],
        compiler_params=pltpu.CompilerParams(vmem_limit_bytes=1024 * 1024),
        name="own_places",
    )(info, slots, rows, cols)


def fill_places(panel, table_ref, rows_ref, col_of, out_ref, kb, lpb, bpr):
    def column(k, carry):
        cols = [col_of(k * bpr + b) for b in range(bpr)]
        for a in range(lpb):
            row = rows_ref[(panel * kb + k) * lpb + a] * CB
            for b in range(bpr):
                out_ref[(k * lpb + a) * bpr + b] = table_ref[row + cols[b]]
        return carry

    lax.fori_loop(0, kb, column, 0)


def panel_places(info, table, turn, rows, even_part, odd_part, kb, lpb, bpr):
    parts = (even_part, odd_part)

    def kernel(info_ref, table_ref, rows_ref, even_ref, odd_ref, out_ref, cols_ref, scalar_ref, sem):
        cols = jnp.where(info_ref[0] == 0, even_ref[...], odd_ref[...])
        cols_ref[...] = cols.astype(jnp.int32)
        copy = pltpu.make_async_copy(cols_ref, scalar_ref, sem)
        copy.start()
        copy.wait()
        fill_places(info_ref[1 + turn], table_ref, rows_ref, lambda n: scalar_ref[0, n], out_ref, kb, lpb, bpr)

    return pl.pallas_call(
        kernel,
        grid=(1,),
        in_specs=[in_smem] * 3 + [pl.BlockSpec((EXTRA, 128), lambda g, at=at: (at // EXTRA, 0)) for _, at in parts],
        out_specs=in_smem,
        out_shape=jax.ShapeDtypeStruct((kb * lpb * bpr,), jnp.int32),
        scratch_shapes=[pltpu.VMEM((EXTRA, 128), jnp.int32), pltpu.SMEM((EXTRA, 128), jnp.int32), pltpu.SemaphoreType.DMA],
        compiler_params=pltpu.CompilerParams(vmem_limit_bytes=1024 * 1024),
        name="panel_places",
    )(info, table, rows, *[array for array, _ in parts])


def combine(kept, other):
    packed, bs, _ = kept[0].shape
    steps = 2 if packed % 2 == 0 else 1
    per = packed // steps

    def kernel(kept_0, kept_1, other_0, other_1, out_ref):
        lower = lower_lanes((bs, bs))
        for p in range(per):
            left = kept_0[p] + other_0[p]
            right = kept_1[p] + other_1[p]
            out_ref[0, p] = jnp.where(lower, left, swap_lanes(right))
            out_ref[1, p] = jnp.where(lower, swap_lanes(left), right)

    return pl.pallas_call(
        kernel,
        grid=(steps,),
        in_specs=[pl.BlockSpec((per, bs, bs), lambda g: (g, 0, 0))] * 4,
        out_specs=pl.BlockSpec((2, per, bs, bs), lambda g: (0, g, 0, 0)),
        out_shape=jax.ShapeDtypeStruct((2, packed, bs, bs), f32),
        compiler_params=pltpu.CompilerParams(vmem_limit_bytes=8 * 1024 * 1024),
        name="combine",
    )(*kept, *other).reshape(2 * packed, bs, bs)


def shards(left_values, left_rows, right_values, right_cols, result_slots):
    rows_n, cols_n = (lax.axis_size(a) for a in ("row", "col"))
    row, col, rep = (lax.axis_index(a) for a in ("row", "col", "rep"))
    panels = left_values[0, 0, 0]
    panel_rows = left_rows.reshape(-1)
    right = right_values[0, 0, 0]
    right_places = right_cols.reshape(-1)
    slots = result_slots[0, 0]
    kb = right.shape[0]
    nc = slots.shape[0]
    place = [(col + turn) // cols_n for turn in range(STEPS)]
    info = jnp.stack([row % 2, *place, rep]).astype(jnp.int32)

    z_pairs = [(r, (r - 2) % rows_n) for r in range(rows_n)]
    x_pairs = [(r, r ^ 1) for r in range(rows_n)]

    def along_z(chunk):
        return lax.ppermute(chunk, "row", z_pairs)

    def along_x(chunk):
        return lax.ppermute(chunk, "row", x_pairs)

    rows, width = quarter_shape(right)
    cols_row = jnp.pad(right_places.astype(f32)[None], ((0, EXTRA - 1), (0, width - right_places.shape[0])))

    def sent(even_part, odd_part, *others, extra=False):
        return pick(info, right, cols_row if extra else None, even_part, odd_part, *others)

    z = {}
    x = {}
    upper = own_quarters(right, (2, 3), None)
    x[1] = along_x(upper)
    z[1] = along_z(own_quarters(right, (0,), cols_row, upper))

    shifts = sorted({turn % cols_n for turn in range(STEPS)})
    held = {
        shift: (panels, panel_rows) if shift == 0 else lax.ppermute((panels, panel_rows), "col", [(c, (c - shift) % cols_n) for c in range(cols_n)])
        for shift in shifts
    }
    lefts = [held[turn % cols_n][0] for turn in range(STEPS)]
    rows_at = [held[turn % cols_n][1] for turn in range(STEPS)]

    lpb, bpr = panels.shape[2], right.shape[1]
    places = {}
    table, places[0] = own_places(info, slots, panel_rows, right_places, kb, lpb)

    def read_places(turn, even_part, odd_part):
        places[turn] = panel_places(info, table, turn, rows_at[turn], even_part, odd_part, kb, lpb, bpr)

    def add(totals, chunks, finish=None):
        return accumulate(info, places, lefts, chunks, totals, nc, finish)

    def along_z_part(stage):
        return (z[stage], 0, Z_CHUNKS[stage])

    def along_x_part(stage):
        return (*((x[1], stage - 1) if stage < 3 else (x[stage], 0)), X_CHUNKS[stage])

    totals, done = accumulate(info, places, [panels] * STEPS, [(right, 0, ((0, 0), (0, 0)))], None, nc)
    second = own_quarters(right, (1,), None, done)
    z[2] = along_z(second)
    x[3] = along_x(sent((z[1], 0), (None, 0), done, extra=True))
    z[3] = along_z(own_quarters(right, (2,), None, z[1], done))
    read_places(2, (z[1], rows), (z[1], rows))
    totals, done = add(totals, [along_z_part(1), along_z_part(2)])
    x[4] = along_x(sent((z[2], 0), (None, 1), done))
    z[4] = along_z(sent((None, 3), (x[3], 0), done, extra=True))
    read_places(1, (x[3], rows), (x[3], rows))
    totals, done = add(totals, [along_x_part(1), along_x_part(2), along_x_part(3)])
    x[5] = along_x(sent((z[3], 0), (z[1], 0), done, extra=True))
    z[5] = along_z(sent((x[1], 1), (x[4], 0), done))
    totals, done = add(totals, [along_z_part(3), along_x_part(4)])
    x[6] = along_x(sent((z[4], 0), (z[2], 0), done))
    z[6] = along_z(x[5])
    read_places(3, (x[5], rows), (z[4], rows))
    totals, done = add(totals, [along_z_part(4), along_x_part(5)])
    x[7] = along_x(sent((z[5], 0), (z[3], 0), done))
    z[7] = along_z(x[6])
    totals, done = add(totals, [along_z_part(5)])

    def to_partner(blocks):
        return lax.ppermute(blocks, "rep", [(0, 1), (1, 0)])

    totals, done, kept_0, send_0 = add(totals, [along_x_part(6)], 0)
    other_0 = to_partner(send_0)
    totals, done = add(totals, [along_z_part(6), along_x_part(7)])
    totals, done, kept_1, send_1 = add(totals, [along_z_part(7)], 1)
    other_1 = to_partner(send_1)
    return combine((kept_0, kept_1), (other_0, other_1))[None, None]


def solution(mesh):
    in_specs = (
        P("row", "rep", "col", None, None, None, None, None),
        P("row", "rep", "col", None, None, None),
        P("rep", "row", "col", None, None, None, None),
        P("rep", "row", "col", None, None),
        P("row", "col", None),
    )
    out_specs = P("row", "col", "rep", None, None)
    return jax.shard_map(shards, mesh=mesh, in_specs=in_specs, out_specs=out_specs, check_vma=False)
```

time: 114 us -> 109 us (0.956)
  starting transfers between devices: 34.5 us -> 22.9 us
  Pallas kernels: 24.8 us -> 35.5 us
  local copies, waits for them, and re-layouts: 8.72 us -> 5.69 us
    pallas_call x7 -> x11, Pallas kernels: 3.77 us -> 13.1 us  [the longest x3 5.92 us: panel_places(): pl.pallas_call(kernel, grid=(1,), in_specs=[in_smem] * 3 + [pl.BlockSpec(...]
    ppermute x7, starting transfers between devices: 19.3 us -> 11.3 us  [along_z(): return lax.ppermute(chunk, 'row', z_pairs)]
    ppermute x3 -> x0, starting transfers between devices: 6.4 us -> none  [right_of(): lax.ppermute(held, 'row', [(r, (r - turn) % rows_n) for r in range(rows_n)])]
    ppermute x6, waiting for transfers between devices: 28.1 us -> 24.8 us  [along_x(): return lax.ppermute(chunk, 'row', x_pairs)]
    unnamed x28 -> x18, local copies, waits for them, and re-layouts: 8.37 us -> 5.27 us
    ppermute x7, waiting for transfers between devices: 7.71 us -> 10.7 us  [along_z(): return lax.ppermute(chunk, 'row', z_pairs)]
    ppermute x6, starting transfers between devices: 5.33 us -> 8.07 us  [along_x(): return lax.ppermute(chunk, 'row', x_pairs)]
    pallas_call x4, Pallas kernels: 0.92 us -> 2.71 us  [own_quarters(): pl.pallas_call(kernel, grid=(1,), in_specs=[own_spec(right, quarter % HAL...]
  transfers between devices with their start and end apart: 20 -> 17, of which waited for: 9 -> 12; matrix products, arithmetic and copies ran while one was open for 1% -> 1% of each run, Pallas kernels for 20% -> 32%
where the time goes in v6:
time: 109 us
  waiting for transfers between devices  43.6 us (40%)
  Pallas kernels  35.5 us (33%)
  starting transfers between devices  22.9 us (21%)
  local copies, waits for them, and re-layouts  5.69 us (5%)
    ppermute x6, waiting for transfers between devices, along_x(): return lax.ppermute(chunk, 'row', x_pairs)  24.8 us
    pallas_call x9, Pallas kernels, accumulate(): pl.pallas_call(kernel, grid_spec=pltpu.PrefetchScalarGridSpec(num_scalar_...  18.6 us
    ppermute x7, starting transfers between devices, along_z(): return lax.ppermute(chunk, 'row', z_pairs)  11.3 us
    ppermute x7, waiting for transfers between devices, along_z(): return lax.ppermute(chunk, 'row', z_pairs)  10.7 us
    ppermute x6, starting transfers between devices, along_x(): return lax.ppermute(chunk, 'row', x_pairs)  8.07 us
    ppermute x2, waiting for transfers between devices, to_partner(): return lax.ppermute(blocks, 'rep', [(0, 1), (1, 0)])  7.76 us
    pallas_call x3, Pallas kernels, panel_places(): pl.pallas_call(kernel, grid=(1,), in_specs=[in_smem] * 3 + [pl.BlockSpec(...  5.92 us
    pallas_call x7, Pallas kernels, pick(): pl.pallas_call(kernel, grid=(1,), in_specs=[in_smem] + [spec(*part) for p...  5.8 us
  transfers between devices with their start and end apart: 17, of which 12 were waited for; matrix products, arithmetic and copies ran while one was open for 1% of the time, Pallas kernels for 32%

profile of v6, /device:TPU:0, one launch (start us, length us, event | category | flops | bytes accessed | tf_op | source)
XLA Modules:
  0.0 108.6 jit_solution(8030782789175596162)
XLA Ops:
  0.5 0.7 convert_element_type.15
  1.3 1.6 %copy-done = f32[1,1,1,8,4,128,128]{6,5,4,3,2,1,0:T(8,128)S(1)} copy-done((f32[1,1,1,8,4,128,128]{6,5,4,3,2,1,0:T(8,128)S(1)}, f32[1,1,1,8,4,128,128]{6,5,4,3,2,1,0:T(8,128)}, u32[]{:S(2)}) %copy-start) | copy-done | bytes 2097176
  2.9 1.3 %own_quarters.4.refs_2_ = f32[1024,256]{1,0:T(8,128)} custom-call(f32[8,4,128,128]{3,2,1,0:T(8,128)S(1)} %bitcast.16, f32[8,4,128,128]{3,2,1,0:T(8,128)S(1)} %bitcast.17), custom_call_target="tpu_custom_call" | custom-call | bytes 3145728 | tf_op jit(solution)/shard_map/own_quarters/pallas_call | solution.py:87
  4.2 1.0 own_quarters.5
  5.2 4.6 %collective-permute-start.1 = (f32[520,256]{1,0:T(8,128)}, f32[520,256]{1,0:T(8,128)}, u32[]{:S(2)}, u32[]{:S(2)}) collective-permute-start(f32[520,256]{1,0:T(8,128)} %own_quarters.5), channel_id=1, source_target_pairs={{0,24},{4,28},{8,0},{12,4},{16,8},{20,12},{24,16},{28,20},{1,25},{... | collective-permute-start | bytes 1597448 | tf_op jit(solution)/shard_map/ppermute | solution.py:363
  9.8 1.5 %collective-permute-start.5 = (f32[1024,256]{1,0:T(8,128)}, f32[1024,256]{1,0:T(8,128)}, u32[]{:S(2)}, u32[]{:S(2)}) collective-permute-start(f32[1024,256]{1,0:T(8,128)} %own_quarters.4.refs_2_), channel_id=1, source_target_pairs={{0,4},{4,0},{8,12},{12,8},{16,20},{20,16},{24,28},{28,24},{1,5},{5... | collective-permute-start | bytes 3145736 | tf_op jit(solution)/shard_map/ppermute | solution.py:366
  11.8 1.4 %own_places.1 = (s32[64]{0:T(128)S(1)}, s32[64]{0:T(128)S(1)}) custom-call(s32[6]{0:T(128)S(1)} %stack.27.info_ref, s32[24]{0:T(128)S(1)} %bitcast.32, s32[48]{0:T(128)S(1)} %reshape.17.rows_ref, s32[32]{0:T(128)S(1)} %reshape.18.cols_ref), custom_call_target="tpu_custom_call" | custom-call | tf_op jit(solution)/shard_map/own_places/pallas_call | solution.py:277
  13.2 1.6 %copy-done.1 = f32[1,1,1,8,4,128,128]{6,5,4,3,2,1,0:T(8,128)S(1)} copy-done((f32[1,1,1,8,4,128,128]{6,5,4,3,2,1,0:T(8,128)S(1)}, f32[1,1,1,8,4,128,128]{6,5,4,3,2,1,0:T(8,128)}, u32[]{:S(2)}) %copy-start.1) | copy-done | bytes 2097176
  14.8 1.9 %copy-done.3 = f32[1,1,1,3,8,2,128,128]{7,6,5,4,3,2,1,0:T(8,128)S(1)} copy-done((f32[1,1,1,3,8,2,128,128]{7,6,5,4,3,2,1,0:T(8,128)S(1)}, f32[1,1,1,3,8,2,128,128]{7,6,5,4,3,2,1,0:T(8,128)}, u32[]{:S(2)}) %copy-start.3) | copy-done | bytes 3145752
  16.7 2.5 %accumulate.9 = (f32[25,128,128]{2,1,0:T(8,128)S(1)}, f32[25,128,128]{2,1,0:T(8,128)S(1)}, s32[8,128]{1,0:T(8,128)S(1)}) custom-call(s32[6]{0:T(128)S(1)} %stack.27.info_ref, s32[64]{0:T(128)S(1)} %get-tuple-element.30.refs_0_, f32[3,8,2,128,128]{4,3,2,1,0:T(8,128)S(1)} %bitcast.26, f32[8,4,128,128]{3,2,1,0:T(8,128)S(1)} %bitcast.19), custom_call_target="tpu_custom_call" | custom-call | flops 805306368 | bytes 4194304 | tf_op jit(solution)/shard_map/accumulate/pallas_call | solution.py:245
  19.8 2.7 %collective-permute-done.1.refs_0_.refs_1_.even_ref.odd_ref.refs_3_ = f32[520,256]{1,0:T(8,128)} collective-permute-done((f32[520,256]{1,0:T(8,128)}, f32[520,256]{1,0:T(8,128)}, u32[]{:S(2)}, u32[]{:S(2)}) %collective-permute-start.1) | collective-permute-done | bytes 532512 | tf_op jit(solution)/shard_map/ppermute | solution.py:363
  22.6 1.1 %pick.7 = f32[520,256]{1,0:T(8,128)S(1)} custom-call(s32[6]{0:T(128)S(1)} %stack.27.info_ref, f32[520,256]{1,0:T(8,128)} %collective-permute-done.1.refs_0_.refs_1_.even_ref.odd_ref.refs_3_, f32[8,4,128,128]{3,2,1,0:T(8,128)S(1)} %bitcast.21, f32[8,256]{1,0:T(8,128)S(1)} %pad.4.refs_1_.refs_2_, s32[8,128]{1,0:T(8,128)S(1)} %get-tuple-element.31.refs_3_.refs_2_.refs_1_), custom_call_target="tpu_custom_call" | custom-call | bytes 1064960 | tf_op jit(solution)/shard_map/pick/pallas_call | solution.py:130
  23.7 1.7 %collective-permute-start.2 = (f32[520,256]{1,0:T(8,128)S(1)}, f32[520,256]{1,0:T(8,128)S(1)}, u32[]{:S(2)}, u32[]{:S(2)}) collective-permute-start(f32[520,256]{1,0:T(8,128)S(1)} %pick.7), channel_id=1, source_target_pairs={{0,4},{4,0},{8,12},{12,8},{16,20},{20,16},{24,28},{28,24},{1,5},{5... | collective-permute-start | bytes 1597448 | tf_op jit(solution)/shard_map/ppermute | solution.py:366
  25.6 4.3 %collective-permute-start.3 = (f32[512,256]{1,0:T(8,128)S(1)}, f32[512,256]{1,0:T(8,128)S(1)}, u32[]{:S(2)}, u32[]{:S(2)}) collective-permute-start(f32[512,256]{1,0:T(8,128)S(1)} %own_quarters.6), channel_id=1, source_target_pairs={{0,24},{4,28},{8,0},{12,4},{16,8},{20,12},{24,16},{28,20},{1,25},{... | collective-permute-start | bytes 1572872 | tf_op jit(solution)/shard_map/ppermute | solution.py:363
  29.9 2.1 %panel_places.4.refs_0_.refs_1_ = s32[64]{0:T(128)S(1)} custom-call(s32[6]{0:T(128)S(1)} %stack.27.info_ref, s32[64]{0:T(128)S(1)} %get-tuple-element.29.table_ref, s32[48]{0:T(128)S(1)} %reshape.17.rows_ref, f32[520,256]{1,0:T(8,128)} %collective-permute-done.1.refs_0_.refs_1_.even_ref.odd_ref.refs_3_, ...), custom_call_target="tpu_custom_call" | custom-call | tf_op jit(solution)/shard_map/panel_places/pallas_call | solution.py:310
  32.1 2.1 %collective-permute-done.6.refs_4_.refs_0_.refs_1_ = f32[512,256]{1,0:T(8,128)S(1)} collective-permute-done((f32[512,256]{1,0:T(8,128)S(1)}, f32[512,256]{1,0:T(8,128)S(1)}, u32[]{:S(2)}, u32[]{:S(2)}) %collective-permute-start.6) | collective-permute-done | bytes 524320 | tf_op jit(solution)/shard_map/ppermute | solution.py:363
  34.2 2.6 %accumulate.10 = (f32[25,128,128]{2,1,0:T(8,128)S(1)}, s32[8,128]{1,0:T(8,128)S(1)}) custom-call(s32[6]{0:T(128)S(1)} %stack.27.info_ref, s32[64]{0:T(128)S(1)} %panel_places.4.refs_0_.refs_1_, f32[3,8,2,128,128]{4,3,2,1,0:T(8,128)S(1)} %bitcast.27, f32[3,8,2,128,128]{4,3,2,1,0:T(8,128)S(1)} %bitcast.28, ...), custom_call_target="tpu_custom_call", output_to_operand_aliasing={{0}: (6, {})} | custom-call | flops 402653184 | bytes 2097152 | tf_op jit(solution)/shard_map/accumulate/pallas_call | solution.py:245
  36.8 0.6 pick.10
  37.4 1.2 %collective-permute-start.9 = (f32[512,256]{1,0:T(8,128)S(1)}, f32[512,256]{1,0:T(8,128)S(1)}, u32[]{:S(2)}, u32[]{:S(2)}) collective-permute-start(f32[512,256]{1,0:T(8,128)S(1)} %pick.10), channel_id=1, source_target_pairs={{0,4},{4,0},{8,12},{12,8},{16,20},{20,16},{24,28},{28,24},{1,5},{5... | collective-permute-start | bytes 1572872 | tf_op jit(solution)/shard_map/ppermute | solution.py:366
  38.6 8.8 %collective-permute-done.2.even_ref.odd_ref.refs_6_.refs_1_ = f32[520,256]{1,0:T(8,128)S(1)} collective-permute-done((f32[520,256]{1,0:T(8,128)S(1)}, f32[520,256]{1,0:T(8,128)S(1)}, u32[]{:S(2)}, u32[]{:S(2)}) %collective-permute-start.2) | collective-permute-done | bytes 532512 | tf_op jit(solution)/shard_map/ppermute | solution.py:366
  47.5 0.7 pick.9
  49.0 1.9 %panel_places.3.refs_0_ = s32[64]{0:T(128)S(1)} custom-call(s32[6]{0:T(128)S(1)} %stack.27.info_ref, s32[64]{0:T(128)S(1)} %get-tuple-element.29.table_ref, s32[48]{0:T(128)S(1)} %collective-permute-done.rows_ref, f32[520,256]{1,0:T(8,128)S(1)} %collective-permute-done.2.even_ref.odd_ref.refs_6_.refs_1_, ...), custom_call_target="tpu_custom_call" | custom-call | tf_op jit(solution)/shard_map/panel_places/pallas_call | solution.py:310
  51.0 3.2 %accumulate.11 = (f32[25,128,128]{2,1,0:T(8,128)S(1)}, f32[25,128,128]{2,1,0:T(8,128)S(1)}, s32[8,128]{1,0:T(8,128)S(1)}) custom-call(s32[6]{0:T(128)S(1)} %stack.27.info_ref, s32[64]{0:T(128)S(1)} %panel_places.3.refs_0_, ...), custom_call_target="tpu_custom_call", output_to_operand_aliasing={{0}: (8, {}), {1}: (9, {})} | custom-call | flops 603979776 | bytes 3145728 | tf_op jit(solution)/shard_map/accumulate/pallas_call | solution.py:245
  54.1 1.1 %pick.8 = f32[520,256]{1,0:T(8,128)S(1)} custom-call(s32[6]{0:T(128)S(1)} %stack.27.info_ref, f32[512,256]{1,0:T(8,128)S(1)} %collective-permute-done.3.refs_0_.refs_4_.refs_1_, f32[520,256]{1,0:T(8,128)} %collective-permute-done.1.refs_0_.refs_1_.even_ref.odd_ref.refs_3_, f32[8,256]{1,0:T(8,128)S(1)} %pad.4.refs_1_.refs_2_, ...), custom_call_target="tpu_custom_call" | custom-call | bytes 1064960 | tf_op jit(solution)/shard_map/pick/pallas_call | solution.py:130
  55.2 0.7 collective-permute-start.7
  55.9 2.2 %collective-permute-done.9.refs_5_.refs_1_ = f32[512,256]{1,0:T(8,128)S(1)} collective-permute-done((f32[512,256]{1,0:T(8,128)S(1)}, f32[512,256]{1,0:T(8,128)S(1)}, u32[]{:S(2)}, u32[]{:S(2)}) %collective-permute-start.9) | collective-permute-done | bytes 524320 | tf_op jit(solution)/shard_map/ppermute | solution.py:366
  58.1 1.1 %pick.12 = f32[512,256]{1,0:T(8,128)S(1)} custom-call(s32[6]{0:T(128)S(1)} %stack.27.info_ref, f32[1024,256]{1,0:T(8,128)} %collective-permute-done.5.refs_4_.refs_5_.refs_0_, f32[512,256]{1,0:T(8,128)S(1)} %collective-permute-done.9.refs_5_.refs_1_, s32[8,128]{1,0:T(8,128)S(1)} %get-tuple-element.35.refs_3_.refs_2_), custom_call_target="tpu_custom_call" | custom-call | bytes 1048576 | tf_op jit(solution)/shard_map/pick/pallas_call | solution.py:130
  59.2 0.5 collective-permute-start.11
  59.7 1.5 %accumulate.12 = (f32[25,128,128]{2,1,0:T(8,128)S(1)}, f32[25,128,128]{2,1,0:T(8,128)S(1)}, s32[8,128]{1,0:T(8,128)S(1)}) custom-call(s32[6]{0:T(128)S(1)} %stack.27.info_ref, s32[64]{0:T(128)S(1)} %panel_places.3.refs_0_, s32[64]{0:T(128)S(1)} %panel_places.4.refs_0_.refs_1_, ...), custom_call_target="tpu_custom_call", output_to_operand_aliasing={{0}: (7, {}), {1}: (8, {})} | custom-call | flops 402653184 | bytes 2097152 | tf_op jit(solution)/shard_map/accumulate/pallas_call | solution.py:245
  61.1 2.4 %collective-permute-done.8.odd_ref.refs_0_.refs_7_ = f32[520,256]{1,0:T(8,128)S(1)} collective-permute-done((f32[520,256]{1,0:T(8,128)S(1)}, f32[520,256]{1,0:T(8,128)S(1)}, u32[]{:S(2)}, u32[]{:S(2)}) %collective-permute-start.8) | collective-permute-done | bytes 532512 | tf_op jit(solution)/shard_map/ppermute | solution.py:363
  63.5 0.6 pick.11
  64.1 1.6 %collective-permute-start.10 = (f32[512,256]{1,0:T(8,128)S(1)}, f32[512,256]{1,0:T(8,128)S(1)}, u32[]{:S(2)}, u32[]{:S(2)}) collective-permute-start(f32[512,256]{1,0:T(8,128)S(1)} %pick.11), channel_id=1, source_target_pairs={{0,4},{4,0},{8,12},{12,8},{16,20},{20,16},{24,28},{28,24},{1,5},{5... | collective-permute-start | bytes 1572872 | tf_op jit(solution)/shard_map/ppermute | solution.py:366
  65.7 4.6 %collective-permute-done.7.even_ref.refs_8_ = f32[520,256]{1,0:T(8,128)S(1)} collective-permute-done((f32[520,256]{1,0:T(8,128)S(1)}, f32[520,256]{1,0:T(8,128)S(1)}, u32[]{:S(2)}, u32[]{:S(2)}) %collective-permute-start.7) | collective-permute-done | bytes 532512 | tf_op jit(solution)/shard_map/ppermute | solution.py:366
  70.3 1.9 %panel_places.5.refs_2_.refs_0_.refs_1_ = s32[64]{0:T(128)S(1)} custom-call(s32[6]{0:T(128)S(1)} %stack.27.info_ref, s32[64]{0:T(128)S(1)} %get-tuple-element.29.table_ref, s32[48]{0:T(128)S(1)} %collective-permute-done.rows_ref, f32[520,256]{1,0:T(8,128)S(1)} %collective-permute-done.7.even_ref.refs_8_, ...), custom_call_target="tpu_custom_call" | custom-call | tf_op jit(solution)/shard_map/panel_places/pallas_call | solution.py:310
  72.7 1.7 %accumulate.13 = (f32[25,128,128]{2,1,0:T(8,128)S(1)}, f32[25,128,128]{2,1,0:T(8,128)S(1)}, s32[8,128]{1,0:T(8,128)S(1)}) custom-call(s32[6]{0:T(128)S(1)} %stack.27.info_ref, s32[64]{0:T(128)S(1)} %panel_places.3.refs_0_, s32[64]{0:T(128)S(1)} %panel_places.4.refs_0_.refs_1_, ...), custom_call_target="tpu_custom_call", output_to_operand_aliasing={{0}: (10, {}), {1}: (11, {})} | custom-call | flops 402653184 | bytes 2097152 | tf_op jit(solution)/shard_map/accumulate/pallas_call | solution.py:245
  74.8 0.6 pick.13
  75.3 1.4 %collective-permute-start.14 = (f32[512,256]{1,0:T(8,128)S(1)}, f32[512,256]{1,0:T(8,128)S(1)}, u32[]{:S(2)}, u32[]{:S(2)}) collective-permute-start(f32[512,256]{1,0:T(8,128)S(1)} %pick.13), channel_id=1, source_target_pairs={{0,4},{4,0},{8,12},{12,8},{16,20},{20,16},{24,28},{28,24},{1,5},{5... | collective-permute-start | bytes 1572872 | tf_op jit(solution)/shard_map/ppermute | solution.py:366
  76.8 4.7 %collective-permute-done.10.refs_4_ = f32[512,256]{1,0:T(8,128)S(1)} collective-permute-done((f32[512,256]{1,0:T(8,128)S(1)}, f32[512,256]{1,0:T(8,128)S(1)}, u32[]{:S(2)}, u32[]{:S(2)}) %collective-permute-start.10) | collective-permute-done | bytes 524320 | tf_op jit(solution)/shard_map/ppermute | solution.py:366
  82.0 1.7 %accumulate.14 = (f32[25,128,128]{2,1,0:T(8,128)S(1)}, f32[25,128,128]{2,1,0:T(8,128)S(1)}, s32[8,128]{1,0:T(8,128)}) custom-call(s32[6]{0:T(128)S(1)} %stack.27.info_ref, s32[64]{0:T(128)S(1)} %panel_places.5.refs_2_.refs_0_.refs_1_, ...), custom_call_target="tpu_custom_call", output_to_operand_aliasing={{0}: (5, {}), {1}: (6, {})} | custom-call | flops 201326592 | bytes 1048576 | tf_op jit(solution)/shard_map/accumulate/pallas_call | solution.py:245
  83.6 2.3 %accumulate.15 = (f32[25,128,128]{2,1,0:T(8,128)S(1)}, f32[25,128,128]{2,1,0:T(8,128)S(1)}, s32[8,128]{1,0:T(8,128)}, f32[6,128,128]{2,1,0:T(8,128)S(1)}, f32[6,128,128]{2,1,0:T(8,128)S(1)}) custom-call(s32[6]{0:T(128)S(1)} %stack.27.info_ref, s32[64]{0:T(128)S(1)} %panel_places.3.refs_0_, ...), custom_call_target="tpu_custom_call", output_to_operand_aliasing={{0}: (6, {}), {1}: (7, {})} | custom-call | flops 201326592 | bytes 1048576 | tf_op jit(solution)/shard_map/accumulate/pallas_call | solution.py:245
  85.9 1.5 %collective-permute-start.15 = (f32[6,128,128]{2,1,0:T(8,128)S(1)}, f32[6,128,128]{2,1,0:T(8,128)S(1)}, u32[]{:S(2)}, u32[]{:S(2)}) collective-permute-start(f32[6,128,128]{2,1,0:T(8,128)S(1)} %get-tuple-element.51), channel_id=1, source_target_pairs={{0,1},{1,0},{2,3},{3,2},{4,5},{5,4},{6,7},{7,6},{8,9},{9,8},{10,11... | collective-permute-start | bytes 1179656 | tf_op jit(solution)/shard_map/ppermute | solution.py:427
  87.4 4.4 %collective-permute-done.14.refs_6_ = f32[512,256]{1,0:T(8,128)S(1)} collective-permute-done((f32[512,256]{1,0:T(8,128)S(1)}, f32[512,256]{1,0:T(8,128)S(1)}, u32[]{:S(2)}, u32[]{:S(2)}) %collective-permute-start.14) | collective-permute-done | bytes 524320 | tf_op jit(solution)/shard_map/ppermute | solution.py:366
  91.9 1.7 %accumulate.16 = (f32[25,128,128]{2,1,0:T(8,128)S(1)}, s32[8,128]{1,0:T(8,128)}) custom-call(s32[6]{0:T(128)S(1)} %stack.27.info_ref, s32[64]{0:T(128)S(1)} %panel_places.4.refs_0_.refs_1_, s32[64]{0:T(128)S(1)} %panel_places.5.refs_2_.refs_0_.refs_1_, ...), custom_call_target="tpu_custom_call", output_to_operand_aliasing={{0}: (8, {})} | custom-call | flops 402653184 | bytes 2097152 | tf_op jit(solution)/shard_map/accumulate/pallas_call | solution.py:245
  93.6 3.1 %collective-permute-done.12.refs_2_ = f32[512,256]{1,0:T(8,128)S(1)} collective-permute-done((f32[512,256]{1,0:T(8,128)S(1)}, f32[512,256]{1,0:T(8,128)S(1)}, u32[]{:S(2)}, u32[]{:S(2)}) %collective-permute-start.12) | collective-permute-done | bytes 524320 | tf_op jit(solution)/shard_map/ppermute | solution.py:363
  96.7 1.5 %accumulate.17 = (f32[25,128,128]{2,1,0:T(8,128)S(1)}, s32[8,128]{1,0:T(8,128)}, f32[6,128,128]{2,1,0:T(8,128)S(1)}, f32[6,128,128]{2,1,0:T(8,128)S(1)}) custom-call(s32[6]{0:T(128)S(1)} %stack.27.info_ref, s32[64]{0:T(128)S(1)} %panel_places.5.refs_2_.refs_0_.refs_1_, ...), custom_call_target="tpu_custom_call", output_to_operand_aliasing={{0}: (4, {})} | custom-call | flops 201326592 | bytes 1048576 | tf_op jit(solution)/shard_map/accumulate/pallas_call | solution.py:245
  98.2 1.5 %collective-permute-start.16 = (f32[6,128,128]{2,1,0:T(8,128)S(1)}, f32[6,128,128]{2,1,0:T(8,128)S(1)}, u32[]{:S(2)}, u32[]{:S(2)}) collective-permute-start(f32[6,128,128]{2,1,0:T(8,128)S(1)} %get-tuple-element.52), channel_id=1, source_target_pairs={{0,1},{1,0},{2,3},{3,2},{4,5},{5,4},{6,7},{7,6},{8,9},{9,8},{10,11... | collective-permute-start | bytes 1179656 | tf_op jit(solution)/shard_map/ppermute | solution.py:427
  99.7 7.8 %collective-permute-done.16.other_1 = f32[6,128,128]{2,1,0:T(8,128)S(1)} collective-permute-done((f32[6,128,128]{2,1,0:T(8,128)S(1)}, f32[6,128,128]{2,1,0:T(8,128)S(1)}, u32[]{:S(2)}, u32[]{:S(2)}) %collective-permute-start.16) | collective-permute-done | bytes 393248 | tf_op jit(solution)/shard_map/ppermute | solution.py:427
  107.5 1.1 %combine.1 = f32[2,6,128,128]{3,2,1,0:T(8,128)} custom-call(f32[6,128,128]{2,1,0:T(8,128)S(1)} %get-tuple-element.46.kept_0, f32[6,128,128]{2,1,0:T(8,128)S(1)} %get-tuple-element.50.kept_1, f32[6,128,128]{2,1,0:T(8,128)S(1)} %collective-permute-done.15.other_0, f32[6,128,128]{2,1,0:T(8,128)S(1)} %collective-permute-done.16.other_1), custom_call_target="tpu_custom_call" | custom-call | tf_op jit(solution)/shard_map/combine/pallas_call | solution.py:335
  (36 shorter events, 4.1 us)
Async XLA Ops:
  0.0 51.0 %collective-permute-start.4 = (f32[3,8,2,128,128]{4,3,2,1,0:T(8,128)}, f32[3,8,2,128,128]{4,3,2,1,0:T(8,128)S(1)}, u32[]{:S(2)}, u32[]{:S(2)}) collective-permute-start(f32[3,8,2,128,128]{4,3,2,1,0:T(8,128)} %bitcast.25), channel_id=1, source_target_pairs={{0,2},{2,0},{1,3},{3,1},{4,6},{6,4},{5,7},{7,5},{8,10},{10,8},{9,1... | collective-permute-start | bytes 9437192 | tf_op jit(solution)/shard_map/ppermute | solution.py:382
  1.3 1.6 %copy-start = (f32[1,1,1,8,4,128,128]{6,5,4,3,2,1,0:T(8,128)S(1)}, f32[1,1,1,8,4,128,128]{6,5,4,3,2,1,0:T(8,128)}, u32[]{:S(2)}) copy-start(f32[1,1,1,8,4,128,128]{6,5,4,3,2,1,0:T(8,128)} %param.7) | copy-start | bytes 6291460
  4.2 7.1 %copy-start.6 = (s32[1,1,1,8,4]{3,4,2,1,0:T(4,128)S(1)}, s32[1,1,1,8,4]{3,4,2,1,0:T(4,128)}, u32[]{:S(2)}) copy-start(s32[1,1,1,8,4]{3,4,2,1,0:T(4,128)} %param.8) | copy-start | bytes 388
  4.2 7.2 %copy-start.7 = (s32[1,1,1,3,8,2]{4,5,3,2,1,0:T(2,128)S(1)}, s32[1,1,1,3,8,2]{4,5,3,2,1,0:T(2,128)}, u32[]{:S(2)}) copy-start(s32[1,1,1,3,8,2]{4,5,3,2,1,0:T(2,128)} %param.6) | copy-start | bytes 580
  4.2 7.5 %copy-start.5 = (s32[1,1,24]{2,1,0:T(1,128)S(1)}, s32[1,1,24]{2,1,0:T(1,128)}, u32[]{:S(2)}) copy-start(s32[1,1,24]{2,1,0:T(1,128)} %param.9) | copy-start | bytes 292
  5.2 17.3 %collective-permute-start.1 = (f32[520,256]{1,0:T(8,128)}, f32[520,256]{1,0:T(8,128)}, u32[]{:S(2)}, u32[]{:S(2)}) collective-permute-start(f32[520,256]{1,0:T(8,128)} %own_quarters.5), channel_id=1, source_target_pairs={{0,24},{4,28},{8,0},{12,4},{16,8},{20,12},{24,16},{28,20},{1,25},{... | collective-permute-start | bytes 1597448 | tf_op jit(solution)/shard_map/ppermute | solution.py:363
  9.8 41.1 %collective-permute-start.5 = (f32[1024,256]{1,0:T(8,128)}, f32[1024,256]{1,0:T(8,128)}, u32[]{:S(2)}, u32[]{:S(2)}) collective-permute-start(f32[1024,256]{1,0:T(8,128)} %own_quarters.4.refs_2_), channel_id=1, source_target_pairs={{0,4},{4,0},{8,12},{12,8},{16,20},{20,16},{24,28},{28,24},{1,5},{5... | collective-permute-start | bytes 3145736 | tf_op jit(solution)/shard_map/ppermute | solution.py:366
  13.2 1.6 %copy-start.1 = (f32[1,1,1,8,4,128,128]{6,5,4,3,2,1,0:T(8,128)S(1)}, f32[1,1,1,8,4,128,128]{6,5,4,3,2,1,0:T(8,128)}, u32[]{:S(2)}) copy-start(f32[1,1,1,8,4,128,128]{6,5,4,3,2,1,0:T(8,128)} %param.7) | copy-start | bytes 6291460
  14.8 1.9 %copy-start.3 = (f32[1,1,1,3,8,2,128,128]{7,6,5,4,3,2,1,0:T(8,128)S(1)}, f32[1,1,1,3,8,2,128,128]{7,6,5,4,3,2,1,0:T(8,128)}, u32[]{:S(2)}) copy-start(f32[1,1,1,3,8,2,128,128]{7,6,5,4,3,2,1,0:T(8,128)} %param.5) | copy-start | bytes 9437188
  19.4 14.8 %collective-permute-start.6 = (f32[512,256]{1,0:T(8,128)S(1)}, f32[512,256]{1,0:T(8,128)S(1)}, u32[]{:S(2)}, u32[]{:S(2)}) collective-permute-start(f32[512,256]{1,0:T(8,128)S(1)} %own_quarters.7), channel_id=1, source_target_pairs={{0,24},{4,28},{8,0},{12,4},{16,8},{20,12},{24,16},{28,20},{1,25},{... | collective-permute-start | bytes 1572872 | tf_op jit(solution)/shard_map/ppermute | solution.py:363
  23.7 10.5 %copy-start.4 = (f32[1,1,1,3,8,2,128,128]{7,6,5,4,3,2,1,0:T(8,128)S(1)}, f32[1,1,1,3,8,2,128,128]{7,6,5,4,3,2,1,0:T(8,128)}, u32[]{:S(2)}) copy-start(f32[1,1,1,3,8,2,128,128]{7,6,5,4,3,2,1,0:T(8,128)} %param.5) | copy-start | bytes 9437188
  23.7 23.8 %collective-permute-start.2 = (f32[520,256]{1,0:T(8,128)S(1)}, f32[520,256]{1,0:T(8,128)S(1)}, u32[]{:S(2)}, u32[]{:S(2)}) collective-permute-start(f32[520,256]{1,0:T(8,128)S(1)} %pick.7), channel_id=1, source_target_pairs={{0,4},{4,0},{8,12},{12,8},{16,20},{20,16},{24,28},{28,24},{1,5},{5... | collective-permute-start | bytes 1597448 | tf_op jit(solution)/shard_map/ppermute | solution.py:366
  25.6 28.5 %collective-permute-start.3 = (f32[512,256]{1,0:T(8,128)S(1)}, f32[512,256]{1,0:T(8,128)S(1)}, u32[]{:S(2)}, u32[]{:S(2)}) collective-permute-start(f32[512,256]{1,0:T(8,128)S(1)} %own_quarters.6), channel_id=1, source_target_pairs={{0,24},{4,28},{8,0},{12,4},{16,8},{20,12},{24,16},{28,20},{1,25},{... | collective-permute-start | bytes 1572872 | tf_op jit(solution)/shard_map/ppermute | solution.py:363
  34.2 2.6 %copy-start.2 = (f32[1,1,1,8,4,128,128]{6,5,4,3,2,1,0:T(8,128)S(1)}, f32[1,1,1,8,4,128,128]{6,5,4,3,2,1,0:T(8,128)}, u32[]{:S(2)}) copy-start(f32[1,1,1,8,4,128,128]{6,5,4,3,2,1,0:T(8,128)} %param.7) | copy-start | bytes 6291460
  37.4 20.6 %collective-permute-start.9 = (f32[512,256]{1,0:T(8,128)S(1)}, f32[512,256]{1,0:T(8,128)S(1)}, u32[]{:S(2)}, u32[]{:S(2)}) collective-permute-start(f32[512,256]{1,0:T(8,128)S(1)} %pick.10), channel_id=1, source_target_pairs={{0,4},{4,0},{8,12},{12,8},{16,20},{20,16},{24,28},{28,24},{1,5},{5... | collective-permute-start | bytes 1572872 | tf_op jit(solution)/shard_map/ppermute | solution.py:366
  47.5 1.1 %collective-permute-start = (s32[48]{0:T(128)S(1)}, s32[48]{0:T(128)S(1)}, u32[]{:S(2)}, u32[]{:S(2)}) collective-permute-start(s32[48]{0:T(128)S(1)} %reshape.17.rows_ref), channel_id=1, source_target_pairs={{0,2},{2,0},{1,3},{3,1},{4,6},{6,4},{5,7},{7,5},{8,10},{10,8},{9,1... | collective-permute-start | bytes 584 | tf_op jit(solution)/shard_map/ppermute | solution.py:382
  48.6 14.9 %collective-permute-start.8 = (f32[520,256]{1,0:T(8,128)S(1)}, f32[520,256]{1,0:T(8,128)S(1)}, u32[]{:S(2)}, u32[]{:S(2)}) collective-permute-start(f32[520,256]{1,0:T(8,128)S(1)} %pick.9), channel_id=1, source_target_pairs={{0,24},{4,28},{8,0},{12,4},{16,8},{20,12},{24,16},{28,20},{1,25},{... | collective-permute-start | bytes 1597448 | tf_op jit(solution)/shard_map/ppermute | solution.py:363
  55.2 15.0 %collective-permute-start.7 = (f32[520,256]{1,0:T(8,128)S(1)}, f32[520,256]{1,0:T(8,128)S(1)}, u32[]{:S(2)}, u32[]{:S(2)}) collective-permute-start(f32[520,256]{1,0:T(8,128)S(1)} %pick.8), channel_id=1, source_target_pairs={{0,4},{4,0},{8,12},{12,8},{16,20},{20,16},{24,28},{28,24},{1,5},{5... | collective-permute-start | bytes 1597448 | tf_op jit(solution)/shard_map/ppermute | solution.py:366
  59.2 15.6 %collective-permute-start.11 = (f32[512,256]{1,0:T(8,128)S(1)}, f32[512,256]{1,0:T(8,128)S(1)}, u32[]{:S(2)}, u32[]{:S(2)}) collective-permute-start(f32[512,256]{1,0:T(8,128)S(1)} %pick.12), channel_id=1, source_target_pairs={{0,24},{4,28},{8,0},{12,4},{16,8},{20,12},{24,16},{28,20},{1,25},{... | collective-permute-start | bytes 1572872 | tf_op jit(solution)/shard_map/ppermute | solution.py:363
  64.1 17.4 %collective-permute-start.10 = (f32[512,256]{1,0:T(8,128)S(1)}, f32[512,256]{1,0:T(8,128)S(1)}, u32[]{:S(2)}, u32[]{:S(2)}) collective-permute-start(f32[512,256]{1,0:T(8,128)S(1)} %pick.11), channel_id=1, source_target_pairs={{0,4},{4,0},{8,12},{12,8},{16,20},{20,16},{24,28},{28,24},{1,5},{5... | collective-permute-start | bytes 1572872 | tf_op jit(solution)/shard_map/ppermute | solution.py:366
  72.2 19.7 %collective-permute-start.13 = (f32[520,256]{1,0:T(8,128)S(1)}, f32[520,256]{1,0:T(8,128)S(1)}, u32[]{:S(2)}, u32[]{:S(2)}) collective-permute-start(f32[520,256]{1,0:T(8,128)S(1)} %collective-permute-done.7.even_ref.refs_8_), channel_id=1, source_target_pairs={{0,24},{4,28},{8,0},{12,4},{16,8},{20,12},{24,16},{28,20},{1,25},{... | collective-permute-start | bytes 1597448 | tf_op jit(solution)/shard_map/ppermute | solution.py:363
  75.3 16.5 %collective-permute-start.14 = (f32[512,256]{1,0:T(8,128)S(1)}, f32[512,256]{1,0:T(8,128)S(1)}, u32[]{:S(2)}, u32[]{:S(2)}) collective-permute-start(f32[512,256]{1,0:T(8,128)S(1)} %pick.13), channel_id=1, source_target_pairs={{0,4},{4,0},{8,12},{12,8},{16,20},{20,16},{24,28},{28,24},{1,5},{5... | collective-permute-start | bytes 1572872 | tf_op jit(solution)/shard_map/ppermute | solution.py:366
  81.5 15.2 %collective-permute-start.12 = (f32[512,256]{1,0:T(8,128)S(1)}, f32[512,256]{1,0:T(8,128)S(1)}, u32[]{:S(2)}, u32[]{:S(2)}) collective-permute-start(f32[512,256]{1,0:T(8,128)S(1)} %collective-permute-done.10.refs_4_), channel_id=1, source_target_pairs={{0,24},{4,28},{8,0},{12,4},{16,8},{20,12},{24,16},{28,20},{1,25},{... | collective-permute-start | bytes 1572872 | tf_op jit(solution)/shard_map/ppermute | solution.py:363
  85.9 13.8 %collective-permute-start.15 = (f32[6,128,128]{2,1,0:T(8,128)S(1)}, f32[6,128,128]{2,1,0:T(8,128)S(1)}, u32[]{:S(2)}, u32[]{:S(2)}) collective-permute-start(f32[6,128,128]{2,1,0:T(8,128)S(1)} %get-tuple-element.51), channel_id=1, source_target_pairs={{0,1},{1,0},{2,3},{3,2},{4,5},{5,4},{6,7},{7,6},{8,9},{9,8},{10,11... | collective-permute-start | bytes 1179656 | tf_op jit(solution)/shard_map/ppermute | solution.py:427
  98.2 9.3 %collective-permute-start.16 = (f32[6,128,128]{2,1,0:T(8,128)S(1)}, f32[6,128,128]{2,1,0:T(8,128)S(1)}, u32[]{:S(2)}, u32[]{:S(2)}) collective-permute-start(f32[6,128,128]{2,1,0:T(8,128)S(1)} %get-tuple-element.52), channel_id=1, source_target_pairs={{0,1},{1,0},{2,3},{3,2},{4,5},{5,4},{6,7},{7,6},{8,9},{9,8},{10,11... | collective-permute-start | bytes 1179656 | tf_op jit(solution)/shard_map/ppermute | solution.py:427

commit v7 on v6

--- a/solution.py
+++ b/solution.py
@@ -13,25 +13,26 @@
 bf16 = jnp.bfloat16
 f32 = jnp.float32
 
+PARTS = 2
 Z_CHUNKS = {
-    1: ((2, 0), (2, 0)),
-    2: ((2, 1), (2, 1)),
-    3: ((2, 2), (2, 2)),
-    4: ((2, 3), (3, 0)),
-    5: ((3, 3), (3, 1)),
-    6: (None, (3, 2)),
-    7: (None, (3, 3)),
+    1: ((2, 0, 0, 2), (2, 0, 0, 2)),
+    2: ((2, 1, 0, 2), (2, 1, 0, 2)),
+    3: ((2, 2, 0, 2), (2, 2, 0, 2)),
+    4: ((2, 3, 0, 2), (3, 0, 0, 2)),
+    5: ((3, 3, 0, 2), (3, 1, 0, 2)),
+    6: ((3, 2, 0, 1), (3, 2, 0, 2)),
+    7: (None, (3, 3, 0, 2)),
 }
 X_CHUNKS = {
-    1: ((1, 2), None),
-    2: ((1, 3), None),
-    3: ((1, 0), (1, 0)),
-    4: ((1, 1), (1, 1)),
-    5: ((3, 0), (1, 2)),
-    6: ((3, 1), (1, 3)),
-    7: ((3, 2), (2, 3)),
+    1: ((1, 3, 0, 2), None),
+    2: ((1, 2, 0, 1), None),
+    3: ((1, 0, 0, 2), (1, 0, 0, 2)),
+    4: ((1, 1, 0, 2), (1, 1, 0, 2)),
+    5: ((3, 0, 0, 2), (1, 2, 0, 2)),
+    6: ((3, 1, 0, 2), (1, 3, 0, 2)),
+    7: ((3, 2, 1, 1), (2, 3, 0, 2)),
+    8: ((1, 2, 1, 1), None),
 }
-EXTRA = 8
 
 in_smem = pl.BlockSpec(memory_space=pltpu.SMEM)
 in_vmem = pl.BlockSpec(memory_space=pltpu.VMEM)
@@ -51,9 +52,9 @@
 
 
 def cut(right_ref, out_ref, half, at=0):
-    per, bpr, bs, _ = right_ref.shape
+    count, bpr, bs, _ = right_ref.shape
     lower = lower_lanes((bs, bs))
-    for k in range(per):
+    for k in range(count):
         for pair in range(bpr // 2):
             even, odd = right_ref[k, 2 * pair], right_ref[k, 2 * pair + 1]
             if half == 0:
@@ -63,8 +64,10 @@
             out_ref[at + k * bs:at + (k + 1) * bs, pair * bs:(pair + 1) * bs] = both
 
 
-def own_spec(right, k_half):
-    return pl.BlockSpec((right.shape[0] // HALVES,) + right.shape[1:], lambda *_: (k_half, 0, 0, 0))
+def own_spec(right, quarter, first=0, parts=PARTS):
+    count = right.shape[0] // (HALVES * PARTS) * parts
+    at = (quarter % HALVES * PARTS + first) // parts
+    return pl.BlockSpec((count,) + right.shape[1:], lambda *_: (at, 0, 0, 0))
 
 
 def quarter_shape(right):
@@ -72,22 +75,28 @@
     return kb // HALVES * bs, bpr * bs // HALVES
 
 
+def put_extra(out_ref, cols_ref, rows):
+    kb, bpr = cols_ref.shape
+    out_ref[rows:rows + kb, :bpr] = cols_ref[...].astype(out_ref.dtype)
+
+
 def own_quarters(right, quarters, cols, *others):
     rows, width = quarter_shape(right)
     extra = [] if cols is None else [cols]
+    starts = [sum(parts for _, _, parts in quarters[:n]) * rows // PARTS for n in range(len(quarters) + 1)]
 
     def kernel(*refs):
         out_ref = refs[-1]
-        for n, quarter in enumerate(quarters):
-            cut(refs[n], out_ref, quarter // HALVES, n * rows)
+        for n, (quarter, _, _) in enumerate(quarters):
+            cut(refs[n], out_ref, quarter // HALVES, starts[n])
         if extra:
-            out_ref[len(quarters) * rows:, :] = refs[len(quarters)][...]
-
-    out_shape = jax.ShapeDtypeStruct((len(quarters) * rows + EXTRA * len(extra), width), right.dtype)
+            put_extra(out_ref, refs[len(quarters)], starts[-1])
+
+    out_shape = jax.ShapeDtypeStruct((starts[-1] + right.shape[0] * len(extra), width), right.dtype)
     return pl.pallas_call(
         kernel,
         grid=(1,),
-        in_specs=[own_spec(right, quarter % HALVES) for quarter in quarters] + [whole(x.shape) for x in extra] + [anywhere] * len(others),
+        in_specs=[own_spec(right, *part) for part in quarters] + [whole(x.shape) for x in extra] + [anywhere] * len(others),
         out_specs=whole(out_shape.shape),
         out_shape=out_shape,
         compiler_params=pltpu.CompilerParams(vmem_limit_bytes=12 * 1024 * 1024),
@@ -96,52 +105,59 @@
     )(*[right] * len(quarters), *extra, *others)
 
 
-def pick(info, right, cols, even_part, odd_part, *others):
-    parts = (even_part, odd_part)
+def pick(info, right, cols, even_parts, odd_parts, *others):
+    sides = (even_parts, odd_parts)
+    kb = right.shape[0]
     rows, width = quarter_shape(right)
     extra = [] if cols is None else [cols]
 
-    def taken(array, at):
-        return array.shape[0] if extra and at == 0 and array.shape[0] == rows + EXTRA else rows
+    def has_extra(part):
+        return part[0] is not None and extra and part[0].shape[0] == rows + kb
+
+    def size(part):
+        return rows + kb if has_extra(part) else part[-1] * rows // PARTS
 
     def kernel(info_ref, *refs):
         out_ref = refs[-1]
 
-        def copy_from(n):
-            array, at = parts[n]
-            if array is None:
-                cut(refs[n], out_ref, at // HALVES)
-                if extra:
-                    out_ref[rows:, :] = refs[2][...]
-                return
-            out_ref[:refs[n].shape[0]] = refs[n][...]
-            if extra and refs[n].shape[0] == rows:
-                out_ref[rows:, :] = jnp.zeros((EXTRA, width), right.dtype)
-
-        pl.when(info_ref[0] == 0)(lambda: copy_from(0))
-        pl.when(info_ref[0] != 0)(lambda: copy_from(1))
-
-    def spec(array, at):
-        if array is None:
-            return own_spec(right, at % HALVES)
-        return pl.BlockSpec((taken(array, at), width), lambda *_: (at, 0))
-
-    out_shape = jax.ShapeDtypeStruct((rows + EXTRA * len(extra), width), right.dtype)
+        def copy_parts(side, refs_of):
+            at = 0
+            for part, ref in zip(sides[side], refs_of):
+                if part[0] is None:
+                    cut(ref, out_ref, part[1] // HALVES, at)
+                else:
+                    out_ref[at:at + size(part)] = ref[...]
+                at += size(part)
+            if at < out_ref.shape[0]:
+                out_ref[at:] = jnp.zeros((out_ref.shape[0] - at, width), out_ref.dtype)
+                if extra and sides[side][0][0] is None:
+                    put_extra(out_ref, refs[len(even_parts) + len(odd_parts)], rows)
+
+        pl.when(info_ref[0] == 0)(lambda: copy_parts(0, refs[:len(even_parts)]))
+        pl.when(info_ref[0] != 0)(lambda: copy_parts(1, refs[len(even_parts):]))
+
+    def spec(part):
+        if part[0] is None:
+            return own_spec(right, *part[1:])
+        return pl.BlockSpec((size(part), width), lambda *_: (part[1], 0))
+
+    parts = [*even_parts, *odd_parts]
+    out_shape = jax.ShapeDtypeStruct((rows + kb * len(extra), width), right.dtype)
     return pl.pallas_call(
         kernel,
         grid=(1,),
-        in_specs=[in_smem] + [spec(*part) for part in parts] + [whole(x.shape) for x in extra] + [anywhere] * len(others),
+        in_specs=[in_smem] + [spec(part) for part in parts] + [whole(x.shape) for x in extra] + [anywhere] * len(others),
         out_specs=whole(out_shape.shape),
         out_shape=out_shape,
         compiler_params=pltpu.CompilerParams(vmem_limit_bytes=8 * 1024 * 1024),
         cost_estimate=pl.CostEstimate(flops=0, bytes_accessed=8 * out_shape.size, transcendentals=0),
         name="pick",
-    )(info, *[right if array is None else array for array, _ in parts], *extra, *others)
+    )(info, *[right if part[0] is None else part[0] for part in parts], *extra, *others)
 
 
 def accumulate(info, places, lefts, chunks, totals, nc, finish=None):
     _, kb, lpb, bs, _ = lefts[0].shape
-    per = kb // HALVES
+    part = kb // (HALVES * PARTS)
     own = totals is None
     bpr = chunks[0][0].shape[1] if own else HALVES * chunks[0][0].shape[1] // bs
     width = bpr * bs // HALVES
@@ -193,11 +209,11 @@
                             total_refs[half][n, :, at] += out[a * bs:(a + 1) * bs, b * bs:(b + 1) * bs][:, at]
 
         def add(c, side):
-            turn, quarter = chunks[c][2][side]
+            turn, quarter, first, parts = chunks[c][2][side]
             half, k_half = divmod(quarter, HALVES)
-            base = k_half * per * products
+            base = (k_half * PARTS + first) * part * products
             left_ref, right_ref, total_ref = left_refs[c, side], right_refs[c], total_refs[half]
-            for k in range(per):
+            for k in range(parts * part):
                 out = products_of(left_ref[0, k], right_ref[k * bs:(k + 1) * bs])
                 for a in range(lpb):
                     for b in range(bpr):
@@ -224,14 +240,19 @@
                     one, two = total_refs[finish][n], total_refs[finish][n + packed]
                     ref[p] = jnp.where(lower, one + swap_lanes(one), two + swap_lanes(two))
 
-    def left_spec(turn, quarter):
-        return pl.BlockSpec((1, per, lpb, bs, bs), lambda g, info_ref, *_: (info_ref[1 + turn], quarter % HALVES, 0, 0, 0))
+    def left_spec(turn, quarter, first, parts):
+        at = (quarter % HALVES * PARTS + first) // parts
+        return pl.BlockSpec((1, parts * part, lpb, bs, bs), lambda g, info_ref, *_: (info_ref[1 + turn], at, 0, 0, 0))
+
+    def right_spec(at, both):
+        parts = max(what[3] for what in both if what is not None)
+        return pl.BlockSpec((parts * part * bs, width), lambda *_: (at, 0))
 
     operands = [lefts[chunks[c][2][side][0]] for c, side in sides] + [c[0] for c in chunks]
     if own:
         in_specs = [pl.BlockSpec((1, kb, lpb, bs, bs), lambda g, info_ref, *_: (info_ref[1], 0, 0, 0, 0)), whole(chunks[0][0].shape)]
     else:
-        in_specs = [left_spec(*chunks[c][2][side]) for c, side in sides] + [pl.BlockSpec((per * bs, width), lambda g, *_, at=at: (at, 0)) for _, at, _ in chunks]
+        in_specs = [left_spec(*chunks[c][2][side]) for c, side in sides] + [right_spec(at, both) for _, at, both in chunks]
     held = len(operands) + 1 + len(turns)
     if not own:
         operands += [totals[half] for half in touched]
@@ -240,6 +261,7 @@
     if finish is not None:
         outs += [jax.ShapeDtypeStruct((packed, bs, bs), f32)] * 2
     parts = QUARTERS if own else len(chunks)
+    per = kb // HALVES
     flops = parts * per * 2 * lpb * bs * 3 * bs * width
     moved = 4 * parts * per * (lpb * bs * bs + bs * width)
     results = pl.pallas_call(
@@ -272,7 +294,7 @@
         behind = nc - nc // 2 * info_ref[1 + STEPS]
         for n in range(nc):
             table_ref[slots_ref[n]] = lax.rem(n + behind, nc)
-        fill_places(info_ref[1], table_ref, rows_ref, lambda n: cols_ref[n], out_ref, kb, lpb, bpr)
+        fill_places(info_ref[1], table_ref, rows_ref, lambda k, b: cols_ref[k * bpr + b], out_ref, kb, lpb, bpr)
 
     return pl.pallas_call(
         kernel,
@@ -286,7 +308,7 @@
 
 def fill_places(panel, table_ref, rows_ref, col_of, out_ref, kb, lpb, bpr):
     def column(k, carry):
-        cols = [col_of(k * bpr + b) for b in range(bpr)]
+        cols = [col_of(k, b) for b in range(bpr)]
         for a in range(lpb):
             row = rows_ref[(panel * kb + k) * lpb + a] * CB
             for b in range(bpr):
@@ -305,15 +327,15 @@
         copy = pltpu.make_async_copy(cols_ref, scalar_ref, sem)
         copy.start()
         copy.wait()
-        fill_places(info_ref[1 + turn], table_ref, rows_ref, lambda n: scalar_ref[0, n], out_ref, kb, lpb, bpr)
+        fill_places(info_ref[1 + turn], table_ref, rows_ref, lambda k, b: scalar_ref[k, b], out_ref, kb, lpb, bpr)
 
     return pl.pallas_call(
         kernel,
         grid=(1,),
-        in_specs=[in_smem] * 3 + [pl.BlockSpec((EXTRA, 128), lambda g, at=at: (at // EXTRA, 0)) for _, at in parts],
+        in_specs=[in_smem] * 3 + [pl.BlockSpec((kb, 128), lambda g, at=at: (at // kb, 0)) for _, at in parts],
         out_specs=in_smem,
         out_shape=jax.ShapeDtypeStruct((kb * lpb * bpr,), jnp.int32),
-        scratch_shapes=[pltpu.VMEM((EXTRA, 128), jnp.int32), pltpu.SMEM((EXTRA, 128), jnp.int32), pltpu.SemaphoreType.DMA],
+        scratch_shapes=[pltpu.VMEM((kb, 128), jnp.int32), pltpu.SMEM((kb, 128), jnp.int32), pltpu.SemaphoreType.DMA],
         compiler_params=pltpu.CompilerParams(vmem_limit_bytes=1024 * 1024),
         name="panel_places",
     )(info, table, rows, *[array for array, _ in parts])
@@ -366,16 +388,24 @@
         return lax.ppermute(chunk, "row", x_pairs)
 
     rows, width = quarter_shape(right)
-    cols_row = jnp.pad(right_places.astype(f32)[None], ((0, EXTRA - 1), (0, width - right_places.shape[0])))
-
-    def sent(even_part, odd_part, *others, extra=False):
-        return pick(info, right, cols_row if extra else None, even_part, odd_part, *others)
+    cols = right_cols[0, 0, 0]
+
+    def sent(even_parts, odd_parts, *others, extra=False):
+        return pick(info, right, cols if extra else None, even_parts, odd_parts, *others)
+
+    def all_of(array):
+        return [(array, 0, PARTS)]
+
+    def own_all(quarter):
+        return [(None, quarter, 0, PARTS)]
 
     z = {}
     x = {}
-    upper = own_quarters(right, (2, 3), None)
-    x[1] = along_x(upper)
-    z[1] = along_z(own_quarters(right, (0,), cols_row, upper))
+    def own_part(quarter, first=0, parts=PARTS):
+        return (quarter, first, parts)
+
+    z[1] = along_z(own_quarters(right, [own_part(0)], cols))
+    x[1] = along_x(own_quarters(right, [own_part(3), own_part(2, 0, 1)], None))
 
     shifts = sorted({turn % cols_n for turn in range(STEPS)})
     held = {
@@ -399,27 +429,31 @@
         return (z[stage], 0, Z_CHUNKS[stage])
 
     def along_x_part(stage):
-        return (*((x[1], stage - 1) if stage < 3 else (x[stage], 0)), X_CHUNKS[stage])
+        if stage == 2:
+            return (x[1], PARTS, X_CHUNKS[stage])
+        if stage == 8:
+            return (x[7], 1, X_CHUNKS[stage])
+        return (x[stage], 0, X_CHUNKS[stage])
 
     totals, done = accumulate(info, places, [panels] * STEPS, [(right, 0, ((0, 0), (0, 0)))], None, nc)
-    second = own_quarters(right, (1,), None, done)
+    second = own_quarters(right, [own_part(1)], None, done)
     z[2] = along_z(second)
-    x[3] = along_x(sent((z[1], 0), (None, 0), done, extra=True))
-    z[3] = along_z(own_quarters(right, (2,), None, z[1], done))
+    x[3] = along_x(sent(all_of(z[1]), own_all(0), done, extra=True))
+    z[3] = along_z(own_quarters(right, [own_part(2)], None, z[1], x[1], done))
     read_places(2, (z[1], rows), (z[1], rows))
     totals, done = add(totals, [along_z_part(1), along_z_part(2)])
-    x[4] = along_x(sent((z[2], 0), (None, 1), done))
-    z[4] = along_z(sent((None, 3), (x[3], 0), done, extra=True))
+    x[4] = along_x(sent(all_of(z[2]), own_all(1), done))
+    z[4] = along_z(sent(own_all(3), all_of(x[3]), done, extra=True))
     read_places(1, (x[3], rows), (x[3], rows))
     totals, done = add(totals, [along_x_part(1), along_x_part(2), along_x_part(3)])
-    x[5] = along_x(sent((z[3], 0), (z[1], 0), done, extra=True))
-    z[5] = along_z(sent((x[1], 1), (x[4], 0), done))
+    x[5] = along_x(sent(all_of(z[3]), all_of(z[1]), done, extra=True))
+    z[5] = along_z(sent(all_of(x[1]), all_of(x[4]), done))
     totals, done = add(totals, [along_z_part(3), along_x_part(4)])
-    x[6] = along_x(sent((z[4], 0), (z[2], 0), done))
-    z[6] = along_z(x[5])
+    x[6] = along_x(sent(all_of(z[4]), all_of(z[2]), done))
+    z[6] = along_z(sent([(x[1], PARTS, 1)], all_of(x[5]), done))
     read_places(3, (x[5], rows), (z[4], rows))
     totals, done = add(totals, [along_z_part(4), along_x_part(5)])
-    x[7] = along_x(sent((z[5], 0), (z[3], 0), done))
+    x[7] = along_x(sent(all_of(z[5]), [(z[3], 1, 1), (None, 2, 1, 1)], done))
     z[7] = along_z(x[6])
     totals, done = add(totals, [along_z_part(5)])
 
@@ -428,7 +462,7 @@
 
     totals, done, kept_0, send_0 = add(totals, [along_x_part(6)], 0)
     other_0 = to_partner(send_0)
-    totals, done = add(totals, [along_z_part(6), along_x_part(7)])
+    totals, done = add(totals, [along_z_part(6), along_x_part(7), along_x_part(8)])
     totals, done, kept_1, send_1 = add(totals, [along_z_part(7)], 1)
     other_1 = to_partner(send_1)
     return combine((kept_0, kept_1), (other_0, other_1))[None, None]

time: 109 us -> 103 us (0.945)
  waiting for transfers between devices: 43.6 us -> 38.3 us
  starting transfers between devices: 22.9 us -> 20.7 us
  Pallas kernels: 35.5 us -> 36.7 us
    ppermute x7, waiting for transfers between devices: 10.7 us -> 3.46 us  [along_z(): return lax.ppermute(chunk, 'row', z_pairs)]
    ppermute x7, starting transfers between devices: 11.3 us -> 8.32 us  [along_z(): return lax.ppermute(chunk, 'row', z_pairs)]
    pallas_call x11 -> x12, Pallas kernels: 8.51 us -> 9.37 us  [the longest x8 6.81 us: pick(): pl.pallas_call(kernel, grid=(1,), in_specs=[in_smem] + [spec(part) for pa...]
  transfers between devices with their start and end apart: 17 -> 17, of which waited for: 12 -> 12; matrix products, arithmetic and copies ran while one was open for 1% -> 1% of each run, Pallas kernels for 32% -> 35%
where the time goes in v7:
time: 103 us; the launch traced here: 102 us
  waiting for transfers between devices  38.3 us (37%)
  Pallas kernels  36.7 us (36%)
  starting transfers between devices  20.7 us (20%)
  local copies, waits for them, and re-layouts  6.28 us (6%)
    ppermute x6, waiting for transfers between devices, along_x(): return lax.ppermute(chunk, 'row', x_pairs)  25.2 us
    pallas_call x9, Pallas kernels, accumulate(): pl.pallas_call(kernel, grid_spec=pltpu.PrefetchScalarGridSpec(num_scalar_...  18.9 us
    ppermute x6, starting transfers between devices, along_x(): return lax.ppermute(chunk, 'row', x_pairs)  8.78 us
    ppermute x2, waiting for transfers between devices, to_partner(): return lax.ppermute(blocks, 'rep', [(0, 1), (1, 0)])  8.46 us
    ppermute x7, starting transfers between devices, along_z(): return lax.ppermute(chunk, 'row', z_pairs)  8.32 us
    pallas_call x8, Pallas kernels, pick(): pl.pallas_call(kernel, grid=(1,), in_specs=[in_smem] + [spec(part) for pa...  6.81 us
    pallas_call x3, Pallas kernels, panel_places(): pl.pallas_call(kernel, grid=(1,), in_specs=[in_smem] * 3 + [pl.BlockSpec(...  5.91 us
    unnamed x18, local copies, waits for them, and re-layouts  5.26 us
  transfers between devices with their start and end apart: 17, of which 12 were waited for; matrix products, arithmetic and copies ran while one was open for 1% of the time, Pallas kernels for 35%

profile of v7, /device:TPU:0, one launch (start us, length us, event | category | flops | bytes accessed | tf_op | source)
XLA Modules:
  0.0 102.2 jit_solution(872212020859961120)
XLA Ops:
  0.5 0.8 copy.27.refs_1_.refs_2_
  1.2 1.6 %copy-done = f32[1,1,1,8,4,128,128]{6,5,4,3,2,1,0:T(8,128)S(1)} copy-done((f32[1,1,1,8,4,128,128]{6,5,4,3,2,1,0:T(8,128)S(1)}, f32[1,1,1,8,4,128,128]{6,5,4,3,2,1,0:T(8,128)}, u32[]{:S(2)}) %copy-start) | copy-done | bytes 2097176
  2.8 1.0 own_quarters.4
  3.8 4.6 %collective-permute-start.1 = (f32[520,256]{1,0:T(8,128)}, f32[520,256]{1,0:T(8,128)}, u32[]{:S(2)}, u32[]{:S(2)}) collective-permute-start(f32[520,256]{1,0:T(8,128)} %own_quarters.4), channel_id=1, source_target_pairs={{0,24},{4,28},{8,0},{12,4},{16,8},{20,12},{24,16},{28,20},{1,25},{... | collective-permute-start | bytes 1597448 | tf_op jit(solution)/shard_map/ppermute | solution.py:385
  8.4 1.1 %own_quarters.5 = f32[768,256]{1,0:T(8,128)} custom-call(f32[8,4,128,128]{3,2,1,0:T(8,128)S(1)} %bitcast.16, f32[8,4,128,128]{3,2,1,0:T(8,128)S(1)} %bitcast.17), custom_call_target="tpu_custom_call" | custom-call | bytes 2359296 | tf_op jit(solution)/shard_map/own_quarters/pallas_call | solution.py:96
  9.6 1.5 %collective-permute-start.3 = (f32[768,256]{1,0:T(8,128)}, f32[768,256]{1,0:T(8,128)}, u32[]{:S(2)}, u32[]{:S(2)}) collective-permute-start(f32[768,256]{1,0:T(8,128)} %own_quarters.5), channel_id=1, source_target_pairs={{0,4},{4,0},{8,12},{12,8},{16,20},{20,16},{24,28},{28,24},{1,5},{5... | collective-permute-start | bytes 2359304 | tf_op jit(solution)/shard_map/ppermute | solution.py:388
  11.5 1.4 %own_places.1 = (s32[64]{0:T(128)S(1)}, s32[64]{0:T(128)S(1)}) custom-call(s32[6]{0:T(128)S(1)} %stack.27.info_ref, s32[24]{0:T(128)S(1)} %bitcast.32, s32[48]{0:T(128)S(1)} %reshape.6.rows_ref, s32[32]{0:T(128)S(1)} %reshape.7.cols_ref), custom_call_target="tpu_custom_call" | custom-call | tf_op jit(solution)/shard_map/own_places/pallas_call | solution.py:299
  12.9 1.6 %copy-done.1 = f32[1,1,1,8,4,128,128]{6,5,4,3,2,1,0:T(8,128)S(1)} copy-done((f32[1,1,1,8,4,128,128]{6,5,4,3,2,1,0:T(8,128)S(1)}, f32[1,1,1,8,4,128,128]{6,5,4,3,2,1,0:T(8,128)}, u32[]{:S(2)}) %copy-start.1) | copy-done | bytes 2097176
  14.5 1.9 %copy-done.3 = f32[1,1,1,3,8,2,128,128]{7,6,5,4,3,2,1,0:T(8,128)S(1)} copy-done((f32[1,1,1,3,8,2,128,128]{7,6,5,4,3,2,1,0:T(8,128)S(1)}, f32[1,1,1,3,8,2,128,128]{7,6,5,4,3,2,1,0:T(8,128)}, u32[]{:S(2)}) %copy-start.3) | copy-done | bytes 3145752
  16.4 2.5 %accumulate.9 = (f32[25,128,128]{2,1,0:T(8,128)S(1)}, f32[25,128,128]{2,1,0:T(8,128)S(1)}, s32[8,128]{1,0:T(8,128)S(1)}) custom-call(s32[6]{0:T(128)S(1)} %stack.27.info_ref, s32[64]{0:T(128)S(1)} %get-tuple-element.30.refs_0_, f32[3,8,2,128,128]{4,3,2,1,0:T(8,128)S(1)} %bitcast.26, f32[8,4,128,128]{3,2,1,0:T(8,128)S(1)} %bitcast.18), custom_call_target="tpu_custom_call" | custom-call | flops 805306368 | bytes 4194304 | tf_op jit(solution)/shard_map/accumulate/pallas_call | solution.py:267
  19.6 1.6 %collective-permute-done.1.refs_0_.refs_1_.even_ref.odd_ref.refs_3_ = f32[520,256]{1,0:T(8,128)} collective-permute-done((f32[520,256]{1,0:T(8,128)}, f32[520,256]{1,0:T(8,128)}, u32[]{:S(2)}, u32[]{:S(2)}) %collective-permute-start.1) | collective-permute-done | bytes 532512 | tf_op jit(solution)/shard_map/ppermute | solution.py:385
  21.2 1.1 %pick.8 = f32[520,256]{1,0:T(8,128)S(1)} custom-call(s32[6]{0:T(128)S(1)} %stack.27.info_ref, f32[520,256]{1,0:T(8,128)} %collective-permute-done.1.refs_0_.refs_1_.even_ref.odd_ref.refs_3_, f32[8,4,128,128]{3,2,1,0:T(8,128)S(1)} %bitcast.20, s32[8,4]{1,0:T(8,128)S(1)} %copy.27.refs_1_.refs_2_, s32[8,128]{1,0:T(8,128)S(1)} %get-tuple-element.31.refs_3_.refs_1_), custom_call_target="tpu_custom_call" | custom-call | bytes 1064960 | tf_op jit(solution)/shard_map/pick/pallas_call | solution.py:146
  22.3 1.7 %collective-permute-start.2 = (f32[520,256]{1,0:T(8,128)S(1)}, f32[520,256]{1,0:T(8,128)S(1)}, u32[]{:S(2)}, u32[]{:S(2)}) collective-permute-start(f32[520,256]{1,0:T(8,128)S(1)} %pick.8), channel_id=1, source_target_pairs={{0,4},{4,0},{8,12},{12,8},{16,20},{20,16},{24,28},{28,24},{1,5},{5... | collective-permute-start | bytes 1597448 | tf_op jit(solution)/shard_map/ppermute | solution.py:388
  24.0 6.3 %collective-permute-done.3.refs_2_.refs_4_.refs_5_.refs_0_ = f32[768,256]{1,0:T(8,128)} collective-permute-done((f32[768,256]{1,0:T(8,128)}, f32[768,256]{1,0:T(8,128)}, u32[]{:S(2)}, u32[]{:S(2)}) %collective-permute-start.3) | collective-permute-done | bytes 786464 | tf_op jit(solution)/shard_map/ppermute | solution.py:388
  31.0 2.1 %panel_places.4.refs_0_.refs_1_ = s32[64]{0:T(128)S(1)} custom-call(s32[6]{0:T(128)S(1)} %stack.27.info_ref, s32[64]{0:T(128)S(1)} %get-tuple-element.29.table_ref, s32[48]{0:T(128)S(1)} %reshape.6.rows_ref, f32[520,256]{1,0:T(8,128)} %collective-permute-done.1.refs_0_.refs_1_.even_ref.odd_ref.refs_3_, ...), custom_call_target="tpu_custom_call" | custom-call | tf_op jit(solution)/shard_map/panel_places/pallas_call | solution.py:332
  33.1 0.9 collective-permute-done.6.refs_4_.refs_0_.refs_1_
  34.0 2.6 %accumulate.10 = (f32[25,128,128]{2,1,0:T(8,128)S(1)}, s32[8,128]{1,0:T(8,128)S(1)}) custom-call(s32[6]{0:T(128)S(1)} %stack.27.info_ref, s32[64]{0:T(128)S(1)} %panel_places.4.refs_0_.refs_1_, f32[3,8,2,128,128]{4,3,2,1,0:T(8,128)S(1)} %bitcast.27, f32[3,8,2,128,128]{4,3,2,1,0:T(8,128)S(1)} %bitcast.28, ...), custom_call_target="tpu_custom_call", output_to_operand_aliasing={{0}: (6, {})} | custom-call | flops 402653184 | bytes 2097152 | tf_op jit(solution)/shard_map/accumulate/pallas_call | solution.py:267
  37.2 0.9 collective-permute-start.9
  38.1 3.5 %collective-permute-done.2.even_ref.odd_ref.refs_6_.refs_1_ = f32[520,256]{1,0:T(8,128)S(1)} collective-permute-done((f32[520,256]{1,0:T(8,128)S(1)}, f32[520,256]{1,0:T(8,128)S(1)}, u32[]{:S(2)}, u32[]{:S(2)}) %collective-permute-start.2) | collective-permute-done | bytes 532512 | tf_op jit(solution)/shard_map/ppermute | solution.py:388
  41.6 0.7 pick.10
  42.5 1.1 %collective-permute-done.rows_ref = s32[48]{0:T(128)S(1)} collective-permute-done((s32[48]{0:T(128)S(1)}, s32[48]{0:T(128)S(1)}, u32[]{:S(2)}, u32[]{:S(2)}) %collective-permute-start) | collective-permute-done | bytes 224 | tf_op jit(solution)/shard_map/ppermute | solution.py:412
  43.6 1.9 %panel_places.3.refs_0_ = s32[64]{0:T(128)S(1)} custom-call(s32[6]{0:T(128)S(1)} %stack.27.info_ref, s32[64]{0:T(128)S(1)} %get-tuple-element.29.table_ref, s32[48]{0:T(128)S(1)} %collective-permute-done.rows_ref, f32[520,256]{1,0:T(8,128)S(1)} %collective-permute-done.2.even_ref.odd_ref.refs_6_.refs_1_, ...), custom_call_target="tpu_custom_call" | custom-call | tf_op jit(solution)/shard_map/panel_places/pallas_call | solution.py:332
  45.5 2.9 %accumulate.11 = (f32[25,128,128]{2,1,0:T(8,128)S(1)}, f32[25,128,128]{2,1,0:T(8,128)S(1)}, s32[8,128]{1,0:T(8,128)S(1)}) custom-call(s32[6]{0:T(128)S(1)} %stack.27.info_ref, s32[64]{0:T(128)S(1)} %panel_places.3.refs_0_, ...), custom_call_target="tpu_custom_call", output_to_operand_aliasing={{0}: (8, {}), {1}: (9, {})} | custom-call | flops 603979776 | bytes 3145728 | tf_op jit(solution)/shard_map/accumulate/pallas_call | solution.py:267
  48.4 1.1 %pick.9 = f32[520,256]{1,0:T(8,128)S(1)} custom-call(s32[6]{0:T(128)S(1)} %stack.27.info_ref, f32[512,256]{1,0:T(8,128)S(1)} %collective-permute-done.4.refs_0_.refs_4_.refs_1_, f32[520,256]{1,0:T(8,128)} %collective-permute-done.1.refs_0_.refs_1_.even_ref.odd_ref.refs_3_, s32[8,4]{1,0:T(8,128)S(1)} %copy.27.refs_1_.refs_2_, ...), custom_call_target="tpu_custom_call" | custom-call | bytes 1064960 | tf_op jit(solution)/shard_map/pick/pallas_call | solution.py:146
  49.5 0.7 collective-permute-start.7
  50.2 1.9 %collective-permute-done.9.refs_5_.refs_1_ = f32[512,256]{1,0:T(8,128)S(1)} collective-permute-done((f32[512,256]{1,0:T(8,128)S(1)}, f32[512,256]{1,0:T(8,128)S(1)}, u32[]{:S(2)}, u32[]{:S(2)}) %collective-permute-start.9) | collective-permute-done | bytes 524320 | tf_op jit(solution)/shard_map/ppermute | solution.py:388
  52.1 1.1 %pick.13 = f32[512,256]{1,0:T(8,128)S(1)} custom-call(s32[6]{0:T(128)S(1)} %stack.27.info_ref, f32[768,256]{1,0:T(8,128)} %collective-permute-done.3.refs_2_.refs_4_.refs_5_.refs_0_, f32[512,256]{1,0:T(8,128)S(1)} %collective-permute-done.9.refs_5_.refs_1_, s32[8,128]{1,0:T(8,128)S(1)} %get-tuple-element.35.refs_3_.refs_2_), custom_call_target="tpu_custom_call" | custom-call | bytes 1048576 | tf_op jit(solution)/shard_map/pick/pallas_call | solution.py:146
  53.2 1.0 collective-permute-start.11
  54.2 1.4 %accumulate.12 = (f32[25,128,128]{2,1,0:T(8,128)S(1)}, f32[25,128,128]{2,1,0:T(8,128)S(1)}, s32[8,128]{1,0:T(8,128)S(1)}) custom-call(s32[6]{0:T(128)S(1)} %stack.27.info_ref, s32[64]{0:T(128)S(1)} %panel_places.3.refs_0_, s32[64]{0:T(128)S(1)} %panel_places.4.refs_0_.refs_1_, ...), custom_call_target="tpu_custom_call", output_to_operand_aliasing={{0}: (7, {}), {1}: (8, {})} | custom-call | flops 402653184 | bytes 2097152 | tf_op jit(solution)/shard_map/accumulate/pallas_call | solution.py:267
  56.4 2.3 %collective-permute-start.10 = (f32[512,256]{1,0:T(8,128)S(1)}, f32[512,256]{1,0:T(8,128)S(1)}, u32[]{:S(2)}, u32[]{:S(2)}) collective-permute-start(f32[512,256]{1,0:T(8,128)S(1)} %pick.12), channel_id=1, source_target_pairs={{0,4},{4,0},{8,12},{12,8},{16,20},{20,16},{24,28},{28,24},{1,5},{5... | collective-permute-start | bytes 1572872 | tf_op jit(solution)/shard_map/ppermute | solution.py:388
  58.7 5.8 %collective-permute-done.7.even_ref.refs_8_.refs_1_ = f32[520,256]{1,0:T(8,128)S(1)} collective-permute-done((f32[520,256]{1,0:T(8,128)S(1)}, f32[520,256]{1,0:T(8,128)S(1)}, u32[]{:S(2)}, u32[]{:S(2)}) %collective-permute-start.7) | collective-permute-done | bytes 532512 | tf_op jit(solution)/shard_map/ppermute | solution.py:388
  64.5 1.0 pick.14
  65.5 0.9 collective-permute-start.13
  66.4 1.9 %panel_places.5.refs_2_.refs_0_.refs_1_ = s32[64]{0:T(128)S(1)} custom-call(s32[6]{0:T(128)S(1)} %stack.27.info_ref, s32[64]{0:T(128)S(1)} %get-tuple-element.29.table_ref, s32[48]{0:T(128)S(1)} %collective-permute-done.rows_ref, f32[520,256]{1,0:T(8,128)S(1)} %collective-permute-done.7.even_ref.refs_8_.refs_1_, ...), custom_call_target="tpu_custom_call" | custom-call | tf_op jit(solution)/shard_map/panel_places/pallas_call | solution.py:332
  68.3 1.7 %accumulate.13 = (f32[25,128,128]{2,1,0:T(8,128)S(1)}, f32[25,128,128]{2,1,0:T(8,128)S(1)}, s32[8,128]{1,0:T(8,128)S(1)}) custom-call(s32[6]{0:T(128)S(1)} %stack.27.info_ref, s32[64]{0:T(128)S(1)} %panel_places.3.refs_0_, s32[64]{0:T(128)S(1)} %panel_places.4.refs_0_.refs_1_, ...), custom_call_target="tpu_custom_call", output_to_operand_aliasing={{0}: (10, {}), {1}: (11, {})} | custom-call | flops 402653184 | bytes 2097152 | tf_op jit(solution)/shard_map/accumulate/pallas_call | solution.py:267
  70.6 1.7 %collective-permute-start.14 = (f32[512,256]{1,0:T(8,128)S(1)}, f32[512,256]{1,0:T(8,128)S(1)}, u32[]{:S(2)}, u32[]{:S(2)}) collective-permute-start(f32[512,256]{1,0:T(8,128)S(1)} %pick.15), channel_id=1, source_target_pairs={{0,4},{4,0},{8,12},{12,8},{16,20},{20,16},{24,28},{28,24},{1,5},{5... | collective-permute-start | bytes 1572872 | tf_op jit(solution)/shard_map/ppermute | solution.py:388
  72.2 3.5 %collective-permute-done.10.refs_4_ = f32[512,256]{1,0:T(8,128)S(1)} collective-permute-done((f32[512,256]{1,0:T(8,128)S(1)}, f32[512,256]{1,0:T(8,128)S(1)}, u32[]{:S(2)}, u32[]{:S(2)}) %collective-permute-start.10) | collective-permute-done | bytes 524320 | tf_op jit(solution)/shard_map/ppermute | solution.py:388
  75.8 0.8 collective-permute-start.12
  76.6 1.7 %accumulate.14 = (f32[25,128,128]{2,1,0:T(8,128)S(1)}, f32[25,128,128]{2,1,0:T(8,128)S(1)}, s32[8,128]{1,0:T(8,128)}) custom-call(s32[6]{0:T(128)S(1)} %stack.27.info_ref, s32[64]{0:T(128)S(1)} %panel_places.5.refs_2_.refs_0_.refs_1_, ...), custom_call_target="tpu_custom_call", output_to_operand_aliasing={{0}: (5, {}), {1}: (6, {})} | custom-call | flops 201326592 | bytes 1048576 | tf_op jit(solution)/shard_map/accumulate/pallas_call | solution.py:267
  78.2 2.3 %accumulate.15 = (f32[25,128,128]{2,1,0:T(8,128)S(1)}, f32[25,128,128]{2,1,0:T(8,128)S(1)}, s32[8,128]{1,0:T(8,128)}, f32[6,128,128]{2,1,0:T(8,128)S(1)}, f32[6,128,128]{2,1,0:T(8,128)S(1)}) custom-call(s32[6]{0:T(128)S(1)} %stack.27.info_ref, s32[64]{0:T(128)S(1)} %panel_places.3.refs_0_, ...), custom_call_target="tpu_custom_call", output_to_operand_aliasing={{0}: (6, {}), {1}: (7, {})} | custom-call | flops 201326592 | bytes 1048576 | tf_op jit(solution)/shard_map/accumulate/pallas_call | solution.py:267
  80.5 1.5 %collective-permute-start.15 = (f32[6,128,128]{2,1,0:T(8,128)S(1)}, f32[6,128,128]{2,1,0:T(8,128)S(1)}, u32[]{:S(2)}, u32[]{:S(2)}) collective-permute-start(f32[6,128,128]{2,1,0:T(8,128)S(1)} %get-tuple-element.51), channel_id=1, source_target_pairs={{0,1},{1,0},{2,3},{3,2},{4,5},{5,4},{6,7},{7,6},{8,9},{9,8},{10,11... | collective-permute-start | bytes 1179656 | tf_op jit(solution)/shard_map/ppermute | solution.py:461
  82.0 4.2 %collective-permute-done.14.refs_9_.refs_10_ = f32[512,256]{1,0:T(8,128)S(1)} collective-permute-done((f32[512,256]{1,0:T(8,128)S(1)}, f32[512,256]{1,0:T(8,128)S(1)}, u32[]{:S(2)}, u32[]{:S(2)}) %collective-permute-start.14) | collective-permute-done | bytes 524320 | tf_op jit(solution)/shard_map/ppermute | solution.py:388
  86.3 2.3 %accumulate.16 = (f32[25,128,128]{2,1,0:T(8,128)S(1)}, s32[8,128]{1,0:T(8,128)}) custom-call(s32[6]{0:T(128)S(1)} %stack.27.info_ref, s32[64]{0:T(128)S(1)} %panel_places.3.refs_0_, s32[64]{0:T(128)S(1)} %panel_places.4.refs_0_.refs_1_, s32[64]{0:T(128)S(1)} %panel_places.5.refs_2_.refs_0_.refs_1_, ...), custom_call_target="tpu_custom_call", output_to_operand_aliasing={{0}: (12, {})} | custom-call | flops 603979776 | bytes 3145728 | tf_op jit(solution)/shard_map/accumulate/pallas_call | solution.py:267
  88.6 0.9 collective-permute-done.12.refs_2_
  89.5 1.5 %accumulate.17 = (f32[25,128,128]{2,1,0:T(8,128)S(1)}, s32[8,128]{1,0:T(8,128)}, f32[6,128,128]{2,1,0:T(8,128)S(1)}, f32[6,128,128]{2,1,0:T(8,128)S(1)}) custom-call(s32[6]{0:T(128)S(1)} %stack.27.info_ref, s32[64]{0:T(128)S(1)} %panel_places.5.refs_2_.refs_0_.refs_1_, ...), custom_call_target="tpu_custom_call", output_to_operand_aliasing={{0}: (4, {})} | custom-call | flops 201326592 | bytes 1048576 | tf_op jit(solution)/shard_map/accumulate/pallas_call | solution.py:267
  91.0 1.5 %collective-permute-start.16 = (f32[6,128,128]{2,1,0:T(8,128)S(1)}, f32[6,128,128]{2,1,0:T(8,128)S(1)}, u32[]{:S(2)}, u32[]{:S(2)}) collective-permute-start(f32[6,128,128]{2,1,0:T(8,128)S(1)} %get-tuple-element.52), channel_id=1, source_target_pairs={{0,1},{1,0},{2,3},{3,2},{4,5},{5,4},{6,7},{7,6},{8,9},{9,8},{10,11... | collective-permute-start | bytes 1179656 | tf_op jit(solution)/shard_map/ppermute | solution.py:461
  92.6 8.5 %collective-permute-done.16.other_1 = f32[6,128,128]{2,1,0:T(8,128)S(1)} collective-permute-done((f32[6,128,128]{2,1,0:T(8,128)S(1)}, f32[6,128,128]{2,1,0:T(8,128)S(1)}, u32[]{:S(2)}, u32[]{:S(2)}) %collective-permute-start.16) | collective-permute-done | bytes 393248 | tf_op jit(solution)/shard_map/ppermute | solution.py:461
  101.0 1.1 %combine.1 = f32[2,6,128,128]{3,2,1,0:T(8,128)} custom-call(f32[6,128,128]{2,1,0:T(8,128)S(1)} %get-tuple-element.46.kept_0, f32[6,128,128]{2,1,0:T(8,128)S(1)} %get-tuple-element.50.kept_1, f32[6,128,128]{2,1,0:T(8,128)S(1)} %collective-permute-done.15.other_0, f32[6,128,128]{2,1,0:T(8,128)S(1)} %collective-permute-done.16.other_1), custom_call_target="tpu_custom_call" | custom-call | tf_op jit(solution)/shard_map/combine/pallas_call | solution.py:357
  (34 shorter events, 4.4 us)
Async XLA Ops:
  0.0 45.5 %collective-permute-start.5 = (f32[3,8,2,128,128]{4,3,2,1,0:T(8,128)}, f32[3,8,2,128,128]{4,3,2,1,0:T(8,128)S(1)}, u32[]{:S(2)}, u32[]{:S(2)}) collective-permute-start(f32[3,8,2,128,128]{4,3,2,1,0:T(8,128)} %bitcast.25), channel_id=1, source_target_pairs={{0,2},{2,0},{1,3},{3,1},{4,6},{6,4},{5,7},{7,5},{8,10},{10,8},{9,1... | collective-permute-start | bytes 9437192 | tf_op jit(solution)/shard_map/ppermute | solution.py:412
  1.2 1.6 %copy-start = (f32[1,1,1,8,4,128,128]{6,5,4,3,2,1,0:T(8,128)S(1)}, f32[1,1,1,8,4,128,128]{6,5,4,3,2,1,0:T(8,128)}, u32[]{:S(2)}) copy-start(f32[1,1,1,8,4,128,128]{6,5,4,3,2,1,0:T(8,128)} %param.7) | copy-start | bytes 6291460
  3.8 7.2 %copy-start.6 = (s32[1,1,1,8,4]{3,4,2,1,0:T(4,128)S(1)}, s32[1,1,1,8,4]{3,4,2,1,0:T(4,128)}, u32[]{:S(2)}) copy-start(s32[1,1,1,8,4]{3,4,2,1,0:T(4,128)} %param.8) | copy-start | bytes 388
  3.8 7.4 %copy-start.7 = (s32[1,1,1,3,8,2]{4,5,3,2,1,0:T(2,128)S(1)}, s32[1,1,1,3,8,2]{4,5,3,2,1,0:T(2,128)}, u32[]{:S(2)}) copy-start(s32[1,1,1,3,8,2]{4,5,3,2,1,0:T(2,128)} %param.6) | copy-start | bytes 580
  3.8 7.7 %copy-start.5 = (s32[1,1,24]{2,1,0:T(1,128)S(1)}, s32[1,1,24]{2,1,0:T(1,128)}, u32[]{:S(2)}) copy-start(s32[1,1,24]{2,1,0:T(1,128)} %param.9) | copy-start | bytes 292
  3.8 17.3 %collective-permute-start.1 = (f32[520,256]{1,0:T(8,128)}, f32[520,256]{1,0:T(8,128)}, u32[]{:S(2)}, u32[]{:S(2)}) collective-permute-start(f32[520,256]{1,0:T(8,128)} %own_quarters.4), channel_id=1, source_target_pairs={{0,24},{4,28},{8,0},{12,4},{16,8},{20,12},{24,16},{28,20},{1,25},{... | collective-permute-start | bytes 1597448 | tf_op jit(solution)/shard_map/ppermute | solution.py:385
  9.6 20.7 %collective-permute-start.3 = (f32[768,256]{1,0:T(8,128)}, f32[768,256]{1,0:T(8,128)}, u32[]{:S(2)}, u32[]{:S(2)}) collective-permute-start(f32[768,256]{1,0:T(8,128)} %own_quarters.5), channel_id=1, source_target_pairs={{0,4},{4,0},{8,12},{12,8},{16,20},{20,16},{24,28},{28,24},{1,5},{5... | collective-permute-start | bytes 2359304 | tf_op jit(solution)/shard_map/ppermute | solution.py:388
  12.9 1.6 %copy-start.1 = (f32[1,1,1,8,4,128,128]{6,5,4,3,2,1,0:T(8,128)S(1)}, f32[1,1,1,8,4,128,128]{6,5,4,3,2,1,0:T(8,128)}, u32[]{:S(2)}) copy-start(f32[1,1,1,8,4,128,128]{6,5,4,3,2,1,0:T(8,128)} %param.7) | copy-start | bytes 6291460
  14.5 1.9 %copy-start.3 = (f32[1,1,1,3,8,2,128,128]{7,6,5,4,3,2,1,0:T(8,128)S(1)}, f32[1,1,1,3,8,2,128,128]{7,6,5,4,3,2,1,0:T(8,128)}, u32[]{:S(2)}) copy-start(f32[1,1,1,3,8,2,128,128]{7,6,5,4,3,2,1,0:T(8,128)} %param.5) | copy-start | bytes 9437188
  19.1 14.8 %collective-permute-start.6 = (f32[512,256]{1,0:T(8,128)S(1)}, f32[512,256]{1,0:T(8,128)S(1)}, u32[]{:S(2)}, u32[]{:S(2)}) collective-permute-start(f32[512,256]{1,0:T(8,128)S(1)} %own_quarters.7), channel_id=1, source_target_pairs={{0,24},{4,28},{8,0},{12,4},{16,8},{20,12},{24,16},{28,20},{1,25},{... | collective-permute-start | bytes 1572872 | tf_op jit(solution)/shard_map/ppermute | solution.py:385
  22.3 11.7 %copy-start.4 = (f32[1,1,1,3,8,2,128,128]{7,6,5,4,3,2,1,0:T(8,128)S(1)}, f32[1,1,1,3,8,2,128,128]{7,6,5,4,3,2,1,0:T(8,128)}, u32[]{:S(2)}) copy-start(f32[1,1,1,3,8,2,128,128]{7,6,5,4,3,2,1,0:T(8,128)} %param.5) | copy-start | bytes 9437188
  22.3 19.3 %collective-permute-start.2 = (f32[520,256]{1,0:T(8,128)S(1)}, f32[520,256]{1,0:T(8,128)S(1)}, u32[]{:S(2)}, u32[]{:S(2)}) collective-permute-start(f32[520,256]{1,0:T(8,128)S(1)} %pick.8), channel_id=1, source_target_pairs={{0,4},{4,0},{8,12},{12,8},{16,20},{20,16},{24,28},{28,24},{1,5},{5... | collective-permute-start | bytes 1597448 | tf_op jit(solution)/shard_map/ppermute | solution.py:388
  30.5 17.9 %collective-permute-start.4 = (f32[512,256]{1,0:T(8,128)S(1)}, f32[512,256]{1,0:T(8,128)S(1)}, u32[]{:S(2)}, u32[]{:S(2)}) collective-permute-start(f32[512,256]{1,0:T(8,128)S(1)} %own_quarters.6), channel_id=1, source_target_pairs={{0,24},{4,28},{8,0},{12,4},{16,8},{20,12},{24,16},{28,20},{1,25},{... | collective-permute-start | bytes 1572872 | tf_op jit(solution)/shard_map/ppermute | solution.py:385
  34.0 2.6 %copy-start.2 = (f32[1,1,1,8,4,128,128]{6,5,4,3,2,1,0:T(8,128)S(1)}, f32[1,1,1,8,4,128,128]{6,5,4,3,2,1,0:T(8,128)}, u32[]{:S(2)}) copy-start(f32[1,1,1,8,4,128,128]{6,5,4,3,2,1,0:T(8,128)} %param.7) | copy-start | bytes 6291460
  37.2 14.9 %collective-permute-start.9 = (f32[512,256]{1,0:T(8,128)S(1)}, f32[512,256]{1,0:T(8,128)S(1)}, u32[]{:S(2)}, u32[]{:S(2)}) collective-permute-start(f32[512,256]{1,0:T(8,128)S(1)} %pick.11), channel_id=1, source_target_pairs={{0,4},{4,0},{8,12},{12,8},{16,20},{20,16},{24,28},{28,24},{1,5},{5... | collective-permute-start | bytes 1572872 | tf_op jit(solution)/shard_map/ppermute | solution.py:388
  42.3 13.5 %collective-permute-start.8 = (f32[520,256]{1,0:T(8,128)S(1)}, f32[520,256]{1,0:T(8,128)S(1)}, u32[]{:S(2)}, u32[]{:S(2)}) collective-permute-start(f32[520,256]{1,0:T(8,128)S(1)} %pick.10), channel_id=1, source_target_pairs={{0,24},{4,28},{8,0},{12,4},{16,8},{20,12},{24,16},{28,20},{1,25},{... | collective-permute-start | bytes 1597448 | tf_op jit(solution)/shard_map/ppermute | solution.py:385
  42.4 1.2 %collective-permute-start = (s32[48]{0:T(128)S(1)}, s32[48]{0:T(128)S(1)}, u32[]{:S(2)}, u32[]{:S(2)}) collective-permute-start(s32[48]{0:T(128)S(1)} %reshape.6.rows_ref), channel_id=1, source_target_pairs={{0,2},{2,0},{1,3},{3,1},{4,6},{6,4},{5,7},{7,5},{8,10},{10,8},{9,1... | collective-permute-start | bytes 584 | tf_op jit(solution)/shard_map/ppermute | solution.py:412
  49.5 15.0 %collective-permute-start.7 = (f32[520,256]{1,0:T(8,128)S(1)}, f32[520,256]{1,0:T(8,128)S(1)}, u32[]{:S(2)}, u32[]{:S(2)}) collective-permute-start(f32[520,256]{1,0:T(8,128)S(1)} %pick.9), channel_id=1, source_target_pairs={{0,4},{4,0},{8,12},{12,8},{16,20},{20,16},{24,28},{28,24},{1,5},{5... | collective-permute-start | bytes 1597448 | tf_op jit(solution)/shard_map/ppermute | solution.py:388
  53.2 16.8 %collective-permute-start.11 = (f32[512,256]{1,0:T(8,128)S(1)}, f32[512,256]{1,0:T(8,128)S(1)}, u32[]{:S(2)}, u32[]{:S(2)}) collective-permute-start(f32[512,256]{1,0:T(8,128)S(1)} %pick.13), channel_id=1, source_target_pairs={{0,24},{4,28},{8,0},{12,4},{16,8},{20,12},{24,16},{28,20},{1,25},{... | collective-permute-start | bytes 1572872 | tf_op jit(solution)/shard_map/ppermute | solution.py:385
  56.4 19.4 %collective-permute-start.10 = (f32[512,256]{1,0:T(8,128)S(1)}, f32[512,256]{1,0:T(8,128)S(1)}, u32[]{:S(2)}, u32[]{:S(2)}) collective-permute-start(f32[512,256]{1,0:T(8,128)S(1)} %pick.12), channel_id=1, source_target_pairs={{0,4},{4,0},{8,12},{12,8},{16,20},{20,16},{24,28},{28,24},{1,5},{5... | collective-permute-start | bytes 1572872 | tf_op jit(solution)/shard_map/ppermute | solution.py:388
  65.5 16.5 %collective-permute-start.13 = (f32[512,256]{1,0:T(8,128)S(1)}, f32[512,256]{1,0:T(8,128)S(1)}, u32[]{:S(2)}, u32[]{:S(2)}) collective-permute-start(f32[512,256]{1,0:T(8,128)S(1)} %pick.14), channel_id=1, source_target_pairs={{0,24},{4,28},{8,0},{12,4},{16,8},{20,12},{24,16},{28,20},{1,25},{... | collective-permute-start | bytes 1572872 | tf_op jit(solution)/shard_map/ppermute | solution.py:385
  70.6 15.7 %collective-permute-start.14 = (f32[512,256]{1,0:T(8,128)S(1)}, f32[512,256]{1,0:T(8,128)S(1)}, u32[]{:S(2)}, u32[]{:S(2)}) collective-permute-start(f32[512,256]{1,0:T(8,128)S(1)} %pick.15), channel_id=1, source_target_pairs={{0,4},{4,0},{8,12},{12,8},{16,20},{20,16},{24,28},{28,24},{1,5},{5... | collective-permute-start | bytes 1572872 | tf_op jit(solution)/shard_map/ppermute | solution.py:388
  75.8 13.7 %collective-permute-start.12 = (f32[512,256]{1,0:T(8,128)S(1)}, f32[512,256]{1,0:T(8,128)S(1)}, u32[]{:S(2)}, u32[]{:S(2)}) collective-permute-start(f32[512,256]{1,0:T(8,128)S(1)} %collective-permute-done.10.refs_4_), channel_id=1, source_target_pairs={{0,24},{4,28},{8,0},{12,4},{16,8},{20,12},{24,16},{28,20},{1,25},{... | collective-permute-start | bytes 1572872 | tf_op jit(solution)/shard_map/ppermute | solution.py:385
  80.5 12.1 %collective-permute-start.15 = (f32[6,128,128]{2,1,0:T(8,128)S(1)}, f32[6,128,128]{2,1,0:T(8,128)S(1)}, u32[]{:S(2)}, u32[]{:S(2)}) collective-permute-start(f32[6,128,128]{2,1,0:T(8,128)S(1)} %get-tuple-element.51), channel_id=1, source_target_pairs={{0,1},{1,0},{2,3},{3,2},{4,5},{5,4},{6,7},{7,6},{8,9},{9,8},{10,11... | collective-permute-start | bytes 1179656 | tf_op jit(solution)/shard_map/ppermute | solution.py:461
  91.0 10.0 %collective-permute-start.16 = (f32[6,128,128]{2,1,0:T(8,128)S(1)}, f32[6,128,128]{2,1,0:T(8,128)S(1)}, u32[]{:S(2)}, u32[]{:S(2)}) collective-permute-start(f32[6,128,128]{2,1,0:T(8,128)S(1)} %get-tuple-element.52), channel_id=1, source_target_pairs={{0,1},{1,0},{2,3},{3,2},{4,5},{5,4},{6,7},{7,6},{8,9},{9,8},{10,11... | collective-permute-start | bytes 1179656 | tf_op jit(solution)/shard_map/ppermute | solution.py:461

commit v8 on v7

--- a/solution.py
+++ b/solution.py
@@ -51,23 +51,52 @@
     return pltpu.roll(x, x.shape[-1] // 2, x.ndim - 1)
 
 
-def cut(right_ref, out_ref, half, at=0):
-    count, bpr, bs, _ = right_ref.shape
+def move_lanes(x, groups):
+    if groups % 4 == 0:
+        return x
+    return pltpu.roll(x, x.shape[-1] // 4 * (groups % 4), x.ndim - 1)
+
+
+def by_group(parts):
+    shape = parts[0].shape
+    group = lax.broadcasted_iota(jnp.int32, shape, len(shape) - 1) // (shape[-1] // 4)
+    out = parts[3]
+    for g in (2, 1, 0):
+        out = jnp.where(group == g, parts[g], out)
+    return out
+
+
+def sum_of(quarter):
+    return max(quarter - 1, 0)
+
+
+def block_rows(kb, quarter, first, parts):
+    if quarter < 2:
+        per = kb // (2 * PARTS)
+        return (quarter * PARTS + first) * per, parts * per
+    per = kb // PARTS
+    return first * per, parts * per
+
+
+def cut(right_ref, out_ref, quarter, at=0, start=0, count=None):
+    count = right_ref.shape[0] if count is None else count
+    _, bpr, bs, _ = right_ref.shape
     lower = lower_lanes((bs, bs))
-    for k in range(count):
-        for pair in range(bpr // 2):
-            even, odd = right_ref[k, 2 * pair], right_ref[k, 2 * pair + 1]
-            if half == 0:
-                both = jnp.where(lower, even, swap_lanes(odd))
-            else:
-                both = jnp.where(lower, swap_lanes(even), odd)
-            out_ref[at + k * bs:at + (k + 1) * bs, pair * bs:(pair + 1) * bs] = both
+    for n in range(count):
+        blocks = [right_ref[start + n, b] for b in range(bpr)]
+        if quarter < 2:
+            for pair in range(bpr // 2):
+                both = jnp.where(lower, blocks[2 * pair], swap_lanes(blocks[2 * pair + 1]))
+                out_ref[at + n * bs:at + (n + 1) * bs, pair * bs:(pair + 1) * bs] = both
+        else:
+            row = at + n // 2 * bs
+            four = by_group([move_lanes(block, b - quarter) for b, block in enumerate(blocks)])
+            out_ref[row:row + bs, n % 2 * bs:(n % 2 + 1) * bs] = four
 
 
 def own_spec(right, quarter, first=0, parts=PARTS):
-    count = right.shape[0] // (HALVES * PARTS) * parts
-    at = (quarter % HALVES * PARTS + first) // parts
-    return pl.BlockSpec((count,) + right.shape[1:], lambda *_: (at, 0, 0, 0))
+    start, count = block_rows(right.shape[0], quarter, first, parts)
+    return pl.BlockSpec((count,) + right.shape[1:], lambda *_: (start // count, 0, 0, 0))
 
 
 def quarter_shape(right):
@@ -83,26 +112,28 @@
 def own_quarters(right, quarters, cols, *others):
     rows, width = quarter_shape(right)
     extra = [] if cols is None else [cols]
+    several = len(quarters) > 1
     starts = [sum(parts for _, _, parts in quarters[:n]) * rows // PARTS for n in range(len(quarters) + 1)]
 
     def kernel(*refs):
         out_ref = refs[-1]
-        for n, (quarter, _, _) in enumerate(quarters):
-            cut(refs[n], out_ref, quarter // HALVES, starts[n])
+        for n, part in enumerate(quarters):
+            start, count = block_rows(right.shape[0], *part)
+            cut(refs[0], out_ref, part[0], starts[n], start if several else 0, count)
         if extra:
-            put_extra(out_ref, refs[len(quarters)], starts[-1])
+            put_extra(out_ref, refs[1], starts[-1])
 
     out_shape = jax.ShapeDtypeStruct((starts[-1] + right.shape[0] * len(extra), width), right.dtype)
     return pl.pallas_call(
         kernel,
         grid=(1,),
-        in_specs=[own_spec(right, *part) for part in quarters] + [whole(x.shape) for x in extra] + [anywhere] * len(others),
+        in_specs=[whole(right.shape) if several else own_spec(right, *quarters[0])] + [whole(x.shape) for x in extra] + [anywhere] * len(others),
         out_specs=whole(out_shape.shape),
         out_shape=out_shape,
         compiler_params=pltpu.CompilerParams(vmem_limit_bytes=12 * 1024 * 1024),
         cost_estimate=pl.CostEstimate(flops=0, bytes_accessed=12 * out_shape.size, transcendentals=0),
         name="own_quarters",
-    )(*[right] * len(quarters), *extra, *others)
+    )(right, *extra, *others)
 
 
 def pick(info, right, cols, even_parts, odd_parts, *others):
@@ -124,7 +155,7 @@
             at = 0
             for part, ref in zip(sides[side], refs_of):
                 if part[0] is None:
-                    cut(ref, out_ref, part[1] // HALVES, at)
+                    cut(ref, out_ref, part[1], at)
                 else:
                     out_ref[at:at + size(part)] = ref[...]
                 at += size(part)
@@ -155,20 +186,18 @@
     )(info, *[right if part[0] is None else part[0] for part in parts], *extra, *others)
 
 
-def accumulate(info, places, lefts, chunks, totals, nc, finish=None):
+def accumulate(info, places, lefts, chunks, totals, nc, finish=None, cost=1):
     _, kb, lpb, bs, _ = lefts[0].shape
-    part = kb // (HALVES * PARTS)
     own = totals is None
     bpr = chunks[0][0].shape[1] if own else HALVES * chunks[0][0].shape[1] // bs
     width = bpr * bs // HALVES
-    lanes = bs // HALVES
     products = lpb * bpr
     turns = sorted({what[0] for _, _, both in chunks for what in both if what is not None})
-    packed = nc // 4
     if own:
-        touched = list(range(HALVES))
+        touched = list(range(3))
     else:
-        touched = sorted({what[1] // HALVES for _, _, both in chunks for what in both if what is not None})
+        touched = {sum_of(what[1]) for _, _, both in chunks for what in both if what is not None}
+        touched = sorted(touched | set(finish or ()))
     sides = [(c, side) for c in range(len(chunks)) for side in range(2) if chunks[c][2][side] is not None]
     sides = [(c, side) for c, side in sides if side == 0 or chunks[c][2][0] != chunks[c][2][1]]
 
@@ -199,27 +228,43 @@
             )
 
         def add_own(left_ref, right_ref):
+            parts = (slice(0, bs // 2), slice(bs // 2, 3 * bs // 4), slice(3 * bs // 4, bs))
             for k in range(kb):
                 out = products_of(left_ref[0, k], jnp.concatenate([right_ref[k, b] for b in range(bpr)], axis=1))
                 for a in range(lpb):
                     for b in range(bpr):
                         n = place_refs[0][k * products + a * bpr + b]
-                        for half in range(HALVES):
-                            at = slice(half * lanes, (half + 1) * lanes)
-                            total_refs[half][n, :, at] += out[a * bs:(a + 1) * bs, b * bs:(b + 1) * bs][:, at]
+                        block = out[a * bs:(a + 1) * bs, b * bs:(b + 1) * bs]
+                        for ref, lanes in zip(total_refs.values(), parts):
+                            ref[n, :, lanes] += block[:, lanes]
 
         def add(c, side):
-            turn, quarter, first, parts = chunks[c][2][side]
-            half, k_half = divmod(quarter, HALVES)
-            base = (k_half * PARTS + first) * part * products
-            left_ref, right_ref, total_ref = left_refs[c, side], right_refs[c], total_refs[half]
-            for k in range(parts * part):
-                out = products_of(left_ref[0, k], right_ref[k * bs:(k + 1) * bs])
+            turn, quarter = chunks[c][2][side][:2]
+            start, count = block_rows(kb, *chunks[c][2][side][1:])
+            left_ref, right_ref, total_ref = left_refs[c, side], right_refs[c], total_refs[sum_of(quarter)]
+            lanes = bs // 2 if quarter < 2 else bs // 4
+            for k in range(count):
+                if quarter < 2:
+                    right = right_ref[k * bs:(k + 1) * bs]
+                else:
+                    right = right_ref[k // 2 * bs:(k // 2 + 1) * bs, k % 2 * bs:(k % 2 + 1) * bs]
+                out = products_of(left_ref[0, k], right)
                 for a in range(lpb):
                     for b in range(bpr):
-                        n = place_refs[turn][base + k * products + a * bpr + b]
-                        at = (b % HALVES) * lanes
+                        n = place_refs[turn][(start + k) * products + a * bpr + b]
+                        at = b * lanes % bs
                         total_ref[n, :, at:at + lanes] += out[a * bs:(a + 1) * bs, b * lanes:(b + 1) * lanes]
+
+        def pack(total_ref, both_refs, quarters):
+            for kept, ref in enumerate(both_refs):
+                packed = ref.shape[0]
+                for p in range(packed):
+                    blocks = [total_ref[nc // 2 * kept + g * packed + p] for g in range(4 if quarters else 2)]
+                    blocks = [block + swap_lanes(block) for block in blocks]
+                    if quarters:
+                        ref[p] = by_group([block + move_lanes(block, 1) for block in blocks])
+                    else:
+                        ref[p] = jnp.where(lower_lanes((bs, bs)), *blocks)
 
         if own:
             add_own(left_refs[0, 0], right_refs[0])
@@ -232,34 +277,33 @@
                 pl.when(odd == 0)(lambda c=c: add(c, 0))
             if both[1] is not None:
                 pl.when(odd != 0)(lambda c=c: add(c, 1))
-        if finish is not None:
-            lower = lower_lanes((bs, bs))
-            for kept, ref in enumerate(outs[1:]):
-                for p in range(packed):
-                    n = 2 * packed * kept + p
-                    one, two = total_refs[finish][n], total_refs[finish][n + packed]
-                    ref[p] = jnp.where(lower, one + swap_lanes(one), two + swap_lanes(two))
-
-    def left_spec(turn, quarter, first, parts):
-        at = (quarter % HALVES * PARTS + first) // parts
-        return pl.BlockSpec((1, parts * part, lpb, bs, bs), lambda g, info_ref, *_: (info_ref[1 + turn], at, 0, 0, 0))
-
-    def right_spec(at, both):
+        if finish is not None and finish[0] == finish[1]:
+            pack(total_refs[finish[0]], outs[1:], finish[0] > 0)
+        elif finish is not None:
+            pl.when(odd == 0)(lambda: pack(total_refs[finish[0]], outs[1:], True))
+            pl.when(odd != 0)(lambda: pack(total_refs[finish[1]], outs[1:], True))
+
+    def left_spec(turn, *what):
+        start, count = block_rows(kb, *what)
+        return pl.BlockSpec((1, count, lpb, bs, bs), lambda g, info_ref, *_: (info_ref[1 + turn], start // count, 0, 0, 0))
+
+    def right_spec(array, at, both):
         parts = max(what[3] for what in both if what is not None)
-        return pl.BlockSpec((parts * part * bs, width), lambda *_: (at, 0))
+        rows = kb // HALVES * bs // PARTS * parts
+        return pl.BlockSpec((rows, width), lambda *_: (at, 0))
 
     operands = [lefts[chunks[c][2][side][0]] for c, side in sides] + [c[0] for c in chunks]
     if own:
         in_specs = [pl.BlockSpec((1, kb, lpb, bs, bs), lambda g, info_ref, *_: (info_ref[1], 0, 0, 0, 0)), whole(chunks[0][0].shape)]
     else:
-        in_specs = [left_spec(*chunks[c][2][side]) for c, side in sides] + [right_spec(at, both) for _, at, both in chunks]
+        in_specs = [left_spec(*chunks[c][2][side]) for c, side in sides] + [right_spec(*chunk) for chunk in chunks]
     held = len(operands) + 1 + len(turns)
     if not own:
-        operands += [totals[half] for half in touched]
+        operands += [totals[n] for n in touched]
         in_specs += [in_vmem] * len(touched)
     outs = [jax.ShapeDtypeStruct((nc + 1, bs, bs), f32)] * len(touched) + [jax.ShapeDtypeStruct((8, 128), jnp.int32)]
     if finish is not None:
-        outs += [jax.ShapeDtypeStruct((packed, bs, bs), f32)] * 2
+        outs += [jax.ShapeDtypeStruct((nc // (8 if finish[0] else 4), bs, bs), f32)] * 2
     parts = QUARTERS if own else len(chunks)
     per = kb // HALVES
     flops = parts * per * 2 * lpb * bs * 3 * bs * width
@@ -274,13 +318,13 @@
         ),
         out_shape=outs,
         input_output_aliases={} if own else {held + n: n for n in range(len(touched))},
-        compiler_params=pltpu.CompilerParams(vmem_limit_bytes=16 * 1024 * 1024),
-        cost_estimate=pl.CostEstimate(flops=flops, bytes_accessed=moved, transcendentals=0),
+        compiler_params=pltpu.CompilerParams(vmem_limit_bytes=20 * 1024 * 1024),
+        cost_estimate=pl.CostEstimate(flops=cost * flops, bytes_accessed=cost * moved, transcendentals=0),
         name="accumulate",
     )(info, *[places[turn] for turn in turns], *operands)
-    totals = [None] * HALVES if own else list(totals)
-    for half, total in zip(touched, results):
-        totals[half] = total
+    totals = [None] * 3 if own else list(totals)
+    for n, total in zip(touched, results):
+        totals[n] = total
     return (totals, *results[len(touched):])
 
 
@@ -341,28 +385,36 @@
     )(info, table, rows, *[array for array, _ in parts])
 
 
-def combine(kept, other):
+def combine(info, kept, other):
     packed, bs, _ = kept[0].shape
-    steps = 2 if packed % 2 == 0 else 1
-    per = packed // steps
-
-    def kernel(kept_0, kept_1, other_0, other_1, out_ref):
+    packed_4 = kept[1].shape[0]
+
+    def kernel(info_ref, *refs):
+        out_ref = refs[-1]
+        even = info_ref[0] == 0
         lower = lower_lanes((bs, bs))
-        for p in range(per):
-            left = kept_0[p] + other_0[p]
-            right = kept_1[p] + other_1[p]
-            out_ref[0, p] = jnp.where(lower, left, swap_lanes(right))
-            out_ref[1, p] = jnp.where(lower, swap_lanes(left), right)
+        halves = [refs[0][p] + refs[3][p] for p in range(packed)]
+        early = [refs[1][p] + refs[4][p] for p in range(packed_4)]
+        late = [refs[2][p] + refs[5][p] for p in range(packed_4)]
+        thirds = [jnp.where(even, x, y) for x, y in zip(late, early)]
+        fourths = [jnp.where(even, x, y) for x, y in zip(early, late)]
+        for p in range(2 * packed):
+            low = halves[p % packed]
+            low = low if p < packed else swap_lanes(low)
+            group = p // packed_4
+            third = move_lanes(thirds[p % packed_4], 2 - group)
+            fourth = move_lanes(fourths[p % packed_4], 3 - group)
+            out_ref[p] = by_group([low, low, third, fourth])
 
     return pl.pallas_call(
         kernel,
-        grid=(steps,),
-        in_specs=[pl.BlockSpec((per, bs, bs), lambda g: (g, 0, 0))] * 4,
-        out_specs=pl.BlockSpec((2, per, bs, bs), lambda g: (0, g, 0, 0)),
-        out_shape=jax.ShapeDtypeStruct((2, packed, bs, bs), f32),
+        grid=(1,),
+        in_specs=[in_smem] + [whole(x.shape) for x in (*kept, *other)],
+        out_specs=whole((2 * packed, bs, bs)),
+        out_shape=jax.ShapeDtypeStruct((2 * packed, bs, bs), f32),
         compiler_params=pltpu.CompilerParams(vmem_limit_bytes=8 * 1024 * 1024),
         name="combine",
-    )(*kept, *other).reshape(2 * packed, bs, bs)
+    )(info, *kept, *other)
 
 
 def shards(left_values, left_rows, right_values, right_cols, result_slots):
@@ -422,8 +474,8 @@
     def read_places(turn, even_part, odd_part):
         places[turn] = panel_places(info, table, turn, rows_at[turn], even_part, odd_part, kb, lpb, bpr)
 
-    def add(totals, chunks, finish=None):
-        return accumulate(info, places, lefts, chunks, totals, nc, finish)
+    def add(totals, chunks, finish=None, cost=1):
+        return accumulate(info, places, lefts, chunks, totals, nc, finish, cost)
 
     def along_z_part(stage):
         return (z[stage], 0, Z_CHUNKS[stage])
@@ -454,18 +506,20 @@
     read_places(3, (x[5], rows), (z[4], rows))
     totals, done = add(totals, [along_z_part(4), along_x_part(5)])
     x[7] = along_x(sent(all_of(z[5]), [(z[3], 1, 1), (None, 2, 1, 1)], done))
-    z[7] = along_z(x[6])
     totals, done = add(totals, [along_z_part(5)])
+    z[7] = along_z(sent(all_of(x[6]), all_of(x[6]), done))
 
     def to_partner(blocks):
         return lax.ppermute(blocks, "rep", [(0, 1), (1, 0)])
 
-    totals, done, kept_0, send_0 = add(totals, [along_x_part(6)], 0)
-    other_0 = to_partner(send_0)
-    totals, done = add(totals, [along_z_part(6), along_x_part(7), along_x_part(8)])
-    totals, done, kept_1, send_1 = add(totals, [along_z_part(7)], 1)
-    other_1 = to_partner(send_1)
-    return combine((kept_0, kept_1), (other_0, other_1))[None, None]
+    totals, done, *both_0 = add(totals, [along_x_part(6)], (0, 0))
+    other_0 = to_partner(both_0[1])
+    totals, done, *both_1 = add(totals, [along_z_part(6)], (2, 1))
+    other_1 = to_partner(both_1[1])
+    totals, done = add(totals, [along_x_part(7), along_x_part(8)], cost=0)
+    totals, done, *both_2 = add(totals, [along_z_part(7)], (1, 2), 0)
+    other_2 = to_partner(both_2[1])
+    return combine(info, [both_0[0], both_1[0], both_2[0]], [other_0, other_1, other_2])[None, None]
 
 
 def solution(mesh):

time: 103 us -> 101 us (0.981)
  Pallas kernels: 36.7 us -> 42.6 us
  starting transfers between devices: 20.7 us -> 16.6 us
  waiting for transfers between devices: 38.3 us -> 34.5 us
    ppermute x2 -> x3, waiting for transfers between devices: 8.46 us -> 4.15 us  [to_partner(): return lax.ppermute(blocks, 'rep', [(0, 1), (1, 0)])]
    ppermute x6, starting transfers between devices: 8.78 us -> 4.56 us  [along_x(): return lax.ppermute(chunk, 'row', x_pairs)]
    pallas_call x9 -> x10, Pallas kernels: 18.9 us -> 22.3 us  [accumulate(): pl.pallas_call(kernel, grid_spec=pltpu.PrefetchScalarGridSpec(num_scalar_...]
    ppermute x7, waiting for transfers between devices: 3.46 us -> 5.94 us  [along_z(): return lax.ppermute(chunk, 'row', z_pairs)]
    ppermute x6, waiting for transfers between devices: 25.2 us -> 23.3 us  [along_x(): return lax.ppermute(chunk, 'row', x_pairs)]
    pallas_call x5, Pallas kernels: 3.7 us -> 5.14 us  [the longest x4 3.23 us: own_quarters(): pl.pallas_call(kernel, grid=(1,), in_specs=[whole(right.shape) if several...]
    pallas_call x8 -> x9, Pallas kernels: 6.81 us -> 7.85 us  [pick(): pl.pallas_call(kernel, grid=(1,), in_specs=[in_smem] + [spec(part) for pa...]
    ppermute x2 -> x3, starting transfers between devices: 3.05 us -> 3.53 us  [to_partner(): return lax.ppermute(blocks, 'rep', [(0, 1), (1, 0)])]
  transfers between devices with their start and end apart: 17 -> 18, of which waited for: 12 -> 13; matrix products, arithmetic and copies ran while one was open for 1% -> 1% of each run, Pallas kernels for 35% -> 41%
where the time goes in v8:
time: 101 us; the launch traced here: 100 us
  Pallas kernels  42.6 us (42%)
  waiting for transfers between devices  34.5 us (34%)
  starting transfers between devices  16.6 us (16%)
  local copies, waits for them, and re-layouts  6.27 us (6%)
    ppermute x6, waiting for transfers between devices, along_x(): return lax.ppermute(chunk, 'row', x_pairs)  23.3 us
    pallas_call x10, Pallas kernels, accumulate(): pl.pallas_call(kernel, grid_spec=pltpu.PrefetchScalarGridSpec(num_scalar_...  22.3 us
    ppermute x7, starting transfers between devices, along_z(): return lax.ppermute(chunk, 'row', z_pairs)  7.96 us
    pallas_call x9, Pallas kernels, pick(): pl.pallas_call(kernel, grid=(1,), in_specs=[in_smem] + [spec(part) for pa...  7.85 us
    ppermute x7, waiting for transfers between devices, along_z(): return lax.ppermute(chunk, 'row', z_pairs)  5.94 us
    pallas_call x3, Pallas kernels, panel_places(): pl.pallas_call(kernel, grid=(1,), in_specs=[in_smem] * 3 + [pl.BlockSpec(...  5.91 us
    unnamed x18, local copies, waits for them, and re-layouts  5.26 us
    ppermute x6, starting transfers between devices, along_x(): return lax.ppermute(chunk, 'row', x_pairs)  4.56 us
  transfers between devices with their start and end apart: 18, of which 13 were waited for; matrix products, arithmetic and copies ran while one was open for 1% of the time, Pallas kernels for 41%

profile of v8, /device:TPU:0, one launch (start us, length us, event | category | flops | bytes accessed | tf_op | source)
XLA Modules:
  0.0 100.2 jit_solution(15903695129794493717)
XLA Ops:
  0.5 0.8 copy.33.refs_1_.refs_2_
  1.2 1.6 %copy-done = f32[1,1,1,8,4,128,128]{6,5,4,3,2,1,0:T(8,128)S(1)} copy-done((f32[1,1,1,8,4,128,128]{6,5,4,3,2,1,0:T(8,128)S(1)}, f32[1,1,1,8,4,128,128]{6,5,4,3,2,1,0:T(8,128)}, u32[]{:S(2)}) %copy-start) | copy-done | bytes 2097176
  2.8 1.0 %own_quarters.4 = f32[520,256]{1,0:T(8,128)} custom-call(f32[8,4,128,128]{3,2,1,0:T(8,128)S(1)} %bitcast.15, s32[8,4]{1,0:T(8,128)S(1)} %copy.33.refs_1_.refs_2_), custom_call_target="tpu_custom_call" | custom-call | bytes 1597440 | tf_op jit(solution)/shard_map/own_quarters/pallas_call | solution.py:127
  3.8 4.6 %collective-permute-start.1 = (f32[520,256]{1,0:T(8,128)}, f32[520,256]{1,0:T(8,128)}, u32[]{:S(2)}, u32[]{:S(2)}) collective-permute-start(f32[520,256]{1,0:T(8,128)} %own_quarters.4), channel_id=1, source_target_pairs={{0,24},{4,28},{8,0},{12,4},{16,8},{20,12},{24,16},{28,20},{1,25},{... | collective-permute-start | bytes 1597448 | tf_op jit(solution)/shard_map/ppermute | solution.py:437
  8.4 1.6 %own_quarters.5 = f32[768,256]{1,0:T(8,128)} custom-call(f32[8,4,128,128]{3,2,1,0:T(8,128)S(1)} %bitcast.16), custom_call_target="tpu_custom_call" | custom-call | bytes 2359296 | tf_op jit(solution)/shard_map/own_quarters/pallas_call | solution.py:127
  10.0 1.5 %collective-permute-start.3 = (f32[768,256]{1,0:T(8,128)}, f32[768,256]{1,0:T(8,128)}, u32[]{:S(2)}, u32[]{:S(2)}) collective-permute-start(f32[768,256]{1,0:T(8,128)} %own_quarters.5), channel_id=1, source_target_pairs={{0,4},{4,0},{8,12},{12,8},{16,20},{20,16},{24,28},{28,24},{1,5},{5... | collective-permute-start | bytes 2359304 | tf_op jit(solution)/shard_map/ppermute | solution.py:440
  11.9 1.4 %own_places.1 = (s32[64]{0:T(128)S(1)}, s32[64]{0:T(128)S(1)}) custom-call(s32[6]{0:T(128)S(1)} %stack.27.info_ref, s32[24]{0:T(128)S(1)} %bitcast.31, s32[48]{0:T(128)S(1)} %reshape.6.rows_ref, s32[32]{0:T(128)S(1)} %reshape.7.cols_ref), custom_call_target="tpu_custom_call" | custom-call | tf_op jit(solution)/shard_map/own_places/pallas_call | solution.py:343
  13.3 1.6 %copy-done.1 = f32[1,1,1,8,4,128,128]{6,5,4,3,2,1,0:T(8,128)S(1)} copy-done((f32[1,1,1,8,4,128,128]{6,5,4,3,2,1,0:T(8,128)S(1)}, f32[1,1,1,8,4,128,128]{6,5,4,3,2,1,0:T(8,128)}, u32[]{:S(2)}) %copy-start.1) | copy-done | bytes 2097176
  14.9 1.9 %copy-done.3 = f32[1,1,1,3,8,2,128,128]{7,6,5,4,3,2,1,0:T(8,128)S(1)} copy-done((f32[1,1,1,3,8,2,128,128]{7,6,5,4,3,2,1,0:T(8,128)S(1)}, f32[1,1,1,3,8,2,128,128]{7,6,5,4,3,2,1,0:T(8,128)}, u32[]{:S(2)}) %copy-start.3) | copy-done | bytes 3145752
  16.8 2.8 %accumulate.10 = (f32[25,128,128]{2,1,0:T(8,128)S(1)}, f32[25,128,128]{2,1,0:T(8,128)S(1)}, f32[25,128,128]{2,1,0:T(8,128)S(1)}, s32[8,128]{1,0:T(8,128)S(1)}) custom-call(s32[6]{0:T(128)S(1)} %stack.27.info_ref, s32[64]{0:T(128)S(1)} %get-tuple-element.39.refs_0_, f32[3,8,2,128,128]{4,3,2,1,0:T(8,128)S(1)} %bitcast.25, f32[8,4,128,128]{3,2,1,0:T(8,128)S(1)} %bitcast.17), custom_call_target="tpu_custom_call" | custom-call | flops 805306368 | bytes 4194304 | tf_op jit(solution)/shard_map/accumulate/pallas_call | solution.py:311
  20.3 0.7 collective-permute-done.1.refs_0_.refs_1_.even_ref.odd_ref.refs_3_
  21.0 1.1 %pick.9 = f32[520,256]{1,0:T(8,128)S(1)} custom-call(s32[6]{0:T(128)S(1)} %stack.27.info_ref, f32[520,256]{1,0:T(8,128)} %collective-permute-done.1.refs_0_.refs_1_.even_ref.odd_ref.refs_3_, f32[8,4,128,128]{3,2,1,0:T(8,128)S(1)} %bitcast.19, s32[8,4]{1,0:T(8,128)S(1)} %copy.33.refs_1_.refs_2_, s32[8,128]{1,0:T(8,128)S(1)} %get-tuple-element.40.refs_3_.refs_1_), custom_call_target="tpu_custom_call" | custom-call | bytes 1064960 | tf_op jit(solution)/shard_map/pick/pallas_call | solution.py:177
  22.1 1.9 %collective-permute-start.2 = (f32[520,256]{1,0:T(8,128)S(1)}, f32[520,256]{1,0:T(8,128)S(1)}, u32[]{:S(2)}, u32[]{:S(2)}) collective-permute-start(f32[520,256]{1,0:T(8,128)S(1)} %pick.9), channel_id=1, source_target_pairs={{0,4},{4,0},{8,12},{12,8},{16,20},{20,16},{24,28},{28,24},{1,5},{5... | collective-permute-start | bytes 1597448 | tf_op jit(solution)/shard_map/ppermute | solution.py:440
  24.0 2.1 %panel_places.4.refs_0_.refs_1_ = s32[64]{0:T(128)S(1)} custom-call(s32[6]{0:T(128)S(1)} %stack.27.info_ref, s32[64]{0:T(128)S(1)} %get-tuple-element.38.table_ref, s32[48]{0:T(128)S(1)} %reshape.6.rows_ref, f32[520,256]{1,0:T(8,128)} %collective-permute-done.1.refs_0_.refs_1_.even_ref.odd_ref.refs_3_, ...), custom_call_target="tpu_custom_call" | custom-call | tf_op jit(solution)/shard_map/panel_places/pallas_call | solution.py:376
  26.1 4.6 %collective-permute-done.3.refs_2_.refs_4_.refs_5_.refs_0_ = f32[768,256]{1,0:T(8,128)} collective-permute-done((f32[768,256]{1,0:T(8,128)}, f32[768,256]{1,0:T(8,128)}, u32[]{:S(2)}, u32[]{:S(2)}) %collective-permute-start.3) | collective-permute-done | bytes 786464 | tf_op jit(solution)/shard_map/ppermute | solution.py:440
  31.6 3.0 %collective-permute-done.6.refs_4_.refs_0_.refs_1_ = f32[512,256]{1,0:T(8,128)S(1)} collective-permute-done((f32[512,256]{1,0:T(8,128)S(1)}, f32[512,256]{1,0:T(8,128)S(1)}, u32[]{:S(2)}, u32[]{:S(2)}) %collective-permute-start.6) | collective-permute-done | bytes 524320 | tf_op jit(solution)/shard_map/ppermute | solution.py:437
  34.7 2.6 %accumulate.11 = (f32[25,128,128]{2,1,0:T(8,128)S(1)}, s32[8,128]{1,0:T(8,128)S(1)}) custom-call(s32[6]{0:T(128)S(1)} %stack.27.info_ref, s32[64]{0:T(128)S(1)} %panel_places.4.refs_0_.refs_1_, f32[3,8,2,128,128]{4,3,2,1,0:T(8,128)S(1)} %bitcast.26, f32[3,8,2,128,128]{4,3,2,1,0:T(8,128)S(1)} %bitcast.27, ...), custom_call_target="tpu_custom_call", output_to_operand_aliasing={{0}: (6, {})} | custom-call | flops 402653184 | bytes 2097152 | tf_op jit(solution)/shard_map/accumulate/pallas_call | solution.py:311
  37.3 0.6 pick.12
  38.0 4.0 %collective-permute-done.2.even_ref.odd_ref.refs_6_.refs_1_ = f32[520,256]{1,0:T(8,128)S(1)} collective-permute-done((f32[520,256]{1,0:T(8,128)S(1)}, f32[520,256]{1,0:T(8,128)S(1)}, u32[]{:S(2)}, u32[]{:S(2)}) %collective-permute-start.2) | collective-permute-done | bytes 532512 | tf_op jit(solution)/shard_map/ppermute | solution.py:440
  42.0 1.0 %pick.11 = f32[520,256]{1,0:T(8,128)S(1)} custom-call(s32[6]{0:T(128)S(1)} %stack.27.info_ref, f32[8,4,128,128]{3,2,1,0:T(8,128)S(1)} %bitcast.22, f32[520,256]{1,0:T(8,128)S(1)} %collective-permute-done.2.even_ref.odd_ref.refs_6_.refs_1_, s32[8,4]{1,0:T(8,128)S(1)} %copy.33.refs_1_.refs_2_, s32[8,128]{1,0:T(8,128)S(1)} %get-tuple-element.46.refs_3_.refs_2_), custom_call_target="tpu_custom_call" | custom-call | bytes 1064960 | tf_op jit(solution)/shard_map/pick/pallas_call | solution.py:177
  43.1 1.1 %collective-permute-done.rows_ref = s32[48]{0:T(128)S(1)} collective-permute-done((s32[48]{0:T(128)S(1)}, s32[48]{0:T(128)S(1)}, u32[]{:S(2)}, u32[]{:S(2)}) %collective-permute-start) | collective-permute-done | bytes 224 | tf_op jit(solution)/shard_map/ppermute | solution.py:464
  44.3 1.9 %panel_places.3.refs_0_ = s32[64]{0:T(128)S(1)} custom-call(s32[6]{0:T(128)S(1)} %stack.27.info_ref, s32[64]{0:T(128)S(1)} %get-tuple-element.38.table_ref, s32[48]{0:T(128)S(1)} %collective-permute-done.rows_ref, f32[520,256]{1,0:T(8,128)S(1)} %collective-permute-done.2.even_ref.odd_ref.refs_6_.refs_1_, ...), custom_call_target="tpu_custom_call" | custom-call | tf_op jit(solution)/shard_map/panel_places/pallas_call | solution.py:376
  46.2 3.3 %accumulate.12 = (f32[25,128,128]{2,1,0:T(8,128)S(1)}, f32[25,128,128]{2,1,0:T(8,128)S(1)}, f32[25,128,128]{2,1,0:T(8,128)S(1)}, s32[8,128]{1,0:T(8,128)S(1)}) custom-call(s32[6]{0:T(128)S(1)} %stack.27.info_ref, s32[64]{0:T(128)S(1)} %panel_places.3.refs_0_, ...), custom_call_target="tpu_custom_call", output_to_operand_aliasing={{0}: (8, {}), {1}: (9, {}), {2}: (10, {})} | custom-call | flops 603979776 | bytes 3145728 | tf_op jit(solution)/shard_map/accumulate/pallas_call | solution.py:311
  49.4 1.1 %pick.10 = f32[520,256]{1,0:T(8,128)S(1)} custom-call(s32[6]{0:T(128)S(1)} %stack.27.info_ref, f32[512,256]{1,0:T(8,128)S(1)} %collective-permute-done.4.refs_0_.refs_4_.refs_1_, f32[520,256]{1,0:T(8,128)} %collective-permute-done.1.refs_0_.refs_1_.even_ref.odd_ref.refs_3_, s32[8,4]{1,0:T(8,128)S(1)} %copy.33.refs_1_.refs_2_, ...), custom_call_target="tpu_custom_call" | custom-call | bytes 1064960 | tf_op jit(solution)/shard_map/pick/pallas_call | solution.py:177
  50.6 1.9 %collective-permute-done.9.refs_5_.refs_1_ = f32[512,256]{1,0:T(8,128)S(1)} collective-permute-done((f32[512,256]{1,0:T(8,128)S(1)}, f32[512,256]{1,0:T(8,128)S(1)}, u32[]{:S(2)}, u32[]{:S(2)}) %collective-permute-start.9) | collective-permute-done | bytes 524320 | tf_op jit(solution)/shard_map/ppermute | solution.py:440
  52.5 1.1 %pick.14 = f32[512,256]{1,0:T(8,128)S(1)} custom-call(s32[6]{0:T(128)S(1)} %stack.27.info_ref, f32[768,256]{1,0:T(8,128)} %collective-permute-done.3.refs_2_.refs_4_.refs_5_.refs_0_, f32[512,256]{1,0:T(8,128)S(1)} %collective-permute-done.9.refs_5_.refs_1_, s32[8,128]{1,0:T(8,128)S(1)} %get-tuple-element.45.refs_3_.refs_2_), custom_call_target="tpu_custom_call" | custom-call | bytes 1048576 | tf_op jit(solution)/shard_map/pick/pallas_call | solution.py:177
  54.1 1.7 %accumulate.13 = (f32[25,128,128]{2,1,0:T(8,128)S(1)}, f32[25,128,128]{2,1,0:T(8,128)S(1)}, s32[8,128]{1,0:T(8,128)S(1)}) custom-call(s32[6]{0:T(128)S(1)} %stack.27.info_ref, s32[64]{0:T(128)S(1)} %panel_places.3.refs_0_, s32[64]{0:T(128)S(1)} %panel_places.4.refs_0_.refs_1_, ...), custom_call_target="tpu_custom_call", output_to_operand_aliasing={{0}: (7, {}), {1}: (8, {})} | custom-call | flops 402653184 | bytes 2097152 | tf_op jit(solution)/shard_map/accumulate/pallas_call | solution.py:311
  55.8 1.0 %collective-permute-done.8.odd_ref.refs_0_.refs_7_ = f32[520,256]{1,0:T(8,128)S(1)} collective-permute-done((f32[520,256]{1,0:T(8,128)S(1)}, f32[520,256]{1,0:T(8,128)S(1)}, u32[]{:S(2)}, u32[]{:S(2)}) %collective-permute-start.8) | collective-permute-done | bytes 532512 | tf_op jit(solution)/shard_map/ppermute | solution.py:437
  57.4 0.8 collective-permute-start.10
  58.3 7.3 %collective-permute-done.7.even_ref.refs_8_.refs_1_ = f32[520,256]{1,0:T(8,128)S(1)} collective-permute-done((f32[520,256]{1,0:T(8,128)S(1)}, f32[520,256]{1,0:T(8,128)S(1)}, u32[]{:S(2)}, u32[]{:S(2)}) %collective-permute-start.7) | collective-permute-done | bytes 532512 | tf_op jit(solution)/shard_map/ppermute | solution.py:440
  65.6 1.0 %pick.15 = f32[512,256]{1,0:T(8,128)S(1)} custom-call(s32[6]{0:T(128)S(1)} %stack.27.info_ref, f32[768,256]{1,0:T(8,128)} %collective-permute-done.3.refs_2_.refs_4_.refs_5_.refs_0_, f32[520,256]{1,0:T(8,128)S(1)} %collective-permute-done.7.even_ref.refs_8_.refs_1_, s32[8,128]{1,0:T(8,128)S(1)} %get-tuple-element.49.refs_2_), custom_call_target="tpu_custom_call" | custom-call | bytes 1048576 | tf_op jit(solution)/shard_map/pick/pallas_call | solution.py:177
  66.6 0.9 collective-permute-start.12
  67.5 1.9 %panel_places.5.refs_2_.refs_0_.refs_1_ = s32[64]{0:T(128)S(1)} custom-call(s32[6]{0:T(128)S(1)} %stack.27.info_ref, s32[64]{0:T(128)S(1)} %get-tuple-element.38.table_ref, s32[48]{0:T(128)S(1)} %collective-permute-done.rows_ref, f32[520,256]{1,0:T(8,128)S(1)} %collective-permute-done.7.even_ref.refs_8_.refs_1_, ...), custom_call_target="tpu_custom_call" | custom-call | tf_op jit(solution)/shard_map/panel_places/pallas_call | solution.py:376
  69.4 1.9 %accumulate.14 = (f32[25,128,128]{2,1,0:T(8,128)S(1)}, f32[25,128,128]{2,1,0:T(8,128)S(1)}, f32[25,128,128]{2,1,0:T(8,128)S(1)}, s32[8,128]{1,0:T(8,128)S(1)}) custom-call(s32[6]{0:T(128)S(1)} %stack.27.info_ref, s32[64]{0:T(128)S(1)} %panel_places.3.refs_0_, ...), custom_call_target="tpu_custom_call", output_to_operand_aliasing={{0}: (10, {}), {1}: (11, {}), {2}: (12, {})} | custom-call | flops 402653184 | bytes 2097152 | tf_op jit(solution)/shard_map/accumulate/pallas_call | solution.py:311
  71.3 0.8 pick.17
  72.3 1.4 %accumulate.15 = (f32[25,128,128]{2,1,0:T(8,128)S(1)}, f32[25,128,128]{2,1,0:T(8,128)S(1)}, s32[8,128]{1,0:T(8,128)S(1)}) custom-call(s32[6]{0:T(128)S(1)} %stack.27.info_ref, s32[64]{0:T(128)S(1)} %panel_places.5.refs_2_.refs_0_.refs_1_, ...), custom_call_target="tpu_custom_call", output_to_operand_aliasing={{0}: (5, {}), {1}: (6, {})} | custom-call | flops 201326592 | bytes 1048576 | tf_op jit(solution)/shard_map/accumulate/pallas_call | solution.py:311
  73.7 3.1 %collective-permute-done.10.refs_4_.refs_0_.refs_1_ = f32[512,256]{1,0:T(8,128)S(1)} collective-permute-done((f32[512,256]{1,0:T(8,128)S(1)}, f32[512,256]{1,0:T(8,128)S(1)}, u32[]{:S(2)}, u32[]{:S(2)}) %collective-permute-start.10) | collective-permute-done | bytes 524320 | tf_op jit(solution)/shard_map/ppermute | solution.py:440
  77.4 0.9 collective-permute-start.13
  78.3 2.1 %accumulate.16 = (f32[25,128,128]{2,1,0:T(8,128)S(1)}, f32[25,128,128]{2,1,0:T(8,128)S(1)}, s32[8,128]{1,0:T(8,128)}, f32[6,128,128]{2,1,0:T(8,128)S(1)}, f32[6,128,128]{2,1,0:T(8,128)S(1)}) custom-call(s32[6]{0:T(128)S(1)} %stack.27.info_ref, s32[64]{0:T(128)S(1)} %panel_places.3.refs_0_, ...), custom_call_target="tpu_custom_call", output_to_operand_aliasing={{0}: (6, {}), {1}: (7, {})} | custom-call | flops 201326592 | bytes 1048576 | tf_op jit(solution)/shard_map/accumulate/pallas_call | solution.py:311
  80.4 1.5 %collective-permute-start.15 = (f32[6,128,128]{2,1,0:T(8,128)S(1)}, f32[6,128,128]{2,1,0:T(8,128)S(1)}, u32[]{:S(2)}, u32[]{:S(2)}) collective-permute-start(f32[6,128,128]{2,1,0:T(8,128)S(1)} %get-tuple-element.68), channel_id=1, source_target_pairs={{0,1},{1,0},{2,3},{3,2},{4,5},{5,4},{6,7},{7,6},{8,9},{9,8},{10,11... | collective-permute-start | bytes 1179656 | tf_op jit(solution)/shard_map/ppermute | solution.py:513
  81.9 2.5 %accumulate.17 = (f32[25,128,128]{2,1,0:T(8,128)S(1)}, f32[25,128,128]{2,1,0:T(8,128)S(1)}, s32[8,128]{1,0:T(8,128)}, f32[3,128,128]{2,1,0:T(8,128)S(1)}, f32[3,128,128]{2,1,0:T(8,128)S(1)}) custom-call(s32[6]{0:T(128)S(1)} %stack.27.info_ref, s32[64]{0:T(128)S(1)} %panel_places.5.refs_2_.refs_0_.refs_1_, ...), custom_call_target="tpu_custom_call", output_to_operand_aliasing={{0}: (5, {}), {1}: (6, {})} | custom-call | flops 201326592 | bytes 1048576 | tf_op jit(solution)/shard_map/accumulate/pallas_call | solution.py:311
  84.9 2.4 %collective-permute-done.14.refs_6_.refs_7_ = f32[512,256]{1,0:T(8,128)S(1)} collective-permute-done((f32[512,256]{1,0:T(8,128)S(1)}, f32[512,256]{1,0:T(8,128)S(1)}, u32[]{:S(2)}, u32[]{:S(2)}) %collective-permute-start.14) | collective-permute-done | bytes 524320 | tf_op jit(solution)/shard_map/ppermute | solution.py:440
  87.3 2.1 %accumulate.18 = (f32[25,128,128]{2,1,0:T(8,128)S(1)}, f32[25,128,128]{2,1,0:T(8,128)S(1)}, s32[8,128]{1,0:T(8,128)}) custom-call(s32[6]{0:T(128)S(1)} %stack.27.info_ref, s32[64]{0:T(128)S(1)} %panel_places.3.refs_0_, s32[64]{0:T(128)S(1)} %panel_places.4.refs_0_.refs_1_, ...), custom_call_target="tpu_custom_call", output_to_operand_aliasing={{0}: (9, {}), {1}: (10, {})} | custom-call | tf_op jit(solution)/shard_map/accumulate/pallas_call | solution.py:311
  89.3 1.2 %collective-permute-done.13.refs_2_ = f32[512,256]{1,0:T(8,128)S(1)} collective-permute-done((f32[512,256]{1,0:T(8,128)S(1)}, f32[512,256]{1,0:T(8,128)S(1)}, u32[]{:S(2)}, u32[]{:S(2)}) %collective-permute-start.13) | collective-permute-done | bytes 524320 | tf_op jit(solution)/shard_map/ppermute | solution.py:437
  90.5 2.0 %accumulate.19 = (f32[25,128,128]{2,1,0:T(8,128)S(1)}, f32[25,128,128]{2,1,0:T(8,128)S(1)}, s32[8,128]{1,0:T(8,128)}, f32[3,128,128]{2,1,0:T(8,128)S(1)}, f32[3,128,128]{2,1,0:T(8,128)S(1)}) custom-call(s32[6]{0:T(128)S(1)} %stack.27.info_ref, s32[64]{0:T(128)S(1)} %panel_places.5.refs_2_.refs_0_.refs_1_, ...), custom_call_target="tpu_custom_call", output_to_operand_aliasing={{0}: (4, {}), {1}: (5, {})} | custom-call | tf_op jit(solution)/shard_map/accumulate/pallas_call | solution.py:311
  92.6 1.5 %collective-permute-start.17 = (f32[3,128,128]{2,1,0:T(8,128)S(1)}, f32[3,128,128]{2,1,0:T(8,128)S(1)}, u32[]{:S(2)}, u32[]{:S(2)}) collective-permute-start(f32[3,128,128]{2,1,0:T(8,128)S(1)} %get-tuple-element.70), channel_id=1, source_target_pairs={{0,1},{1,0},{2,3},{3,2},{4,5},{5,4},{6,7},{7,6},{8,9},{9,8},{10,11... | collective-permute-start | bytes 589832 | tf_op jit(solution)/shard_map/ppermute | solution.py:513
  94.2 4.0 %collective-permute-done.17.refs_5_ = f32[3,128,128]{2,1,0:T(8,128)S(1)} collective-permute-done((f32[3,128,128]{2,1,0:T(8,128)S(1)}, f32[3,128,128]{2,1,0:T(8,128)S(1)}, u32[]{:S(2)}, u32[]{:S(2)}) %collective-permute-start.17) | collective-permute-done | bytes 196640 | tf_op jit(solution)/shard_map/ppermute | solution.py:513
  98.3 1.9 %combine.1 = f32[12,128,128]{2,1,0:T(8,128)} custom-call(s32[6]{0:T(128)S(1)} %stack.27.info_ref, f32[6,128,128]{2,1,0:T(8,128)S(1)} %get-tuple-element.57.refs_0_, f32[3,128,128]{2,1,0:T(8,128)S(1)} %get-tuple-element.60.refs_1_, f32[3,128,128]{2,1,0:T(8,128)S(1)} %get-tuple-element.67.refs_2_, f32[6,128,128]{2,1,0:T(8,128)S(1)} %collective-permute-done.15.refs_3_, ...), custom_call_target="tpu_custom_call" | custom-call | tf_op jit(solution)/shard_map/combine/pallas_call | solution.py:409
  (38 shorter events, 5.4 us)
Async XLA Ops:
  0.0 46.2 %collective-permute-start.5 = (f32[3,8,2,128,128]{4,3,2,1,0:T(8,128)}, f32[3,8,2,128,128]{4,3,2,1,0:T(8,128)S(1)}, u32[]{:S(2)}, u32[]{:S(2)}) collective-permute-start(f32[3,8,2,128,128]{4,3,2,1,0:T(8,128)} %bitcast.24), channel_id=1, source_target_pairs={{0,2},{2,0},{1,3},{3,1},{4,6},{6,4},{5,7},{7,5},{8,10},{10,8},{9,1... | collective-permute-start | bytes 9437192 | tf_op jit(solution)/shard_map/ppermute | solution.py:464
  1.2 1.6 %copy-start = (f32[1,1,1,8,4,128,128]{6,5,4,3,2,1,0:T(8,128)S(1)}, f32[1,1,1,8,4,128,128]{6,5,4,3,2,1,0:T(8,128)}, u32[]{:S(2)}) copy-start(f32[1,1,1,8,4,128,128]{6,5,4,3,2,1,0:T(8,128)} %param.7) | copy-start | bytes 6291460
  3.8 7.7 %copy-start.6 = (s32[1,1,1,8,4]{3,4,2,1,0:T(4,128)S(1)}, s32[1,1,1,8,4]{3,4,2,1,0:T(4,128)}, u32[]{:S(2)}) copy-start(s32[1,1,1,8,4]{3,4,2,1,0:T(4,128)} %param.8) | copy-start | bytes 388
  3.8 7.7 %copy-start.7 = (s32[1,1,1,3,8,2]{4,5,3,2,1,0:T(2,128)S(1)}, s32[1,1,1,3,8,2]{4,5,3,2,1,0:T(2,128)}, u32[]{:S(2)}) copy-start(s32[1,1,1,3,8,2]{4,5,3,2,1,0:T(2,128)} %param.6) | copy-start | bytes 580
  3.8 8.1 %copy-start.5 = (s32[1,1,24]{2,1,0:T(1,128)S(1)}, s32[1,1,24]{2,1,0:T(1,128)}, u32[]{:S(2)}) copy-start(s32[1,1,24]{2,1,0:T(1,128)} %param.9) | copy-start | bytes 292
  3.8 17.2 %collective-permute-start.1 = (f32[520,256]{1,0:T(8,128)}, f32[520,256]{1,0:T(8,128)}, u32[]{:S(2)}, u32[]{:S(2)}) collective-permute-start(f32[520,256]{1,0:T(8,128)} %own_quarters.4), channel_id=1, source_target_pairs={{0,24},{4,28},{8,0},{12,4},{16,8},{20,12},{24,16},{28,20},{1,25},{... | collective-permute-start | bytes 1597448 | tf_op jit(solution)/shard_map/ppermute | solution.py:437
  10.0 20.7 %collective-permute-start.3 = (f32[768,256]{1,0:T(8,128)}, f32[768,256]{1,0:T(8,128)}, u32[]{:S(2)}, u32[]{:S(2)}) collective-permute-start(f32[768,256]{1,0:T(8,128)} %own_quarters.5), channel_id=1, source_target_pairs={{0,4},{4,0},{8,12},{12,8},{16,20},{20,16},{24,28},{28,24},{1,5},{5... | collective-permute-start | bytes 2359304 | tf_op jit(solution)/shard_map/ppermute | solution.py:440
  13.3 1.6 %copy-start.1 = (f32[1,1,1,8,4,128,128]{6,5,4,3,2,1,0:T(8,128)S(1)}, f32[1,1,1,8,4,128,128]{6,5,4,3,2,1,0:T(8,128)}, u32[]{:S(2)}) copy-start(f32[1,1,1,8,4,128,128]{6,5,4,3,2,1,0:T(8,128)} %param.7) | copy-start | bytes 6291460
  14.9 1.9 %copy-start.3 = (f32[1,1,1,3,8,2,128,128]{7,6,5,4,3,2,1,0:T(8,128)S(1)}, f32[1,1,1,3,8,2,128,128]{7,6,5,4,3,2,1,0:T(8,128)}, u32[]{:S(2)}) copy-start(f32[1,1,1,3,8,2,128,128]{7,6,5,4,3,2,1,0:T(8,128)} %param.5) | copy-start | bytes 9437188
  19.8 14.8 %collective-permute-start.6 = (f32[512,256]{1,0:T(8,128)S(1)}, f32[512,256]{1,0:T(8,128)S(1)}, u32[]{:S(2)}, u32[]{:S(2)}) collective-permute-start(f32[512,256]{1,0:T(8,128)S(1)} %own_quarters.7), channel_id=1, source_target_pairs={{0,24},{4,28},{8,0},{12,4},{16,8},{20,12},{24,16},{28,20},{1,25},{... | collective-permute-start | bytes 1572872 | tf_op jit(solution)/shard_map/ppermute | solution.py:437
  22.1 19.9 %collective-permute-start.2 = (f32[520,256]{1,0:T(8,128)S(1)}, f32[520,256]{1,0:T(8,128)S(1)}, u32[]{:S(2)}, u32[]{:S(2)}) collective-permute-start(f32[520,256]{1,0:T(8,128)S(1)} %pick.9), channel_id=1, source_target_pairs={{0,4},{4,0},{8,12},{12,8},{16,20},{20,16},{24,28},{28,24},{1,5},{5... | collective-permute-start | bytes 1597448 | tf_op jit(solution)/shard_map/ppermute | solution.py:440
  26.1 8.6 %copy-start.4 = (f32[1,1,1,3,8,2,128,128]{7,6,5,4,3,2,1,0:T(8,128)S(1)}, f32[1,1,1,3,8,2,128,128]{7,6,5,4,3,2,1,0:T(8,128)}, u32[]{:S(2)}) copy-start(f32[1,1,1,3,8,2,128,128]{7,6,5,4,3,2,1,0:T(8,128)} %param.5) | copy-start | bytes 9437188
  31.1 18.3 %collective-permute-start.4 = (f32[512,256]{1,0:T(8,128)S(1)}, f32[512,256]{1,0:T(8,128)S(1)}, u32[]{:S(2)}, u32[]{:S(2)}) collective-permute-start(f32[512,256]{1,0:T(8,128)S(1)} %own_quarters.6), channel_id=1, source_target_pairs={{0,24},{4,28},{8,0},{12,4},{16,8},{20,12},{24,16},{28,20},{1,25},{... | collective-permute-start | bytes 1572872 | tf_op jit(solution)/shard_map/ppermute | solution.py:437
  34.7 2.6 %copy-start.2 = (f32[1,1,1,8,4,128,128]{6,5,4,3,2,1,0:T(8,128)S(1)}, f32[1,1,1,8,4,128,128]{6,5,4,3,2,1,0:T(8,128)}, u32[]{:S(2)}) copy-start(f32[1,1,1,8,4,128,128]{6,5,4,3,2,1,0:T(8,128)} %param.7) | copy-start | bytes 6291460
  37.9 14.6 %collective-permute-start.9 = (f32[512,256]{1,0:T(8,128)S(1)}, f32[512,256]{1,0:T(8,128)S(1)}, u32[]{:S(2)}, u32[]{:S(2)}) collective-permute-start(f32[512,256]{1,0:T(8,128)S(1)} %pick.12), channel_id=1, source_target_pairs={{0,4},{4,0},{8,12},{12,8},{16,20},{20,16},{24,28},{28,24},{1,5},{5... | collective-permute-start | bytes 1572872 | tf_op jit(solution)/shard_map/ppermute | solution.py:440
  43.0 13.8 %collective-permute-start.8 = (f32[520,256]{1,0:T(8,128)S(1)}, f32[520,256]{1,0:T(8,128)S(1)}, u32[]{:S(2)}, u32[]{:S(2)}) collective-permute-start(f32[520,256]{1,0:T(8,128)S(1)} %pick.11), channel_id=1, source_target_pairs={{0,24},{4,28},{8,0},{12,4},{16,8},{20,12},{24,16},{28,20},{1,25},{... | collective-permute-start | bytes 1597448 | tf_op jit(solution)/shard_map/ppermute | solution.py:437
  43.1 1.2 %collective-permute-start = (s32[48]{0:T(128)S(1)}, s32[48]{0:T(128)S(1)}, u32[]{:S(2)}, u32[]{:S(2)}) collective-permute-start(s32[48]{0:T(128)S(1)} %reshape.6.rows_ref), channel_id=1, source_target_pairs={{0,2},{2,0},{1,3},{3,1},{4,6},{6,4},{5,7},{7,5},{8,10},{10,8},{9,1... | collective-permute-start | bytes 584 | tf_op jit(solution)/shard_map/ppermute | solution.py:464
  50.6 15.0 %collective-permute-start.7 = (f32[520,256]{1,0:T(8,128)S(1)}, f32[520,256]{1,0:T(8,128)S(1)}, u32[]{:S(2)}, u32[]{:S(2)}) collective-permute-start(f32[520,256]{1,0:T(8,128)S(1)} %pick.10), channel_id=1, source_target_pairs={{0,4},{4,0},{8,12},{12,8},{16,20},{20,16},{24,28},{28,24},{1,5},{5... | collective-permute-start | bytes 1597448 | tf_op jit(solution)/shard_map/ppermute | solution.py:440
  53.6 17.7 %collective-permute-start.11 = (f32[512,256]{1,0:T(8,128)S(1)}, f32[512,256]{1,0:T(8,128)S(1)}, u32[]{:S(2)}, u32[]{:S(2)}) collective-permute-start(f32[512,256]{1,0:T(8,128)S(1)} %pick.14), channel_id=1, source_target_pairs={{0,24},{4,28},{8,0},{12,4},{16,8},{20,12},{24,16},{28,20},{1,25},{... | collective-permute-start | bytes 1572872 | tf_op jit(solution)/shard_map/ppermute | solution.py:437
  57.4 19.4 %collective-permute-start.10 = (f32[512,256]{1,0:T(8,128)S(1)}, f32[512,256]{1,0:T(8,128)S(1)}, u32[]{:S(2)}, u32[]{:S(2)}) collective-permute-start(f32[512,256]{1,0:T(8,128)S(1)} %pick.13), channel_id=1, source_target_pairs={{0,4},{4,0},{8,12},{12,8},{16,20},{20,16},{24,28},{28,24},{1,5},{5... | collective-permute-start | bytes 1572872 | tf_op jit(solution)/shard_map/ppermute | solution.py:440
  66.6 15.3 %collective-permute-start.12 = (f32[512,256]{1,0:T(8,128)S(1)}, f32[512,256]{1,0:T(8,128)S(1)}, u32[]{:S(2)}, u32[]{:S(2)}) collective-permute-start(f32[512,256]{1,0:T(8,128)S(1)} %pick.15), channel_id=1, source_target_pairs={{0,24},{4,28},{8,0},{12,4},{16,8},{20,12},{24,16},{28,20},{1,25},{... | collective-permute-start | bytes 1572872 | tf_op jit(solution)/shard_map/ppermute | solution.py:437
  72.1 15.2 %collective-permute-start.14 = (f32[512,256]{1,0:T(8,128)S(1)}, f32[512,256]{1,0:T(8,128)S(1)}, u32[]{:S(2)}, u32[]{:S(2)}) collective-permute-start(f32[512,256]{1,0:T(8,128)S(1)} %pick.17), channel_id=1, source_target_pairs={{0,4},{4,0},{8,12},{12,8},{16,20},{20,16},{24,28},{28,24},{1,5},{5... | collective-permute-start | bytes 1572872 | tf_op jit(solution)/shard_map/ppermute | solution.py:440
  77.4 13.2 %collective-permute-start.13 = (f32[512,256]{1,0:T(8,128)S(1)}, f32[512,256]{1,0:T(8,128)S(1)}, u32[]{:S(2)}, u32[]{:S(2)}) collective-permute-start(f32[512,256]{1,0:T(8,128)S(1)} %pick.16), channel_id=1, source_target_pairs={{0,24},{4,28},{8,0},{12,4},{16,8},{20,12},{24,16},{28,20},{1,25},{... | collective-permute-start | bytes 1572872 | tf_op jit(solution)/shard_map/ppermute | solution.py:437
  80.4 13.7 %collective-permute-start.15 = (f32[6,128,128]{2,1,0:T(8,128)S(1)}, f32[6,128,128]{2,1,0:T(8,128)S(1)}, u32[]{:S(2)}, u32[]{:S(2)}) collective-permute-start(f32[6,128,128]{2,1,0:T(8,128)S(1)} %get-tuple-element.68), channel_id=1, source_target_pairs={{0,1},{1,0},{2,3},{3,2},{4,5},{5,4},{6,7},{7,6},{8,9},{9,8},{10,11... | collective-permute-start | bytes 1179656 | tf_op jit(solution)/shard_map/ppermute | solution.py:513
  84.4 9.8 %collective-permute-start.16 = (f32[3,128,128]{2,1,0:T(8,128)S(1)}, f32[3,128,128]{2,1,0:T(8,128)S(1)}, u32[]{:S(2)}, u32[]{:S(2)}) collective-permute-start(f32[3,128,128]{2,1,0:T(8,128)S(1)} %get-tuple-element.69), channel_id=1, source_target_pairs={{0,1},{1,0},{2,3},{3,2},{4,5},{5,4},{6,7},{7,6},{8,9},{9,8},{10,11... | collective-permute-start | bytes 589832 | tf_op jit(solution)/shard_map/ppermute | solution.py:513
  92.6 5.7 %collective-permute-start.17 = (f32[3,128,128]{2,1,0:T(8,128)S(1)}, f32[3,128,128]{2,1,0:T(8,128)S(1)}, u32[]{:S(2)}, u32[]{:S(2)}) collective-permute-start(f32[3,128,128]{2,1,0:T(8,128)S(1)} %get-tuple-element.70), channel_id=1, source_target_pairs={{0,1},{1,0},{2,3},{3,2},{4,5},{5,4},{6,7},{7,6},{8,9},{9,8},{10,11... | collective-permute-start | bytes 589832 | tf_op jit(solution)/shard_map/ppermute | solution.py:513

commit v9 on v8

--- a/solution.py
+++ b/solution.py
@@ -105,8 +105,8 @@
 
 
 def put_extra(out_ref, cols_ref, rows):
-    kb, bpr = cols_ref.shape
-    out_ref[rows:rows + kb, :bpr] = cols_ref[...].astype(out_ref.dtype)
+    bpr, kb = cols_ref.shape
+    out_ref[rows:rows + bpr, :kb] = cols_ref[...].astype(out_ref.dtype)
 
 
 def own_quarters(right, quarters, cols, *others):
@@ -330,7 +330,7 @@
 
 def own_places(info, slots, rows, cols, kb, lpb):
     nc = slots.shape[0]
-    bpr = cols.shape[0] // kb
+    bpr = cols.shape[0]
 
     def kernel(info_ref, slots_ref, rows_ref, cols_ref, table_ref, out_ref):
         for code in range(CB * CB):
@@ -338,7 +338,7 @@
         behind = nc - nc // 2 * info_ref[1 + STEPS]
         for n in range(nc):
             table_ref[slots_ref[n]] = lax.rem(n + behind, nc)
-        fill_places(info_ref[1], table_ref, rows_ref, lambda k, b: cols_ref[k * bpr + b], out_ref, kb, lpb, bpr)
+        fill_places(info_ref[1], table_ref, rows_ref, lambda k, b: cols_ref[b, k], out_ref, kb, lpb, bpr)
 
     return pl.pallas_call(
         kernel,
@@ -354,7 +354,7 @@
     def column(k, carry):
         cols = [col_of(k, b) for b in range(bpr)]
         for a in range(lpb):
-            row = rows_ref[(panel * kb + k) * lpb + a] * CB
+            row = rows_ref[panel, a, k] * CB
             for b in range(bpr):
                 out_ref[(k * lpb + a) * bpr + b] = table_ref[row + cols[b]]
         return carry
@@ -371,7 +371,7 @@
         copy = pltpu.make_async_copy(cols_ref, scalar_ref, sem)
         copy.start()
         copy.wait()
-        fill_places(info_ref[1 + turn], table_ref, rows_ref, lambda k, b: scalar_ref[k, b], out_ref, kb, lpb, bpr)
+        fill_places(info_ref[1 + turn], table_ref, rows_ref, lambda k, b: scalar_ref[b, k], out_ref, kb, lpb, bpr)
 
     return pl.pallas_call(
         kernel,
@@ -392,25 +392,27 @@
     def kernel(info_ref, *refs):
         out_ref = refs[-1]
         even = info_ref[0] == 0
-        lower = lower_lanes((bs, bs))
-        halves = [refs[0][p] + refs[3][p] for p in range(packed)]
-        early = [refs[1][p] + refs[4][p] for p in range(packed_4)]
-        late = [refs[2][p] + refs[5][p] for p in range(packed_4)]
-        thirds = [jnp.where(even, x, y) for x, y in zip(late, early)]
-        fourths = [jnp.where(even, x, y) for x, y in zip(early, late)]
-        for p in range(2 * packed):
-            low = halves[p % packed]
-            low = low if p < packed else swap_lanes(low)
-            group = p // packed_4
-            third = move_lanes(thirds[p % packed_4], 2 - group)
-            fourth = move_lanes(fourths[p % packed_4], 3 - group)
-            out_ref[p] = by_group([low, low, third, fourth])
+
+        def step(first):
+            for n in range(packed):
+                p = first * packed + n
+                low = refs[0][n] + refs[3][n]
+                early = refs[1][p % packed_4] + refs[4][p % packed_4]
+                late = refs[2][p % packed_4] + refs[5][p % packed_4]
+                group = p // packed_4
+                third = move_lanes(jnp.where(even, late, early), 2 - group)
+                fourth = move_lanes(jnp.where(even, early, late), 3 - group)
+                low = low if first == 0 else swap_lanes(low)
+                out_ref[n] = by_group([low, low, third, fourth])
+
+        for first in range(2):
+            pl.when(pl.program_id(0) == first)(lambda first=first: step(first))
 
     return pl.pallas_call(
         kernel,
-        grid=(1,),
-        in_specs=[in_smem] + [whole(x.shape) for x in (*kept, *other)],
-        out_specs=whole((2 * packed, bs, bs)),
+        grid=(2,),
+        in_specs=[in_smem] + [in_vmem] * 6,
+        out_specs=pl.BlockSpec((packed, bs, bs), lambda g: (g, 0, 0)),
         out_shape=jax.ShapeDtypeStruct((2 * packed, bs, bs), f32),
         compiler_params=pltpu.CompilerParams(vmem_limit_bytes=8 * 1024 * 1024),
         name="combine",
@@ -421,9 +423,9 @@
     rows_n, cols_n = (lax.axis_size(a) for a in ("row", "col"))
     row, col, rep = (lax.axis_index(a) for a in ("row", "col", "rep"))
     panels = left_values[0, 0, 0]
-    panel_rows = left_rows.reshape(-1)
+    panel_rows = jnp.swapaxes(left_rows[0, 0, 0], 1, 2)
     right = right_values[0, 0, 0]
-    right_places = right_cols.reshape(-1)
+    cols = jnp.swapaxes(right_cols[0, 0, 0], 0, 1)
     slots = result_slots[0, 0]
     kb = right.shape[0]
     nc = slots.shape[0]
@@ -440,8 +442,6 @@
         return lax.ppermute(chunk, "row", x_pairs)
 
     rows, width = quarter_shape(right)
-    cols = right_cols[0, 0, 0]
-
     def sent(even_parts, odd_parts, *others, extra=False):
         return pick(info, right, cols if extra else None, even_parts, odd_parts, *others)
 
@@ -456,8 +456,9 @@
     def own_part(quarter, first=0, parts=PARTS):
         return (quarter, first, parts)
 
-    z[1] = along_z(own_quarters(right, [own_part(0)], cols))
-    x[1] = along_x(own_quarters(right, [own_part(3), own_part(2, 0, 1)], None))
+    small = (info,)
+    z[1] = along_z(own_quarters(right, [own_part(0)], cols, *small))
+    x[1] = along_x(own_quarters(right, [own_part(3), own_part(2, 0, 1)], None, *small))
 
     shifts = sorted({turn % cols_n for turn in range(STEPS)})
     held = {
@@ -469,7 +470,7 @@
 
     lpb, bpr = panels.shape[2], right.shape[1]
     places = {}
-    table, places[0] = own_places(info, slots, panel_rows, right_places, kb, lpb)
+    table, places[0] = own_places(info, slots, panel_rows, cols, kb, lpb)
 
     def read_places(turn, even_part, odd_part):
         places[turn] = panel_places(info, table, turn, rows_at[turn], even_part, odd_part, kb, lpb, bpr)

time: 101 us -> 98.7 us (0.977)
  starting transfers between devices: 16.6 us -> 24.6 us
  Pallas kernels: 42.6 us -> 36.6 us
  local copies, waits for them, and re-layouts: 6.27 us -> 2.38 us
    ppermute x7, starting transfers between devices: 7.96 us -> 12.2 us  [along_z(): return lax.ppermute(chunk, 'row', z_pairs)]
    ppermute x6, starting transfers between devices: 4.56 us -> 8.37 us  [along_x(): return lax.ppermute(chunk, 'row', x_pairs)]
    unnamed x18 -> x14, local copies, waits for them, and re-layouts: 5.26 us -> 2.3 us
    pallas_call x10, Pallas kernels: 22.3 us -> 20.1 us  [accumulate(): pl.pallas_call(kernel, grid_spec=pltpu.PrefetchScalarGridSpec(num_scalar_...]
    pallas_call x9, Pallas kernels: 7.85 us -> 5.72 us  [pick(): pl.pallas_call(kernel, grid=(1,), in_specs=[in_smem] + [spec(part) for pa...]
    pallas_call x4, Pallas kernels: 3.23 us -> 1.53 us  [own_quarters(): pl.pallas_call(kernel, grid=(1,), in_specs=[whole(right.shape) if several...]
    ppermute x3, waiting for transfers between devices: 4.15 us -> 5.31 us  [to_partner(): return lax.ppermute(blocks, 'rep', [(0, 1), (1, 0)])]
  transfers between devices with their start and end apart: 18 -> 18, of which waited for: 13 -> 12; matrix products, arithmetic and copies ran while one was open for 1% -> 0% of each run, Pallas kernels for 41% -> 35%
where the time goes in v9:
time: 98.7 us; the launch traced here: 98.5 us
  Pallas kernels  36.6 us (37%)
  waiting for transfers between devices  34.7 us (35%)
  starting transfers between devices  24.6 us (25%)
  local copies, waits for them, and re-layouts  2.38 us (2%)
    ppermute x6, waiting for transfers between devices, along_x(): return lax.ppermute(chunk, 'row', x_pairs)  22.6 us
    pallas_call x10, Pallas kernels, accumulate(): pl.pallas_call(kernel, grid_spec=pltpu.PrefetchScalarGridSpec(num_scalar_...  20.1 us
    ppermute x7, starting transfers between devices, along_z(): return lax.ppermute(chunk, 'row', z_pairs)  12.2 us
    ppermute x6, starting transfers between devices, along_x(): return lax.ppermute(chunk, 'row', x_pairs)  8.37 us
    pallas_call x3, Pallas kernels, panel_places(): pl.pallas_call(kernel, grid=(1,), in_specs=[in_smem] * 3 + [pl.BlockSpec(...  5.86 us
    pallas_call x9, Pallas kernels, pick(): pl.pallas_call(kernel, grid=(1,), in_specs=[in_smem] + [spec(part) for pa...  5.72 us
    ppermute x7, waiting for transfers between devices, along_z(): return lax.ppermute(chunk, 'row', z_pairs)  5.62 us
    ppermute x3, waiting for transfers between devices, to_partner(): return lax.ppermute(blocks, 'rep', [(0, 1), (1, 0)])  5.31 us
  transfers between devices with their start and end apart: 18, of which 12 were waited for; matrix products, arithmetic and copies ran while one was open for 0% of the time, Pallas kernels for 35%

profile of v9, /device:TPU:0, one launch (start us, length us, event | category | flops | bytes accessed | tf_op | source)
XLA Modules:
  0.0 98.5 jit_solution(8966067274812672238)
XLA Ops:
  0.5 1.6 %copy-done = f32[1,1,1,8,4,128,128]{6,5,4,3,2,1,0:T(8,128)S(1)} copy-done((f32[1,1,1,8,4,128,128]{6,5,4,3,2,1,0:T(8,128)S(1)}, f32[1,1,1,8,4,128,128]{6,5,4,3,2,1,0:T(8,128)}, u32[]{:S(2)}) %copy-start) | copy-done | bytes 2097176
  2.1 0.7 copy-done.3
  3.0 4.7 %collective-permute-start.1 = (f32[520,256]{1,0:T(8,128)S(1)}, f32[520,256]{1,0:T(8,128)S(1)}, u32[]{:S(2)}, u32[]{:S(2)}) collective-permute-start(f32[520,256]{1,0:T(8,128)S(1)} %own_quarters.4), channel_id=1, source_target_pairs={{0,24},{4,28},{8,0},{12,4},{16,8},{20,12},{24,16},{28,20},{1,25},{... | collective-permute-start | bytes 1597448 | tf_op jit(solution)/shard_map/ppermute | solution.py:439
  7.7 0.7 own_quarters.5
  8.4 1.6 %collective-permute-start.3 = (f32[768,256]{1,0:T(8,128)S(1)}, f32[768,256]{1,0:T(8,128)S(1)}, u32[]{:S(2)}, u32[]{:S(2)}) collective-permute-start(f32[768,256]{1,0:T(8,128)S(1)} %own_quarters.5), channel_id=1, source_target_pairs={{0,4},{4,0},{8,12},{12,8},{16,20},{20,16},{24,28},{28,24},{1,5},{5... | collective-permute-start | bytes 2359304 | tf_op jit(solution)/shard_map/ppermute | solution.py:442
  9.9 1.5 %own_places.1 = (s32[64]{0:T(128)S(1)}, s32[64]{0:T(128)S(1)}) custom-call(s32[6]{0:T(128)S(1)} %stack.27.info_ref.refs_2_.refs_1_, s32[24]{0:T(128)S(1)} %bitcast.40, s32[3,2,8]{2,1,0:T(2,128)S(1)} %bitcast.37, s32[4,8]{1,0:T(4,128)S(1)} %bitcast.33), custom_call_target="tpu_custom_call" | custom-call | tf_op jit(solution)/shard_map/own_places/pallas_call | solution.py:343
  11.4 2.7 %accumulate.10 = (f32[25,128,128]{2,1,0:T(8,128)S(1)}, f32[25,128,128]{2,1,0:T(8,128)S(1)}, f32[25,128,128]{2,1,0:T(8,128)S(1)}, s32[8,128]{1,0:T(8,128)S(1)}) custom-call(s32[6]{0:T(128)S(1)} %stack.27.info_ref.refs_2_.refs_1_, s32[64]{0:T(128)S(1)} %get-tuple-element.39.refs_0_, f32[3,8,2,128,128]{4,3,2,1,0:T(8,128)S(1)} %bitcast.26, ...), custom_call_target="tpu_custom_call" | custom-call | flops 805306368 | bytes 4194304 | tf_op jit(solution)/shard_map/accumulate/pallas_call | solution.py:311
  14.3 1.4 %collective-permute-start.6 = (f32[512,256]{1,0:T(8,128)S(1)}, f32[512,256]{1,0:T(8,128)S(1)}, u32[]{:S(2)}, u32[]{:S(2)}) collective-permute-start(f32[512,256]{1,0:T(8,128)S(1)} %own_quarters.7), channel_id=1, source_target_pairs={{0,24},{4,28},{8,0},{12,4},{16,8},{20,12},{24,16},{28,20},{1,25},{... | collective-permute-start | bytes 1572872 | tf_op jit(solution)/shard_map/ppermute | solution.py:439
  15.7 4.4 %collective-permute-done.1.refs_0_.refs_1_.even_ref.odd_ref.refs_3_ = f32[520,256]{1,0:T(8,128)S(1)} collective-permute-done((f32[520,256]{1,0:T(8,128)S(1)}, f32[520,256]{1,0:T(8,128)S(1)}, u32[]{:S(2)}, u32[]{:S(2)}) %collective-permute-start.1) | collective-permute-done | bytes 532512 | tf_op jit(solution)/shard_map/ppermute | solution.py:439
  20.7 1.7 %collective-permute-start.2 = (f32[520,256]{1,0:T(8,128)S(1)}, f32[520,256]{1,0:T(8,128)S(1)}, u32[]{:S(2)}, u32[]{:S(2)}) collective-permute-start(f32[520,256]{1,0:T(8,128)S(1)} %pick.9), channel_id=1, source_target_pairs={{0,4},{4,0},{8,12},{12,8},{16,20},{20,16},{24,28},{28,24},{1,5},{5... | collective-permute-start | bytes 1597448 | tf_op jit(solution)/shard_map/ppermute | solution.py:442
  22.4 2.0 %panel_places.4.refs_0_.refs_1_ = s32[64]{0:T(128)S(1)} custom-call(s32[6]{0:T(128)S(1)} %stack.27.info_ref.refs_2_.refs_1_, s32[64]{0:T(128)S(1)} %get-tuple-element.38.table_ref, s32[3,2,8]{2,1,0:T(2,128)S(1)} %bitcast.38, f32[520,256]{1,0:T(8,128)S(1)} %collective-permute-done.1.refs_0_.refs_1_.even_ref.odd_ref.refs_3_, ...), custom_call_target="tpu_custom_call" | custom-call | tf_op jit(solution)/shard_map/panel_places/pallas_call | solution.py:376
  24.4 4.4 %collective-permute-done.3.refs_2_.refs_4_.refs_5_.refs_0_ = f32[768,256]{1,0:T(8,128)S(1)} collective-permute-done((f32[768,256]{1,0:T(8,128)S(1)}, f32[768,256]{1,0:T(8,128)S(1)}, u32[]{:S(2)}, u32[]{:S(2)}) %collective-permute-start.3) | collective-permute-done | bytes 786464 | tf_op jit(solution)/shard_map/ppermute | solution.py:442
  29.3 1.4 %collective-permute-start.4 = (f32[512,256]{1,0:T(8,128)S(1)}, f32[512,256]{1,0:T(8,128)S(1)}, u32[]{:S(2)}, u32[]{:S(2)}) collective-permute-start(f32[512,256]{1,0:T(8,128)S(1)} %own_quarters.6), channel_id=1, source_target_pairs={{0,24},{4,28},{8,0},{12,4},{16,8},{20,12},{24,16},{28,20},{1,25},{... | collective-permute-start | bytes 1572872 | tf_op jit(solution)/shard_map/ppermute | solution.py:439
  30.6 0.7 collective-permute-done.6.refs_4_.refs_0_.refs_1_
  31.3 1.5 %accumulate.11 = (f32[25,128,128]{2,1,0:T(8,128)S(1)}, s32[8,128]{1,0:T(8,128)S(1)}) custom-call(s32[6]{0:T(128)S(1)} %stack.27.info_ref.refs_2_.refs_1_, s32[64]{0:T(128)S(1)} %panel_places.4.refs_0_.refs_1_, f32[3,8,2,128,128]{4,3,2,1,0:T(8,128)S(1)} %bitcast.27, f32[3,8,2,128,128]{4,3,2,1,0:T(8,128)S(1)} %bitcast.28, ...), custom_call_target="tpu_custom_call", output_to_operand_aliasing={{0}: (6, {})} | custom-call | flops 402653184 | bytes 2097152 | tf_op jit(solution)/shard_map/accumulate/pallas_call | solution.py:311
  32.8 0.6 pick.12
  33.4 1.7 %collective-permute-start.9 = (f32[512,256]{1,0:T(8,128)S(1)}, f32[512,256]{1,0:T(8,128)S(1)}, u32[]{:S(2)}, u32[]{:S(2)}) collective-permute-start(f32[512,256]{1,0:T(8,128)S(1)} %pick.12), channel_id=1, source_target_pairs={{0,4},{4,0},{8,12},{12,8},{16,20},{20,16},{24,28},{28,24},{1,5},{5... | collective-permute-start | bytes 1572872 | tf_op jit(solution)/shard_map/ppermute | solution.py:442
  35.1 5.1 %collective-permute-done.2.even_ref.odd_ref.refs_6_.refs_1_ = f32[520,256]{1,0:T(8,128)S(1)} collective-permute-done((f32[520,256]{1,0:T(8,128)S(1)}, f32[520,256]{1,0:T(8,128)S(1)}, u32[]{:S(2)}, u32[]{:S(2)}) %collective-permute-start.2) | collective-permute-done | bytes 532512 | tf_op jit(solution)/shard_map/ppermute | solution.py:442
  40.2 1.0 %pick.11 = f32[520,256]{1,0:T(8,128)S(1)} custom-call(s32[6]{0:T(128)S(1)} %stack.27.info_ref.refs_2_.refs_1_, f32[8,4,128,128]{3,2,1,0:T(8,128)S(1)} %bitcast.23, f32[520,256]{1,0:T(8,128)S(1)} %collective-permute-done.2.even_ref.odd_ref.refs_6_.refs_1_, s32[4,8]{1,0:T(4,128)S(1)} %bitcast.35, s32[8,128]{1,0:T(8,128)S(1)} %get-tuple-element.46.refs_3_.refs_2_), custom_call_target="tpu_custom_call" | custom-call | bytes 1064960 | tf_op jit(solution)/shard_map/pick/pallas_call | solution.py:177
  41.3 1.4 %collective-permute-start.8 = (f32[520,256]{1,0:T(8,128)S(1)}, f32[520,256]{1,0:T(8,128)S(1)}, u32[]{:S(2)}, u32[]{:S(2)}) collective-permute-start(f32[520,256]{1,0:T(8,128)S(1)} %pick.11), channel_id=1, source_target_pairs={{0,24},{4,28},{8,0},{12,4},{16,8},{20,12},{24,16},{28,20},{1,25},{... | collective-permute-start | bytes 1597448 | tf_op jit(solution)/shard_map/ppermute | solution.py:439
  42.6 1.2 %collective-permute-done.rows_ref = s32[3,2,8]{2,1,0:T(2,128)S(1)} collective-permute-done((s32[3,2,8]{2,1,0:T(2,128)S(1)}, s32[3,2,8]{2,1,0:T(2,128)S(1)}, u32[]{:S(2)}, u32[]{:S(2)}) %collective-permute-start) | collective-permute-done | bytes 224 | tf_op jit(solution)/shard_map/ppermute | solution.py:465
  43.8 2.0 %panel_places.3.refs_0_ = s32[64]{0:T(128)S(1)} custom-call(s32[6]{0:T(128)S(1)} %stack.27.info_ref.refs_2_.refs_1_, s32[64]{0:T(128)S(1)} %get-tuple-element.38.table_ref, s32[3,2,8]{2,1,0:T(2,128)S(1)} %collective-permute-done.rows_ref, f32[520,256]{1,0:T(8,128)S(1)} %collective-permute-done.2.even_ref.odd_ref.refs_6_.refs_1_, ...), custom_call_target="tpu_custom_call" | custom-call | tf_op jit(solution)/shard_map/panel_places/pallas_call | solution.py:376
  45.7 2.1 %accumulate.12 = (f32[25,128,128]{2,1,0:T(8,128)S(1)}, f32[25,128,128]{2,1,0:T(8,128)S(1)}, f32[25,128,128]{2,1,0:T(8,128)S(1)}, s32[8,128]{1,0:T(8,128)S(1)}) custom-call(s32[6]{0:T(128)S(1)} %stack.27.info_ref.refs_2_.refs_1_, s32[64]{0:T(128)S(1)} %panel_places.3.refs_0_, ...), custom_call_target="tpu_custom_call", output_to_operand_aliasing={{0}: (8, {}), {1}: (9, {}), {2}: (10, {})} | custom-call | flops 603979776 | bytes 3145728 | tf_op jit(solution)/shard_map/accumulate/pallas_call | solution.py:311
  47.9 0.6 pick.10
  48.6 2.2 %collective-permute-done.9.refs_5_.refs_1_ = f32[512,256]{1,0:T(8,128)S(1)} collective-permute-done((f32[512,256]{1,0:T(8,128)S(1)}, f32[512,256]{1,0:T(8,128)S(1)}, u32[]{:S(2)}, u32[]{:S(2)}) %collective-permute-start.9) | collective-permute-done | bytes 524320 | tf_op jit(solution)/shard_map/ppermute | solution.py:442
  51.4 2.1 %collective-permute-start.11 = (f32[512,256]{1,0:T(8,128)S(1)}, f32[512,256]{1,0:T(8,128)S(1)}, u32[]{:S(2)}, u32[]{:S(2)}) collective-permute-start(f32[512,256]{1,0:T(8,128)S(1)} %pick.14), channel_id=1, source_target_pairs={{0,24},{4,28},{8,0},{12,4},{16,8},{20,12},{24,16},{28,20},{1,25},{... | collective-permute-start | bytes 1572872 | tf_op jit(solution)/shard_map/ppermute | solution.py:439
  53.4 1.7 %accumulate.13 = (f32[25,128,128]{2,1,0:T(8,128)S(1)}, f32[25,128,128]{2,1,0:T(8,128)S(1)}, s32[8,128]{1,0:T(8,128)S(1)}) custom-call(s32[6]{0:T(128)S(1)} %stack.27.info_ref.refs_2_.refs_1_, s32[64]{0:T(128)S(1)} %panel_places.3.refs_0_, s32[64]{0:T(128)S(1)} %panel_places.4.refs_0_.refs_1_, ...), custom_call_target="tpu_custom_call", output_to_operand_aliasing={{0}: (7, {}), {1}: (8, {})} | custom-call | flops 402653184 | bytes 2097152 | tf_op jit(solution)/shard_map/accumulate/pallas_call | solution.py:311
  55.1 0.6 pick.13
  55.7 1.6 %collective-permute-start.10 = (f32[512,256]{1,0:T(8,128)S(1)}, f32[512,256]{1,0:T(8,128)S(1)}, u32[]{:S(2)}, u32[]{:S(2)}) collective-permute-start(f32[512,256]{1,0:T(8,128)S(1)} %pick.13), channel_id=1, source_target_pairs={{0,4},{4,0},{8,12},{12,8},{16,20},{20,16},{24,28},{28,24},{1,5},{5... | collective-permute-start | bytes 1572872 | tf_op jit(solution)/shard_map/ppermute | solution.py:442
  57.3 6.2 %collective-permute-done.7.even_ref.refs_8_.refs_1_ = f32[520,256]{1,0:T(8,128)S(1)} collective-permute-done((f32[520,256]{1,0:T(8,128)S(1)}, f32[520,256]{1,0:T(8,128)S(1)}, u32[]{:S(2)}, u32[]{:S(2)}) %collective-permute-start.7) | collective-permute-done | bytes 532512 | tf_op jit(solution)/shard_map/ppermute | solution.py:442
  64.1 0.7 collective-permute-start.12
  64.8 2.0 %panel_places.5.refs_2_.refs_0_.refs_1_ = s32[64]{0:T(128)S(1)} custom-call(s32[6]{0:T(128)S(1)} %stack.27.info_ref.refs_2_.refs_1_, s32[64]{0:T(128)S(1)} %get-tuple-element.38.table_ref, s32[3,2,8]{2,1,0:T(2,128)S(1)} %collective-permute-done.rows_ref, f32[520,256]{1,0:T(8,128)S(1)} %collective-permute-done.7.even_ref.refs_8_.refs_1_, ...), custom_call_target="tpu_custom_call" | custom-call | tf_op jit(solution)/shard_map/panel_places/pallas_call | solution.py:376
  66.8 1.9 %accumulate.14 = (f32[25,128,128]{2,1,0:T(8,128)S(1)}, f32[25,128,128]{2,1,0:T(8,128)S(1)}, f32[25,128,128]{2,1,0:T(8,128)S(1)}, s32[8,128]{1,0:T(8,128)S(1)}) custom-call(s32[6]{0:T(128)S(1)} %stack.27.info_ref.refs_2_.refs_1_, s32[64]{0:T(128)S(1)} %panel_places.3.refs_0_, ...), custom_call_target="tpu_custom_call", output_to_operand_aliasing={{0}: (10, {}), {1}: (11, {}), {2}: (12, {})} | custom-call | flops 402653184 | bytes 2097152 | tf_op jit(solution)/shard_map/accumulate/pallas_call | solution.py:311
  68.7 0.6 pick.17
  69.3 1.8 %collective-permute-start.14 = (f32[512,256]{1,0:T(8,128)S(1)}, f32[512,256]{1,0:T(8,128)S(1)}, u32[]{:S(2)}, u32[]{:S(2)}) collective-permute-start(f32[512,256]{1,0:T(8,128)S(1)} %pick.17), channel_id=1, source_target_pairs={{0,4},{4,0},{8,12},{12,8},{16,20},{20,16},{24,28},{28,24},{1,5},{5... | collective-permute-start | bytes 1572872 | tf_op jit(solution)/shard_map/ppermute | solution.py:442
  71.0 1.5 %accumulate.15 = (f32[25,128,128]{2,1,0:T(8,128)S(1)}, f32[25,128,128]{2,1,0:T(8,128)S(1)}, s32[8,128]{1,0:T(8,128)S(1)}) custom-call(s32[6]{0:T(128)S(1)} %stack.27.info_ref.refs_2_.refs_1_, s32[64]{0:T(128)S(1)} %panel_places.5.refs_2_.refs_0_.refs_1_, ...), custom_call_target="tpu_custom_call", output_to_operand_aliasing={{0}: (5, {}), {1}: (6, {})} | custom-call | flops 201326592 | bytes 1048576 | tf_op jit(solution)/shard_map/accumulate/pallas_call | solution.py:311
  72.6 2.2 %collective-permute-done.10.refs_4_.refs_0_.refs_1_ = f32[512,256]{1,0:T(8,128)S(1)} collective-permute-done((f32[512,256]{1,0:T(8,128)S(1)}, f32[512,256]{1,0:T(8,128)S(1)}, u32[]{:S(2)}, u32[]{:S(2)}) %collective-permute-start.10) | collective-permute-done | bytes 524320 | tf_op jit(solution)/shard_map/ppermute | solution.py:442
  75.3 0.7 collective-permute-start.13
  76.1 2.1 %accumulate.16 = (f32[25,128,128]{2,1,0:T(8,128)S(1)}, f32[25,128,128]{2,1,0:T(8,128)S(1)}, s32[8,128]{1,0:T(8,128)}, f32[6,128,128]{2,1,0:T(8,128)S(1)}, f32[6,128,128]{2,1,0:T(8,128)S(1)}) custom-call(s32[6]{0:T(128)S(1)} %stack.27.info_ref.refs_2_.refs_1_, s32[64]{0:T(128)S(1)} %panel_places.3.refs_0_, ...), custom_call_target="tpu_custom_call", output_to_operand_aliasing={{0}: (6, {}), {1}: (7, {})} | custom-call | flops 201326592 | bytes 1048576 | tf_op jit(solution)/shard_map/accumulate/pallas_call | solution.py:311
  78.2 1.5 %collective-permute-start.15 = (f32[6,128,128]{2,1,0:T(8,128)S(1)}, f32[6,128,128]{2,1,0:T(8,128)S(1)}, u32[]{:S(2)}, u32[]{:S(2)}) collective-permute-start(f32[6,128,128]{2,1,0:T(8,128)S(1)} %get-tuple-element.68), channel_id=1, source_target_pairs={{0,1},{1,0},{2,3},{3,2},{4,5},{5,4},{6,7},{7,6},{8,9},{9,8},{10,11... | collective-permute-start | bytes 1179656 | tf_op jit(solution)/shard_map/ppermute | solution.py:514
  79.7 2.5 %accumulate.17 = (f32[25,128,128]{2,1,0:T(8,128)S(1)}, f32[25,128,128]{2,1,0:T(8,128)S(1)}, s32[8,128]{1,0:T(8,128)}, f32[3,128,128]{2,1,0:T(8,128)S(1)}, f32[3,128,128]{2,1,0:T(8,128)S(1)}) custom-call(s32[6]{0:T(128)S(1)} %stack.27.info_ref.refs_2_.refs_1_, ...), custom_call_target="tpu_custom_call", output_to_operand_aliasing={{0}: (5, {}), {1}: (6, {})} | custom-call | flops 201326592 | bytes 1048576 | tf_op jit(solution)/shard_map/accumulate/pallas_call | solution.py:311
  82.7 2.5 %collective-permute-done.14.refs_6_.refs_7_ = f32[512,256]{1,0:T(8,128)S(1)} collective-permute-done((f32[512,256]{1,0:T(8,128)S(1)}, f32[512,256]{1,0:T(8,128)S(1)}, u32[]{:S(2)}, u32[]{:S(2)}) %collective-permute-start.14) | collective-permute-done | bytes 524320 | tf_op jit(solution)/shard_map/ppermute | solution.py:442
  85.2 2.0 %accumulate.18 = (f32[25,128,128]{2,1,0:T(8,128)S(1)}, f32[25,128,128]{2,1,0:T(8,128)S(1)}, s32[8,128]{1,0:T(8,128)}) custom-call(s32[6]{0:T(128)S(1)} %stack.27.info_ref.refs_2_.refs_1_, s32[64]{0:T(128)S(1)} %panel_places.3.refs_0_, s32[64]{0:T(128)S(1)} %panel_places.4.refs_0_.refs_1_, ...), custom_call_target="tpu_custom_call", output_to_operand_aliasing={{0}: (9, {}), {1}: (10, {})} | custom-call | tf_op jit(solution)/shard_map/accumulate/pallas_call | solution.py:311
  87.8 2.0 %accumulate.19 = (f32[25,128,128]{2,1,0:T(8,128)S(1)}, f32[25,128,128]{2,1,0:T(8,128)S(1)}, s32[8,128]{1,0:T(8,128)}, f32[3,128,128]{2,1,0:T(8,128)S(1)}, f32[3,128,128]{2,1,0:T(8,128)S(1)}) custom-call(s32[6]{0:T(128)S(1)} %stack.27.info_ref.refs_2_.refs_1_, ...), custom_call_target="tpu_custom_call", output_to_operand_aliasing={{0}: (4, {}), {1}: (5, {})} | custom-call | tf_op jit(solution)/shard_map/accumulate/pallas_call | solution.py:311
  89.8 1.5 %collective-permute-start.17 = (f32[3,128,128]{2,1,0:T(8,128)S(1)}, f32[3,128,128]{2,1,0:T(8,128)S(1)}, u32[]{:S(2)}, u32[]{:S(2)}) collective-permute-start(f32[3,128,128]{2,1,0:T(8,128)S(1)} %get-tuple-element.70), channel_id=1, source_target_pairs={{0,1},{1,0},{2,3},{3,2},{4,5},{5,4},{6,7},{7,6},{8,9},{9,8},{10,11... | collective-permute-start | bytes 589832 | tf_op jit(solution)/shard_map/ppermute | solution.py:514
  91.3 2.2 %collective-permute-done.16.refs_4_ = f32[3,128,128]{2,1,0:T(8,128)S(1)} collective-permute-done((f32[3,128,128]{2,1,0:T(8,128)S(1)}, f32[3,128,128]{2,1,0:T(8,128)S(1)}, u32[]{:S(2)}, u32[]{:S(2)}) %collective-permute-start.16) | collective-permute-done | bytes 196640 | tf_op jit(solution)/shard_map/ppermute | solution.py:514
  93.6 3.1 %collective-permute-done.17.refs_5_ = f32[3,128,128]{2,1,0:T(8,128)S(1)} collective-permute-done((f32[3,128,128]{2,1,0:T(8,128)S(1)}, f32[3,128,128]{2,1,0:T(8,128)S(1)}, u32[]{:S(2)}, u32[]{:S(2)}) %collective-permute-start.17) | collective-permute-done | bytes 196640 | tf_op jit(solution)/shard_map/ppermute | solution.py:514
  96.7 1.9 %combine.1 = f32[12,128,128]{2,1,0:T(8,128)} custom-call(s32[6]{0:T(128)S(1)} %stack.27.info_ref.refs_2_.refs_1_, f32[6,128,128]{2,1,0:T(8,128)S(1)} %get-tuple-element.57.refs_0_, f32[3,128,128]{2,1,0:T(8,128)S(1)} %get-tuple-element.60.refs_1_, f32[3,128,128]{2,1,0:T(8,128)S(1)} %get-tuple-element.67.refs_2_, ...), custom_call_target="tpu_custom_call" | custom-call | tf_op jit(solution)/shard_map/combine/pallas_call | solution.py:411
  (31 shorter events, 4.9 us)
Async XLA Ops:
  0.0 45.7 %collective-permute-start.5 = (f32[3,8,2,128,128]{4,3,2,1,0:T(8,128)}, f32[3,8,2,128,128]{4,3,2,1,0:T(8,128)S(1)}, u32[]{:S(2)}, u32[]{:S(2)}) collective-permute-start(f32[3,8,2,128,128]{4,3,2,1,0:T(8,128)} %bitcast.25), channel_id=1, source_target_pairs={{0,2},{2,0},{1,3},{3,1},{4,6},{6,4},{5,7},{7,5},{8,10},{10,8},{9,1... | collective-permute-start | bytes 9437192 | tf_op jit(solution)/shard_map/ppermute | solution.py:465
  0.5 1.6 %copy-start = (f32[1,1,1,8,4,128,128]{6,5,4,3,2,1,0:T(8,128)S(1)}, f32[1,1,1,8,4,128,128]{6,5,4,3,2,1,0:T(8,128)}, u32[]{:S(2)}) copy-start(f32[1,1,1,8,4,128,128]{6,5,4,3,2,1,0:T(8,128)} %param.7) | copy-start | bytes 6291460
  2.1 0.7 copy-start.3
  2.8 4.9 %copy-start.1 = (f32[1,1,1,8,4,128,128]{6,5,4,3,2,1,0:T(8,128)S(1)}, f32[1,1,1,8,4,128,128]{6,5,4,3,2,1,0:T(8,128)}, u32[]{:S(2)}) copy-start(f32[1,1,1,8,4,128,128]{6,5,4,3,2,1,0:T(8,128)} %param.7) | copy-start | bytes 6291460
  2.8 8.6 %copy-start.2 = (f32[1,1,1,3,8,2,128,128]{7,6,5,4,3,2,1,0:T(8,128)S(1)}, f32[1,1,1,3,8,2,128,128]{7,6,5,4,3,2,1,0:T(8,128)}, u32[]{:S(2)}) copy-start(f32[1,1,1,3,8,2,128,128]{7,6,5,4,3,2,1,0:T(8,128)} %param.5) | copy-start | bytes 9437188
  3.0 6.9 %copy-start.5 = (s32[1,1,1,3,8,2]{4,5,3,2,1,0:T(2,128)S(1)}, s32[1,1,1,3,8,2]{4,5,3,2,1,0:T(2,128)}, u32[]{:S(2)}) copy-start(s32[1,1,1,3,8,2]{4,5,3,2,1,0:T(2,128)} %param.6) | copy-start | bytes 580
  3.0 6.9 %copy-start.6 = (s32[1,1,24]{2,1,0:T(1,128)S(1)}, s32[1,1,24]{2,1,0:T(1,128)}, u32[]{:S(2)}) copy-start(s32[1,1,24]{2,1,0:T(1,128)} %param.9) | copy-start | bytes 292
  3.0 17.1 %collective-permute-start.1 = (f32[520,256]{1,0:T(8,128)S(1)}, f32[520,256]{1,0:T(8,128)S(1)}, u32[]{:S(2)}, u32[]{:S(2)}) collective-permute-start(f32[520,256]{1,0:T(8,128)S(1)} %own_quarters.4), channel_id=1, source_target_pairs={{0,24},{4,28},{8,0},{12,4},{16,8},{20,12},{24,16},{28,20},{1,25},{... | collective-permute-start | bytes 1597448 | tf_op jit(solution)/shard_map/ppermute | solution.py:439
  8.4 20.4 %collective-permute-start.3 = (f32[768,256]{1,0:T(8,128)S(1)}, f32[768,256]{1,0:T(8,128)S(1)}, u32[]{:S(2)}, u32[]{:S(2)}) collective-permute-start(f32[768,256]{1,0:T(8,128)S(1)} %own_quarters.5), channel_id=1, source_target_pairs={{0,4},{4,0},{8,12},{12,8},{16,20},{20,16},{24,28},{28,24},{1,5},{5... | collective-permute-start | bytes 2359304 | tf_op jit(solution)/shard_map/ppermute | solution.py:442
  14.1 6.0 %copy-start.4 = (s32[1,1,1,8,4]{3,4,2,1,0:T(4,128)S(1)}, s32[1,1,1,8,4]{3,4,2,1,0:T(4,128)}, u32[]{:S(2)}) copy-start(s32[1,1,1,8,4]{3,4,2,1,0:T(4,128)} %param.8) | copy-start | bytes 388
  14.3 17.0 %collective-permute-start.6 = (f32[512,256]{1,0:T(8,128)S(1)}, f32[512,256]{1,0:T(8,128)S(1)}, u32[]{:S(2)}, u32[]{:S(2)}) collective-permute-start(f32[512,256]{1,0:T(8,128)S(1)} %own_quarters.7), channel_id=1, source_target_pairs={{0,24},{4,28},{8,0},{12,4},{16,8},{20,12},{24,16},{28,20},{1,25},{... | collective-permute-start | bytes 1572872 | tf_op jit(solution)/shard_map/ppermute | solution.py:439
  20.7 19.5 %collective-permute-start.2 = (f32[520,256]{1,0:T(8,128)S(1)}, f32[520,256]{1,0:T(8,128)S(1)}, u32[]{:S(2)}, u32[]{:S(2)}) collective-permute-start(f32[520,256]{1,0:T(8,128)S(1)} %pick.9), channel_id=1, source_target_pairs={{0,4},{4,0},{8,12},{12,8},{16,20},{20,16},{24,28},{28,24},{1,5},{5... | collective-permute-start | bytes 1597448 | tf_op jit(solution)/shard_map/ppermute | solution.py:442
  29.3 18.6 %collective-permute-start.4 = (f32[512,256]{1,0:T(8,128)S(1)}, f32[512,256]{1,0:T(8,128)S(1)}, u32[]{:S(2)}, u32[]{:S(2)}) collective-permute-start(f32[512,256]{1,0:T(8,128)S(1)} %own_quarters.6), channel_id=1, source_target_pairs={{0,24},{4,28},{8,0},{12,4},{16,8},{20,12},{24,16},{28,20},{1,25},{... | collective-permute-start | bytes 1572872 | tf_op jit(solution)/shard_map/ppermute | solution.py:439
  33.4 17.3 %collective-permute-start.9 = (f32[512,256]{1,0:T(8,128)S(1)}, f32[512,256]{1,0:T(8,128)S(1)}, u32[]{:S(2)}, u32[]{:S(2)}) collective-permute-start(f32[512,256]{1,0:T(8,128)S(1)} %pick.12), channel_id=1, source_target_pairs={{0,4},{4,0},{8,12},{12,8},{16,20},{20,16},{24,28},{28,24},{1,5},{5... | collective-permute-start | bytes 1572872 | tf_op jit(solution)/shard_map/ppermute | solution.py:442
  41.3 13.9 %collective-permute-start.8 = (f32[520,256]{1,0:T(8,128)S(1)}, f32[520,256]{1,0:T(8,128)S(1)}, u32[]{:S(2)}, u32[]{:S(2)}) collective-permute-start(f32[520,256]{1,0:T(8,128)S(1)} %pick.11), channel_id=1, source_target_pairs={{0,24},{4,28},{8,0},{12,4},{16,8},{20,12},{24,16},{28,20},{1,25},{... | collective-permute-start | bytes 1597448 | tf_op jit(solution)/shard_map/ppermute | solution.py:439
  42.6 1.2 %collective-permute-start = (s32[3,2,8]{2,1,0:T(2,128)S(1)}, s32[3,2,8]{2,1,0:T(2,128)S(1)}, u32[]{:S(2)}, u32[]{:S(2)}) collective-permute-start(s32[3,2,8]{2,1,0:T(2,128)S(1)} %bitcast.39), channel_id=1, source_target_pairs={{0,2},{2,0},{1,3},{3,1},{4,6},{6,4},{5,7},{7,5},{8,10},{10,8},{9,1... | collective-permute-start | bytes 584 | tf_op jit(solution)/shard_map/ppermute | solution.py:465
  48.5 15.0 %collective-permute-start.7 = (f32[520,256]{1,0:T(8,128)S(1)}, f32[520,256]{1,0:T(8,128)S(1)}, u32[]{:S(2)}, u32[]{:S(2)}) collective-permute-start(f32[520,256]{1,0:T(8,128)S(1)} %pick.10), channel_id=1, source_target_pairs={{0,4},{4,0},{8,12},{12,8},{16,20},{20,16},{24,28},{28,24},{1,5},{5... | collective-permute-start | bytes 1597448 | tf_op jit(solution)/shard_map/ppermute | solution.py:442
  51.4 17.3 %collective-permute-start.11 = (f32[512,256]{1,0:T(8,128)S(1)}, f32[512,256]{1,0:T(8,128)S(1)}, u32[]{:S(2)}, u32[]{:S(2)}) collective-permute-start(f32[512,256]{1,0:T(8,128)S(1)} %pick.14), channel_id=1, source_target_pairs={{0,24},{4,28},{8,0},{12,4},{16,8},{20,12},{24,16},{28,20},{1,25},{... | collective-permute-start | bytes 1572872 | tf_op jit(solution)/shard_map/ppermute | solution.py:439
  55.7 19.0 %collective-permute-start.10 = (f32[512,256]{1,0:T(8,128)S(1)}, f32[512,256]{1,0:T(8,128)S(1)}, u32[]{:S(2)}, u32[]{:S(2)}) collective-permute-start(f32[512,256]{1,0:T(8,128)S(1)} %pick.13), channel_id=1, source_target_pairs={{0,4},{4,0},{8,12},{12,8},{16,20},{20,16},{24,28},{28,24},{1,5},{5... | collective-permute-start | bytes 1572872 | tf_op jit(solution)/shard_map/ppermute | solution.py:442
  64.1 15.6 %collective-permute-start.12 = (f32[512,256]{1,0:T(8,128)S(1)}, f32[512,256]{1,0:T(8,128)S(1)}, u32[]{:S(2)}, u32[]{:S(2)}) collective-permute-start(f32[512,256]{1,0:T(8,128)S(1)} %pick.15), channel_id=1, source_target_pairs={{0,24},{4,28},{8,0},{12,4},{16,8},{20,12},{24,16},{28,20},{1,25},{... | collective-permute-start | bytes 1572872 | tf_op jit(solution)/shard_map/ppermute | solution.py:439
  69.3 15.9 %collective-permute-start.14 = (f32[512,256]{1,0:T(8,128)S(1)}, f32[512,256]{1,0:T(8,128)S(1)}, u32[]{:S(2)}, u32[]{:S(2)}) collective-permute-start(f32[512,256]{1,0:T(8,128)S(1)} %pick.17), channel_id=1, source_target_pairs={{0,4},{4,0},{8,12},{12,8},{16,20},{20,16},{24,28},{28,24},{1,5},{5... | collective-permute-start | bytes 1572872 | tf_op jit(solution)/shard_map/ppermute | solution.py:442
  75.3 12.4 %collective-permute-start.13 = (f32[512,256]{1,0:T(8,128)S(1)}, f32[512,256]{1,0:T(8,128)S(1)}, u32[]{:S(2)}, u32[]{:S(2)}) collective-permute-start(f32[512,256]{1,0:T(8,128)S(1)} %pick.16), channel_id=1, source_target_pairs={{0,24},{4,28},{8,0},{12,4},{16,8},{20,12},{24,16},{28,20},{1,25},{... | collective-permute-start | bytes 1572872 | tf_op jit(solution)/shard_map/ppermute | solution.py:439
  78.2 13.2 %collective-permute-start.15 = (f32[6,128,128]{2,1,0:T(8,128)S(1)}, f32[6,128,128]{2,1,0:T(8,128)S(1)}, u32[]{:S(2)}, u32[]{:S(2)}) collective-permute-start(f32[6,128,128]{2,1,0:T(8,128)S(1)} %get-tuple-element.68), channel_id=1, source_target_pairs={{0,1},{1,0},{2,3},{3,2},{4,5},{5,4},{6,7},{7,6},{8,9},{9,8},{10,11... | collective-permute-start | bytes 1179656 | tf_op jit(solution)/shard_map/ppermute | solution.py:514
  82.2 11.4 %collective-permute-start.16 = (f32[3,128,128]{2,1,0:T(8,128)S(1)}, f32[3,128,128]{2,1,0:T(8,128)S(1)}, u32[]{:S(2)}, u32[]{:S(2)}) collective-permute-start(f32[3,128,128]{2,1,0:T(8,128)S(1)} %get-tuple-element.69), channel_id=1, source_target_pairs={{0,1},{1,0},{2,3},{3,2},{4,5},{5,4},{6,7},{7,6},{8,9},{9,8},{10,11... | collective-permute-start | bytes 589832 | tf_op jit(solution)/shard_map/ppermute | solution.py:514
  89.8 6.8 %collective-permute-start.17 = (f32[3,128,128]{2,1,0:T(8,128)S(1)}, f32[3,128,128]{2,1,0:T(8,128)S(1)}, u32[]{:S(2)}, u32[]{:S(2)}) collective-permute-start(f32[3,128,128]{2,1,0:T(8,128)S(1)} %get-tuple-element.70), channel_id=1, source_target_pairs={{0,1},{1,0},{2,3},{3,2},{4,5},{5,4},{6,7},{7,6},{8,9},{9,8},{10,11... | collective-permute-start | bytes 589832 | tf_op jit(solution)/shard_map/ppermute | solution.py:514

commit v10 on v9

--- a/solution.py
+++ b/solution.py
@@ -57,9 +57,17 @@
     return pltpu.roll(x, x.shape[-1] // 4 * (groups % 4), x.ndim - 1)
 
 
+def lane_group(shape):
+    return lax.broadcasted_iota(jnp.int32, shape, len(shape) - 1) // (shape[-1] // 4)
+
+
+def fold_half(group, one, two):
+    lower = group < 2
+    return jnp.where(lower, one, two) + swap_lanes(jnp.where(lower, two, one))
+
+
 def by_group(parts):
-    shape = parts[0].shape
-    group = lax.broadcasted_iota(jnp.int32, shape, len(shape) - 1) // (shape[-1] // 4)
+    group = lane_group(parts[0].shape)
     out = parts[3]
     for g in (2, 1, 0):
         out = jnp.where(group == g, parts[g], out)
@@ -134,6 +142,41 @@
         cost_estimate=pl.CostEstimate(flops=0, bytes_accessed=12 * out_shape.size, transcendentals=0),
         name="own_quarters",
     )(right, *extra, *others)
+
+
+def first_quarter(right, cols, *others):
+    rows, width = quarter_shape(right)
+    start, count = block_rows(right.shape[0], 0, 0, PARTS)
+
+    def kernel(right_ref, cols_ref, *refs):
+        out_ref, blocks_ref, small_ref, sems = refs[-4:]
+        copies = [
+            pltpu.make_async_copy(cols_ref, small_ref, sems.at[count]),
+            *(pltpu.make_async_copy(right_ref.at[start + n], blocks_ref.at[n], sems.at[n]) for n in range(count)),
+        ]
+        for copy in copies:
+            copy.start()
+        copies[0].wait()
+        put_extra(out_ref, small_ref, rows)
+        for n in range(count):
+            copies[1 + n].wait()
+            cut(blocks_ref, out_ref, 0, n * right.shape[2], n, 1)
+
+    in_hbm = pl.BlockSpec(memory_space=pltpu.HBM)
+    return pl.pallas_call(
+        kernel,
+        in_specs=[in_hbm] * 2 + [anywhere] * len(others),
+        out_specs=in_vmem,
+        out_shape=jax.ShapeDtypeStruct((rows + right.shape[0], width), right.dtype),
+        scratch_shapes=[
+            pltpu.VMEM((count,) + right.shape[1:], right.dtype),
+            pltpu.VMEM(cols.shape, cols.dtype),
+            pltpu.SemaphoreType.DMA((count + 1,)),
+        ],
+        compiler_params=pltpu.CompilerParams(vmem_limit_bytes=12 * 1024 * 1024),
+        cost_estimate=pl.CostEstimate(flops=0, bytes_accessed=12 * rows * width, transcendentals=0),
+        name="first_quarter",
+    )(*(pltpu.with_memory_space_constraint(x, pltpu.HBM) for x in (right, cols)), *others)
 
 
 def pick(info, right, cols, even_parts, odd_parts, *others):
@@ -255,16 +298,19 @@
                         at = b * lanes % bs
                         total_ref[n, :, at:at + lanes] += out[a * bs:(a + 1) * bs, b * lanes:(b + 1) * lanes]
 
-        def pack(total_ref, both_refs, quarters):
-            for kept, ref in enumerate(both_refs):
-                packed = ref.shape[0]
-                for p in range(packed):
-                    blocks = [total_ref[nc // 2 * kept + g * packed + p] for g in range(4 if quarters else 2)]
-                    blocks = [block + swap_lanes(block) for block in blocks]
-                    if quarters:
-                        ref[p] = by_group([block + move_lanes(block, 1) for block in blocks])
-                    else:
-                        ref[p] = jnp.where(lower_lanes((bs, bs)), *blocks)
+        def pack(total_ref, ref, quarters):
+            packed = ref.shape[0]
+            group = lane_group((bs, bs))
+            for p in range(packed):
+                blocks = [total_ref[nc // 2 + g * packed + p] for g in range(4 if quarters else 2)]
+                if not quarters:
+                    ref[p] = fold_half(group, *blocks)
+                    continue
+                one = fold_half(group, blocks[0], blocks[2])
+                two = fold_half(group, blocks[1], blocks[3])
+                even = group % 2 == 0
+                moved = jnp.where(even, two, one)
+                ref[p] = jnp.where(even, one + move_lanes(moved, 3), two + move_lanes(moved, 1))
 
         if own:
             add_own(left_refs[0, 0], right_refs[0])
@@ -278,10 +324,10 @@
             if both[1] is not None:
                 pl.when(odd != 0)(lambda c=c: add(c, 1))
         if finish is not None and finish[0] == finish[1]:
-            pack(total_refs[finish[0]], outs[1:], finish[0] > 0)
+            pack(total_refs[finish[0]], outs[1], finish[0] > 0)
         elif finish is not None:
-            pl.when(odd == 0)(lambda: pack(total_refs[finish[0]], outs[1:], True))
-            pl.when(odd != 0)(lambda: pack(total_refs[finish[1]], outs[1:], True))
+            pl.when(odd == 0)(lambda: pack(total_refs[finish[0]], outs[1], True))
+            pl.when(odd != 0)(lambda: pack(total_refs[finish[1]], outs[1], True))
 
     def left_spec(turn, *what):
         start, count = block_rows(kb, *what)
@@ -303,7 +349,7 @@
         in_specs += [in_vmem] * len(touched)
     outs = [jax.ShapeDtypeStruct((nc + 1, bs, bs), f32)] * len(touched) + [jax.ShapeDtypeStruct((8, 128), jnp.int32)]
     if finish is not None:
-        outs += [jax.ShapeDtypeStruct((nc // (8 if finish[0] else 4), bs, bs), f32)] * 2
+        outs.append(jax.ShapeDtypeStruct((nc // (8 if finish[0] else 4), bs, bs), f32))
     parts = QUARTERS if own else len(chunks)
     per = kb // HALVES
     flops = parts * per * 2 * lpb * bs * 3 * bs * width
@@ -385,25 +431,43 @@
     )(info, table, rows, *[array for array, _ in parts])
 
 
+def kept_blocks(totals, nc):
+    bs = totals[0].shape[-1]
+
+    def kernel(half_ref, third_ref, fourth_ref, out_ref):
+        for n in range(nc // 2):
+            half = half_ref[n]
+            upper = [ref[n] + swap_lanes(ref[n]) for ref in (third_ref, fourth_ref)]
+            half = half + swap_lanes(half)
+            out_ref[n] = by_group([half, half, *(x + move_lanes(x, 1) for x in upper)])
+
+    return pl.pallas_call(
+        kernel,
+        in_specs=[in_vmem] * 3,
+        out_specs=in_vmem,
+        out_shape=jax.ShapeDtypeStruct((nc // 2, bs, bs), f32),
+        compiler_params=pltpu.CompilerParams(vmem_limit_bytes=8 * 1024 * 1024),
+        cost_estimate=pl.CostEstimate(flops=0, bytes_accessed=0, transcendentals=0),
+        name="kept_blocks",
+    )(*totals)
+
+
 def combine(info, kept, other):
-    packed, bs, _ = kept[0].shape
-    packed_4 = kept[1].shape[0]
-
-    def kernel(info_ref, *refs):
-        out_ref = refs[-1]
+    packed, bs, _ = other[0].shape
+    packed_4 = other[1].shape[0]
+
+    def kernel(info_ref, kept_ref, half_ref, early_ref, late_ref, out_ref):
         even = info_ref[0] == 0
 
         def step(first):
             for n in range(packed):
                 p = first * packed + n
-                low = refs[0][n] + refs[3][n]
-                early = refs[1][p % packed_4] + refs[4][p % packed_4]
-                late = refs[2][p % packed_4] + refs[5][p % packed_4]
+                low = half_ref[n] if first == 0 else swap_lanes(half_ref[n])
+                early, late = early_ref[p % packed_4], late_ref[p % packed_4]
                 group = p // packed_4
                 third = move_lanes(jnp.where(even, late, early), 2 - group)
                 fourth = move_lanes(jnp.where(even, early, late), 3 - group)
-                low = low if first == 0 else swap_lanes(low)
-                out_ref[n] = by_group([low, low, third, fourth])
+                out_ref[n] = kept_ref[p] + by_group([low, low, third, fourth])
 
         for first in range(2):
             pl.when(pl.program_id(0) == first)(lambda first=first: step(first))
@@ -411,12 +475,12 @@
     return pl.pallas_call(
         kernel,
         grid=(2,),
-        in_specs=[in_smem] + [in_vmem] * 6,
+        in_specs=[in_smem] + [in_vmem] * 4,
         out_specs=pl.BlockSpec((packed, bs, bs), lambda g: (g, 0, 0)),
         out_shape=jax.ShapeDtypeStruct((2 * packed, bs, bs), f32),
         compiler_params=pltpu.CompilerParams(vmem_limit_bytes=8 * 1024 * 1024),
         name="combine",
-    )(info, *kept, *other)
+    )(info, kept, *other)
 
 
 def shards(left_values, left_rows, right_values, right_cols, result_slots):
@@ -457,7 +521,7 @@
         return (quarter, first, parts)
 
     small = (info,)
-    z[1] = along_z(own_quarters(right, [own_part(0)], cols, *small))
+    z[1] = along_z(first_quarter(right, cols, *small))
     x[1] = along_x(own_quarters(right, [own_part(3), own_part(2, 0, 1)], None, *small))
 
     shifts = sorted({turn % cols_n for turn in range(STEPS)})
@@ -513,14 +577,14 @@
     def to_partner(blocks):
         return lax.ppermute(blocks, "rep", [(0, 1), (1, 0)])
 
-    totals, done, *both_0 = add(totals, [along_x_part(6)], (0, 0))
-    other_0 = to_partner(both_0[1])
-    totals, done, *both_1 = add(totals, [along_z_part(6)], (2, 1))
-    other_1 = to_partner(both_1[1])
+    totals, done, send_0 = add(totals, [along_x_part(6)], (0, 0))
+    other_0 = to_partner(send_0)
+    totals, done, send_1 = add(totals, [along_z_part(6)], (2, 1))
+    other_1 = to_partner(send_1)
     totals, done = add(totals, [along_x_part(7), along_x_part(8)], cost=0)
-    totals, done, *both_2 = add(totals, [along_z_part(7)], (1, 2), 0)
-    other_2 = to_partner(both_2[1])
-    return combine(info, [both_0[0], both_1[0], both_2[0]], [other_0, other_1, other_2])[None, None]
+    totals, done, send_2 = add(totals, [along_z_part(7)], (1, 2), 0)
+    other_2 = to_partner(send_2)
+    return combine(info, kept_blocks(totals, nc), [other_0, other_1, other_2])[None, None]
 
 
 def solution(mesh):

time: 98.7 us -> 96.6 us (0.979)
  starting transfers between devices: 24.6 us -> 21.4 us
  local copies, waits for them, and re-layouts: 2.38 us -> 0.11 us
  waiting for transfers between devices: 34.7 us -> 36.7 us
  Pallas kernels: 36.6 us -> 37.8 us
    ppermute x7, starting transfers between devices: 12.2 us -> 7.51 us  [along_z(): return lax.ppermute(chunk, 'row', z_pairs)]
    pallas_call x1 -> x3, Pallas kernels: 1.88 us -> 4.76 us  [the longest x1 1.9 us: combine(): pl.pallas_call(kernel, grid=(2,), in_specs=[in_smem] + [in_vmem] * 4, out...]
    ppermute x7, waiting for transfers between devices: 5.62 us -> 8.29 us  [along_z(): return lax.ppermute(chunk, 'row', z_pairs)]
    unnamed x14 -> x10, local copies, waits for them, and re-layouts: 2.3 us -> 0.03 us
    ppermute x3, waiting for transfers between devices: 5.31 us -> 3.29 us  [to_partner(): return lax.ppermute(blocks, 'rep', [(0, 1), (1, 0)])]
    ppermute x6, starting transfers between devices: 8.37 us -> 9.94 us  [along_x(): return lax.ppermute(chunk, 'row', x_pairs)]
    pallas_call x10, Pallas kernels: 20.1 us -> 18.7 us  [accumulate(): pl.pallas_call(kernel, grid_spec=pltpu.PrefetchScalarGridSpec(num_scalar_...]
    ppermute x6, waiting for transfers between devices: 22.6 us -> 24 us  [along_x(): return lax.ppermute(chunk, 'row', x_pairs)]
  transfers between devices with their start and end apart: 18 -> 18, of which waited for: 12 -> 12; matrix products, arithmetic and copies ran while one was open for 0% -> 0% of each run, Pallas kernels for 35% -> 37%
where the time goes in v10:
time: 96.6 us; the launch traced here: 96.4 us
  Pallas kernels  37.8 us (39%)
  waiting for transfers between devices  36.7 us (38%)
  starting transfers between devices  21.4 us (22%)
    ppermute x6, waiting for transfers between devices, along_x(): return lax.ppermute(chunk, 'row', x_pairs)  24 us
    pallas_call x10, Pallas kernels, accumulate(): pl.pallas_call(kernel, grid_spec=pltpu.PrefetchScalarGridSpec(num_scalar_...  18.7 us
    ppermute x6, starting transfers between devices, along_x(): return lax.ppermute(chunk, 'row', x_pairs)  9.94 us
    ppermute x7, waiting for transfers between devices, along_z(): return lax.ppermute(chunk, 'row', z_pairs)  8.29 us
    ppermute x7, starting transfers between devices, along_z(): return lax.ppermute(chunk, 'row', z_pairs)  7.51 us
    pallas_call x3, Pallas kernels, panel_places(): pl.pallas_call(kernel, grid=(1,), in_specs=[in_smem] * 3 + [pl.BlockSpec(...  5.86 us
    pallas_call x9, Pallas kernels, pick(): pl.pallas_call(kernel, grid=(1,), in_specs=[in_smem] + [spec(part) for pa...  5.71 us
    ppermute x3, starting transfers between devices, to_partner(): return lax.ppermute(blocks, 'rep', [(0, 1), (1, 0)])  3.54 us
  transfers between devices with their start and end apart: 18, of which 12 were waited for; matrix products, arithmetic and copies ran while one was open for 0% of the time, Pallas kernels for 37%

profile of v10, /device:TPU:0, one launch (start us, length us, event | category | flops | bytes accessed | tf_op | source)
XLA Modules:
  0.0 96.4 jit_solution(5339194188576680301)
XLA Ops:
  0.5 1.6 %first_quarter.1 = f32[520,256]{1,0:T(8,128)S(1)} custom-call(f32[8,4,128,128]{3,2,1,0:T(8,128)} %bitcast.16, s32[4,8]{1,0:T(4,128)} %bitcast.32, s32[6]{0:T(128)S(1)} %stack.27.info_ref.refs_0_.refs_1_), custom_call_target="tpu_custom_call" | custom-call | bytes 1572864 | tf_op jit(solution)/shard_map/first_quarter/pallas_call | solution.py:166
  2.2 4.7 %collective-permute-start.1 = (f32[520,256]{1,0:T(8,128)S(1)}, f32[520,256]{1,0:T(8,128)S(1)}, u32[]{:S(2)}, u32[]{:S(2)}) collective-permute-start(f32[520,256]{1,0:T(8,128)S(1)} %first_quarter.1), channel_id=1, source_target_pairs={{0,24},{4,28},{8,0},{12,4},{16,8},{20,12},{24,16},{28,20},{1,25},{... | collective-permute-start | bytes 1597448 | tf_op jit(solution)/shard_map/ppermute | solution.py:503
  6.8 0.7 own_quarters.3
  7.5 1.6 %collective-permute-start.3 = (f32[768,256]{1,0:T(8,128)S(1)}, f32[768,256]{1,0:T(8,128)S(1)}, u32[]{:S(2)}, u32[]{:S(2)}) collective-permute-start(f32[768,256]{1,0:T(8,128)S(1)} %own_quarters.3), channel_id=1, source_target_pairs={{0,4},{4,0},{8,12},{12,8},{16,20},{20,16},{24,28},{28,24},{1,5},{5... | collective-permute-start | bytes 2359304 | tf_op jit(solution)/shard_map/ppermute | solution.py:506
  9.0 1.5 %own_places.1 = (s32[64]{0:T(128)S(1)}, s32[64]{0:T(128)S(1)}) custom-call(s32[6]{0:T(128)S(1)} %stack.27.info_ref.refs_0_.refs_1_, s32[24]{0:T(128)S(1)} %bitcast.40, s32[3,2,8]{2,1,0:T(2,128)S(1)} %bitcast.37, s32[4,8]{1,0:T(4,128)S(1)} %bitcast.33), custom_call_target="tpu_custom_call" | custom-call | tf_op jit(solution)/shard_map/own_places/pallas_call | solution.py:389
  10.5 2.7 %accumulate.10 = (f32[25,128,128]{2,1,0:T(8,128)S(1)}, f32[25,128,128]{2,1,0:T(8,128)S(1)}, f32[25,128,128]{2,1,0:T(8,128)S(1)}, s32[8,128]{1,0:T(8,128)S(1)}) custom-call(s32[6]{0:T(128)S(1)} %stack.27.info_ref.refs_0_.refs_1_, s32[64]{0:T(128)S(1)} %get-tuple-element.39.refs_0_, f32[3,8,2,128,128]{4,3,2,1,0:T(8,128)S(1)} %bitcast.26, ...), custom_call_target="tpu_custom_call" | custom-call | flops 805306368 | bytes 4194304 | tf_op jit(solution)/shard_map/accumulate/pallas_call | solution.py:357
  14.0 5.3 %collective-permute-done.1.refs_0_.refs_1_.even_ref.odd_ref.refs_3_ = f32[520,256]{1,0:T(8,128)S(1)} collective-permute-done((f32[520,256]{1,0:T(8,128)S(1)}, f32[520,256]{1,0:T(8,128)S(1)}, u32[]{:S(2)}, u32[]{:S(2)}) %collective-permute-start.1) | collective-permute-done | bytes 532512 | tf_op jit(solution)/shard_map/ppermute | solution.py:503
  19.2 0.6 pick.9
  19.8 1.7 %collective-permute-start.2 = (f32[520,256]{1,0:T(8,128)S(1)}, f32[520,256]{1,0:T(8,128)S(1)}, u32[]{:S(2)}, u32[]{:S(2)}) collective-permute-start(f32[520,256]{1,0:T(8,128)S(1)} %pick.9), channel_id=1, source_target_pairs={{0,4},{4,0},{8,12},{12,8},{16,20},{20,16},{24,28},{28,24},{1,5},{5... | collective-permute-start | bytes 1597448 | tf_op jit(solution)/shard_map/ppermute | solution.py:506
  21.5 2.0 %panel_places.4.refs_0_.refs_1_ = s32[64]{0:T(128)S(1)} custom-call(s32[6]{0:T(128)S(1)} %stack.27.info_ref.refs_0_.refs_1_, s32[64]{0:T(128)S(1)} %get-tuple-element.38.table_ref, s32[3,2,8]{2,1,0:T(2,128)S(1)} %bitcast.38, f32[520,256]{1,0:T(8,128)S(1)} %collective-permute-done.1.refs_0_.refs_1_.even_ref.odd_ref.refs_3_, ...), custom_call_target="tpu_custom_call" | custom-call | tf_op jit(solution)/shard_map/panel_places/pallas_call | solution.py:422
  23.5 4.4 %collective-permute-done.3.refs_2_.refs_4_.refs_5_.refs_0_ = f32[768,256]{1,0:T(8,128)S(1)} collective-permute-done((f32[768,256]{1,0:T(8,128)S(1)}, f32[768,256]{1,0:T(8,128)S(1)}, u32[]{:S(2)}, u32[]{:S(2)}) %collective-permute-start.3) | collective-permute-done | bytes 786464 | tf_op jit(solution)/shard_map/ppermute | solution.py:506
  28.9 1.6 %collective-permute-done.6.refs_4_.refs_0_.refs_1_ = f32[512,256]{1,0:T(8,128)S(1)} collective-permute-done((f32[512,256]{1,0:T(8,128)S(1)}, f32[512,256]{1,0:T(8,128)S(1)}, u32[]{:S(2)}, u32[]{:S(2)}) %collective-permute-start.6) | collective-permute-done | bytes 524320 | tf_op jit(solution)/shard_map/ppermute | solution.py:503
  30.5 1.5 %accumulate.11 = (f32[25,128,128]{2,1,0:T(8,128)S(1)}, s32[8,128]{1,0:T(8,128)S(1)}) custom-call(s32[6]{0:T(128)S(1)} %stack.27.info_ref.refs_0_.refs_1_, s32[64]{0:T(128)S(1)} %panel_places.4.refs_0_.refs_1_, f32[3,8,2,128,128]{4,3,2,1,0:T(8,128)S(1)} %bitcast.27, f32[3,8,2,128,128]{4,3,2,1,0:T(8,128)S(1)} %bitcast.28, ...), custom_call_target="tpu_custom_call", output_to_operand_aliasing={{0}: (6, {})} | custom-call | flops 402653184 | bytes 2097152 | tf_op jit(solution)/shard_map/accumulate/pallas_call | solution.py:357
  31.9 0.6 pick.12
  32.5 1.7 %collective-permute-start.9 = (f32[512,256]{1,0:T(8,128)S(1)}, f32[512,256]{1,0:T(8,128)S(1)}, u32[]{:S(2)}, u32[]{:S(2)}) collective-permute-start(f32[512,256]{1,0:T(8,128)S(1)} %pick.12), channel_id=1, source_target_pairs={{0,4},{4,0},{8,12},{12,8},{16,20},{20,16},{24,28},{28,24},{1,5},{5... | collective-permute-start | bytes 1572872 | tf_op jit(solution)/shard_map/ppermute | solution.py:506
  34.2 5.1 %collective-permute-done.2.even_ref.odd_ref.refs_6_.refs_1_ = f32[520,256]{1,0:T(8,128)S(1)} collective-permute-done((f32[520,256]{1,0:T(8,128)S(1)}, f32[520,256]{1,0:T(8,128)S(1)}, u32[]{:S(2)}, u32[]{:S(2)}) %collective-permute-start.2) | collective-permute-done | bytes 532512 | tf_op jit(solution)/shard_map/ppermute | solution.py:506
  39.3 1.0 %pick.11 = f32[520,256]{1,0:T(8,128)S(1)} custom-call(s32[6]{0:T(128)S(1)} %stack.27.info_ref.refs_0_.refs_1_, f32[8,4,128,128]{3,2,1,0:T(8,128)S(1)} %bitcast.23, f32[520,256]{1,0:T(8,128)S(1)} %collective-permute-done.2.even_ref.odd_ref.refs_6_.refs_1_, s32[4,8]{1,0:T(4,128)S(1)} %bitcast.35, s32[8,128]{1,0:T(8,128)S(1)} %get-tuple-element.46.refs_3_.refs_2_), custom_call_target="tpu_custom_call" | custom-call | bytes 1064960 | tf_op jit(solution)/shard_map/pick/pallas_call | solution.py:220
  40.5 1.2 %collective-permute-done.rows_ref = s32[3,2,8]{2,1,0:T(2,128)S(1)} collective-permute-done((s32[3,2,8]{2,1,0:T(2,128)S(1)}, s32[3,2,8]{2,1,0:T(2,128)S(1)}, u32[]{:S(2)}, u32[]{:S(2)}) %collective-permute-start) | collective-permute-done | bytes 224 | tf_op jit(solution)/shard_map/ppermute | solution.py:529
  41.7 2.0 %panel_places.3.refs_0_ = s32[64]{0:T(128)S(1)} custom-call(s32[6]{0:T(128)S(1)} %stack.27.info_ref.refs_0_.refs_1_, s32[64]{0:T(128)S(1)} %get-tuple-element.38.table_ref, s32[3,2,8]{2,1,0:T(2,128)S(1)} %collective-permute-done.rows_ref, f32[520,256]{1,0:T(8,128)S(1)} %collective-permute-done.2.even_ref.odd_ref.refs_6_.refs_1_, ...), custom_call_target="tpu_custom_call" | custom-call | tf_op jit(solution)/shard_map/panel_places/pallas_call | solution.py:422
  43.7 2.2 %accumulate.12 = (f32[25,128,128]{2,1,0:T(8,128)S(1)}, f32[25,128,128]{2,1,0:T(8,128)S(1)}, f32[25,128,128]{2,1,0:T(8,128)S(1)}, s32[8,128]{1,0:T(8,128)S(1)}) custom-call(s32[6]{0:T(128)S(1)} %stack.27.info_ref.refs_0_.refs_1_, s32[64]{0:T(128)S(1)} %panel_places.3.refs_0_, ...), custom_call_target="tpu_custom_call", output_to_operand_aliasing={{0}: (8, {}), {1}: (9, {}), {2}: (10, {})} | custom-call | flops 603979776 | bytes 3145728 | tf_op jit(solution)/shard_map/accumulate/pallas_call | solution.py:357
  45.8 0.6 pick.10
  46.5 3.9 %collective-permute-done.9.refs_5_.refs_1_ = f32[512,256]{1,0:T(8,128)S(1)} collective-permute-done((f32[512,256]{1,0:T(8,128)S(1)}, f32[512,256]{1,0:T(8,128)S(1)}, u32[]{:S(2)}, u32[]{:S(2)}) %collective-permute-start.9) | collective-permute-done | bytes 524320 | tf_op jit(solution)/shard_map/ppermute | solution.py:506
  50.4 0.6 pick.14
  51.0 0.6 collective-permute-start.11
  51.5 1.7 %accumulate.13 = (f32[25,128,128]{2,1,0:T(8,128)S(1)}, f32[25,128,128]{2,1,0:T(8,128)S(1)}, s32[8,128]{1,0:T(8,128)S(1)}) custom-call(s32[6]{0:T(128)S(1)} %stack.27.info_ref.refs_0_.refs_1_, s32[64]{0:T(128)S(1)} %panel_places.3.refs_0_, s32[64]{0:T(128)S(1)} %panel_places.4.refs_0_.refs_1_, ...), custom_call_target="tpu_custom_call", output_to_operand_aliasing={{0}: (7, {}), {1}: (8, {})} | custom-call | flops 402653184 | bytes 2097152 | tf_op jit(solution)/shard_map/accumulate/pallas_call | solution.py:357
  53.7 0.6 pick.13
  54.3 2.1 %collective-permute-start.10 = (f32[512,256]{1,0:T(8,128)S(1)}, f32[512,256]{1,0:T(8,128)S(1)}, u32[]{:S(2)}, u32[]{:S(2)}) collective-permute-start(f32[512,256]{1,0:T(8,128)S(1)} %pick.13), channel_id=1, source_target_pairs={{0,4},{4,0},{8,12},{12,8},{16,20},{20,16},{24,28},{28,24},{1,5},{5... | collective-permute-start | bytes 1572872 | tf_op jit(solution)/shard_map/ppermute | solution.py:506
  56.4 5.4 %collective-permute-done.7.even_ref.refs_8_.refs_1_ = f32[520,256]{1,0:T(8,128)S(1)} collective-permute-done((f32[520,256]{1,0:T(8,128)S(1)}, f32[520,256]{1,0:T(8,128)S(1)}, u32[]{:S(2)}, u32[]{:S(2)}) %collective-permute-start.7) | collective-permute-done | bytes 532512 | tf_op jit(solution)/shard_map/ppermute | solution.py:506
  61.8 0.6 pick.17
  62.4 0.6 collective-permute-start.14
  62.9 2.0 %panel_places.5.refs_2_.refs_0_.refs_1_ = s32[64]{0:T(128)S(1)} custom-call(s32[6]{0:T(128)S(1)} %stack.27.info_ref.refs_0_.refs_1_, s32[64]{0:T(128)S(1)} %get-tuple-element.38.table_ref, s32[3,2,8]{2,1,0:T(2,128)S(1)} %collective-permute-done.rows_ref, f32[520,256]{1,0:T(8,128)S(1)} %collective-permute-done.7.even_ref.refs_8_.refs_1_, ...), custom_call_target="tpu_custom_call" | custom-call | tf_op jit(solution)/shard_map/panel_places/pallas_call | solution.py:422
  64.9 1.9 %accumulate.14 = (f32[25,128,128]{2,1,0:T(8,128)S(1)}, f32[25,128,128]{2,1,0:T(8,128)S(1)}, f32[25,128,128]{2,1,0:T(8,128)S(1)}, s32[8,128]{1,0:T(8,128)S(1)}) custom-call(s32[6]{0:T(128)S(1)} %stack.27.info_ref.refs_0_.refs_1_, s32[64]{0:T(128)S(1)} %panel_places.3.refs_0_, ...), custom_call_target="tpu_custom_call", output_to_operand_aliasing={{0}: (10, {}), {1}: (11, {}), {2}: (12, {})} | custom-call | flops 402653184 | bytes 2097152 | tf_op jit(solution)/shard_map/accumulate/pallas_call | solution.py:357
  66.8 0.6 pick.16
  67.4 2.7 %collective-permute-start.13 = (f32[512,256]{1,0:T(8,128)S(1)}, f32[512,256]{1,0:T(8,128)S(1)}, u32[]{:S(2)}, u32[]{:S(2)}) collective-permute-start(f32[512,256]{1,0:T(8,128)S(1)} %pick.16), channel_id=1, source_target_pairs={{0,4},{4,0},{8,12},{12,8},{16,20},{20,16},{24,28},{28,24},{1,5},{5... | collective-permute-start | bytes 1572872 | tf_op jit(solution)/shard_map/ppermute | solution.py:506
  70.2 1.5 %accumulate.15 = (f32[25,128,128]{2,1,0:T(8,128)S(1)}, f32[25,128,128]{2,1,0:T(8,128)S(1)}, s32[8,128]{1,0:T(8,128)S(1)}) custom-call(s32[6]{0:T(128)S(1)} %stack.27.info_ref.refs_0_.refs_1_, s32[64]{0:T(128)S(1)} %panel_places.5.refs_2_.refs_0_.refs_1_, ...), custom_call_target="tpu_custom_call", output_to_operand_aliasing={{0}: (5, {}), {1}: (6, {})} | custom-call | flops 201326592 | bytes 1048576 | tf_op jit(solution)/shard_map/accumulate/pallas_call | solution.py:357
  71.7 1.3 %collective-permute-done.10.refs_4_.refs_0_.refs_1_ = f32[512,256]{1,0:T(8,128)S(1)} collective-permute-done((f32[512,256]{1,0:T(8,128)S(1)}, f32[512,256]{1,0:T(8,128)S(1)}, u32[]{:S(2)}, u32[]{:S(2)}) %collective-permute-start.10) | collective-permute-done | bytes 524320 | tf_op jit(solution)/shard_map/ppermute | solution.py:506
  73.0 0.6 pick.15
  74.2 1.7 %accumulate.16 = (f32[25,128,128]{2,1,0:T(8,128)S(1)}, f32[25,128,128]{2,1,0:T(8,128)S(1)}, s32[8,128]{1,0:T(8,128)}, f32[6,128,128]{2,1,0:T(8,128)S(1)}) custom-call(s32[6]{0:T(128)S(1)} %stack.27.info_ref.refs_0_.refs_1_, s32[64]{0:T(128)S(1)} %panel_places.3.refs_0_, ...), custom_call_target="tpu_custom_call", output_to_operand_aliasing={{0}: (6, {}), {1}: (7, {})} | custom-call | flops 201326592 | bytes 1048576 | tf_op jit(solution)/shard_map/accumulate/pallas_call | solution.py:357
  75.9 1.5 %collective-permute-start.15 = (f32[6,128,128]{2,1,0:T(8,128)S(1)}, f32[6,128,128]{2,1,0:T(8,128)S(1)}, u32[]{:S(2)}, u32[]{:S(2)}) collective-permute-start(f32[6,128,128]{2,1,0:T(8,128)S(1)} %get-tuple-element.68), channel_id=1, source_target_pairs={{0,1},{1,0},{2,3},{3,2},{4,5},{5,4},{6,7},{7,6},{8,9},{9,8},{10,11... | collective-permute-start | bytes 1179656 | tf_op jit(solution)/shard_map/ppermute | solution.py:578
  77.4 2.0 %accumulate.17 = (f32[25,128,128]{2,1,0:T(8,128)S(1)}, f32[25,128,128]{2,1,0:T(8,128)S(1)}, s32[8,128]{1,0:T(8,128)}, f32[3,128,128]{2,1,0:T(8,128)S(1)}) custom-call(s32[6]{0:T(128)S(1)} %stack.27.info_ref.refs_0_.refs_1_, s32[64]{0:T(128)S(1)} %panel_places.5.refs_2_.refs_0_.refs_1_, ...), custom_call_target="tpu_custom_call", output_to_operand_aliasing={{0}: (5, {}), {1}: (6, {})} | custom-call | flops 201326592 | bytes 1048576 | tf_op jit(solution)/shard_map/accumulate/pallas_call | solution.py:357
  79.9 3.9 %collective-permute-done.13.refs_6_.refs_7_ = f32[512,256]{1,0:T(8,128)S(1)} collective-permute-done((f32[512,256]{1,0:T(8,128)S(1)}, f32[512,256]{1,0:T(8,128)S(1)}, u32[]{:S(2)}, u32[]{:S(2)}) %collective-permute-start.13) | collective-permute-done | bytes 524320 | tf_op jit(solution)/shard_map/ppermute | solution.py:506
  83.8 2.0 %accumulate.18 = (f32[25,128,128]{2,1,0:T(8,128)S(1)}, f32[25,128,128]{2,1,0:T(8,128)S(1)}, s32[8,128]{1,0:T(8,128)}) custom-call(s32[6]{0:T(128)S(1)} %stack.27.info_ref.refs_0_.refs_1_, s32[64]{0:T(128)S(1)} %panel_places.3.refs_0_, s32[64]{0:T(128)S(1)} %panel_places.4.refs_0_.refs_1_, ...), custom_call_target="tpu_custom_call", output_to_operand_aliasing={{0}: (9, {}), {1}: (10, {})} | custom-call | tf_op jit(solution)/shard_map/accumulate/pallas_call | solution.py:357
  85.8 1.0 %collective-permute-done.12.refs_2_ = f32[512,256]{1,0:T(8,128)S(1)} collective-permute-done((f32[512,256]{1,0:T(8,128)S(1)}, f32[512,256]{1,0:T(8,128)S(1)}, u32[]{:S(2)}, u32[]{:S(2)}) %collective-permute-start.12) | collective-permute-done | bytes 524320 | tf_op jit(solution)/shard_map/ppermute | solution.py:503
  86.8 1.6 %accumulate.19 = (f32[25,128,128]{2,1,0:T(8,128)S(1)}, f32[25,128,128]{2,1,0:T(8,128)S(1)}, s32[8,128]{1,0:T(8,128)}, f32[3,128,128]{2,1,0:T(8,128)S(1)}) custom-call(s32[6]{0:T(128)S(1)} %stack.27.info_ref.refs_0_.refs_1_, s32[64]{0:T(128)S(1)} %panel_places.5.refs_2_.refs_0_.refs_1_, ...), custom_call_target="tpu_custom_call", output_to_operand_aliasing={{0}: (4, {}), {1}: (5, {})} | custom-call | tf_op jit(solution)/shard_map/accumulate/pallas_call | solution.py:357
  88.4 1.5 %collective-permute-start.17 = (f32[3,128,128]{2,1,0:T(8,128)S(1)}, f32[3,128,128]{2,1,0:T(8,128)S(1)}, u32[]{:S(2)}, u32[]{:S(2)}) collective-permute-start(f32[3,128,128]{2,1,0:T(8,128)S(1)} %get-tuple-element.70), channel_id=1, source_target_pairs={{0,1},{1,0},{2,3},{3,2},{4,5},{5,4},{6,7},{7,6},{8,9},{9,8},{10,11... | collective-permute-start | bytes 589832 | tf_op jit(solution)/shard_map/ppermute | solution.py:578
  89.9 1.3 %kept_blocks.1.kept_ref = f32[12,128,128]{2,1,0:T(8,128)S(1)} custom-call(f32[25,128,128]{2,1,0:T(8,128)S(1)} %get-tuple-element.57.half_ref, f32[25,128,128]{2,1,0:T(8,128)S(1)} %get-tuple-element.66.third_ref, f32[25,128,128]{2,1,0:T(8,128)S(1)} %get-tuple-element.67.fourth_ref), custom_call_target="tpu_custom_call" | custom-call | tf_op jit(solution)/shard_map/kept_blocks/pallas_call | solution.py:444
  91.2 3.3 %collective-permute-done.17.late_ref = f32[3,128,128]{2,1,0:T(8,128)S(1)} collective-permute-done((f32[3,128,128]{2,1,0:T(8,128)S(1)}, f32[3,128,128]{2,1,0:T(8,128)S(1)}, u32[]{:S(2)}, u32[]{:S(2)}) %collective-permute-start.17) | collective-permute-done | bytes 196640 | tf_op jit(solution)/shard_map/ppermute | solution.py:578
  94.5 1.9 %combine.1 = f32[12,128,128]{2,1,0:T(8,128)} custom-call(s32[6]{0:T(128)S(1)} %stack.27.info_ref.refs_0_.refs_1_, f32[12,128,128]{2,1,0:T(8,128)S(1)} %kept_blocks.1.kept_ref, f32[6,128,128]{2,1,0:T(8,128)S(1)} %collective-permute-done.15.half_ref, f32[3,128,128]{2,1,0:T(8,128)S(1)} %collective-permute-done.16.early_ref, ...), custom_call_target="tpu_custom_call" | custom-call | tf_op jit(solution)/shard_map/combine/pallas_call | solution.py:475
  (28 shorter events, 4.0 us)
Async XLA Ops:
  0.0 43.7 %collective-permute-start.5 = (f32[3,8,2,128,128]{4,3,2,1,0:T(8,128)}, f32[3,8,2,128,128]{4,3,2,1,0:T(8,128)S(1)}, u32[]{:S(2)}, u32[]{:S(2)}) collective-permute-start(f32[3,8,2,128,128]{4,3,2,1,0:T(8,128)} %bitcast.25), channel_id=1, source_target_pairs={{0,2},{2,0},{1,3},{3,1},{4,6},{6,4},{5,7},{7,5},{8,10},{10,8},{9,1... | collective-permute-start | bytes 9437192 | tf_op jit(solution)/shard_map/ppermute | solution.py:529
  0.5 6.3 %copy-start = (f32[1,1,1,8,4,128,128]{6,5,4,3,2,1,0:T(8,128)S(1)}, f32[1,1,1,8,4,128,128]{6,5,4,3,2,1,0:T(8,128)}, u32[]{:S(2)}) copy-start(f32[1,1,1,8,4,128,128]{6,5,4,3,2,1,0:T(8,128)} %param.7) | copy-start | bytes 6291460
  0.5 10.0 %copy-start.1 = (f32[1,1,1,3,8,2,128,128]{7,6,5,4,3,2,1,0:T(8,128)S(1)}, f32[1,1,1,3,8,2,128,128]{7,6,5,4,3,2,1,0:T(8,128)}, u32[]{:S(2)}) copy-start(f32[1,1,1,3,8,2,128,128]{7,6,5,4,3,2,1,0:T(8,128)} %param.5) | copy-start | bytes 9437188
  2.1 6.9 %copy-start.2 = (s32[1,1,1,8,4]{3,4,2,1,0:T(4,128)S(1)}, s32[1,1,1,8,4]{3,4,2,1,0:T(4,128)}, u32[]{:S(2)}) copy-start(s32[1,1,1,8,4]{3,4,2,1,0:T(4,128)} %param.8) | copy-start | bytes 388
  2.1 6.9 %copy-start.3 = (s32[1,1,1,3,8,2]{4,5,3,2,1,0:T(2,128)S(1)}, s32[1,1,1,3,8,2]{4,5,3,2,1,0:T(2,128)}, u32[]{:S(2)}) copy-start(s32[1,1,1,3,8,2]{4,5,3,2,1,0:T(2,128)} %param.6) | copy-start | bytes 580
  2.1 6.9 %copy-start.4 = (s32[1,1,24]{2,1,0:T(1,128)S(1)}, s32[1,1,24]{2,1,0:T(1,128)}, u32[]{:S(2)}) copy-start(s32[1,1,24]{2,1,0:T(1,128)} %param.9) | copy-start | bytes 292
  2.2 17.1 %collective-permute-start.1 = (f32[520,256]{1,0:T(8,128)S(1)}, f32[520,256]{1,0:T(8,128)S(1)}, u32[]{:S(2)}, u32[]{:S(2)}) collective-permute-start(f32[520,256]{1,0:T(8,128)S(1)} %first_quarter.1), channel_id=1, source_target_pairs={{0,24},{4,28},{8,0},{12,4},{16,8},{20,12},{24,16},{28,20},{1,25},{... | collective-permute-start | bytes 1597448 | tf_op jit(solution)/shard_map/ppermute | solution.py:503
  7.5 20.4 %collective-permute-start.3 = (f32[768,256]{1,0:T(8,128)S(1)}, f32[768,256]{1,0:T(8,128)S(1)}, u32[]{:S(2)}, u32[]{:S(2)}) collective-permute-start(f32[768,256]{1,0:T(8,128)S(1)} %own_quarters.3), channel_id=1, source_target_pairs={{0,4},{4,0},{8,12},{12,8},{16,20},{20,16},{24,28},{28,24},{1,5},{5... | collective-permute-start | bytes 2359304 | tf_op jit(solution)/shard_map/ppermute | solution.py:506
  13.4 17.0 %collective-permute-start.6 = (f32[512,256]{1,0:T(8,128)S(1)}, f32[512,256]{1,0:T(8,128)S(1)}, u32[]{:S(2)}, u32[]{:S(2)}) collective-permute-start(f32[512,256]{1,0:T(8,128)S(1)} %own_quarters.5), channel_id=1, source_target_pairs={{0,24},{4,28},{8,0},{12,4},{16,8},{20,12},{24,16},{28,20},{1,25},{... | collective-permute-start | bytes 1572872 | tf_op jit(solution)/shard_map/ppermute | solution.py:503
  19.8 19.5 %collective-permute-start.2 = (f32[520,256]{1,0:T(8,128)S(1)}, f32[520,256]{1,0:T(8,128)S(1)}, u32[]{:S(2)}, u32[]{:S(2)}) collective-permute-start(f32[520,256]{1,0:T(8,128)S(1)} %pick.9), channel_id=1, source_target_pairs={{0,4},{4,0},{8,12},{12,8},{16,20},{20,16},{24,28},{28,24},{1,5},{5... | collective-permute-start | bytes 1597448 | tf_op jit(solution)/shard_map/ppermute | solution.py:506
  28.4 17.4 %collective-permute-start.4 = (f32[512,256]{1,0:T(8,128)S(1)}, f32[512,256]{1,0:T(8,128)S(1)}, u32[]{:S(2)}, u32[]{:S(2)}) collective-permute-start(f32[512,256]{1,0:T(8,128)S(1)} %own_quarters.4), channel_id=1, source_target_pairs={{0,24},{4,28},{8,0},{12,4},{16,8},{20,12},{24,16},{28,20},{1,25},{... | collective-permute-start | bytes 1572872 | tf_op jit(solution)/shard_map/ppermute | solution.py:503
  32.5 17.9 %collective-permute-start.9 = (f32[512,256]{1,0:T(8,128)S(1)}, f32[512,256]{1,0:T(8,128)S(1)}, u32[]{:S(2)}, u32[]{:S(2)}) collective-permute-start(f32[512,256]{1,0:T(8,128)S(1)} %pick.12), channel_id=1, source_target_pairs={{0,4},{4,0},{8,12},{12,8},{16,20},{20,16},{24,28},{28,24},{1,5},{5... | collective-permute-start | bytes 1572872 | tf_op jit(solution)/shard_map/ppermute | solution.py:506
  40.4 13.3 %collective-permute-start.8 = (f32[520,256]{1,0:T(8,128)S(1)}, f32[520,256]{1,0:T(8,128)S(1)}, u32[]{:S(2)}, u32[]{:S(2)}) collective-permute-start(f32[520,256]{1,0:T(8,128)S(1)} %pick.11), channel_id=1, source_target_pairs={{0,24},{4,28},{8,0},{12,4},{16,8},{20,12},{24,16},{28,20},{1,25},{... | collective-permute-start | bytes 1597448 | tf_op jit(solution)/shard_map/ppermute | solution.py:503
  40.5 1.2 %collective-permute-start = (s32[3,2,8]{2,1,0:T(2,128)S(1)}, s32[3,2,8]{2,1,0:T(2,128)S(1)}, u32[]{:S(2)}, u32[]{:S(2)}) collective-permute-start(s32[3,2,8]{2,1,0:T(2,128)S(1)} %bitcast.39), channel_id=1, source_target_pairs={{0,2},{2,0},{1,3},{3,1},{4,6},{6,4},{5,7},{7,5},{8,10},{10,8},{9,1... | collective-permute-start | bytes 584 | tf_op jit(solution)/shard_map/ppermute | solution.py:529
  46.4 15.4 %collective-permute-start.7 = (f32[520,256]{1,0:T(8,128)S(1)}, f32[520,256]{1,0:T(8,128)S(1)}, u32[]{:S(2)}, u32[]{:S(2)}) collective-permute-start(f32[520,256]{1,0:T(8,128)S(1)} %pick.10), channel_id=1, source_target_pairs={{0,4},{4,0},{8,12},{12,8},{16,20},{20,16},{24,28},{28,24},{1,5},{5... | collective-permute-start | bytes 1597448 | tf_op jit(solution)/shard_map/ppermute | solution.py:506
  51.0 15.8 %collective-permute-start.11 = (f32[512,256]{1,0:T(8,128)S(1)}, f32[512,256]{1,0:T(8,128)S(1)}, u32[]{:S(2)}, u32[]{:S(2)}) collective-permute-start(f32[512,256]{1,0:T(8,128)S(1)} %pick.14), channel_id=1, source_target_pairs={{0,24},{4,28},{8,0},{12,4},{16,8},{20,12},{24,16},{28,20},{1,25},{... | collective-permute-start | bytes 1572872 | tf_op jit(solution)/shard_map/ppermute | solution.py:503
  54.3 18.8 %collective-permute-start.10 = (f32[512,256]{1,0:T(8,128)S(1)}, f32[512,256]{1,0:T(8,128)S(1)}, u32[]{:S(2)}, u32[]{:S(2)}) collective-permute-start(f32[512,256]{1,0:T(8,128)S(1)} %pick.13), channel_id=1, source_target_pairs={{0,4},{4,0},{8,12},{12,8},{16,20},{20,16},{24,28},{28,24},{1,5},{5... | collective-permute-start | bytes 1572872 | tf_op jit(solution)/shard_map/ppermute | solution.py:506
  62.4 15.0 %collective-permute-start.14 = (f32[512,256]{1,0:T(8,128)S(1)}, f32[512,256]{1,0:T(8,128)S(1)}, u32[]{:S(2)}, u32[]{:S(2)}) collective-permute-start(f32[512,256]{1,0:T(8,128)S(1)} %pick.17), channel_id=1, source_target_pairs={{0,24},{4,28},{8,0},{12,4},{16,8},{20,12},{24,16},{28,20},{1,25},{... | collective-permute-start | bytes 1572872 | tf_op jit(solution)/shard_map/ppermute | solution.py:503
  67.4 16.3 %collective-permute-start.13 = (f32[512,256]{1,0:T(8,128)S(1)}, f32[512,256]{1,0:T(8,128)S(1)}, u32[]{:S(2)}, u32[]{:S(2)}) collective-permute-start(f32[512,256]{1,0:T(8,128)S(1)} %pick.16), channel_id=1, source_target_pairs={{0,4},{4,0},{8,12},{12,8},{16,20},{20,16},{24,28},{28,24},{1,5},{5... | collective-permute-start | bytes 1572872 | tf_op jit(solution)/shard_map/ppermute | solution.py:506
  73.6 13.2 %collective-permute-start.12 = (f32[512,256]{1,0:T(8,128)S(1)}, f32[512,256]{1,0:T(8,128)S(1)}, u32[]{:S(2)}, u32[]{:S(2)}) collective-permute-start(f32[512,256]{1,0:T(8,128)S(1)} %pick.15), channel_id=1, source_target_pairs={{0,24},{4,28},{8,0},{12,4},{16,8},{20,12},{24,16},{28,20},{1,25},{... | collective-permute-start | bytes 1572872 | tf_op jit(solution)/shard_map/ppermute | solution.py:503
  75.9 15.4 %collective-permute-start.15 = (f32[6,128,128]{2,1,0:T(8,128)S(1)}, f32[6,128,128]{2,1,0:T(8,128)S(1)}, u32[]{:S(2)}, u32[]{:S(2)}) collective-permute-start(f32[6,128,128]{2,1,0:T(8,128)S(1)} %get-tuple-element.68), channel_id=1, source_target_pairs={{0,1},{1,0},{2,3},{3,2},{4,5},{5,4},{6,7},{7,6},{8,9},{9,8},{10,11... | collective-permute-start | bytes 1179656 | tf_op jit(solution)/shard_map/ppermute | solution.py:578
  79.4 11.8 %collective-permute-start.16 = (f32[3,128,128]{2,1,0:T(8,128)S(1)}, f32[3,128,128]{2,1,0:T(8,128)S(1)}, u32[]{:S(2)}, u32[]{:S(2)}) collective-permute-start(f32[3,128,128]{2,1,0:T(8,128)S(1)} %get-tuple-element.69), channel_id=1, source_target_pairs={{0,1},{1,0},{2,3},{3,2},{4,5},{5,4},{6,7},{7,6},{8,9},{9,8},{10,11... | collective-permute-start | bytes 589832 | tf_op jit(solution)/shard_map/ppermute | solution.py:578
  88.4 6.1 %collective-permute-start.17 = (f32[3,128,128]{2,1,0:T(8,128)S(1)}, f32[3,128,128]{2,1,0:T(8,128)S(1)}, u32[]{:S(2)}, u32[]{:S(2)}) collective-permute-start(f32[3,128,128]{2,1,0:T(8,128)S(1)} %get-tuple-element.70), channel_id=1, source_target_pairs={{0,1},{1,0},{2,3},{3,2},{4,5},{5,4},{6,7},{7,6},{8,9},{9,8},{10,11... | collective-permute-start | bytes 589832 | tf_op jit(solution)/shard_map/ppermute | solution.py:578

commit v11 on v10

--- a/solution.py
+++ b/solution.py
@@ -521,12 +521,14 @@
         return (quarter, first, parts)
 
     small = (info,)
-    z[1] = along_z(first_quarter(right, cols, *small))
+    first = first_quarter(right, cols, *small)
+    z[1] = along_z(first)
+    sent_panels, _ = lax.optimization_barrier((panels, first))
     x[1] = along_x(own_quarters(right, [own_part(3), own_part(2, 0, 1)], None, *small))
 
     shifts = sorted({turn % cols_n for turn in range(STEPS)})
     held = {
-        shift: (panels, panel_rows) if shift == 0 else lax.ppermute((panels, panel_rows), "col", [(c, (c - shift) % cols_n) for c in range(cols_n)])
+        shift: (panels, panel_rows) if shift == 0 else lax.ppermute((sent_panels, panel_rows), "col", [(c, (c - shift) % cols_n) for c in range(cols_n)])
         for shift in shifts
     }
     lefts = [held[turn % cols_n][0] for turn in range(STEPS)]

time: 96.6 us -> 96.5 us (level)
  transfers between devices with their start and end apart: 18 -> 18, of which waited for: 12 -> 12; matrix products, arithmetic and copies ran while one was open for 0% -> 0% of each run, Pallas kernels for 37% -> 36%
where the time goes in v11:
time: 96.5 us; the launch traced here: 96.3 us
  Pallas kernels  37.9 us (39%)
  waiting for transfers between devices  37.1 us (38%)
  starting transfers between devices  20.8 us (22%)
    ppermute x6, waiting for transfers between devices, along_x(): return lax.ppermute(chunk, 'row', x_pairs)  24.3 us
    pallas_call x10, Pallas kernels, accumulate(): pl.pallas_call(kernel, grid_spec=pltpu.PrefetchScalarGridSpec(num_scalar_...  18.8 us
    ppermute x6, starting transfers between devices, along_x(): return lax.ppermute(chunk, 'row', x_pairs)  9.48 us
    ppermute x7, waiting for transfers between devices, along_z(): return lax.ppermute(chunk, 'row', z_pairs)  8.39 us
    ppermute x7, starting transfers between devices, along_z(): return lax.ppermute(chunk, 'row', z_pairs)  7.24 us
    pallas_call x3, Pallas kernels, panel_places(): pl.pallas_call(kernel, grid=(1,), in_specs=[in_smem] * 3 + [pl.BlockSpec(...  5.86 us
    pallas_call x9, Pallas kernels, pick(): pl.pallas_call(kernel, grid=(1,), in_specs=[in_smem] + [spec(part) for pa...  5.71 us
    ppermute x3, starting transfers between devices, to_partner(): return lax.ppermute(blocks, 'rep', [(0, 1), (1, 0)])  3.54 us
  transfers between devices with their start and end apart: 18, of which 12 were waited for; matrix products, arithmetic and copies ran while one was open for 0% of the time, Pallas kernels for 36%

profile of v11, /device:TPU:0, one launch (start us, length us, event | category | flops | bytes accessed | tf_op | source)
XLA Modules:
  0.0 96.3 jit_solution(15313105862422081846)
XLA Ops:
  0.1 1.6 %first_quarter.1 = f32[520,256]{1,0:T(8,128)S(1)} custom-call(f32[8,4,128,128]{3,2,1,0:T(8,128)} %bitcast.16, s32[4,8]{1,0:T(4,128)} %bitcast.32, s32[6]{0:T(128)S(1)} %stack.27.info_ref.refs_0_.refs_1_), custom_call_target="tpu_custom_call" | custom-call | bytes 1572864 | tf_op jit(solution)/shard_map/first_quarter/pallas_call | solution.py:166
  2.2 4.7 %collective-permute-start.1 = (f32[520,256]{1,0:T(8,128)S(1)}, f32[520,256]{1,0:T(8,128)S(1)}, u32[]{:S(2)}, u32[]{:S(2)}) collective-permute-start(f32[520,256]{1,0:T(8,128)S(1)} %first_quarter.1), channel_id=1, source_target_pairs={{0,24},{4,28},{8,0},{12,4},{16,8},{20,12},{24,16},{28,20},{1,25},{... | collective-permute-start | bytes 1597448 | tf_op jit(solution)/shard_map/ppermute | solution.py:503
  6.9 0.7 own_quarters.3
  7.6 1.6 %collective-permute-start.3 = (f32[768,256]{1,0:T(8,128)S(1)}, f32[768,256]{1,0:T(8,128)S(1)}, u32[]{:S(2)}, u32[]{:S(2)}) collective-permute-start(f32[768,256]{1,0:T(8,128)S(1)} %own_quarters.3), channel_id=1, source_target_pairs={{0,4},{4,0},{8,12},{12,8},{16,20},{20,16},{24,28},{28,24},{1,5},{5... | collective-permute-start | bytes 2359304 | tf_op jit(solution)/shard_map/ppermute | solution.py:506
  9.1 1.5 %own_places.1 = (s32[64]{0:T(128)S(1)}, s32[64]{0:T(128)S(1)}) custom-call(s32[6]{0:T(128)S(1)} %stack.27.info_ref.refs_0_.refs_1_, s32[24]{0:T(128)S(1)} %bitcast.40, s32[3,2,8]{2,1,0:T(2,128)S(1)} %bitcast.37, s32[4,8]{1,0:T(4,128)S(1)} %bitcast.33), custom_call_target="tpu_custom_call" | custom-call | tf_op jit(solution)/shard_map/own_places/pallas_call | solution.py:389
  10.6 2.7 %accumulate.10 = (f32[25,128,128]{2,1,0:T(8,128)S(1)}, f32[25,128,128]{2,1,0:T(8,128)S(1)}, f32[25,128,128]{2,1,0:T(8,128)S(1)}, s32[8,128]{1,0:T(8,128)S(1)}) custom-call(s32[6]{0:T(128)S(1)} %stack.27.info_ref.refs_0_.refs_1_, s32[64]{0:T(128)S(1)} %get-tuple-element.40.refs_0_, f32[3,8,2,128,128]{4,3,2,1,0:T(8,128)S(1)} %bitcast.26, ...), custom_call_target="tpu_custom_call" | custom-call | flops 805306368 | bytes 4194304 | tf_op jit(solution)/shard_map/accumulate/pallas_call | solution.py:357
  14.0 5.3 %collective-permute-done.1.refs_0_.refs_1_.even_ref.odd_ref.refs_3_ = f32[520,256]{1,0:T(8,128)S(1)} collective-permute-done((f32[520,256]{1,0:T(8,128)S(1)}, f32[520,256]{1,0:T(8,128)S(1)}, u32[]{:S(2)}, u32[]{:S(2)}) %collective-permute-start.1) | collective-permute-done | bytes 532512 | tf_op jit(solution)/shard_map/ppermute | solution.py:503
  19.3 0.6 pick.9
  19.9 1.7 %collective-permute-start.2 = (f32[520,256]{1,0:T(8,128)S(1)}, f32[520,256]{1,0:T(8,128)S(1)}, u32[]{:S(2)}, u32[]{:S(2)}) collective-permute-start(f32[520,256]{1,0:T(8,128)S(1)} %pick.9), channel_id=1, source_target_pairs={{0,4},{4,0},{8,12},{12,8},{16,20},{20,16},{24,28},{28,24},{1,5},{5... | collective-permute-start | bytes 1597448 | tf_op jit(solution)/shard_map/ppermute | solution.py:506
  21.6 2.0 %panel_places.4.refs_0_.refs_1_ = s32[64]{0:T(128)S(1)} custom-call(s32[6]{0:T(128)S(1)} %stack.27.info_ref.refs_0_.refs_1_, s32[64]{0:T(128)S(1)} %get-tuple-element.39.table_ref, s32[3,2,8]{2,1,0:T(2,128)S(1)} %bitcast.38, f32[520,256]{1,0:T(8,128)S(1)} %collective-permute-done.1.refs_0_.refs_1_.even_ref.odd_ref.refs_3_, ...), custom_call_target="tpu_custom_call" | custom-call | tf_op jit(solution)/shard_map/panel_places/pallas_call | solution.py:422
  23.6 4.4 %collective-permute-done.3.refs_2_.refs_4_.refs_5_.refs_0_ = f32[768,256]{1,0:T(8,128)S(1)} collective-permute-done((f32[768,256]{1,0:T(8,128)S(1)}, f32[768,256]{1,0:T(8,128)S(1)}, u32[]{:S(2)}, u32[]{:S(2)}) %collective-permute-start.3) | collective-permute-done | bytes 786464 | tf_op jit(solution)/shard_map/ppermute | solution.py:506
  29.0 1.6 %collective-permute-done.6.refs_4_.refs_0_.refs_1_ = f32[512,256]{1,0:T(8,128)S(1)} collective-permute-done((f32[512,256]{1,0:T(8,128)S(1)}, f32[512,256]{1,0:T(8,128)S(1)}, u32[]{:S(2)}, u32[]{:S(2)}) %collective-permute-start.6) | collective-permute-done | bytes 524320 | tf_op jit(solution)/shard_map/ppermute | solution.py:503
  30.5 1.5 %accumulate.11 = (f32[25,128,128]{2,1,0:T(8,128)S(1)}, s32[8,128]{1,0:T(8,128)S(1)}) custom-call(s32[6]{0:T(128)S(1)} %stack.27.info_ref.refs_0_.refs_1_, s32[64]{0:T(128)S(1)} %panel_places.4.refs_0_.refs_1_, f32[3,8,2,128,128]{4,3,2,1,0:T(8,128)S(1)} %bitcast.27, f32[3,8,2,128,128]{4,3,2,1,0:T(8,128)S(1)} %bitcast.28, ...), custom_call_target="tpu_custom_call", output_to_operand_aliasing={{0}: (6, {})} | custom-call | flops 402653184 | bytes 2097152 | tf_op jit(solution)/shard_map/accumulate/pallas_call | solution.py:357
  32.0 0.6 pick.12
  32.6 1.7 %collective-permute-start.9 = (f32[512,256]{1,0:T(8,128)S(1)}, f32[512,256]{1,0:T(8,128)S(1)}, u32[]{:S(2)}, u32[]{:S(2)}) collective-permute-start(f32[512,256]{1,0:T(8,128)S(1)} %pick.12), channel_id=1, source_target_pairs={{0,4},{4,0},{8,12},{12,8},{16,20},{20,16},{24,28},{28,24},{1,5},{5... | collective-permute-start | bytes 1572872 | tf_op jit(solution)/shard_map/ppermute | solution.py:506
  34.3 5.1 %collective-permute-done.2.even_ref.odd_ref.refs_6_.refs_1_ = f32[520,256]{1,0:T(8,128)S(1)} collective-permute-done((f32[520,256]{1,0:T(8,128)S(1)}, f32[520,256]{1,0:T(8,128)S(1)}, u32[]{:S(2)}, u32[]{:S(2)}) %collective-permute-start.2) | collective-permute-done | bytes 532512 | tf_op jit(solution)/shard_map/ppermute | solution.py:506
  39.4 1.0 %pick.11 = f32[520,256]{1,0:T(8,128)S(1)} custom-call(s32[6]{0:T(128)S(1)} %stack.27.info_ref.refs_0_.refs_1_, f32[8,4,128,128]{3,2,1,0:T(8,128)S(1)} %bitcast.23, f32[520,256]{1,0:T(8,128)S(1)} %collective-permute-done.2.even_ref.odd_ref.refs_6_.refs_1_, s32[4,8]{1,0:T(4,128)S(1)} %bitcast.35, s32[8,128]{1,0:T(8,128)S(1)} %get-tuple-element.48.refs_3_.refs_2_), custom_call_target="tpu_custom_call" | custom-call | bytes 1064960 | tf_op jit(solution)/shard_map/pick/pallas_call | solution.py:220
  40.6 1.1 %collective-permute-done.rows_ref = s32[3,2,8]{2,1,0:T(2,128)S(1)} collective-permute-done((s32[3,2,8]{2,1,0:T(2,128)S(1)}, s32[3,2,8]{2,1,0:T(2,128)S(1)}, u32[]{:S(2)}, u32[]{:S(2)}) %collective-permute-start) | collective-permute-done | bytes 224 | tf_op jit(solution)/shard_map/ppermute | solution.py:531
  41.7 2.0 %panel_places.3.refs_0_ = s32[64]{0:T(128)S(1)} custom-call(s32[6]{0:T(128)S(1)} %stack.27.info_ref.refs_0_.refs_1_, s32[64]{0:T(128)S(1)} %get-tuple-element.39.table_ref, s32[3,2,8]{2,1,0:T(2,128)S(1)} %collective-permute-done.rows_ref, f32[520,256]{1,0:T(8,128)S(1)} %collective-permute-done.2.even_ref.odd_ref.refs_6_.refs_1_, ...), custom_call_target="tpu_custom_call" | custom-call | tf_op jit(solution)/shard_map/panel_places/pallas_call | solution.py:422
  43.7 2.2 %accumulate.12 = (f32[25,128,128]{2,1,0:T(8,128)S(1)}, f32[25,128,128]{2,1,0:T(8,128)S(1)}, f32[25,128,128]{2,1,0:T(8,128)S(1)}, s32[8,128]{1,0:T(8,128)S(1)}) custom-call(s32[6]{0:T(128)S(1)} %stack.27.info_ref.refs_0_.refs_1_, s32[64]{0:T(128)S(1)} %panel_places.3.refs_0_, ...), custom_call_target="tpu_custom_call", output_to_operand_aliasing={{0}: (8, {}), {1}: (9, {}), {2}: (10, {})} | custom-call | flops 603979776 | bytes 3145728 | tf_op jit(solution)/shard_map/accumulate/pallas_call | solution.py:357
  45.9 0.6 pick.10
  46.6 3.8 %collective-permute-done.9.refs_5_.refs_1_ = f32[512,256]{1,0:T(8,128)S(1)} collective-permute-done((f32[512,256]{1,0:T(8,128)S(1)}, f32[512,256]{1,0:T(8,128)S(1)}, u32[]{:S(2)}, u32[]{:S(2)}) %collective-permute-start.9) | collective-permute-done | bytes 524320 | tf_op jit(solution)/shard_map/ppermute | solution.py:506
  50.4 0.6 pick.14
  51.3 1.7 %accumulate.13 = (f32[25,128,128]{2,1,0:T(8,128)S(1)}, f32[25,128,128]{2,1,0:T(8,128)S(1)}, s32[8,128]{1,0:T(8,128)S(1)}) custom-call(s32[6]{0:T(128)S(1)} %stack.27.info_ref.refs_0_.refs_1_, s32[64]{0:T(128)S(1)} %panel_places.3.refs_0_, s32[64]{0:T(128)S(1)} %panel_places.4.refs_0_.refs_1_, ...), custom_call_target="tpu_custom_call", output_to_operand_aliasing={{0}: (7, {}), {1}: (8, {})} | custom-call | flops 402653184 | bytes 2097152 | tf_op jit(solution)/shard_map/accumulate/pallas_call | solution.py:357
  53.0 0.6 collective-permute-done.8.odd_ref.refs_0_.refs_7_
  53.6 0.6 pick.13
  54.2 2.0 %collective-permute-start.10 = (f32[512,256]{1,0:T(8,128)S(1)}, f32[512,256]{1,0:T(8,128)S(1)}, u32[]{:S(2)}, u32[]{:S(2)}) collective-permute-start(f32[512,256]{1,0:T(8,128)S(1)} %pick.13), channel_id=1, source_target_pairs={{0,4},{4,0},{8,12},{12,8},{16,20},{20,16},{24,28},{28,24},{1,5},{5... | collective-permute-start | bytes 1572872 | tf_op jit(solution)/shard_map/ppermute | solution.py:506
  56.1 5.6 %collective-permute-done.7.even_ref.refs_8_.refs_1_ = f32[520,256]{1,0:T(8,128)S(1)} collective-permute-done((f32[520,256]{1,0:T(8,128)S(1)}, f32[520,256]{1,0:T(8,128)S(1)}, u32[]{:S(2)}, u32[]{:S(2)}) %collective-permute-start.7) | collective-permute-done | bytes 532512 | tf_op jit(solution)/shard_map/ppermute | solution.py:506
  62.4 0.6 collective-permute-start.14
  63.0 2.0 %panel_places.5.refs_2_.refs_0_.refs_1_ = s32[64]{0:T(128)S(1)} custom-call(s32[6]{0:T(128)S(1)} %stack.27.info_ref.refs_0_.refs_1_, s32[64]{0:T(128)S(1)} %get-tuple-element.39.table_ref, s32[3,2,8]{2,1,0:T(2,128)S(1)} %collective-permute-done.rows_ref, f32[520,256]{1,0:T(8,128)S(1)} %collective-permute-done.7.even_ref.refs_8_.refs_1_, ...), custom_call_target="tpu_custom_call" | custom-call | tf_op jit(solution)/shard_map/panel_places/pallas_call | solution.py:422
  64.9 1.9 %accumulate.14 = (f32[25,128,128]{2,1,0:T(8,128)S(1)}, f32[25,128,128]{2,1,0:T(8,128)S(1)}, f32[25,128,128]{2,1,0:T(8,128)S(1)}, s32[8,128]{1,0:T(8,128)S(1)}) custom-call(s32[6]{0:T(128)S(1)} %stack.27.info_ref.refs_0_.refs_1_, s32[64]{0:T(128)S(1)} %panel_places.3.refs_0_, ...), custom_call_target="tpu_custom_call", output_to_operand_aliasing={{0}: (10, {}), {1}: (11, {}), {2}: (12, {})} | custom-call | flops 402653184 | bytes 2097152 | tf_op jit(solution)/shard_map/accumulate/pallas_call | solution.py:357
  66.9 0.6 pick.16
  67.4 2.5 %collective-permute-start.13 = (f32[512,256]{1,0:T(8,128)S(1)}, f32[512,256]{1,0:T(8,128)S(1)}, u32[]{:S(2)}, u32[]{:S(2)}) collective-permute-start(f32[512,256]{1,0:T(8,128)S(1)} %pick.16), channel_id=1, source_target_pairs={{0,4},{4,0},{8,12},{12,8},{16,20},{20,16},{24,28},{28,24},{1,5},{5... | collective-permute-start | bytes 1572872 | tf_op jit(solution)/shard_map/ppermute | solution.py:506
  69.9 1.5 %accumulate.15 = (f32[25,128,128]{2,1,0:T(8,128)S(1)}, f32[25,128,128]{2,1,0:T(8,128)S(1)}, s32[8,128]{1,0:T(8,128)S(1)}) custom-call(s32[6]{0:T(128)S(1)} %stack.27.info_ref.refs_0_.refs_1_, s32[64]{0:T(128)S(1)} %panel_places.5.refs_2_.refs_0_.refs_1_, ...), custom_call_target="tpu_custom_call", output_to_operand_aliasing={{0}: (5, {}), {1}: (6, {})} | custom-call | flops 201326592 | bytes 1048576 | tf_op jit(solution)/shard_map/accumulate/pallas_call | solution.py:357
  71.5 1.5 %collective-permute-done.10.refs_4_.refs_0_.refs_1_ = f32[512,256]{1,0:T(8,128)S(1)} collective-permute-done((f32[512,256]{1,0:T(8,128)S(1)}, f32[512,256]{1,0:T(8,128)S(1)}, u32[]{:S(2)}, u32[]{:S(2)}) %collective-permute-start.10) | collective-permute-done | bytes 524320 | tf_op jit(solution)/shard_map/ppermute | solution.py:506
  73.0 0.6 pick.15
  73.6 0.6 collective-permute-start.12
  74.2 1.7 %accumulate.16 = (f32[25,128,128]{2,1,0:T(8,128)S(1)}, f32[25,128,128]{2,1,0:T(8,128)S(1)}, s32[8,128]{1,0:T(8,128)}, f32[6,128,128]{2,1,0:T(8,128)S(1)}) custom-call(s32[6]{0:T(128)S(1)} %stack.27.info_ref.refs_0_.refs_1_, s32[64]{0:T(128)S(1)} %panel_places.3.refs_0_, ...), custom_call_target="tpu_custom_call", output_to_operand_aliasing={{0}: (6, {}), {1}: (7, {})} | custom-call | flops 201326592 | bytes 1048576 | tf_op jit(solution)/shard_map/accumulate/pallas_call | solution.py:357
  75.9 1.5 %collective-permute-start.15 = (f32[6,128,128]{2,1,0:T(8,128)S(1)}, f32[6,128,128]{2,1,0:T(8,128)S(1)}, u32[]{:S(2)}, u32[]{:S(2)}) collective-permute-start(f32[6,128,128]{2,1,0:T(8,128)S(1)} %get-tuple-element.70), channel_id=1, source_target_pairs={{0,1},{1,0},{2,3},{3,2},{4,5},{5,4},{6,7},{7,6},{8,9},{9,8},{10,11... | collective-permute-start | bytes 1179656 | tf_op jit(solution)/shard_map/ppermute | solution.py:580
  77.4 2.0 %accumulate.17 = (f32[25,128,128]{2,1,0:T(8,128)S(1)}, f32[25,128,128]{2,1,0:T(8,128)S(1)}, s32[8,128]{1,0:T(8,128)}, f32[3,128,128]{2,1,0:T(8,128)S(1)}) custom-call(s32[6]{0:T(128)S(1)} %stack.27.info_ref.refs_0_.refs_1_, s32[64]{0:T(128)S(1)} %panel_places.5.refs_2_.refs_0_.refs_1_, ...), custom_call_target="tpu_custom_call", output_to_operand_aliasing={{0}: (5, {}), {1}: (6, {})} | custom-call | flops 201326592 | bytes 1048576 | tf_op jit(solution)/shard_map/accumulate/pallas_call | solution.py:357
  79.9 3.8 %collective-permute-done.13.refs_6_.refs_7_ = f32[512,256]{1,0:T(8,128)S(1)} collective-permute-done((f32[512,256]{1,0:T(8,128)S(1)}, f32[512,256]{1,0:T(8,128)S(1)}, u32[]{:S(2)}, u32[]{:S(2)}) %collective-permute-start.13) | collective-permute-done | bytes 524320 | tf_op jit(solution)/shard_map/ppermute | solution.py:506
  83.8 2.1 %accumulate.18 = (f32[25,128,128]{2,1,0:T(8,128)S(1)}, f32[25,128,128]{2,1,0:T(8,128)S(1)}, s32[8,128]{1,0:T(8,128)}) custom-call(s32[6]{0:T(128)S(1)} %stack.27.info_ref.refs_0_.refs_1_, s32[64]{0:T(128)S(1)} %panel_places.3.refs_0_, s32[64]{0:T(128)S(1)} %panel_places.4.refs_0_.refs_1_, ...), custom_call_target="tpu_custom_call", output_to_operand_aliasing={{0}: (9, {}), {1}: (10, {})} | custom-call | tf_op jit(solution)/shard_map/accumulate/pallas_call | solution.py:357
  85.8 0.9 collective-permute-done.12.refs_2_
  86.8 1.6 %accumulate.19 = (f32[25,128,128]{2,1,0:T(8,128)S(1)}, f32[25,128,128]{2,1,0:T(8,128)S(1)}, s32[8,128]{1,0:T(8,128)}, f32[3,128,128]{2,1,0:T(8,128)S(1)}) custom-call(s32[6]{0:T(128)S(1)} %stack.27.info_ref.refs_0_.refs_1_, s32[64]{0:T(128)S(1)} %panel_places.5.refs_2_.refs_0_.refs_1_, ...), custom_call_target="tpu_custom_call", output_to_operand_aliasing={{0}: (4, {}), {1}: (5, {})} | custom-call | tf_op jit(solution)/shard_map/accumulate/pallas_call | solution.py:357
  88.3 1.5 %collective-permute-start.17 = (f32[3,128,128]{2,1,0:T(8,128)S(1)}, f32[3,128,128]{2,1,0:T(8,128)S(1)}, u32[]{:S(2)}, u32[]{:S(2)}) collective-permute-start(f32[3,128,128]{2,1,0:T(8,128)S(1)} %get-tuple-element.72), channel_id=1, source_target_pairs={{0,1},{1,0},{2,3},{3,2},{4,5},{5,4},{6,7},{7,6},{8,9},{9,8},{10,11... | collective-permute-start | bytes 589832 | tf_op jit(solution)/shard_map/ppermute | solution.py:580
  89.8 1.3 %kept_blocks.1.kept_ref = f32[12,128,128]{2,1,0:T(8,128)S(1)} custom-call(f32[25,128,128]{2,1,0:T(8,128)S(1)} %get-tuple-element.59.half_ref, f32[25,128,128]{2,1,0:T(8,128)S(1)} %get-tuple-element.68.third_ref, f32[25,128,128]{2,1,0:T(8,128)S(1)} %get-tuple-element.69.fourth_ref), custom_call_target="tpu_custom_call" | custom-call | tf_op jit(solution)/shard_map/kept_blocks/pallas_call | solution.py:444
  91.2 3.3 %collective-permute-done.17.late_ref = f32[3,128,128]{2,1,0:T(8,128)S(1)} collective-permute-done((f32[3,128,128]{2,1,0:T(8,128)S(1)}, f32[3,128,128]{2,1,0:T(8,128)S(1)}, u32[]{:S(2)}, u32[]{:S(2)}) %collective-permute-start.17) | collective-permute-done | bytes 196640 | tf_op jit(solution)/shard_map/ppermute | solution.py:580
  94.5 1.9 %combine.1 = f32[12,128,128]{2,1,0:T(8,128)} custom-call(s32[6]{0:T(128)S(1)} %stack.27.info_ref.refs_0_.refs_1_, f32[12,128,128]{2,1,0:T(8,128)S(1)} %kept_blocks.1.kept_ref, f32[6,128,128]{2,1,0:T(8,128)S(1)} %collective-permute-done.15.half_ref, f32[3,128,128]{2,1,0:T(8,128)S(1)} %collective-permute-done.16.early_ref, ...), custom_call_target="tpu_custom_call" | custom-call | tf_op jit(solution)/shard_map/combine/pallas_call | solution.py:475
  (28 shorter events, 3.9 us)
Async XLA Ops:
  0.0 6.9 %copy-start = (f32[1,1,1,8,4,128,128]{6,5,4,3,2,1,0:T(8,128)S(1)}, f32[1,1,1,8,4,128,128]{6,5,4,3,2,1,0:T(8,128)}, u32[]{:S(2)}) copy-start(f32[1,1,1,8,4,128,128]{6,5,4,3,2,1,0:T(8,128)} %param.7) | copy-start | bytes 6291460
  0.1 10.5 %copy-start.1 = (f32[1,1,1,3,8,2,128,128]{7,6,5,4,3,2,1,0:T(8,128)S(1)}, f32[1,1,1,3,8,2,128,128]{7,6,5,4,3,2,1,0:T(8,128)}, u32[]{:S(2)}) copy-start(f32[1,1,1,3,8,2,128,128]{7,6,5,4,3,2,1,0:T(8,128)} %param.5) | copy-start | bytes 9437188
  1.7 7.5 %copy-start.2 = (s32[1,1,1,8,4]{3,4,2,1,0:T(4,128)S(1)}, s32[1,1,1,8,4]{3,4,2,1,0:T(4,128)}, u32[]{:S(2)}) copy-start(s32[1,1,1,8,4]{3,4,2,1,0:T(4,128)} %param.8) | copy-start | bytes 388
  1.7 7.4 %copy-start.3 = (s32[1,1,1,3,8,2]{4,5,3,2,1,0:T(2,128)S(1)}, s32[1,1,1,3,8,2]{4,5,3,2,1,0:T(2,128)}, u32[]{:S(2)}) copy-start(s32[1,1,1,3,8,2]{4,5,3,2,1,0:T(2,128)} %param.6) | copy-start | bytes 580
  1.7 7.4 %copy-start.4 = (s32[1,1,24]{2,1,0:T(1,128)S(1)}, s32[1,1,24]{2,1,0:T(1,128)}, u32[]{:S(2)}) copy-start(s32[1,1,24]{2,1,0:T(1,128)} %param.9) | copy-start | bytes 292
  1.7 42.0 %collective-permute-start.5 = (f32[3,8,2,128,128]{4,3,2,1,0:T(8,128)}, f32[3,8,2,128,128]{4,3,2,1,0:T(8,128)S(1)}, u32[]{:S(2)}, u32[]{:S(2)}) collective-permute-start(f32[3,8,2,128,128]{4,3,2,1,0:T(8,128)} %bitcast.25), channel_id=1, source_target_pairs={{0,2},{2,0},{1,3},{3,1},{4,6},{6,4},{5,7},{7,5},{8,10},{10,8},{9,1... | collective-permute-start | bytes 9437192 | tf_op jit(solution)/shard_map/ppermute | solution.py:531
  2.2 17.1 %collective-permute-start.1 = (f32[520,256]{1,0:T(8,128)S(1)}, f32[520,256]{1,0:T(8,128)S(1)}, u32[]{:S(2)}, u32[]{:S(2)}) collective-permute-start(f32[520,256]{1,0:T(8,128)S(1)} %first_quarter.1), channel_id=1, source_target_pairs={{0,24},{4,28},{8,0},{12,4},{16,8},{20,12},{24,16},{28,20},{1,25},{... | collective-permute-start | bytes 1597448 | tf_op jit(solution)/shard_map/ppermute | solution.py:503
  7.6 20.5 %collective-permute-start.3 = (f32[768,256]{1,0:T(8,128)S(1)}, f32[768,256]{1,0:T(8,128)S(1)}, u32[]{:S(2)}, u32[]{:S(2)}) collective-permute-start(f32[768,256]{1,0:T(8,128)S(1)} %own_quarters.3), channel_id=1, source_target_pairs={{0,4},{4,0},{8,12},{12,8},{16,20},{20,16},{24,28},{28,24},{1,5},{5... | collective-permute-start | bytes 2359304 | tf_op jit(solution)/shard_map/ppermute | solution.py:506
  13.5 17.0 %collective-permute-start.6 = (f32[512,256]{1,0:T(8,128)S(1)}, f32[512,256]{1,0:T(8,128)S(1)}, u32[]{:S(2)}, u32[]{:S(2)}) collective-permute-start(f32[512,256]{1,0:T(8,128)S(1)} %own_quarters.5), channel_id=1, source_target_pairs={{0,24},{4,28},{8,0},{12,4},{16,8},{20,12},{24,16},{28,20},{1,25},{... | collective-permute-start | bytes 1572872 | tf_op jit(solution)/shard_map/ppermute | solution.py:503
  19.9 19.5 %collective-permute-start.2 = (f32[520,256]{1,0:T(8,128)S(1)}, f32[520,256]{1,0:T(8,128)S(1)}, u32[]{:S(2)}, u32[]{:S(2)}) collective-permute-start(f32[520,256]{1,0:T(8,128)S(1)} %pick.9), channel_id=1, source_target_pairs={{0,4},{4,0},{8,12},{12,8},{16,20},{20,16},{24,28},{28,24},{1,5},{5... | collective-permute-start | bytes 1597448 | tf_op jit(solution)/shard_map/ppermute | solution.py:506
  28.5 17.4 %collective-permute-start.4 = (f32[512,256]{1,0:T(8,128)S(1)}, f32[512,256]{1,0:T(8,128)S(1)}, u32[]{:S(2)}, u32[]{:S(2)}) collective-permute-start(f32[512,256]{1,0:T(8,128)S(1)} %own_quarters.4), channel_id=1, source_target_pairs={{0,24},{4,28},{8,0},{12,4},{16,8},{20,12},{24,16},{28,20},{1,25},{... | collective-permute-start | bytes 1572872 | tf_op jit(solution)/shard_map/ppermute | solution.py:503
  32.6 17.8 %collective-permute-start.9 = (f32[512,256]{1,0:T(8,128)S(1)}, f32[512,256]{1,0:T(8,128)S(1)}, u32[]{:S(2)}, u32[]{:S(2)}) collective-permute-start(f32[512,256]{1,0:T(8,128)S(1)} %pick.12), channel_id=1, source_target_pairs={{0,4},{4,0},{8,12},{12,8},{16,20},{20,16},{24,28},{28,24},{1,5},{5... | collective-permute-start | bytes 1572872 | tf_op jit(solution)/shard_map/ppermute | solution.py:506
  40.5 13.1 %collective-permute-start.8 = (f32[520,256]{1,0:T(8,128)S(1)}, f32[520,256]{1,0:T(8,128)S(1)}, u32[]{:S(2)}, u32[]{:S(2)}) collective-permute-start(f32[520,256]{1,0:T(8,128)S(1)} %pick.11), channel_id=1, source_target_pairs={{0,24},{4,28},{8,0},{12,4},{16,8},{20,12},{24,16},{28,20},{1,25},{... | collective-permute-start | bytes 1597448 | tf_op jit(solution)/shard_map/ppermute | solution.py:503
  40.5 1.2 %collective-permute-start = (s32[3,2,8]{2,1,0:T(2,128)S(1)}, s32[3,2,8]{2,1,0:T(2,128)S(1)}, u32[]{:S(2)}, u32[]{:S(2)}) collective-permute-start(s32[3,2,8]{2,1,0:T(2,128)S(1)} %bitcast.39), channel_id=1, source_target_pairs={{0,2},{2,0},{1,3},{3,1},{4,6},{6,4},{5,7},{7,5},{8,10},{10,8},{9,1... | collective-permute-start | bytes 584 | tf_op jit(solution)/shard_map/ppermute | solution.py:531
  46.5 15.2 %collective-permute-start.7 = (f32[520,256]{1,0:T(8,128)S(1)}, f32[520,256]{1,0:T(8,128)S(1)}, u32[]{:S(2)}, u32[]{:S(2)}) collective-permute-start(f32[520,256]{1,0:T(8,128)S(1)} %pick.10), channel_id=1, source_target_pairs={{0,4},{4,0},{8,12},{12,8},{16,20},{20,16},{24,28},{28,24},{1,5},{5... | collective-permute-start | bytes 1597448 | tf_op jit(solution)/shard_map/ppermute | solution.py:506
  51.0 15.9 %collective-permute-start.11 = (f32[512,256]{1,0:T(8,128)S(1)}, f32[512,256]{1,0:T(8,128)S(1)}, u32[]{:S(2)}, u32[]{:S(2)}) collective-permute-start(f32[512,256]{1,0:T(8,128)S(1)} %pick.14), channel_id=1, source_target_pairs={{0,24},{4,28},{8,0},{12,4},{16,8},{20,12},{24,16},{28,20},{1,25},{... | collective-permute-start | bytes 1572872 | tf_op jit(solution)/shard_map/ppermute | solution.py:503
  54.2 18.8 %collective-permute-start.10 = (f32[512,256]{1,0:T(8,128)S(1)}, f32[512,256]{1,0:T(8,128)S(1)}, u32[]{:S(2)}, u32[]{:S(2)}) collective-permute-start(f32[512,256]{1,0:T(8,128)S(1)} %pick.13), channel_id=1, source_target_pairs={{0,4},{4,0},{8,12},{12,8},{16,20},{20,16},{24,28},{28,24},{1,5},{5... | collective-permute-start | bytes 1572872 | tf_op jit(solution)/shard_map/ppermute | solution.py:506
  62.4 15.0 %collective-permute-start.14 = (f32[512,256]{1,0:T(8,128)S(1)}, f32[512,256]{1,0:T(8,128)S(1)}, u32[]{:S(2)}, u32[]{:S(2)}) collective-permute-start(f32[512,256]{1,0:T(8,128)S(1)} %pick.17), channel_id=1, source_target_pairs={{0,24},{4,28},{8,0},{12,4},{16,8},{20,12},{24,16},{28,20},{1,25},{... | collective-permute-start | bytes 1572872 | tf_op jit(solution)/shard_map/ppermute | solution.py:503
  67.4 16.3 %collective-permute-start.13 = (f32[512,256]{1,0:T(8,128)S(1)}, f32[512,256]{1,0:T(8,128)S(1)}, u32[]{:S(2)}, u32[]{:S(2)}) collective-permute-start(f32[512,256]{1,0:T(8,128)S(1)} %pick.16), channel_id=1, source_target_pairs={{0,4},{4,0},{8,12},{12,8},{16,20},{20,16},{24,28},{28,24},{1,5},{5... | collective-permute-start | bytes 1572872 | tf_op jit(solution)/shard_map/ppermute | solution.py:506
  73.6 13.2 %collective-permute-start.12 = (f32[512,256]{1,0:T(8,128)S(1)}, f32[512,256]{1,0:T(8,128)S(1)}, u32[]{:S(2)}, u32[]{:S(2)}) collective-permute-start(f32[512,256]{1,0:T(8,128)S(1)} %pick.15), channel_id=1, source_target_pairs={{0,24},{4,28},{8,0},{12,4},{16,8},{20,12},{24,16},{28,20},{1,25},{... | collective-permute-start | bytes 1572872 | tf_op jit(solution)/shard_map/ppermute | solution.py:503
  75.9 15.3 %collective-permute-start.15 = (f32[6,128,128]{2,1,0:T(8,128)S(1)}, f32[6,128,128]{2,1,0:T(8,128)S(1)}, u32[]{:S(2)}, u32[]{:S(2)}) collective-permute-start(f32[6,128,128]{2,1,0:T(8,128)S(1)} %get-tuple-element.70), channel_id=1, source_target_pairs={{0,1},{1,0},{2,3},{3,2},{4,5},{5,4},{6,7},{7,6},{8,9},{9,8},{10,11... | collective-permute-start | bytes 1179656 | tf_op jit(solution)/shard_map/ppermute | solution.py:580
  79.4 11.8 %collective-permute-start.16 = (f32[3,128,128]{2,1,0:T(8,128)S(1)}, f32[3,128,128]{2,1,0:T(8,128)S(1)}, u32[]{:S(2)}, u32[]{:S(2)}) collective-permute-start(f32[3,128,128]{2,1,0:T(8,128)S(1)} %get-tuple-element.71), channel_id=1, source_target_pairs={{0,1},{1,0},{2,3},{3,2},{4,5},{5,4},{6,7},{7,6},{8,9},{9,8},{10,11... | collective-permute-start | bytes 589832 | tf_op jit(solution)/shard_map/ppermute | solution.py:580
  88.3 6.1 %collective-permute-start.17 = (f32[3,128,128]{2,1,0:T(8,128)S(1)}, f32[3,128,128]{2,1,0:T(8,128)S(1)}, u32[]{:S(2)}, u32[]{:S(2)}) collective-permute-start(f32[3,128,128]{2,1,0:T(8,128)S(1)} %get-tuple-element.72), channel_id=1, source_target_pairs={{0,1},{1,0},{2,3},{3,2},{4,5},{5,4},{6,7},{7,6},{8,9},{9,8},{10,11... | collective-permute-start | bytes 589832 | tf_op jit(solution)/shard_map/ppermute | solution.py:580
